TPU v7x, 32 devices: a whole 2x2x4 slice. The times are simulated.
32 devices in a mesh: groups: 2 (over x), patch: 16 (over z, y, core).
Axes of the slice: x: 2, y: 2, z: 4, core: 2. Of those that a mesh axis runs over, the one named last changes fastest.
Arguments:
- query: bfloat16 [768, 1536], P(('groups', 'patch')), parts along dimension 0, may hold values from -140 to 140
- key_new: bfloat16 [768, 1536], P(('groups', 'patch')), parts along dimension 0, may hold values from -5 to 5
- value_new: bfloat16 [768, 1536], P(('groups', 'patch')), parts along dimension 0, may hold values from -5 to 5
- key_stale: bfloat16 [768, 1536], P('groups'), parts along dimension 0, may hold values from -4.2 to 4.2
- value_stale: bfloat16 [768, 1536], P('groups'), parts along dimension 0, may hold values from -4 to 4
- exponents: int32 [768, 24], P('groups'), parts along dimension 0, may hold values from -2 to 1
- w_out: bfloat16 [1536, 3072], P('patch'), may hold values from -0.15625 to 0.15625
- gate: float32 [6144], P('groups'), parts along dimension 0, may hold values from 0.5 to 4
Outputs:
- branch: bfloat16 [768, 3072], P(('groups', 'patch')), parts along dimension 0
There are 2 independent parts, one for each index of `groups`. A program takes and returns all parts, laid end to end along the dimension named above; an argument that names none is the same for every part. Nothing has to cross between parts.
All inputs are finite; a program needn't handle non-finite values.
Results may differ from a plain program's by a relative error of at most 0.012.
Values may be sent and summed in bfloat16 or wider, within the bound.
No kernel may reach another device: no remote copies, remote signals or barrier semaphores. Data moves between devices by JAX's collectives and lax.ppermute only.
A program may use at most 128 MiB of HBM per device.

v0:
```python
import jax
import jax.numpy as jnp
from jax import lax
from jax.sharding import PartitionSpec as P

CLIP_LIMIT = 2.0


def encode(fresh, stale, powers):
    count = fresh.shape[0]
    heads = powers.shape[1]
    resid = fresh.astype(jnp.float32).reshape(count, heads, -1) - stale.astype(jnp.float32).reshape(
        count, heads, -1
    )
    codes = jnp.clip(resid * jnp.exp2(-powers)[:, :, None], -CLIP_LIMIT, CLIP_LIMIT)
    return codes.reshape(count, -1).astype(jnp.bfloat16)


def decode(codes, stale, powers):
    count = codes.shape[0]
    heads = powers.shape[1]
    shaped = stale.astype(jnp.float32).reshape(count, heads, -1) + jnp.exp2(powers)[
        :, :, None
    ] * codes.astype(jnp.float32).reshape(count, heads, -1)
    return shaped.reshape(count, -1).astype(jnp.bfloat16)


def per_device(query, key_new, value_new, key_stale, value_stale, exponents, w_out, gate):
    rows = query.shape[0]
    width = query.shape[1]
    heads = exponents.shape[1] // 2
    head_dim = width // heads
    first = lax.axis_index("patch") * rows
    powers = exponents.astype(jnp.float32)
    own_powers = lax.dynamic_slice_in_dim(powers, first, rows, 0)
    own_kstale = lax.dynamic_slice_in_dim(key_stale, first, rows, 0)
    own_vstale = lax.dynamic_slice_in_dim(value_stale, first, rows, 0)
    key_codes = encode(key_new, own_kstale, own_powers[:, :heads])
    value_codes = encode(value_new, own_vstale, own_powers[:, heads:])

    def open_values(piece):
        power_rows = powers[:, heads:]
        return decode(piece, value_stale, power_rows)

    inverse = 1.0 / head_dim**0.5
    query3 = query.reshape(rows, heads, head_dim)
    stacked = jnp.concatenate([key_codes, value_codes], axis=1)
    piece = lax.all_gather(stacked, "patch", axis=0, tiled=True)
    open_piece = piece[:, :width]
    power_rows = powers[:, :heads]
    both = jnp.concatenate(
        [decode(open_piece, key_stale, power_rows), open_values(piece[:, width:])], axis=1
    )
    keys = both[:, :width]
    keys3 = keys.reshape(keys.shape[0], heads, head_dim)
    scores = jnp.einsum("qhd,khd->hqk", query3, keys3, preferred_element_type=jnp.float32) * inverse
    peak = jnp.max(scores, axis=2, keepdims=True)
    expo = jnp.exp(scores - peak)
    weights = expo.astype(jnp.bfloat16)
    total = jnp.sum(expo, axis=2)
    values = both[:, width:]
    values3 = values.reshape(values.shape[0], heads, head_dim)
    numer = jnp.einsum("hqk,khd->qhd", weights, values3, preferred_element_type=jnp.float32)
    attended = (numer / jnp.transpose(total)[:, :, None]).astype(jnp.bfloat16).reshape(rows, width)
    projected = jnp.dot(
        attended,
        lax.all_gather(w_out, "patch", axis=0, tiled=True),
        preferred_element_type=jnp.float32,
    )
    return (projected * gate[None, :]).astype(jnp.bfloat16)


def solution(mesh):
    return jax.shard_map(
        per_device,
        mesh=mesh,
        in_specs=(
            P(("groups", "patch"), None),
            P(("groups", "patch"), None),
            P(("groups", "patch"), None),
            P("groups", None),
            P("groups", None),
            P("groups", None),
            P("patch", None),
            P("groups"),
        ),
        out_specs=P(("groups", "patch"), None),
        check_vma=False,
    )
```

profile of v0, /device:TPU:0, one launch (start us, length us, event | category | flops | bytes accessed | tf_op | source)
XLA Modules:
  0.0 149.8 jit_solution(14557653581684727218)
XLA Ops:
  6.5 0.0 copy-start
  6.5 0.0 all-gather.3.cloned.1.call-start
  6.5 0.8 convert_element_type.49
  7.3 0.1 fusion.26
  7.4 0.0 copy-start.2
  7.4 0.1 copy.31
  7.5 0.1 copy.32
  7.6 0.1 mul.67
  7.7 0.1 mul.70
  7.8 1.1 fusion.14
  9.0 0.7 pad_maximum_fusion
  9.6 0.0 all-gather.3.cloned.1.call-update
  9.6 0.0 all-gather.5.cloned.1.call-start
  9.7 0.7 all-gather.5.cloned.1.call-update
  10.4 0.0 copy-done.2
  10.4 0.7 copy.34
  11.2 1.7 %copy.30 = bf16[384,1536]{0,1:T(8,128)(2,1)S(1)} copy(bf16[384,1536]{1,0:T(8,128)(2,1)} %param.12) | data formatting | bytes 2359296 | tf_op args[4]
  12.9 41.8 %all-gather.3.cloned.1.call-done = bf16[384,3072]{1,0:T(8,128)(2,1)} async-done(((bf16[24,3072]{1,0:T(8,128)(2,1)}), bf16[384,3072]{1,0:T(8,128)(2,1)}) %all-gather.3.cloned.1.call-update) | async-done | bytes 2359312 | tf_op jit(solution)/shard_map/all_gather | solution.py:48
  54.7 3.2 %fusion.27 = (bf16[384,1536]{1,0:T(8,128)(2,1)}, bf16[384,1536]{1,0:T(8,128)(2,1)}) fusion(bf16[384,3072]{1,0:T(8,128)(2,1)} %all-gather.3.cloned.1.call-done), kind=kLoop, calls=%fused_computation.39 | loop fusion | bytes 4718592 | tf_op jit(solution)/shard_map/slice | solution.py:49
  58.0 2.4 %copy.43 = bf16[384,1536]{0,1:T(8,128)(2,1)} copy(bf16[384,1536]{1,0:T(8,128)(2,1)} %get-tuple-element.5) | data formatting | bytes 2359296
  60.4 2.4 %copy.42 = bf16[384,1536]{0,1:T(8,128)(2,1)} copy(bf16[384,1536]{1,0:T(8,128)(2,1)} %get-tuple-element.6) | data formatting | bytes 2359296
  62.7 0.0 copy-start.1
  62.7 1.9 %fusion.2 = bf16[384,1536]{0,1:T(8,128)(2,1)S(1)} fusion(bf16[384,1536]{0,1:T(8,128)(2,1)} %copy.43, bf16[384,1536]{0,1:T(8,128)(2,1)S(1)} %copy.34, f32[384,12]{0,1:T(8,128)S(1)} %get-tuple-element.7), kind=kLoop, calls=%fused_computation.4 | loop fusion | flops 2949120 | bytes 3557376 | tf_op jit(solution)/shard_map/convert_element_type | solution.py:25
  64.6 0.0 copy-done.1
  64.6 0.4 fusion.4
  65.0 0.0 copy-done
  65.0 0.4 fusion.28
  65.4 0.0 copy-start.3
  65.4 0.2 fusion.9
  65.6 0.6 fusion.8
  66.2 71.1 %all-gather.5.cloned.1.call-done = bf16[1536,3072]{1,0:T(8,128)(2,1)} async-done(((bf16[96,3072]{1,0:T(8,128)(2,1)}), bf16[1536,3072]{1,0:T(8,128)(2,1)}) %all-gather.5.cloned.1.call-update) | async-done | bytes 9437200 | tf_op jit(solution)/shard_map/all_gather | solution.py:67
  137.3 0.0 copy-done.3
  137.3 5.7 %fusion = bf16[24,3072]{1,0:T(8,128)(2,1)} fusion(bf16[1536,3072]{1,0:T(8,128)(2,1)} %all-gather.5.cloned.1.call-done, f32[3072]{0:T(1024)S(1)} %copy-done.3, bf16[12,3,8,128]{3,2,1,0:T(8,128)(2,1)S(1)} %fusion.8), kind=kOutput, calls=%fused_computation.1 | convolution fusion | flops 226639872 | bytes 9670656 | tf_op jit(solution)/shard_map/dot_general | solution.py:65
  (1 shorter events, 0.0 us)
Async XLA Ops:
  6.5 58.5 %copy-start = (bf16[24,1536]{1,0:T(8,128)(2,1)S(1)}, bf16[24,1536]{1,0:T(8,128)(2,1)}, u32[]{:S(2)}) copy-start(bf16[24,1536]{1,0:T(8,128)(2,1)} %param.8) | copy-start | bytes 221188
  6.5 48.2 %all-gather.3.cloned.1.call-start = ((), (), s32[]{:S(2)}) async-start(), calls=%async_computation | async-start | bytes 2506752 | tf_op jit(solution)/shard_map/all_gather | solution.py:48
  7.4 3.0 %copy-start.2 = (bf16[384,1536]{1,0:T(8,128)(2,1)S(1)}, bf16[384,1536]{1,0:T(8,128)(2,1)}, u32[]{:S(2)}) copy-start(bf16[384,1536]{1,0:T(8,128)(2,1)} %param.11) | copy-start | bytes 3538948
  9.6 127.6 %all-gather.5.cloned.1.call-start = ((), (), s32[]{:S(2)}) async-start(), calls=%async_computation.1 | async-start | bytes 10027008 | tf_op jit(solution)/shard_map/all_gather | solution.py:67
  62.7 1.9 %copy-start.1 = (bf16[384,1536]{0,1:T(8,128)(2,1)S(1)}, bf16[384,1536]{0,1:T(8,128)(2,1)}, u32[]{:S(2)}) copy-start(bf16[384,1536]{0,1:T(8,128)(2,1)} %copy.42) | copy-start | bytes 3538948
  65.4 71.9 %copy-start.3 = (f32[3072]{0:T(1024)S(1)}, f32[3072]{0:T(1024)}, u32[]{:S(2)}) copy-start(f32[3072]{0:T(1024)} %param.15) | copy-start | bytes 36868
Sparse Core Ops, SparseCore 0:
  9.8 44.9 all-gather.2
  57.0 80.2 all-gather.4
where the time goes:
time: 150 us
  waiting for transfers between devices  114 us (76%)
  between operations  13.5 us (9%)
  local copies, waits for them, and re-layouts  10.8 us (7%)
  matrix products  6.65 us (4%)
  other arithmetic  5.16 us (3%)
    all_gather x1, waiting for transfers between devices, per_device(): lax.all_gather(w_out, 'patch', axis=0, tiled=True)  71.1 us
    all_gather x1, waiting for transfers between devices, per_device(): piece = lax.all_gather(stacked, 'patch', axis=0, tiled=True)  41.8 us
    unnamed x12, local copies, waits for them, and re-layouts  7.22 us
    dot_general x1, matrix products, per_device(): jnp.dot(attended, lax.all_gather(w_out, 'patch', axis=0, tiled=True), pre...  5.69 us
    slice x1, local copies, waits for them, and re-layouts, per_device(): open_piece = piece[:, :width]  3.25 us
  transfers between devices with their start and end apart: 2, of which 2 were waited for; matrix products, arithmetic and copies ran while one was open for 9% of the time, Pallas kernels for 0%

commit v1 on v0

v1 whole, which is shorter than its diff:
```python
import functools
import math

import jax
import jax.numpy as jnp
from jax import lax
from jax.experimental import pallas as pl
from jax.experimental.pallas import tpu as pltpu
from jax.sharding import PartitionSpec as P

CLIP_LIMIT = 2.0
VMEM = pl.BlockSpec(memory_space=pltpu.VMEM)
ANY = pl.BlockSpec(memory_space=pl.ANY)


def prepare_kernel(
    groups,
    members,
    query_ref,
    key_ref,
    value_ref,
    kstale_ref,
    vstale_ref,
    expo_ref,
    *rest,
):
    outs = rest[:groups]
    kst, vst, est, packed, sems = rest[groups:]
    rows, width = query_ref.shape
    me = lax.axis_index("patch")
    first = pl.multiple_of((me // 2) * (2 * rows), 2 * rows)
    copies = [
        pltpu.make_async_copy(src.at[pl.ds(first, 2 * rows)], dst, sems.at[i])
        for i, (src, dst) in enumerate(((kstale_ref, kst), (vstale_ref, vst), (expo_ref, est)))
    ]
    for c in copies:
        c.start()
    for c in copies:
        c.wait()
    heads = expo_ref.shape[1] // 2
    dim = width // heads
    odd = me % 2 == 1

    def own(ref, cols):
        both = ref[:, cols].astype(jnp.float32)
        return jnp.where(odd, both[rows:], both[:rows])

    powers = jnp.where(odd, est[rows:, :], est[:rows, :]).astype(jnp.float32)
    scale = jnp.exp2(powers)
    inverse = jnp.exp2(-powers)
    for part, (fresh, stale) in enumerate(((key_ref, kst), (value_ref, vst))):
        for h in range(heads):
            cols = slice(h * dim, (h + 1) * dim)
            col = part * heads + h
            base = own(stale, cols)
            resid = fresh[:, cols].astype(jnp.float32) - base
            codes = jnp.clip(resid * inverse[:, col : col + 1], -CLIP_LIMIT, CLIP_LIMIT)
            codes = codes.astype(jnp.bfloat16).astype(jnp.float32)
            packed[part, :, cols] = (base + scale[:, col : col + 1] * codes).astype(jnp.bfloat16)
    share = width // groups
    for k in range(groups):
        target = (me // members) ^ k
        cols = pl.ds(pl.multiple_of(target * share, share), share)
        outs[k][:, :share] = query_ref[:, cols]
        outs[k][:, share : 2 * share] = packed[0, :, cols]
        outs[k][:, 2 * share :] = packed[1, :, cols]


def prepare(groups, members, query, key_new, value_new, key_stale, value_stale, exponents):
    rows, width = query.shape
    share = width // groups
    return pl.pallas_call(
        functools.partial(prepare_kernel, groups, members),
        out_shape=[jax.ShapeDtypeStruct((rows, 3 * share), jnp.bfloat16)] * groups,
        in_specs=[VMEM] * 3 + [pl.BlockSpec(memory_space=pltpu.HBM)] * 3,
        out_specs=[VMEM] * groups,
        scratch_shapes=[
            pltpu.VMEM((2 * rows, width), jnp.bfloat16),
            pltpu.VMEM((2 * rows, width), jnp.bfloat16),
            pltpu.VMEM((2 * rows, exponents.shape[1]), jnp.int32),
            pltpu.VMEM((2, rows, width), jnp.bfloat16),
            pltpu.SemaphoreType.DMA((3,)),
        ],
        cost_estimate=pl.CostEstimate(flops=10 * rows * width, bytes_accessed=14 * rows * width, transcendentals=0),
    )(query, key_new, value_new, key_stale, value_stale, exponents)


def attend_kernel(groups, members, dim, *refs):
    packs = refs[:groups]
    kvs = refs[groups : groups + members]
    att, kv = refs[groups + members :]
    share = att.shape[1]
    block = kvs[0].shape[0]
    for j in range(members):
        kv[j * block : (j + 1) * block] = kvs[j][...]
    queries = jnp.concatenate([p[:, :share].astype(jnp.float32) for p in packs], axis=0).astype(jnp.bfloat16)
    inverse = 1.0 / dim**0.5
    for h in range(share // dim):
        cols = slice(h * dim, (h + 1) * dim)
        scores = (
            lax.dot_general(queries[:, cols], kv[:, cols], (((1,), (1,)), ((), ())), preferred_element_type=jnp.float32)
            * inverse
        )
        peak = jnp.max(scores, axis=1, keepdims=True)
        expo = jnp.exp(scores - peak)
        total = jnp.sum(expo, axis=1, keepdims=True)
        numer = jnp.dot(
            expo.astype(jnp.bfloat16),
            kv[:, share + h * dim : share + (h + 1) * dim],
            preferred_element_type=jnp.float32,
        )
        att[:, cols] = (numer / total).astype(jnp.bfloat16)


def attend(groups, members, dim, packs, kvs):
    rows = packs[0].shape[0]
    share = packs[0].shape[1] // 3
    block = kvs[0].shape[0]
    return pl.pallas_call(
        functools.partial(attend_kernel, groups, members, dim),
        out_shape=jax.ShapeDtypeStruct((groups * rows, share), jnp.bfloat16),
        in_specs=[VMEM] * (groups + members),
        out_specs=VMEM,
        scratch_shapes=[pltpu.VMEM((members * block, 2 * share), jnp.bfloat16)],
        compiler_params=pltpu.CompilerParams(vmem_limit_bytes=24 * 1024 * 1024),
        cost_estimate=pl.CostEstimate(
            flops=4 * groups * rows * members * block * share,
            bytes_accessed=4 * members * block * share,
            transcendentals=groups * rows * members * block * share // dim,
        ),
    )(*packs, *kvs)


def project_kernel(groups, members, pieces, att, *refs):
    ws = refs[:pieces]
    outs = refs[pieces : pieces + groups]
    wide, sems = refs[pieces + groups :]
    depth = ws[0].shape[0]
    q = lax.axis_index("patch") % members
    copies = []
    for j in range(pieces):
        at = pl.multiple_of((q ^ j) * depth, depth) if pieces > 1 else 0
        copies.append(pltpu.make_async_copy(ws[j], wide.at[pl.ds(at, depth)], sems.at[j]))
    for c in copies:
        c.start()
    for c in copies:
        c.wait()
    rows, width = outs[0].shape
    tile = 512 if width % 512 == 0 else width
    for t in range(width // tile):
        cols = slice(t * tile, (t + 1) * tile)
        part = jnp.dot(att[...], wide[:, cols], preferred_element_type=jnp.float32)
        for k in range(groups):
            outs[k][:, cols] = part[k * rows : (k + 1) * rows].astype(outs[k].dtype)


def project(groups, members, att, ws):
    rows = att.shape[0] // groups
    share = att.shape[1]
    model = ws[0].shape[1]
    return pl.pallas_call(
        functools.partial(project_kernel, groups, members, len(ws)),
        out_shape=[jax.ShapeDtypeStruct((rows, model), jnp.float32)]
        + [jax.ShapeDtypeStruct((rows, model), jnp.bfloat16)] * (groups - 1),
        in_specs=[VMEM] + [ANY] * len(ws),
        out_specs=[VMEM] * groups,
        scratch_shapes=[pltpu.VMEM((share, model), jnp.bfloat16), pltpu.SemaphoreType.DMA((len(ws),))],
        compiler_params=pltpu.CompilerParams(vmem_limit_bytes=24 * 1024 * 1024),
        cost_estimate=pl.CostEstimate(
            flops=2 * groups * rows * share * model, bytes_accessed=2 * share * model, transcendentals=0
        ),
    )(att, *ws)


def per_device(patch, query, key_new, value_new, key_stale, value_stale, exponents, w_out, gate):
    heads = exponents.shape[1] // 2
    dim = query.shape[1] // heads
    groups = math.gcd(patch, heads)
    members = patch // groups
    share = query.shape[1] // groups

    def across(x, k):
        return lax.ppermute(x, "patch", [(p, ((p // members) ^ k) * members + p % members) for p in range(patch)])

    def within(x, j):
        return lax.ppermute(x, "patch", [(p, p ^ j) for p in range(patch)])

    def spread(x, after=None):
        pieces = {0: x}
        bit = members // 2
        while bit:
            for j in list(pieces):
                piece = pieces[j]
                if j and after is not None:
                    piece, _ = lax.optimization_barrier((piece, after))
                pieces[j ^ bit] = within(piece, bit)
            bit //= 2
        return [pieces[j] for j in range(members)]

    packs = prepare(groups, members, query, key_new, value_new, key_stale, value_stale, exponents)
    packs = [packs[0]] + [across(packs[k], k) for k in range(1, groups)]
    kvs = spread(jnp.concatenate([p[:, share:] for p in packs], axis=0))
    att = attend(groups, members, dim, packs, kvs)
    ws = spread(w_out, after=kvs)
    if w_out.shape[0] % 16:
        order = (lax.axis_index("patch") % members) ^ jnp.arange(members)
        ws = [jnp.stack(ws)[order].reshape(-1, w_out.shape[1])]
    parts = project(groups, members, att, ws)
    total = parts[0]
    for k in range(1, groups):
        total = total + across(parts[k], k).astype(jnp.float32)
    return (total * gate[None, :]).astype(jnp.bfloat16)


def solution(mesh):
    return jax.shard_map(
        functools.partial(per_device, mesh.shape["patch"]),
        mesh=mesh,
        in_specs=(
            P(("groups", "patch"), None),
            P(("groups", "patch"), None),
            P(("groups", "patch"), None),
            P("groups", None),
            P("groups", None),
            P("groups", None),
            P("patch", None),
            P("groups"),
        ),
        out_specs=P(("groups", "patch"), None),
        check_vma=False,
    )
```

time: 150 us -> 42.9 us (0.29)
  waiting for transfers between devices: 114 us -> 20.4 us
  between operations: 13.5 us -> 0.06 us
  starting transfers between devices: 0.04 us -> 13.1 us
  local copies, waits for them, and re-layouts: 10.8 us -> 3.18 us
  matrix products: 6.65 us -> 0 us
  Pallas kernels: 0 us -> 5 us
  other arithmetic: 5.16 us -> 0.76 us
    all_gather x2 -> x0, waiting for transfers between devices: 113 us -> none  [the longest x1 71.1 us: per_device(): lax.all_gather(w_out, 'patch', axis=0, tiled=True)]
    ppermute x0 -> x12, waiting for transfers between devices: none -> 20.4 us  [the longest x6 14.8 us: across(): lax.ppermute(x, 'patch', [(p, (p // members ^ k) * members + p % members)...]
    ppermute x0 -> x12, starting transfers between devices: none -> 13.1 us  [the longest x6 8.9 us: across(): lax.ppermute(x, 'patch', [(p, (p // members ^ k) * members + p % members)...]
    dot_general x3 -> x0, matrix products: 6.65 us -> none  [the longest x1 5.69 us: per_device(): jnp.dot(attended, lax.all_gather(w_out, 'patch', axis=0, tiled=True), pre...]
    pallas_call x0 -> x3, Pallas kernels: none -> 5 us  [the longest x1 2.98 us: prepare(): pl.pallas_call(functools.partial(prepare_kernel, groups, members), out_sh...]
    unnamed x12 -> x7, local copies, waits for them, and re-layouts: 7.22 us -> 2.4 us
    convert_element_type x4 -> x1, other arithmetic: 4.17 us -> 0.75 us  [per_device(): return (total * gate[None, :]).astype(jnp.bfloat16)]
    slice x1 -> x4, local copies, waits for them, and re-layouts: 3.25 us -> 0.78 us  [per_device(): kvs = spread(jnp.concatenate([p[:, share:] for p in packs], axis=0))]
  transfers between devices with their start and end apart: 2 -> 12, of which waited for: 2 -> 7; matrix products, arithmetic and copies ran while one was open for 9% -> 6% of each run, Pallas kernels for 0% -> 9%
where the time goes in v1:
time: 42.9 us; the launch traced here: 42.5 us
  waiting for transfers between devices  20.4 us (48%)
  starting transfers between devices  13.1 us (31%)
  Pallas kernels  5 us (12%)
  local copies, waits for them, and re-layouts  3.18 us (7%)
  other arithmetic  0.76 us (2%)
    ppermute x6, waiting for transfers between devices, across(): lax.ppermute(x, 'patch', [(p, (p // members ^ k) * members + p % members)...  14.8 us
    ppermute x6, starting transfers between devices, across(): lax.ppermute(x, 'patch', [(p, (p // members ^ k) * members + p % members)...  8.9 us
    ppermute x6, waiting for transfers between devices, within(): return lax.ppermute(x, 'patch', [(p, p ^ j) for p in range(patch)])  5.59 us
    ppermute x6, starting transfers between devices, within(): return lax.ppermute(x, 'patch', [(p, p ^ j) for p in range(patch)])  4.2 us
    pallas_call x1, Pallas kernels, prepare(): pl.pallas_call(functools.partial(prepare_kernel, groups, members), out_sh...  2.98 us
    unnamed x7, local copies, waits for them, and re-layouts  2.4 us
    pallas_call x1, Pallas kernels, project(): pl.pallas_call(functools.partial(project_kernel, groups, members, len(ws)...  1.1 us
    pallas_call x1, Pallas kernels, attend(): pl.pallas_call(functools.partial(attend_kernel, groups, members, dim), ou...  0.92 us
  transfers between devices with their start and end apart: 12, of which 7 were waited for; matrix products, arithmetic and copies ran while one was open for 6% of the time, Pallas kernels for 9%

profile of v1, /device:TPU:0, one launch (start us, length us, event | category | flops | bytes accessed | tf_op | source)
XLA Modules:
  0.0 42.5 jit_solution(5688319965871038698)
XLA Ops:
  0.0 3.0 %collective-permute-start.7 = (bf16[96,3072]{1,0:T(8,128)(2,1)}, bf16[96,3072]{1,0:T(8,128)(2,1)S(1)}, u32[]{:S(2)}, u32[]{:S(2)}) collective-permute-start(bf16[96,3072]{1,0:T(8,128)(2,1)} %refs_0_.1), channel_id=1, source_target_pairs={{0,2},{1,3},{2,0},{3,1},{4,6},{5,7},{6,4},{7,5},{8,10},{9,11},{10,... | collective-permute-start | bytes 1769480 | tf_op jit(solution)/shard_map/ppermute | solution.py:186
  3.0 1.6 %copy.9.expo_ref = s32[384,24]{1,0:T(8,128)} copy(s32[384,24]{0,1:T(8,128)} %param.13) | data formatting | bytes 73728 | tf_op args[5]
  4.5 0.0 copy-start
  4.5 3.0 %shard_map.82 = (bf16[24,1152]{1,0:T(8,128)(2,1)}, bf16[24,1152]{1,0:T(8,128)(2,1)}, bf16[24,1152]{1,0:T(8,128)(2,1)}, bf16[24,1152]{1,0:T(8,128)(2,1)}) custom-call(bf16[24,1536]{1,0:T(8,128)(2,1)} %query_ref.1, bf16[24,1536]{1,0:T(8,128)(2,1)} %key_ref.1, bf16[24,1536]{1,0:T(8,128)(2,1)} %value_ref.1, bf16[384,1536]{1,0:T(8,128)(2,1)} %kstale_ref.1, ...), custom_call_target="tpu_custom_call" | custom-call | flops 368640 | bytes 516096 | tf_op jit(solution)/shard_map/pallas_call | solution.py:72
  7.5 1.6 %collective-permute-start = (bf16[24,1152]{1,0:T(8,128)(2,1)}, bf16[24,1152]{1,0:T(8,128)(2,1)S(1)}, u32[]{:S(2)}, u32[]{:S(2)}) collective-permute-start(bf16[24,1152]{1,0:T(8,128)(2,1)} %get-tuple-element.15), channel_id=1, source_target_pairs={{0,4},{1,5},{2,6},{3,7},{4,0},{5,1},{6,2},{7,3},{8,12},{9,13},{10,... | collective-permute-start | bytes 165896 | tf_op jit(solution)/shard_map/ppermute | solution.py:183
  9.2 2.6 %collective-permute-start.1 = (bf16[24,1152]{1,0:T(8,128)(2,1)}, bf16[24,1152]{1,0:T(8,128)(2,1)S(1)}, u32[]{:S(2)}, u32[]{:S(2)}) collective-permute-start(bf16[24,1152]{1,0:T(8,128)(2,1)} %get-tuple-element.16), channel_id=1, source_target_pairs={{0,8},{1,9},{2,10},{3,11},{4,12},{5,13},{6,14},{7,15},{8,0},{9,1},... | collective-permute-start | bytes 165896 | tf_op jit(solution)/shard_map/ppermute | solution.py:183
  11.8 0.2 collective-permute-start.2
  12.0 0.8 %slice.12 = bf16[24,768]{1,0:T(8,128)(2,1)S(1)} slice(bf16[24,1152]{1,0:T(8,128)(2,1)} %get-tuple-element.14.refs_0_), slice={[0:24], [384:1152]} | slice | bytes 73728 | tf_op jit(solution)/shard_map/slice | solution.py:202
  12.8 0.0 collective-permute-done.refs_1_
  12.8 2.5 %collective-permute-done.1.refs_2_ = bf16[24,1152]{1,0:T(8,128)(2,1)S(1)} collective-permute-done((bf16[24,1152]{1,0:T(8,128)(2,1)}, bf16[24,1152]{1,0:T(8,128)(2,1)S(1)}, u32[]{:S(2)}, u32[]{:S(2)}) %collective-permute-start.1) | collective-permute-done | bytes 55328 | tf_op jit(solution)/shard_map/ppermute | solution.py:183
  15.2 2.7 %collective-permute-done.2.refs_3_ = bf16[24,1152]{1,0:T(8,128)(2,1)S(1)} collective-permute-done((bf16[24,1152]{1,0:T(8,128)(2,1)}, bf16[24,1152]{1,0:T(8,128)(2,1)S(1)}, u32[]{:S(2)}, u32[]{:S(2)}) %collective-permute-start.2) | collective-permute-done | bytes 55328 | tf_op jit(solution)/shard_map/ppermute | solution.py:183
  17.9 0.6 %collective-permute-start.4 = (bf16[96,768]{1,0:T(8,128)(2,1)S(1)}, bf16[96,768]{1,0:T(8,128)(2,1)S(1)}, u32[]{:S(2)}, u32[]{:S(2)}) collective-permute-start(bf16[96,768]{1,0:T(8,128)(2,1)S(1)} %pad_maximum_fusion.refs_4_), channel_id=1, source_target_pairs={{0,2},{1,3},{2,0},{3,1},{4,6},{5,7},{6,4},{7,5},{8,10},{9,11},{10,... | collective-permute-start | bytes 442376 | tf_op jit(solution)/shard_map/ppermute | solution.py:186
  18.5 0.0 collective-permute-start.3
  18.5 4.6 %collective-permute-done.4.refs_6_ = bf16[96,768]{1,0:T(8,128)(2,1)S(1)} collective-permute-done((bf16[96,768]{1,0:T(8,128)(2,1)S(1)}, bf16[96,768]{1,0:T(8,128)(2,1)S(1)}, u32[]{:S(2)}, u32[]{:S(2)}) %collective-permute-start.4) | collective-permute-done | bytes 147488 | tf_op jit(solution)/shard_map/ppermute | solution.py:186
  23.2 0.0 collective-permute-start.5
  23.2 0.0 copy-done
  23.2 0.5 %collective-permute-start.6 = (bf16[96,3072]{1,0:T(8,128)(2,1)S(1)}, bf16[96,3072]{1,0:T(8,128)(2,1)S(1)}, u32[]{:S(2)}, u32[]{:S(2)}) collective-permute-start(bf16[96,3072]{1,0:T(8,128)(2,1)S(1)} %copy-done), channel_id=1, source_target_pairs={{0,1},{1,0},{2,3},{3,2},{4,5},{5,4},{6,7},{7,6},{8,9},{9,8},{10,11... | collective-permute-start | bytes 1769480 | tf_op jit(solution)/shard_map/ppermute | solution.py:186
  23.7 0.0 collective-permute-done.3.refs_5_
  23.7 0.9 %collective-permute-done.5.refs_7_ = bf16[96,768]{1,0:T(8,128)(2,1)S(1)} collective-permute-done((bf16[96,768]{1,0:T(8,128)(2,1)S(1)}, bf16[96,768]{1,0:T(8,128)(2,1)S(1)}, u32[]{:S(2)}, u32[]{:S(2)}) %collective-permute-start.5) | collective-permute-done | bytes 147488 | tf_op jit(solution)/shard_map/ppermute | solution.py:186
  24.5 0.0 collective-permute-done.7.refs_2_
  24.5 0.1 collective-permute-start.8
  24.7 0.0 copy-start.1
  24.7 0.8 %copy-done.1 = bf16[24,1152]{1,0:T(8,128)(2,1)S(1)} copy-done((bf16[24,1152]{1,0:T(8,128)(2,1)S(1)}, bf16[24,1152]{1,0:T(8,128)(2,1)}, u32[]{:S(2)}) %copy-start.1) | copy-done | bytes 55320
  25.5 0.9 %shard_map.83.att = bf16[96,384]{1,0:T(8,128)(2,1)S(1)} custom-call(bf16[24,1152]{1,0:T(8,128)(2,1)S(1)} %copy-done.1, bf16[24,1152]{1,0:T(8,128)(2,1)S(1)} %collective-permute-done.refs_1_, bf16[24,1152]{1,0:T(8,128)(2,1)S(1)} %collective-permute-done.1.refs_2_, bf16[24,1152]{1,0:T(8,128)(2,1)S(1)} %collective-permute-done.2.refs_3_, ...), custom_call_target="tpu_custom_call" | custom-call | flops 56623104 | bytes 589824 | tf_op jit(solution)/shard_map/pallas_call | solution.py:119
  26.4 0.0 copy-start.2
  26.4 0.0 collective-permute-done.6.refs_1_
  26.4 0.1 collective-permute-done.8.refs_3_
  26.5 1.1 %shard_map.84 = (f32[24,3072]{1,0:T(8,128)S(1)}, bf16[24,3072]{1,0:T(8,128)(2,1)S(1)}, bf16[24,3072]{1,0:T(8,128)(2,1)S(1)}, bf16[24,3072]{1,0:T(8,128)(2,1)S(1)}) custom-call(bf16[96,384]{1,0:T(8,128)(2,1)S(1)} %shard_map.83.att, bf16[96,3072]{1,0:T(8,128)(2,1)S(1)} %copy-done, bf16[96,3072]{1,0:T(8,128)(2,1)S(1)} %collective-permute-done.6.refs_1_, ...), custom_call_target="tpu_custom_call" | custom-call | flops 226492416 | bytes 2359296 | tf_op jit(solution)/shard_map/pallas_call | solution.py:161
  27.6 0.1 collective-permute-start.9
  27.7 1.4 %collective-permute-start.10 = (bf16[24,3072]{1,0:T(8,128)(2,1)S(1)}, bf16[24,3072]{1,0:T(8,128)(2,1)S(1)}, u32[]{:S(2)}, u32[]{:S(2)}) collective-permute-start(bf16[24,3072]{1,0:T(8,128)(2,1)S(1)} %get-tuple-element.21), channel_id=1, source_target_pairs={{0,8},{1,9},{2,10},{3,11},{4,12},{5,13},{6,14},{7,15},{8,0},{9,1},... | collective-permute-start | bytes 442376 | tf_op jit(solution)/shard_map/ppermute | solution.py:183
  29.1 3.0 %collective-permute-start.11 = (bf16[24,3072]{1,0:T(8,128)(2,1)S(1)}, bf16[24,3072]{1,0:T(8,128)(2,1)S(1)}, u32[]{:S(2)}, u32[]{:S(2)}) collective-permute-start(bf16[24,3072]{1,0:T(8,128)(2,1)S(1)} %get-tuple-element.22), channel_id=1, source_target_pairs={{0,12},{1,13},{2,14},{3,15},{4,8},{5,9},{6,10},{7,11},{8,4},{9,5},... | collective-permute-start | bytes 442376 | tf_op jit(solution)/shard_map/ppermute | solution.py:183
  32.1 3.9 %collective-permute-done.9 = bf16[24,3072]{1,0:T(8,128)(2,1)S(1)} collective-permute-done((bf16[24,3072]{1,0:T(8,128)(2,1)S(1)}, bf16[24,3072]{1,0:T(8,128)(2,1)S(1)}, u32[]{:S(2)}, u32[]{:S(2)}) %collective-permute-start.9) | collective-permute-done | bytes 147488 | tf_op jit(solution)/shard_map/ppermute | solution.py:183
  36.0 5.7 %collective-permute-done.10 = bf16[24,3072]{1,0:T(8,128)(2,1)S(1)} collective-permute-done((bf16[24,3072]{1,0:T(8,128)(2,1)S(1)}, bf16[24,3072]{1,0:T(8,128)(2,1)S(1)}, u32[]{:S(2)}, u32[]{:S(2)}) %collective-permute-start.10) | collective-permute-done | bytes 147488 | tf_op jit(solution)/shard_map/ppermute | solution.py:183
  41.7 0.0 collective-permute-done.11
  41.7 0.0 copy-done.2
  41.7 0.8 %multiply_convert_fusion = bf16[24,3072]{1,0:T(8,128)(2,1)} fusion(bf16[24,3072]{1,0:T(8,128)(2,1)S(1)} %collective-permute-done.11, bf16[24,3072]{1,0:T(8,128)(2,1)S(1)} %collective-permute-done.10, f32[24,3072]{1,0:T(8,128)S(1)} %get-tuple-element.19, bf16[24,3072]{1,0:T(8,128)(2,1)S(1)} %collective-permute-done.9, f32[3072]{0:T(1024)S(1)} %copy-done.2), kind=kLoop, calls=%fused_computation | loop fusion | flops 589824 | bytes 897024 | tf_op jit(solution)/shard_map/convert_element_type | solution.py:212
  (4 shorter events, 0.0 us)
Async XLA Ops:
  0.0 24.5 %collective-permute-start.7 = (bf16[96,3072]{1,0:T(8,128)(2,1)}, bf16[96,3072]{1,0:T(8,128)(2,1)S(1)}, u32[]{:S(2)}, u32[]{:S(2)}) collective-permute-start(bf16[96,3072]{1,0:T(8,128)(2,1)} %refs_0_.1), channel_id=1, source_target_pairs={{0,2},{1,3},{2,0},{3,1},{4,6},{5,7},{6,4},{7,5},{8,10},{9,11},{10,... | collective-permute-start | bytes 1769480 | tf_op jit(solution)/shard_map/ppermute | solution.py:186
  4.5 18.6 %copy-start = (bf16[96,3072]{1,0:T(8,128)(2,1)S(1)}, bf16[96,3072]{1,0:T(8,128)(2,1)}, u32[]{:S(2)}) copy-start(bf16[96,3072]{1,0:T(8,128)(2,1)} %refs_0_.1) | copy-start | bytes 1769476
  7.5 5.2 %collective-permute-start = (bf16[24,1152]{1,0:T(8,128)(2,1)}, bf16[24,1152]{1,0:T(8,128)(2,1)S(1)}, u32[]{:S(2)}, u32[]{:S(2)}) collective-permute-start(bf16[24,1152]{1,0:T(8,128)(2,1)} %get-tuple-element.15), channel_id=1, source_target_pairs={{0,4},{1,5},{2,6},{3,7},{4,0},{5,1},{6,2},{7,3},{8,12},{9,13},{10,... | collective-permute-start | bytes 165896 | tf_op jit(solution)/shard_map/ppermute | solution.py:183
  9.2 6.1 %collective-permute-start.1 = (bf16[24,1152]{1,0:T(8,128)(2,1)}, bf16[24,1152]{1,0:T(8,128)(2,1)S(1)}, u32[]{:S(2)}, u32[]{:S(2)}) collective-permute-start(bf16[24,1152]{1,0:T(8,128)(2,1)} %get-tuple-element.16), channel_id=1, source_target_pairs={{0,8},{1,9},{2,10},{3,11},{4,12},{5,13},{6,14},{7,15},{8,0},{9,1},... | collective-permute-start | bytes 165896 | tf_op jit(solution)/shard_map/ppermute | solution.py:183
  11.8 6.2 %collective-permute-start.2 = (bf16[24,1152]{1,0:T(8,128)(2,1)}, bf16[24,1152]{1,0:T(8,128)(2,1)S(1)}, u32[]{:S(2)}, u32[]{:S(2)}) collective-permute-start(bf16[24,1152]{1,0:T(8,128)(2,1)} %get-tuple-element.17), channel_id=1, source_target_pairs={{0,12},{1,13},{2,14},{3,15},{4,8},{5,9},{6,10},{7,11},{8,4},{9,5},... | collective-permute-start | bytes 165896 | tf_op jit(solution)/shard_map/ppermute | solution.py:183
  17.9 5.2 %collective-permute-start.4 = (bf16[96,768]{1,0:T(8,128)(2,1)S(1)}, bf16[96,768]{1,0:T(8,128)(2,1)S(1)}, u32[]{:S(2)}, u32[]{:S(2)}) collective-permute-start(bf16[96,768]{1,0:T(8,128)(2,1)S(1)} %pad_maximum_fusion.refs_4_), channel_id=1, source_target_pairs={{0,2},{1,3},{2,0},{3,1},{4,6},{5,7},{6,4},{7,5},{8,10},{9,11},{10,... | collective-permute-start | bytes 442376 | tf_op jit(solution)/shard_map/ppermute | solution.py:186
  18.5 5.2 %collective-permute-start.3 = (bf16[96,768]{1,0:T(8,128)(2,1)S(1)}, bf16[96,768]{1,0:T(8,128)(2,1)S(1)}, u32[]{:S(2)}, u32[]{:S(2)}) collective-permute-start(bf16[96,768]{1,0:T(8,128)(2,1)S(1)} %pad_maximum_fusion.refs_4_), channel_id=1, source_target_pairs={{0,1},{1,0},{2,3},{3,2},{4,5},{5,4},{6,7},{7,6},{8,9},{9,8},{10,11... | collective-permute-start | bytes 442376 | tf_op jit(solution)/shard_map/ppermute | solution.py:186
  23.2 1.4 %collective-permute-start.5 = (bf16[96,768]{1,0:T(8,128)(2,1)S(1)}, bf16[96,768]{1,0:T(8,128)(2,1)S(1)}, u32[]{:S(2)}, u32[]{:S(2)}) collective-permute-start(bf16[96,768]{1,0:T(8,128)(2,1)S(1)} %collective-permute-done.4.refs_6_), channel_id=1, source_target_pairs={{0,1},{1,0},{2,3},{3,2},{4,5},{5,4},{6,7},{7,6},{8,9},{9,8},{10,11... | collective-permute-start | bytes 442376 | tf_op jit(solution)/shard_map/ppermute | solution.py:186
  23.2 3.3 %collective-permute-start.6 = (bf16[96,3072]{1,0:T(8,128)(2,1)S(1)}, bf16[96,3072]{1,0:T(8,128)(2,1)S(1)}, u32[]{:S(2)}, u32[]{:S(2)}) collective-permute-start(bf16[96,3072]{1,0:T(8,128)(2,1)S(1)} %copy-done), channel_id=1, source_target_pairs={{0,1},{1,0},{2,3},{3,2},{4,5},{5,4},{6,7},{7,6},{8,9},{9,8},{10,11... | collective-permute-start | bytes 1769480 | tf_op jit(solution)/shard_map/ppermute | solution.py:186
  24.5 2.0 %collective-permute-start.8 = (bf16[96,3072]{1,0:T(8,128)(2,1)S(1)}, bf16[96,3072]{1,0:T(8,128)(2,1)S(1)}, u32[]{:S(2)}, u32[]{:S(2)}) collective-permute-start(bf16[96,3072]{1,0:T(8,128)(2,1)S(1)} %collective-permute-done.7.refs_2_), channel_id=1, source_target_pairs={{0,1},{1,0},{2,3},{3,2},{4,5},{5,4},{6,7},{7,6},{8,9},{9,8},{10,11... | collective-permute-start | bytes 1769480 | tf_op jit(solution)/shard_map/ppermute | solution.py:186
  24.7 0.8 %copy-start.1 = (bf16[24,1152]{1,0:T(8,128)(2,1)S(1)}, bf16[24,1152]{1,0:T(8,128)(2,1)}, u32[]{:S(2)}) copy-start(bf16[24,1152]{1,0:T(8,128)(2,1)} %get-tuple-element.14.refs_0_) | copy-start | bytes 165892
  26.4 15.3 %copy-start.2 = (f32[3072]{0:T(1024)S(1)}, f32[3072]{0:T(1024)}, u32[]{:S(2)}) copy-start(f32[3072]{0:T(1024)} %param.15) | copy-start | bytes 36868
  27.6 8.3 %collective-permute-start.9 = (bf16[24,3072]{1,0:T(8,128)(2,1)S(1)}, bf16[24,3072]{1,0:T(8,128)(2,1)S(1)}, u32[]{:S(2)}, u32[]{:S(2)}) collective-permute-start(bf16[24,3072]{1,0:T(8,128)(2,1)S(1)} %get-tuple-element.20), channel_id=1, source_target_pairs={{0,4},{1,5},{2,6},{3,7},{4,0},{5,1},{6,2},{7,3},{8,12},{9,13},{10,... | collective-permute-start | bytes 442376 | tf_op jit(solution)/shard_map/ppermute | solution.py:183
  27.7 14.0 %collective-permute-start.10 = (bf16[24,3072]{1,0:T(8,128)(2,1)S(1)}, bf16[24,3072]{1,0:T(8,128)(2,1)S(1)}, u32[]{:S(2)}, u32[]{:S(2)}) collective-permute-start(bf16[24,3072]{1,0:T(8,128)(2,1)S(1)} %get-tuple-element.21), channel_id=1, source_target_pairs={{0,8},{1,9},{2,10},{3,11},{4,12},{5,13},{6,14},{7,15},{8,0},{9,1},... | collective-permute-start | bytes 442376 | tf_op jit(solution)/shard_map/ppermute | solution.py:183
  29.1 12.6 %collective-permute-start.11 = (bf16[24,3072]{1,0:T(8,128)(2,1)S(1)}, bf16[24,3072]{1,0:T(8,128)(2,1)S(1)}, u32[]{:S(2)}, u32[]{:S(2)}) collective-permute-start(bf16[24,3072]{1,0:T(8,128)(2,1)S(1)} %get-tuple-element.22), channel_id=1, source_target_pairs={{0,12},{1,13},{2,14},{3,15},{4,8},{5,9},{6,10},{7,11},{8,4},{9,5},... | collective-permute-start | bytes 442376 | tf_op jit(solution)/shard_map/ppermute | solution.py:183

commit v2 on v1

v2 whole, which is shorter than its diff:
```python
import functools
import math

import jax
import jax.numpy as jnp
from jax import lax
from jax.experimental import pallas as pl
from jax.experimental.pallas import tpu as pltpu
from jax.sharding import PartitionSpec as P

CLIP_LIMIT = 2.0
VMEM = pl.BlockSpec(memory_space=pltpu.VMEM)
ANY = pl.BlockSpec(memory_space=pl.ANY)
HBM = pl.BlockSpec(memory_space=pltpu.HBM)


def prepare_kernel(groups, query_ref, key_ref, value_ref, power_ref, kstale_ref, vstale_ref, qout, kvout, kst, vst, sems):
    rows, width = query_ref.shape
    me = lax.axis_index("patch")
    first = pl.multiple_of((me // 2) * (2 * rows), 2 * rows)
    copies = [
        pltpu.make_async_copy(src.at[pl.ds(first, 2 * rows)], dst, sems.at[i])
        for i, (src, dst) in enumerate(((kstale_ref, kst), (vstale_ref, vst)))
    ]
    for c in copies:
        c.start()
    heads = power_ref.shape[1] // 2
    dim = width // heads
    share = width // groups
    odd = me % 2 == 1
    powers = power_ref[...].astype(jnp.float32)
    scale = jnp.exp2(powers)
    inverse = jnp.exp2(-powers)
    for z in range(groups):
        qout[z] = query_ref[:, z * share : (z + 1) * share]
    for part, (fresh, stale) in enumerate(((key_ref, kst), (value_ref, vst))):
        copies[part].wait()
        for h in range(heads):
            cols = slice(h * dim, (h + 1) * dim)
            col = part * heads + h
            both = stale[:, cols].astype(jnp.float32)
            base = jnp.where(odd, both[rows:], both[:rows])
            resid = fresh[:, cols].astype(jnp.float32) - base
            codes = jnp.clip(resid * inverse[:, col : col + 1], -CLIP_LIMIT, CLIP_LIMIT)
            codes = codes.astype(jnp.bfloat16).astype(jnp.float32)
            at = part * share + (h * dim) % share
            kvout[h * dim // share, :, at : at + dim] = (base + scale[:, col : col + 1] * codes).astype(jnp.bfloat16)


def prepare(groups, query, key_new, value_new, powers, key_stale, value_stale):
    rows, width = query.shape
    share = width // groups
    return pl.pallas_call(
        functools.partial(prepare_kernel, groups),
        out_shape=[
            jax.ShapeDtypeStruct((groups, rows, share), jnp.bfloat16),
            jax.ShapeDtypeStruct((groups, rows, 2 * share), jnp.bfloat16),
        ],
        in_specs=[VMEM] * 4 + [HBM] * 2,
        out_specs=[VMEM] * 2,
        scratch_shapes=[
            pltpu.VMEM((2 * rows, width), jnp.bfloat16),
            pltpu.VMEM((2 * rows, width), jnp.bfloat16),
            pltpu.SemaphoreType.DMA((2,)),
        ],
        cost_estimate=pl.CostEstimate(flops=10 * rows * width, bytes_accessed=14 * rows * width, transcendentals=0),
    )(query, key_new, value_new, powers, key_stale, value_stale)


def attend_kernel(members, dim, *refs):
    query = refs[0]
    kvs = refs[1 : 1 + members]
    att, kv = refs[1 + members :]
    share = att.shape[1]
    block = kvs[0].shape[0]
    for j in range(members):
        kv[j * block : (j + 1) * block] = kvs[j][...]
    inverse = 1.0 / dim**0.5
    for h in range(share // dim):
        cols = slice(h * dim, (h + 1) * dim)
        scores = (
            lax.dot_general(query[:, cols], kv[:, cols], (((1,), (1,)), ((), ())), preferred_element_type=jnp.float32)
            * inverse
        )
        peak = jnp.max(scores, axis=1, keepdims=True)
        expo = jnp.exp(scores - peak)
        total = jnp.sum(expo, axis=1, keepdims=True)
        numer = jnp.dot(
            expo.astype(jnp.bfloat16),
            kv[:, share + h * dim : share + (h + 1) * dim],
            preferred_element_type=jnp.float32,
        )
        att[:, cols] = (numer / total).astype(jnp.bfloat16)


def attend(members, dim, query, kvs):
    rows, share = query.shape
    block = kvs[0].shape[0]
    return pl.pallas_call(
        functools.partial(attend_kernel, members, dim),
        out_shape=jax.ShapeDtypeStruct((rows, share), jnp.bfloat16),
        in_specs=[VMEM] * (1 + members),
        out_specs=VMEM,
        scratch_shapes=[pltpu.VMEM((members * block, 2 * share), jnp.bfloat16)],
        compiler_params=pltpu.CompilerParams(vmem_limit_bytes=24 * 1024 * 1024),
        cost_estimate=pl.CostEstimate(
            flops=4 * rows * members * block * share,
            bytes_accessed=4 * members * block * share,
            transcendentals=rows * members * block * share // dim,
        ),
    )(query, *kvs)


def project_kernel(groups, members, pieces, att, *refs):
    ws = refs[:pieces]
    out, wide, sems = refs[pieces:]
    depth = ws[0].shape[0]
    q = lax.axis_index("patch") % members
    copies = []
    for j in range(pieces):
        at = pl.multiple_of((q ^ j) * depth, depth) if pieces > 1 else 0
        copies.append(pltpu.make_async_copy(ws[j], wide.at[pl.ds(at, depth)], sems.at[j]))
    for c in copies:
        c.start()
    for c in copies:
        c.wait()
    _, rows, width = out.shape
    tile = 512 if width % 512 == 0 else width
    for t in range(width // tile):
        cols = slice(t * tile, (t + 1) * tile)
        part = jnp.dot(att[...], wide[:, cols], preferred_element_type=jnp.float32)
        for k in range(groups):
            out[k, :, cols] = part[k * rows : (k + 1) * rows].astype(out.dtype)


def project(groups, members, att, ws):
    rows = att.shape[0] // groups
    share = att.shape[1]
    model = ws[0].shape[1]
    return pl.pallas_call(
        functools.partial(project_kernel, groups, members, len(ws)),
        out_shape=jax.ShapeDtypeStruct((groups, rows, model), jnp.bfloat16),
        in_specs=[VMEM] + [ANY] * len(ws),
        out_specs=VMEM,
        scratch_shapes=[pltpu.VMEM((share, model), jnp.bfloat16), pltpu.SemaphoreType.DMA((len(ws),))],
        compiler_params=pltpu.CompilerParams(vmem_limit_bytes=24 * 1024 * 1024),
        cost_estimate=pl.CostEstimate(
            flops=2 * groups * rows * share * model, bytes_accessed=2 * share * model, transcendentals=0
        ),
    )(att, *ws)


def per_device(patch, query, key_new, value_new, key_stale, value_stale, exponents, w_out, gate):
    heads = exponents.shape[1] // 2
    dim = query.shape[1] // heads
    groups = math.gcd(patch, heads)
    members = patch // groups
    share = query.shape[1] // groups

    lines = [[z * members + q for z in range(groups)] for q in range(members)]

    def across(x):
        return lax.all_to_all(x, "patch", 0, 0, axis_index_groups=lines, tiled=True)

    def within(x, j):
        return lax.ppermute(x, "patch", [(p, p ^ j) for p in range(patch)])

    def spread(x, after=None):
        pieces = {0: x}
        bit = members // 2
        while bit:
            for j in list(pieces):
                piece = pieces[j]
                if j and after is not None:
                    piece, _ = lax.optimization_barrier((piece, after))
                pieces[j ^ bit] = within(piece, bit)
            bit //= 2
        return [pieces[j] for j in range(members)]

    rows = query.shape[0]
    powers = lax.dynamic_slice_in_dim(exponents, lax.axis_index("patch") * rows, rows, 0)
    queries, both = prepare(groups, query, key_new, value_new, powers, key_stale, value_stale)
    both = across(both)
    queries = across(queries)
    kvs = spread(both.reshape(groups * rows, 2 * share))
    att = attend(members, dim, queries.reshape(groups * rows, share), kvs)
    ws = spread(w_out, after=kvs)
    if w_out.shape[0] % 16:
        order = (lax.axis_index("patch") % members) ^ jnp.arange(members)
        ws = [jnp.stack(ws)[order].reshape(-1, w_out.shape[1])]
    parts = project(groups, members, att, ws)
    parts = across(parts)
    total = parts[0].astype(jnp.float32)
    for z in range(1, groups):
        total = total + parts[z].astype(jnp.float32)
    return (total * gate[None, :]).astype(jnp.bfloat16)


def solution(mesh):
    return jax.shard_map(
        functools.partial(per_device, mesh.shape["patch"]),
        mesh=mesh,
        in_specs=(
            P(("groups", "patch"), None),
            P(("groups", "patch"), None),
            P(("groups", "patch"), None),
            P("groups", None),
            P("groups", None),
            P("groups", None),
            P("patch", None),
            P("groups"),
        ),
        out_specs=P(("groups", "patch"), None),
        check_vma=False,
    )
```

time: 42.9 us -> 55.2 us (1.29)
  blocking collectives: 0 us -> 38.6 us
  waiting for transfers between devices: 20.4 us -> 5.24 us
  starting transfers between devices: 13.1 us -> 4.39 us
  local copies, waits for them, and re-layouts: 3.18 us -> 0.76 us
    all_to_all x0 -> x3, blocking collectives: none -> 38.6 us  [across(): return lax.all_to_all(x, 'patch', 0, 0, axis_index_groups=lines, tiled=True)]
    ppermute x6 -> x0, waiting for transfers between devices: 14.8 us -> none  [across(): lax.ppermute(x, 'patch', [(p, (p // members ^ k) * members + p % members)...]
    ppermute x6 -> x0, starting transfers between devices: 8.9 us -> none  [across(): lax.ppermute(x, 'patch', [(p, (p // members ^ k) * members + p % members)...]
    unnamed x7, local copies, waits for them, and re-layouts: 2.4 us -> 0.69 us
    slice x4 -> x0, local copies, waits for them, and re-layouts: 0.78 us -> none  [per_device(): kvs = spread(jnp.concatenate([p[:, share:] for p in packs], axis=0))]
  transfers between devices with their start and end apart: 12 -> 6, of which waited for: 7 -> 2; matrix products, arithmetic and copies ran while one was open for 6% -> 1% of each run, Pallas kernels for 9% -> 7%
where the time goes in v2:
time: 55.2 us; the launch traced here: 54.8 us
  blocking collectives  38.6 us (70%)
  waiting for transfers between devices  5.24 us (9%)
  Pallas kernels  5 us (9%)
  starting transfers between devices  4.39 us (8%)
  local copies, waits for them, and re-layouts  0.76 us (1%)
  other arithmetic  0.75 us (1%)
    all_to_all x3, blocking collectives, across(): return lax.all_to_all(x, 'patch', 0, 0, axis_index_groups=lines, tiled=True)  38.6 us
    ppermute x6, waiting for transfers between devices, within(): return lax.ppermute(x, 'patch', [(p, p ^ j) for p in range(patch)])  5.24 us
    ppermute x6, starting transfers between devices, within(): return lax.ppermute(x, 'patch', [(p, p ^ j) for p in range(patch)])  4.39 us
    pallas_call x1, Pallas kernels, prepare(): pl.pallas_call(functools.partial(prepare_kernel, groups), out_shape=[jax....  2.96 us
    pallas_call x1, Pallas kernels, project(): pl.pallas_call(functools.partial(project_kernel, groups, members, len(ws)...  1.12 us
  transfers between devices with their start and end apart: 6, of which 2 were waited for; matrix products, arithmetic and copies ran while one was open for 1% of the time, Pallas kernels for 7%

profile of v2, /device:TPU:0, one launch (start us, length us, event | category | flops | bytes accessed | tf_op | source)
XLA Modules:
  0.0 54.8 jit_solution(9881403839336903827)
XLA Ops:
  0.0 0.0 copy-start
  0.0 3.0 %collective-permute-start.4 = (bf16[96,3072]{1,0:T(8,128)(2,1)}, bf16[96,3072]{1,0:T(8,128)(2,1)S(1)}, u32[]{:S(2)}, u32[]{:S(2)}) collective-permute-start(bf16[96,3072]{1,0:T(8,128)(2,1)} %refs_0_.1), channel_id=1, source_target_pairs={{0,2},{1,3},{2,0},{3,1},{4,6},{5,7},{6,4},{7,5},{8,10},{9,11},{10,... | collective-permute-start | bytes 1769480 | tf_op jit(solution)/shard_map/ppermute | solution.py:166
  3.0 0.0 copy-done
  3.0 0.1 constant_dynamic-slice_fusion
  3.0 0.7 %copy.10.power_ref = s32[24,24]{1,0:T(8,128)} copy(s32[24,24]{0,1:T(8,128)S(1)} %constant_dynamic-slice_fusion) | data formatting | bytes 4608
  3.7 0.0 copy-start.1
  3.7 3.0 %shard_map.82 = (bf16[4,24,384]{2,1,0:T(8,128)(2,1)}, bf16[4,24,768]{2,1,0:T(8,128)(2,1)}) custom-call(bf16[24,1536]{1,0:T(8,128)(2,1)} %query_ref.1, bf16[24,1536]{1,0:T(8,128)(2,1)} %key_ref.1, bf16[24,1536]{1,0:T(8,128)(2,1)} %value_ref.1, s32[24,24]{1,0:T(8,128)} %copy.10.power_ref, bf16[384,1536]{1,0:T(8,128)(2,1)} %kstale_ref.1, ...), custom_call_target="tpu_custom_call" | custom-call | flops 368640 | bytes 516096 | tf_op jit(solution)/shard_map/pallas_call | solution.py:53
  6.7 11.5 %all_to_all.15 = bf16[4,24,768]{2,1,0:T(8,128)(2,1)S(1)} all-to-all(bf16[4,24,768]{2,1,0:T(8,128)(2,1)} %get-tuple-element.9), channel_id=1, replica_groups={{0,4,8,12},{1,5,9,13},{2,6,10,14},{3,7,11,15},{16,20,24,28},{17,21,25,2..., dimensions={0} | all-to-all | bytes 294912 | tf_op jit(solution)/shard_map/all_to_all | solution.py:163
  18.2 0.8 %collective-permute-start.1 = (bf16[96,768]{1,0:T(8,128)(2,1)S(1)}, bf16[96,768]{1,0:T(8,128)(2,1)S(1)}, u32[]{:S(2)}, u32[]{:S(2)}) collective-permute-start(bf16[96,768]{1,0:T(8,128)(2,1)S(1)} %bitcast.6), channel_id=1, source_target_pairs={{0,2},{1,3},{2,0},{3,1},{4,6},{5,7},{6,4},{7,5},{8,10},{9,11},{10,... | collective-permute-start | bytes 442376 | tf_op jit(solution)/shard_map/ppermute | solution.py:166
  19.0 0.0 collective-permute-start
  19.0 4.4 %collective-permute-done.1.refs_3_ = bf16[96,768]{1,0:T(8,128)(2,1)S(1)} collective-permute-done((bf16[96,768]{1,0:T(8,128)(2,1)S(1)}, bf16[96,768]{1,0:T(8,128)(2,1)S(1)}, u32[]{:S(2)}, u32[]{:S(2)}) %collective-permute-start.1) | collective-permute-done | bytes 147488 | tf_op jit(solution)/shard_map/ppermute | solution.py:166
  23.4 0.0 collective-permute-start.2
  23.4 0.0 copy-done.1
  23.4 0.5 collective-permute-start.3
  23.9 0.0 collective-permute-done.refs_2_
  23.9 0.9 %collective-permute-done.2.refs_4_ = bf16[96,768]{1,0:T(8,128)(2,1)S(1)} collective-permute-done((bf16[96,768]{1,0:T(8,128)(2,1)S(1)}, bf16[96,768]{1,0:T(8,128)(2,1)S(1)}, u32[]{:S(2)}, u32[]{:S(2)}) %collective-permute-start.2) | collective-permute-done | bytes 147488 | tf_op jit(solution)/shard_map/ppermute | solution.py:166
  24.8 0.0 collective-permute-done.4.refs_2_
  24.8 0.1 collective-permute-start.5
  24.9 9.0 %all_to_all.16 = bf16[4,24,384]{2,1,0:T(8,128)(2,1)S(1)} all-to-all(bf16[4,24,384]{2,1,0:T(8,128)(2,1)} %get-tuple-element.8), channel_id=1, replica_groups={{0,4,8,12},{1,5,9,13},{2,6,10,14},{3,7,11,15},{16,20,24,28},{17,21,25,2..., dimensions={0} | all-to-all | bytes 147456 | tf_op jit(solution)/shard_map/all_to_all | solution.py:163
  33.9 0.9 %shard_map.83.att = bf16[96,384]{1,0:T(8,128)(2,1)S(1)} custom-call(bf16[96,384]{1,0:T(8,128)(2,1)S(1)} %bitcast.9, bf16[96,768]{1,0:T(8,128)(2,1)S(1)} %bitcast.8, bf16[96,768]{1,0:T(8,128)(2,1)S(1)} %collective-permute-done.refs_2_, bf16[96,768]{1,0:T(8,128)(2,1)S(1)} %collective-permute-done.1.refs_3_, bf16[96,768]{1,0:T(8,128)(2,1)S(1)} %collective-permute-done.2.refs_4_), custom_call_target="tpu_custom_call" | custom-call | flops 56623104 | bytes 589824 | tf_op jit(solution)/shard_map/pallas_call | solution.py:99
  34.9 0.0 collective-permute-done.3.refs_1_
  34.9 0.0 collective-permute-done.5.refs_3_
  34.9 1.1 %shard_map.84 = bf16[4,24,3072]{2,1,0:T(8,128)(2,1)S(1)} custom-call(bf16[96,384]{1,0:T(8,128)(2,1)S(1)} %shard_map.83.att, bf16[96,3072]{1,0:T(8,128)(2,1)S(1)} %copy-done.1, bf16[96,3072]{1,0:T(8,128)(2,1)S(1)} %collective-permute-done.3.refs_1_, bf16[96,3072]{1,0:T(8,128)(2,1)S(1)} %collective-permute-done.4.refs_2_, ...), custom_call_target="tpu_custom_call" | custom-call | flops 226492416 | bytes 2359296 | tf_op jit(solution)/shard_map/pallas_call | solution.py:140
  36.0 0.0 copy-start.2
  36.0 18.0 %all_to_all.17 = bf16[4,24,3072]{2,1,0:T(8,128)(2,1)S(1)} all-to-all(bf16[4,24,3072]{2,1,0:T(8,128)(2,1)S(1)} %shard_map.84), channel_id=1, replica_groups={{0,4,8,12},{1,5,9,13},{2,6,10,14},{3,7,11,15},{16,20,24,28},{17,21,25,2..., dimensions={0} | all-to-all | bytes 1179648 | tf_op jit(solution)/shard_map/all_to_all | solution.py:163
  54.1 0.0 copy-done.2
  54.1 0.7 %fusion = bf16[24,3072]{1,0:T(8,128)(2,1)} fusion(bf16[4,24,3072]{2,1,0:T(8,128)(2,1)S(1)} %all_to_all.17, f32[3072]{0:T(1024)S(1)} %copy-done.2), kind=kLoop, calls=%fused_computation.1 | loop fusion | flops 663552 | bytes 749568 | tf_op jit(solution)/shard_map/convert_element_type | solution.py:196
Async XLA Ops:
  0.0 3.0 %copy-start = (s32[384,24]{0,1:T(8,128)S(1)}, s32[384,24]{0,1:T(8,128)}, u32[]{:S(2)}) copy-start(s32[384,24]{0,1:T(8,128)} %param.13) | copy-start | bytes 110596
  0.0 24.8 %collective-permute-start.4 = (bf16[96,3072]{1,0:T(8,128)(2,1)}, bf16[96,3072]{1,0:T(8,128)(2,1)S(1)}, u32[]{:S(2)}, u32[]{:S(2)}) collective-permute-start(bf16[96,3072]{1,0:T(8,128)(2,1)} %refs_0_.1), channel_id=1, source_target_pairs={{0,2},{1,3},{2,0},{3,1},{4,6},{5,7},{6,4},{7,5},{8,10},{9,11},{10,... | collective-permute-start | bytes 1769480 | tf_op jit(solution)/shard_map/ppermute | solution.py:166
  3.7 19.7 %copy-start.1 = (bf16[96,3072]{1,0:T(8,128)(2,1)S(1)}, bf16[96,3072]{1,0:T(8,128)(2,1)}, u32[]{:S(2)}) copy-start(bf16[96,3072]{1,0:T(8,128)(2,1)} %refs_0_.1) | copy-start | bytes 1769476
  18.2 5.1 %collective-permute-start.1 = (bf16[96,768]{1,0:T(8,128)(2,1)S(1)}, bf16[96,768]{1,0:T(8,128)(2,1)S(1)}, u32[]{:S(2)}, u32[]{:S(2)}) collective-permute-start(bf16[96,768]{1,0:T(8,128)(2,1)S(1)} %bitcast.6), channel_id=1, source_target_pairs={{0,2},{1,3},{2,0},{3,1},{4,6},{5,7},{6,4},{7,5},{8,10},{9,11},{10,... | collective-permute-start | bytes 442376 | tf_op jit(solution)/shard_map/ppermute | solution.py:166
  19.0 4.9 %collective-permute-start = (bf16[96,768]{1,0:T(8,128)(2,1)S(1)}, bf16[96,768]{1,0:T(8,128)(2,1)S(1)}, u32[]{:S(2)}, u32[]{:S(2)}) collective-permute-start(bf16[96,768]{1,0:T(8,128)(2,1)S(1)} %bitcast.7), channel_id=1, source_target_pairs={{0,1},{1,0},{2,3},{3,2},{4,5},{5,4},{6,7},{7,6},{8,9},{9,8},{10,11... | collective-permute-start | bytes 442376 | tf_op jit(solution)/shard_map/ppermute | solution.py:166
  23.4 1.4 %collective-permute-start.2 = (bf16[96,768]{1,0:T(8,128)(2,1)S(1)}, bf16[96,768]{1,0:T(8,128)(2,1)S(1)}, u32[]{:S(2)}, u32[]{:S(2)}) collective-permute-start(bf16[96,768]{1,0:T(8,128)(2,1)S(1)} %collective-permute-done.1.refs_3_), channel_id=1, source_target_pairs={{0,1},{1,0},{2,3},{3,2},{4,5},{5,4},{6,7},{7,6},{8,9},{9,8},{10,11... | collective-permute-start | bytes 442376 | tf_op jit(solution)/shard_map/ppermute | solution.py:166
  23.4 11.5 %collective-permute-start.3 = (bf16[96,3072]{1,0:T(8,128)(2,1)S(1)}, bf16[96,3072]{1,0:T(8,128)(2,1)S(1)}, u32[]{:S(2)}, u32[]{:S(2)}) collective-permute-start(bf16[96,3072]{1,0:T(8,128)(2,1)S(1)} %copy-done.1), channel_id=1, source_target_pairs={{0,1},{1,0},{2,3},{3,2},{4,5},{5,4},{6,7},{7,6},{8,9},{9,8},{10,11... | collective-permute-start | bytes 1769480 | tf_op jit(solution)/shard_map/ppermute | solution.py:166
  24.8 10.1 %collective-permute-start.5 = (bf16[96,3072]{1,0:T(8,128)(2,1)S(1)}, bf16[96,3072]{1,0:T(8,128)(2,1)S(1)}, u32[]{:S(2)}, u32[]{:S(2)}) collective-permute-start(bf16[96,3072]{1,0:T(8,128)(2,1)S(1)} %collective-permute-done.4.refs_2_), channel_id=1, source_target_pairs={{0,1},{1,0},{2,3},{3,2},{4,5},{5,4},{6,7},{7,6},{8,9},{9,8},{10,11... | collective-permute-start | bytes 1769480 | tf_op jit(solution)/shard_map/ppermute | solution.py:166
  36.0 18.0 %copy-start.2 = (f32[3072]{0:T(1024)S(1)}, f32[3072]{0:T(1024)}, u32[]{:S(2)}) copy-start(f32[3072]{0:T(1024)} %param.15) | copy-start | bytes 36868

commit v3 on v1

v3 whole, which is shorter than its diff:
```python
import functools
import math

import jax
import jax.numpy as jnp
from jax import lax
from jax.experimental import pallas as pl
from jax.experimental.pallas import tpu as pltpu
from jax.sharding import PartitionSpec as P

CLIP_LIMIT = 2.0
VMEM = pl.BlockSpec(memory_space=pltpu.VMEM)
ANY = pl.BlockSpec(memory_space=pl.ANY)
HBM = pl.BlockSpec(memory_space=pltpu.HBM)


def prepare_kernel(groups, members, chunks, *refs):
    sources, (w_ref,) = refs[:6], refs[6:7]
    qouts, kvouts, wouts = refs[7 : 7 + groups], refs[7 + groups : 7 + 2 * groups], refs[7 + 2 * groups :][:chunks]
    query, key_new, value_new, kst, vst, est, packed, sems = refs[7 + 2 * groups + chunks :]
    rows, width = query.shape
    me = lax.axis_index("patch")
    first = pl.multiple_of((me // 2) * (2 * rows), 2 * rows)
    pair = pl.ds(first, 2 * rows)
    views = [sources[0], sources[1], sources[2], sources[3].at[pair], sources[4].at[pair], sources[5]]
    order = (5, 3, 1, 4, 2, 0)
    copies = {
        i: pltpu.make_async_copy(views[i], (query, key_new, value_new, kst, vst, est)[i], sems.at[i]) for i in order
    }
    for i in order:
        copies[i].start()
    part = w_ref.shape[1] // chunks
    moves = [
        pltpu.make_async_copy(w_ref.at[:, pl.ds(i * part, part)], wouts[i], sems.at[6 + i]) for i in range(chunks)
    ]
    for m in moves:
        m.start()
    heads = est.shape[0] // 2
    dim = width // heads
    share = width // groups
    odd = me % 2 == 1
    copies[5].wait()
    spot = lax.broadcasted_iota(jnp.int32, (rows, est.shape[1]), 1) == me * rows + lax.broadcasted_iota(
        jnp.int32, (rows, est.shape[1]), 0
    )
    powers = lax.dot_general(
        spot.astype(jnp.float32).astype(jnp.bfloat16),
        est[...].astype(jnp.float32).astype(jnp.bfloat16),
        (((1,), (1,)), ((), ())),
        preferred_element_type=jnp.float32,
    )
    scale = jnp.exp2(powers)
    inverse = jnp.exp2(-powers)
    for side, (fresh, stale) in enumerate(((key_new, kst), (value_new, vst))):
        copies[1 + side].wait()
        copies[3 + side].wait()
        for h in range(heads):
            cols = slice(h * dim, (h + 1) * dim)
            col = side * heads + h
            both = stale[:, cols].astype(jnp.float32)
            base = jnp.where(odd, both[rows:], both[:rows])
            resid = fresh[:, cols].astype(jnp.float32) - base
            codes = jnp.clip(resid * inverse[:, col : col + 1], -CLIP_LIMIT, CLIP_LIMIT)
            codes = codes.astype(jnp.bfloat16).astype(jnp.float32)
            at = side * share + (h * dim) % share
            packed[h * dim // share, :, at : at + dim] = (base + scale[:, col : col + 1] * codes).astype(jnp.bfloat16)
    copies[0].wait()
    for k in range(groups):
        target = (me // members) ^ k
        kvouts[k][...] = packed[target]
        qouts[k][...] = query[:, pl.ds(pl.multiple_of(target * share, share), share)]
    for m in moves:
        m.wait()


def prepare(groups, members, chunks, query, key_new, value_new, key_stale, value_stale, powers, w_out):
    rows, width = query.shape
    share = width // groups
    depth, model = w_out.shape
    outs = (
        [((rows, share), jnp.bfloat16)] * groups
        + [((rows, 2 * share), jnp.bfloat16)] * groups
        + [((depth, model // chunks), jnp.bfloat16)] * chunks
    )
    result = pl.pallas_call(
        functools.partial(prepare_kernel, groups, members, chunks),
        out_shape=[jax.ShapeDtypeStruct(*o) for o in outs],
        in_specs=[HBM] * 7,
        out_specs=[VMEM] * len(outs),
        scratch_shapes=[pltpu.VMEM((rows, width), jnp.bfloat16)] * 3
        + [pltpu.VMEM((2 * rows, width), jnp.bfloat16)] * 2
        + [
            pltpu.VMEM(powers.shape, jnp.int32),
            pltpu.VMEM((groups, rows, 2 * share), jnp.bfloat16),
            pltpu.SemaphoreType.DMA((6 + chunks,)),
        ],
        compiler_params=pltpu.CompilerParams(vmem_limit_bytes=24 * 1024 * 1024),
        cost_estimate=pl.CostEstimate(
            flops=10 * rows * width, bytes_accessed=14 * rows * width + 4 * depth * model, transcendentals=0
        ),
    )(query, key_new, value_new, key_stale, value_stale, powers, w_out)
    return result[:groups], result[groups : 2 * groups], result[2 * groups :]


def attend_kernel(groups, members, dim, *refs):
    queries = refs[:groups]
    kvs = refs[groups : groups + members]
    att, kv = refs[groups + members :]
    share = att.shape[1]
    block = kvs[0].shape[0]
    for j in range(members):
        kv[j * block : (j + 1) * block] = kvs[j][...]
    query = jnp.concatenate([q[...].astype(jnp.float32) for q in queries], axis=0).astype(jnp.bfloat16)
    inverse = 1.0 / dim**0.5
    for h in range(share // dim):
        cols = slice(h * dim, (h + 1) * dim)
        scores = (
            lax.dot_general(query[:, cols], kv[:, cols], (((1,), (1,)), ((), ())), preferred_element_type=jnp.float32)
            * inverse
        )
        peak = jnp.max(scores, axis=1, keepdims=True)
        expo = jnp.exp(scores - peak)
        total = jnp.sum(expo, axis=1, keepdims=True)
        numer = jnp.dot(
            expo.astype(jnp.bfloat16),
            kv[:, share + h * dim : share + (h + 1) * dim],
            preferred_element_type=jnp.float32,
        )
        att[:, cols] = (numer / total).astype(jnp.bfloat16)


def attend(groups, members, dim, queries, kvs):
    rows, share = queries[0].shape
    block = kvs[0].shape[0]
    return pl.pallas_call(
        functools.partial(attend_kernel, groups, members, dim),
        out_shape=jax.ShapeDtypeStruct((groups * rows, share), jnp.bfloat16),
        in_specs=[VMEM] * (groups + members),
        out_specs=VMEM,
        scratch_shapes=[pltpu.VMEM((members * block, 2 * share), jnp.bfloat16)],
        compiler_params=pltpu.CompilerParams(vmem_limit_bytes=24 * 1024 * 1024),
        cost_estimate=pl.CostEstimate(
            flops=4 * groups * rows * members * block * share,
            bytes_accessed=4 * members * block * share,
            transcendentals=groups * rows * members * block * share // dim,
        ),
    )(*queries, *kvs)


def project_kernel(groups, members, pieces, att, *refs):
    ws = refs[:pieces]
    outs = refs[pieces : pieces + groups]
    wide, sems = refs[pieces + groups :]
    depth = ws[0].shape[0]
    q = lax.axis_index("patch") % members
    copies = []
    for j in range(pieces):
        at = pl.multiple_of((q ^ j) * depth, depth) if pieces > 1 else 0
        copies.append(pltpu.make_async_copy(ws[j], wide.at[pl.ds(at, depth)], sems.at[j]))
    for c in copies:
        c.start()
    for c in copies:
        c.wait()
    rows, width = outs[0].shape
    tile = 512 if width % 512 == 0 else width
    for t in range(width // tile):
        cols = slice(t * tile, (t + 1) * tile)
        part = jnp.dot(att[...], wide[:, cols], preferred_element_type=jnp.float32)
        for k in range(groups):
            outs[k][:, cols] = part[k * rows : (k + 1) * rows].astype(outs[k].dtype)


def project(groups, members, att, ws):
    rows = att.shape[0] // groups
    share = att.shape[1]
    model = ws[0].shape[1]
    return pl.pallas_call(
        functools.partial(project_kernel, groups, members, len(ws)),
        out_shape=[jax.ShapeDtypeStruct((rows, model), jnp.float32)]
        + [jax.ShapeDtypeStruct((rows, model), jnp.bfloat16)] * (groups - 1),
        in_specs=[VMEM] + [ANY] * len(ws),
        out_specs=[VMEM] * groups,
        scratch_shapes=[pltpu.VMEM((share, model), jnp.bfloat16), pltpu.SemaphoreType.DMA((len(ws),))],
        compiler_params=pltpu.CompilerParams(vmem_limit_bytes=24 * 1024 * 1024),
        cost_estimate=pl.CostEstimate(
            flops=2 * groups * rows * share * model, bytes_accessed=2 * share * model, transcendentals=0
        ),
    )(att, *ws)


def after(x, *others):
    return lax.optimization_barrier((x, *others))[0]


def per_device(patch, query, key_new, value_new, key_stale, value_stale, exponents, w_out, gate):
    heads = exponents.shape[1] // 2
    dim = query.shape[1] // heads
    groups = math.gcd(patch, heads)
    members = patch // groups
    chunks = 2

    def across(x, k):
        return lax.ppermute(x, "patch", [(p, ((p // members) ^ k) * members + p % members) for p in range(patch)])

    def within(x, j):
        return lax.ppermute(x, "patch", [(p, p ^ j) for p in range(patch)])

    def spread(pieces, bit):
        while bit:
            for j in list(pieces):
                pieces[j ^ bit] = within(pieces[j], bit)
            bit //= 2
        return [pieces[j] for j in range(members)]

    far = members // 2
    queries, fresh, ws = prepare(
        groups, members, chunks, query, key_new, value_new, key_stale, value_stale, exponents.T, w_out
    )
    fresh = [fresh[0]] + [across(fresh[k], k) for k in range(1, groups)]
    both = jnp.concatenate(fresh, axis=0)
    kvs = spread({0: both}, far)
    queries = [queries[0]] + [across(after(queries[k], both), k) for k in range(1, groups)]
    att = attend(groups, members, dim, queries, kvs)
    sums = []
    done = None
    for c in range(chunks):
        own = ws[c] if c == 0 else after(ws[c], both)
        other = within(own, far)
        if done is not None:
            other = after(other, *done)
        pieces = spread({0: ws[c], far: other}, far // 2)
        if w_out.shape[0] % 16:
            order = (lax.axis_index("patch") % members) ^ jnp.arange(members)
            pieces = [jnp.stack(pieces)[order].reshape(-1, pieces[0].shape[1])]
        done = project(groups, members, att, pieces)
        total = done[0]
        for k in range(1, groups):
            total = total + across(done[k], k).astype(jnp.float32)
        sums.append(total)
    return (jnp.concatenate(sums, axis=1) * gate[None, :]).astype(jnp.bfloat16)


def solution(mesh):
    return jax.shard_map(
        functools.partial(per_device, mesh.shape["patch"]),
        mesh=mesh,
        in_specs=(
            P(("groups", "patch"), None),
            P(("groups", "patch"), None),
            P(("groups", "patch"), None),
            P("groups", None),
            P("groups", None),
            P("groups", None),
            P("patch", None),
            P("groups"),
        ),
        out_specs=P(("groups", "patch"), None),
        check_vma=False,
    )
```

time: 42.9 us -> 60.6 us (1.41)
  starting transfers between devices: 13.1 us -> 25.2 us
  local copies, waits for them, and re-layouts: 3.18 us -> 7.04 us
  waiting for transfers between devices: 20.4 us -> 23.5 us
  Pallas kernels: 5 us -> 3.56 us
    ppermute x6 -> x12, starting transfers between devices: 8.9 us -> 19.3 us  [across(): lax.ppermute(x, 'patch', [(p, (p // members ^ k) * members + p % members)...]
    ppermute x6 -> x12, waiting for transfers between devices: 14.8 us -> 20.1 us  [across(): lax.ppermute(x, 'patch', [(p, (p // members ^ k) * members + p % members)...]
    unnamed x7 -> x19, local copies, waits for them, and re-layouts: 2.4 us -> 7.04 us
    ppermute x6 -> x9, waiting for transfers between devices: 5.59 us -> 3.38 us  [within(): return lax.ppermute(x, 'patch', [(p, p ^ j) for p in range(patch)])]
    pallas_call x1, Pallas kernels: 2.98 us -> 1.35 us  [prepare(): pl.pallas_call(functools.partial(prepare_kernel, groups, members, chunks)...]
    ppermute x6 -> x9, starting transfers between devices: 4.2 us -> 5.82 us  [within(): return lax.ppermute(x, 'patch', [(p, p ^ j) for p in range(patch)])]
    slice x4 -> x0, local copies, waits for them, and re-layouts: 0.78 us -> none  [per_device(): kvs = spread(jnp.concatenate([p[:, share:] for p in packs], axis=0))]
    pallas_call x1 -> x2, Pallas kernels: 1.1 us -> 1.29 us  [project(): pl.pallas_call(functools.partial(project_kernel, groups, members, len(ws)...]
  transfers between devices with their start and end apart: 12 -> 21, of which waited for: 7 -> 10; matrix products, arithmetic and copies ran while one was open for 6% -> 0% of each run, Pallas kernels for 9% -> 4%
where the time goes in v3:
time: 60.6 us; the launch traced here: 60.2 us
  starting transfers between devices  25.2 us (42%)
  waiting for transfers between devices  23.5 us (39%)
  local copies, waits for them, and re-layouts  7.04 us (12%)
  Pallas kernels  3.56 us (6%)
  other arithmetic  0.75 us (1%)
    ppermute x12, waiting for transfers between devices, across(): lax.ppermute(x, 'patch', [(p, (p // members ^ k) * members + p % members)...  20.1 us
    ppermute x12, starting transfers between devices, across(): lax.ppermute(x, 'patch', [(p, (p // members ^ k) * members + p % members)...  19.3 us
    unnamed x19, local copies, waits for them, and re-layouts  7.04 us
    ppermute x9, starting transfers between devices, within(): return lax.ppermute(x, 'patch', [(p, p ^ j) for p in range(patch)])  5.82 us
    ppermute x9, waiting for transfers between devices, within(): return lax.ppermute(x, 'patch', [(p, p ^ j) for p in range(patch)])  3.38 us
    pallas_call x1, Pallas kernels, prepare(): pl.pallas_call(functools.partial(prepare_kernel, groups, members, chunks)...  1.35 us
    pallas_call x2, Pallas kernels, project(): pl.pallas_call(functools.partial(project_kernel, groups, members, len(ws)...  1.29 us
  transfers between devices with their start and end apart: 21, of which 10 were waited for; matrix products, arithmetic and copies ran while one was open for 0% of the time, Pallas kernels for 4%

profile of v3, /device:TPU:0, one launch (start us, length us, event | category | flops | bytes accessed | tf_op | source)
XLA Modules:
  0.0 60.2 jit_solution(8559274809677472792)
XLA Ops:
  0.0 1.3 %copy-done = bf16[384,1536]{1,0:T(8,128)(2,1)S(1)} copy-done((bf16[384,1536]{1,0:T(8,128)(2,1)S(1)}, bf16[384,1536]{1,0:T(8,128)(2,1)}, u32[]{:S(2)}) %copy-start) | copy-done | bytes 1179672
  1.3 1.3 %copy-done.1 = bf16[384,1536]{1,0:T(8,128)(2,1)S(1)} copy-done((bf16[384,1536]{1,0:T(8,128)(2,1)S(1)}, bf16[384,1536]{1,0:T(8,128)(2,1)}, u32[]{:S(2)}) %copy-start.1) | copy-done | bytes 1179672
  2.5 1.1 %copy-done.2 = bf16[96,3072]{1,0:T(8,128)(2,1)S(1)} copy-done((bf16[96,3072]{1,0:T(8,128)(2,1)S(1)}, bf16[96,3072]{1,0:T(8,128)(2,1)}, u32[]{:S(2)}) %copy-start.2) | copy-done | bytes 589848
  3.6 0.9 %copy-done.3 = bf16[24,1536]{1,0:T(8,128)(2,1)S(1)} copy-done((bf16[24,1536]{1,0:T(8,128)(2,1)S(1)}, bf16[24,1536]{1,0:T(8,128)(2,1)}, u32[]{:S(2)}) %copy-start.3) | copy-done | bytes 73752
  4.5 0.9 %copy-done.4 = bf16[24,1536]{1,0:T(8,128)(2,1)S(1)} copy-done((bf16[24,1536]{1,0:T(8,128)(2,1)S(1)}, bf16[24,1536]{1,0:T(8,128)(2,1)}, u32[]{:S(2)}) %copy-start.4) | copy-done | bytes 73752
  5.4 0.9 %copy-done.5 = bf16[24,1536]{1,0:T(8,128)(2,1)S(1)} copy-done((bf16[24,1536]{1,0:T(8,128)(2,1)S(1)}, bf16[24,1536]{1,0:T(8,128)(2,1)}, u32[]{:S(2)}) %copy-start.5) | copy-done | bytes 73752
  6.3 0.8 %copy-done.6 = s32[384,24]{0,1:T(8,128)S(1)} copy-done((s32[384,24]{0,1:T(8,128)S(1)}, s32[384,24]{0,1:T(8,128)}, u32[]{:S(2)}) %copy-start.6) | copy-done | bytes 36888
  7.0 1.4 %shard_map.82 = (bf16[24,384]{1,0:T(8,128)(2,1)S(1)}, bf16[24,384]{1,0:T(8,128)(2,1)S(1)}, bf16[24,384]{1,0:T(8,128)(2,1)S(1)}, bf16[24,384]{1,0:T(8,128)(2,1)S(...) custom-call(bf16[24,1536]{1,0:T(8,128)(2,1)S(1)} %copy-done.3, ...), custom_call_target="tpu_custom_call" | custom-call | flops 368640 | bytes 1695744 | tf_op jit(solution)/shard_map/pallas_call | solution.py:85
  8.4 3.1 %collective-permute-start = (bf16[24,768]{1,0:T(8,128)(2,1)S(1)}, bf16[24,768]{1,0:T(8,128)(2,1)S(1)}, u32[]{:S(2)}, u32[]{:S(2)}) collective-permute-start(bf16[24,768]{1,0:T(8,128)(2,1)S(1)} %get-tuple-element.31), channel_id=1, source_target_pairs={{0,4},{1,5},{2,6},{3,7},{4,0},{5,1},{6,2},{7,3},{8,12},{9,13},{10,... | collective-permute-start | bytes 110600 | tf_op jit(solution)/shard_map/ppermute | solution.py:203
  11.5 2.6 %collective-permute-start.1 = (bf16[24,768]{1,0:T(8,128)(2,1)S(1)}, bf16[24,768]{1,0:T(8,128)(2,1)S(1)}, u32[]{:S(2)}, u32[]{:S(2)}) collective-permute-start(bf16[24,768]{1,0:T(8,128)(2,1)S(1)} %get-tuple-element.32), channel_id=1, source_target_pairs={{0,8},{1,9},{2,10},{3,11},{4,12},{5,13},{6,14},{7,15},{8,0},{9,1},... | collective-permute-start | bytes 110600 | tf_op jit(solution)/shard_map/ppermute | solution.py:203
  14.1 0.0 collective-permute-start.2
  14.1 1.7 %collective-permute-start.10 = (bf16[96,1536]{1,0:T(8,128)(2,1)S(1)}, bf16[96,1536]{1,0:T(8,128)(2,1)S(1)}, u32[]{:S(2)}, u32[]{:S(2)}) collective-permute-start(bf16[96,1536]{1,0:T(8,128)(2,1)S(1)} %get-tuple-element.39.refs_0_), channel_id=1, source_target_pairs={{0,2},{1,3},{2,0},{3,1},{4,6},{5,7},{6,4},{7,5},{8,10},{9,11},{10,... | collective-permute-start | bytes 884744 | tf_op jit(solution)/shard_map/ppermute | solution.py:206
  15.8 0.0 collective-permute-done
  15.8 1.2 %collective-permute-done.1 = bf16[24,768]{1,0:T(8,128)(2,1)S(1)} collective-permute-done((bf16[24,768]{1,0:T(8,128)(2,1)S(1)}, bf16[24,768]{1,0:T(8,128)(2,1)S(1)}, u32[]{:S(2)}, u32[]{:S(2)}) %collective-permute-start.1) | collective-permute-done | bytes 36896 | tf_op jit(solution)/shard_map/ppermute | solution.py:203
  17.0 2.8 %collective-permute-done.2 = bf16[24,768]{1,0:T(8,128)(2,1)S(1)} collective-permute-done((bf16[24,768]{1,0:T(8,128)(2,1)S(1)}, bf16[24,768]{1,0:T(8,128)(2,1)S(1)}, u32[]{:S(2)}, u32[]{:S(2)}) %collective-permute-start.2) | collective-permute-done | bytes 36896 | tf_op jit(solution)/shard_map/ppermute | solution.py:203
  19.8 1.5 %collective-permute-start.7 = (bf16[96,768]{1,0:T(8,128)(2,1)S(1)}, bf16[96,768]{1,0:T(8,128)(2,1)S(1)}, u32[]{:S(2)}, u32[]{:S(2)}) collective-permute-start(bf16[96,768]{1,0:T(8,128)(2,1)S(1)} %constant_dynamic-update-slice_fusion.refs_4_), channel_id=1, source_target_pairs={{0,2},{1,3},{2,0},{3,1},{4,6},{5,7},{6,4},{7,5},{8,10},{9,11},{10,... | collective-permute-start | bytes 442376 | tf_op jit(solution)/shard_map/ppermute | solution.py:206
  21.4 0.0 collective-permute-start.9
  21.4 2.4 %collective-permute-done.10.refs_2_ = bf16[96,1536]{1,0:T(8,128)(2,1)S(1)} collective-permute-done((bf16[96,1536]{1,0:T(8,128)(2,1)S(1)}, bf16[96,1536]{1,0:T(8,128)(2,1)S(1)}, u32[]{:S(2)}, u32[]{:S(2)}) %collective-permute-start.10) | collective-permute-done | bytes 294944 | tf_op jit(solution)/shard_map/ppermute | solution.py:206
  23.8 0.0 collective-permute-start.11
  23.8 1.5 %collective-permute-start.16 = (bf16[96,1536]{1,0:T(8,128)(2,1)S(1)}, bf16[96,1536]{1,0:T(8,128)(2,1)S(1)}, u32[]{:S(2)}, u32[]{:S(2)}) collective-permute-start(bf16[96,1536]{1,0:T(8,128)(2,1)S(1)} %get-tuple-element.45.refs_0_), channel_id=1, source_target_pairs={{0,2},{1,3},{2,0},{3,1},{4,6},{5,7},{6,4},{7,5},{8,10},{9,11},{10,... | collective-permute-start | bytes 884744 | tf_op jit(solution)/shard_map/ppermute | solution.py:206
  25.3 3.6 %collective-permute-start.5 = (bf16[24,384]{1,0:T(8,128)(2,1)S(1)}, bf16[24,384]{1,0:T(8,128)(2,1)S(1)}, u32[]{:S(2)}, u32[]{:S(2)}) collective-permute-start(bf16[24,384]{1,0:T(8,128)(2,1)S(1)} %get-tuple-element.38), channel_id=1, source_target_pairs={{0,12},{1,13},{2,14},{3,15},{4,8},{5,9},{6,10},{7,11},{8,4},{9,5},... | collective-permute-start | bytes 55304 | tf_op jit(solution)/shard_map/ppermute | solution.py:203
  28.9 2.0 %collective-permute-done.5.refs_3_ = bf16[24,384]{1,0:T(8,128)(2,1)S(1)} collective-permute-done((bf16[24,384]{1,0:T(8,128)(2,1)S(1)}, bf16[24,384]{1,0:T(8,128)(2,1)S(1)}, u32[]{:S(2)}, u32[]{:S(2)}) %collective-permute-start.5) | collective-permute-done | bytes 18464 | tf_op jit(solution)/shard_map/ppermute | solution.py:203
  30.9 0.0 collective-permute-start.4
  30.9 4.7 %collective-permute-done.4.refs_2_ = bf16[24,384]{1,0:T(8,128)(2,1)S(1)} collective-permute-done((bf16[24,384]{1,0:T(8,128)(2,1)S(1)}, bf16[24,384]{1,0:T(8,128)(2,1)S(1)}, u32[]{:S(2)}, u32[]{:S(2)}) %collective-permute-start.4) | collective-permute-done | bytes 18464 | tf_op jit(solution)/shard_map/ppermute | solution.py:203
  35.5 1.2 %collective-permute-start.3 = (bf16[24,384]{1,0:T(8,128)(2,1)S(1)}, bf16[24,384]{1,0:T(8,128)(2,1)S(1)}, u32[]{:S(2)}, u32[]{:S(2)}) collective-permute-start(bf16[24,384]{1,0:T(8,128)(2,1)S(1)} %get-tuple-element.34), channel_id=1, source_target_pairs={{0,4},{1,5},{2,6},{3,7},{4,0},{5,1},{6,2},{7,3},{8,12},{9,13},{10,... | collective-permute-start | bytes 55304 | tf_op jit(solution)/shard_map/ppermute | solution.py:203
  36.8 2.5 %collective-permute-done.3.refs_1_ = bf16[24,384]{1,0:T(8,128)(2,1)S(1)} collective-permute-done((bf16[24,384]{1,0:T(8,128)(2,1)S(1)}, bf16[24,384]{1,0:T(8,128)(2,1)S(1)}, u32[]{:S(2)}, u32[]{:S(2)}) %collective-permute-start.3) | collective-permute-done | bytes 18464 | tf_op jit(solution)/shard_map/ppermute | solution.py:203
  39.3 0.0 collective-permute-start.6
  39.3 0.5 collective-permute-start.8
  39.8 0.9 %collective-permute-done.6.refs_5_ = bf16[96,768]{1,0:T(8,128)(2,1)S(1)} collective-permute-done((bf16[96,768]{1,0:T(8,128)(2,1)S(1)}, bf16[96,768]{1,0:T(8,128)(2,1)S(1)}, u32[]{:S(2)}, u32[]{:S(2)}) %collective-permute-start.6) | collective-permute-done | bytes 147488 | tf_op jit(solution)/shard_map/ppermute | solution.py:206
  40.7 0.1 collective-permute-start.15
  40.8 0.1 collective-permute-done.8.refs_7_
  40.9 0.9 %shard_map.83.att = bf16[96,384]{1,0:T(8,128)(2,1)S(1)} custom-call(bf16[24,384]{1,0:T(8,128)(2,1)S(1)} %get-tuple-element.28.refs_0_, bf16[24,384]{1,0:T(8,128)(2,1)S(1)} %collective-permute-done.3.refs_1_, bf16[24,384]{1,0:T(8,128)(2,1)S(1)} %collective-permute-done.4.refs_2_, bf16[24,384]{1,0:T(8,128)(2,1)S(1)} %collective-permute-done.5.refs_3_, ...), custom_call_target="tpu_custom_call" | custom-call | flops 56623104 | bytes 589824 | tf_op jit(solution)/shard_map/pallas_call | solution.py:135
  41.8 0.0 collective-permute-done.9.refs_1_
  41.8 0.7 %shard_map.84 = (f32[24,1536]{1,0:T(8,128)S(1)}, bf16[24,1536]{1,0:T(8,128)(2,1)S(1)}, bf16[24,1536]{1,0:T(8,128)(2,1)S(1)}, bf16[24,1536]{1,0:T(8,128)(2,1)S(1)}) custom-call(bf16[96,384]{1,0:T(8,128)(2,1)S(1)} %shard_map.83.att, bf16[96,1536]{1,0:T(8,128)(2,1)S(1)} %get-tuple-element.39.refs_0_, bf16[96,1536]{1,0:T(8,128)(2,1)S(1)} %collective-permute-done.9.refs_1_, ...), custom_call_target="tpu_custom_call" | custom-call | flops 113246208 | bytes 1179648 | tf_op jit(solution)/shard_map/pallas_call | solution.py:177
  42.5 0.0 copy-start.7
  42.5 0.4 collective-permute-start.17
  42.9 1.2 %collective-permute-start.12 = (bf16[24,1536]{1,0:T(8,128)(2,1)S(1)}, bf16[24,1536]{1,0:T(8,128)(2,1)S(1)}, u32[]{:S(2)}, u32[]{:S(2)}) collective-permute-start(bf16[24,1536]{1,0:T(8,128)(2,1)S(1)} %get-tuple-element.41), channel_id=1, source_target_pairs={{0,4},{1,5},{2,6},{3,7},{4,0},{5,1},{6,2},{7,3},{8,12},{9,13},{10,... | collective-permute-start | bytes 221192 | tf_op jit(solution)/shard_map/ppermute | solution.py:203
  44.1 2.9 %collective-permute-start.13 = (bf16[24,1536]{1,0:T(8,128)(2,1)S(1)}, bf16[24,1536]{1,0:T(8,128)(2,1)S(1)}, u32[]{:S(2)}, u32[]{:S(2)}) collective-permute-start(bf16[24,1536]{1,0:T(8,128)(2,1)S(1)} %get-tuple-element.42), channel_id=1, source_target_pairs={{0,8},{1,9},{2,10},{3,11},{4,12},{5,13},{6,14},{7,15},{8,0},{9,1},... | collective-permute-start | bytes 221192 | tf_op jit(solution)/shard_map/ppermute | solution.py:203
  47.0 0.3 collective-permute-start.14
  47.3 0.6 %shard_map.85 = (f32[24,1536]{1,0:T(8,128)S(1)}, bf16[24,1536]{1,0:T(8,128)(2,1)S(1)}, bf16[24,1536]{1,0:T(8,128)(2,1)S(1)}, bf16[24,1536]{1,0:T(8,128)(2,1)S(1)}) custom-call(bf16[96,384]{1,0:T(8,128)(2,1)S(1)} %shard_map.83.att, bf16[96,1536]{1,0:T(8,128)(2,1)S(1)} %get-tuple-element.45.refs_0_, bf16[96,1536]{1,0:T(8,128)(2,1)S(1)} %collective-permute-done.15.refs_1_, ...), custom_call_target="tpu_custom_call" | custom-call | flops 113246208 | bytes 1179648 | tf_op jit(solution)/shard_map/pallas_call | solution.py:177
  47.9 0.4 collective-permute-start.18
  48.3 3.8 %collective-permute-start.19 = (bf16[24,1536]{1,0:T(8,128)(2,1)S(1)}, bf16[24,1536]{1,0:T(8,128)(2,1)S(1)}, u32[]{:S(2)}, u32[]{:S(2)}) collective-permute-start(bf16[24,1536]{1,0:T(8,128)(2,1)S(1)} %get-tuple-element.49), channel_id=1, source_target_pairs={{0,8},{1,9},{2,10},{3,11},{4,12},{5,13},{6,14},{7,15},{8,0},{9,1},... | collective-permute-start | bytes 221192 | tf_op jit(solution)/shard_map/ppermute | solution.py:203
  52.1 0.0 collective-permute-done.12
  52.1 0.3 collective-permute-start.20
  52.4 1.7 %collective-permute-done.14 = bf16[24,1536]{1,0:T(8,128)(2,1)S(1)} collective-permute-done((bf16[24,1536]{1,0:T(8,128)(2,1)S(1)}, bf16[24,1536]{1,0:T(8,128)(2,1)S(1)}, u32[]{:S(2)}, u32[]{:S(2)}) %collective-permute-start.14) | collective-permute-done | bytes 73760 | tf_op jit(solution)/shard_map/ppermute | solution.py:203
  54.2 5.3 %collective-permute-done.19 = bf16[24,1536]{1,0:T(8,128)(2,1)S(1)} collective-permute-done((bf16[24,1536]{1,0:T(8,128)(2,1)S(1)}, bf16[24,1536]{1,0:T(8,128)(2,1)S(1)}, u32[]{:S(2)}, u32[]{:S(2)}) %collective-permute-start.19) | collective-permute-done | bytes 73760 | tf_op jit(solution)/shard_map/ppermute | solution.py:203
  59.4 0.0 collective-permute-done.20
  59.5 0.7 %fusion = bf16[24,3072]{1,0:T(8,128)(2,1)} fusion(f32[24,1536]{1,0:T(8,128)S(1)} %convert_add_fusion, f32[24,1536]{1,0:T(8,128)S(1)} %convert_add_fusion.1, f32[3072]{0:T(1024)S(1)} %copy-done.7), kind=kLoop, calls=%fused_computation.1 | loop fusion | flops 221184 | bytes 454656 | tf_op jit(solution)/shard_map/convert_element_type | solution.py:240
  (21 shorter events, 0.1 us)
Async XLA Ops:
  0.0 1.3 %copy-start = (bf16[384,1536]{1,0:T(8,128)(2,1)S(1)}, bf16[384,1536]{1,0:T(8,128)(2,1)}, u32[]{:S(2)}) copy-start(bf16[384,1536]{1,0:T(8,128)(2,1)} %refs_3_.1) | copy-start | bytes 3538948
  1.3 1.3 %copy-start.1 = (bf16[384,1536]{1,0:T(8,128)(2,1)S(1)}, bf16[384,1536]{1,0:T(8,128)(2,1)}, u32[]{:S(2)}) copy-start(bf16[384,1536]{1,0:T(8,128)(2,1)} %refs_4_.1) | copy-start | bytes 3538948
  2.5 1.1 %copy-start.2 = (bf16[96,3072]{1,0:T(8,128)(2,1)S(1)}, bf16[96,3072]{1,0:T(8,128)(2,1)}, u32[]{:S(2)}) copy-start(bf16[96,3072]{1,0:T(8,128)(2,1)} %refs_6_.1) | copy-start | bytes 1769476
  3.6 0.9 %copy-start.3 = (bf16[24,1536]{1,0:T(8,128)(2,1)S(1)}, bf16[24,1536]{1,0:T(8,128)(2,1)}, u32[]{:S(2)}) copy-start(bf16[24,1536]{1,0:T(8,128)(2,1)} %refs_0_.1) | copy-start | bytes 221188
  4.5 0.9 %copy-start.4 = (bf16[24,1536]{1,0:T(8,128)(2,1)S(1)}, bf16[24,1536]{1,0:T(8,128)(2,1)}, u32[]{:S(2)}) copy-start(bf16[24,1536]{1,0:T(8,128)(2,1)} %refs_1_.1) | copy-start | bytes 221188
  5.4 0.9 %copy-start.5 = (bf16[24,1536]{1,0:T(8,128)(2,1)S(1)}, bf16[24,1536]{1,0:T(8,128)(2,1)}, u32[]{:S(2)}) copy-start(bf16[24,1536]{1,0:T(8,128)(2,1)} %refs_2_.1) | copy-start | bytes 221188
  6.3 0.8 %copy-start.6 = (s32[384,24]{0,1:T(8,128)S(1)}, s32[384,24]{0,1:T(8,128)}, u32[]{:S(2)}) copy-start(s32[384,24]{0,1:T(8,128)} %param.13) | copy-start | bytes 110596
  8.4 7.4 %collective-permute-start = (bf16[24,768]{1,0:T(8,128)(2,1)S(1)}, bf16[24,768]{1,0:T(8,128)(2,1)S(1)}, u32[]{:S(2)}, u32[]{:S(2)}) collective-permute-start(bf16[24,768]{1,0:T(8,128)(2,1)S(1)} %get-tuple-element.31), channel_id=1, source_target_pairs={{0,4},{1,5},{2,6},{3,7},{4,0},{5,1},{6,2},{7,3},{8,12},{9,13},{10,... | collective-permute-start | bytes 110600 | tf_op jit(solution)/shard_map/ppermute | solution.py:203
  11.5 5.5 %collective-permute-start.1 = (bf16[24,768]{1,0:T(8,128)(2,1)S(1)}, bf16[24,768]{1,0:T(8,128)(2,1)S(1)}, u32[]{:S(2)}, u32[]{:S(2)}) collective-permute-start(bf16[24,768]{1,0:T(8,128)(2,1)S(1)} %get-tuple-element.32), channel_id=1, source_target_pairs={{0,8},{1,9},{2,10},{3,11},{4,12},{5,13},{6,14},{7,15},{8,0},{9,1},... | collective-permute-start | bytes 110600 | tf_op jit(solution)/shard_map/ppermute | solution.py:203
  14.1 5.8 %collective-permute-start.2 = (bf16[24,768]{1,0:T(8,128)(2,1)S(1)}, bf16[24,768]{1,0:T(8,128)(2,1)S(1)}, u32[]{:S(2)}, u32[]{:S(2)}) collective-permute-start(bf16[24,768]{1,0:T(8,128)(2,1)S(1)} %get-tuple-element.33), channel_id=1, source_target_pairs={{0,12},{1,13},{2,14},{3,15},{4,8},{5,9},{6,10},{7,11},{8,4},{9,5},... | collective-permute-start | bytes 110600 | tf_op jit(solution)/shard_map/ppermute | solution.py:203
  14.1 9.7 %collective-permute-start.10 = (bf16[96,1536]{1,0:T(8,128)(2,1)S(1)}, bf16[96,1536]{1,0:T(8,128)(2,1)S(1)}, u32[]{:S(2)}, u32[]{:S(2)}) collective-permute-start(bf16[96,1536]{1,0:T(8,128)(2,1)S(1)} %get-tuple-element.39.refs_0_), channel_id=1, source_target_pairs={{0,2},{1,3},{2,0},{3,1},{4,6},{5,7},{6,4},{7,5},{8,10},{9,11},{10,... | collective-permute-start | bytes 884744 | tf_op jit(solution)/shard_map/ppermute | solution.py:206
  19.8 19.5 %collective-permute-start.7 = (bf16[96,768]{1,0:T(8,128)(2,1)S(1)}, bf16[96,768]{1,0:T(8,128)(2,1)S(1)}, u32[]{:S(2)}, u32[]{:S(2)}) collective-permute-start(bf16[96,768]{1,0:T(8,128)(2,1)S(1)} %constant_dynamic-update-slice_fusion.refs_4_), channel_id=1, source_target_pairs={{0,2},{1,3},{2,0},{3,1},{4,6},{5,7},{6,4},{7,5},{8,10},{9,11},{10,... | collective-permute-start | bytes 442376 | tf_op jit(solution)/shard_map/ppermute | solution.py:206
  21.4 20.5 %collective-permute-start.9 = (bf16[96,1536]{1,0:T(8,128)(2,1)S(1)}, bf16[96,1536]{1,0:T(8,128)(2,1)S(1)}, u32[]{:S(2)}, u32[]{:S(2)}) collective-permute-start(bf16[96,1536]{1,0:T(8,128)(2,1)S(1)} %get-tuple-element.39.refs_0_), channel_id=1, source_target_pairs={{0,1},{1,0},{2,3},{3,2},{4,5},{5,4},{6,7},{7,6},{8,9},{9,8},{10,11... | collective-permute-start | bytes 884744 | tf_op jit(solution)/shard_map/ppermute | solution.py:206
  23.8 18.0 %collective-permute-start.11 = (bf16[96,1536]{1,0:T(8,128)(2,1)S(1)}, bf16[96,1536]{1,0:T(8,128)(2,1)S(1)}, u32[]{:S(2)}, u32[]{:S(2)}) collective-permute-start(bf16[96,1536]{1,0:T(8,128)(2,1)S(1)} %collective-permute-done.10.refs_2_), channel_id=1, source_target_pairs={{0,1},{1,0},{2,3},{3,2},{4,5},{5,4},{6,7},{7,6},{8,9},{9,8},{10,11... | collective-permute-start | bytes 884744 | tf_op jit(solution)/shard_map/ppermute | solution.py:206
  23.8 18.7 %collective-permute-start.16 = (bf16[96,1536]{1,0:T(8,128)(2,1)S(1)}, bf16[96,1536]{1,0:T(8,128)(2,1)S(1)}, u32[]{:S(2)}, u32[]{:S(2)}) collective-permute-start(bf16[96,1536]{1,0:T(8,128)(2,1)S(1)} %get-tuple-element.45.refs_0_), channel_id=1, source_target_pairs={{0,2},{1,3},{2,0},{3,1},{4,6},{5,7},{6,4},{7,5},{8,10},{9,11},{10,... | collective-permute-start | bytes 884744 | tf_op jit(solution)/shard_map/ppermute | solution.py:206
  25.3 5.6 %collective-permute-start.5 = (bf16[24,384]{1,0:T(8,128)(2,1)S(1)}, bf16[24,384]{1,0:T(8,128)(2,1)S(1)}, u32[]{:S(2)}, u32[]{:S(2)}) collective-permute-start(bf16[24,384]{1,0:T(8,128)(2,1)S(1)} %get-tuple-element.38), channel_id=1, source_target_pairs={{0,12},{1,13},{2,14},{3,15},{4,8},{5,9},{6,10},{7,11},{8,4},{9,5},... | collective-permute-start | bytes 55304 | tf_op jit(solution)/shard_map/ppermute | solution.py:203
  30.9 4.7 %collective-permute-start.4 = (bf16[24,384]{1,0:T(8,128)(2,1)S(1)}, bf16[24,384]{1,0:T(8,128)(2,1)S(1)}, u32[]{:S(2)}, u32[]{:S(2)}) collective-permute-start(bf16[24,384]{1,0:T(8,128)(2,1)S(1)} %get-tuple-element.36), channel_id=1, source_target_pairs={{0,8},{1,9},{2,10},{3,11},{4,12},{5,13},{6,14},{7,15},{8,0},{9,1},... | collective-permute-start | bytes 55304 | tf_op jit(solution)/shard_map/ppermute | solution.py:203
  35.5 3.8 %collective-permute-start.3 = (bf16[24,384]{1,0:T(8,128)(2,1)S(1)}, bf16[24,384]{1,0:T(8,128)(2,1)S(1)}, u32[]{:S(2)}, u32[]{:S(2)}) collective-permute-start(bf16[24,384]{1,0:T(8,128)(2,1)S(1)} %get-tuple-element.34), channel_id=1, source_target_pairs={{0,4},{1,5},{2,6},{3,7},{4,0},{5,1},{6,2},{7,3},{8,12},{9,13},{10,... | collective-permute-start | bytes 55304 | tf_op jit(solution)/shard_map/ppermute | solution.py:203
  39.3 1.4 %collective-permute-start.6 = (bf16[96,768]{1,0:T(8,128)(2,1)S(1)}, bf16[96,768]{1,0:T(8,128)(2,1)S(1)}, u32[]{:S(2)}, u32[]{:S(2)}) collective-permute-start(bf16[96,768]{1,0:T(8,128)(2,1)S(1)} %constant_dynamic-update-slice_fusion.refs_4_), channel_id=1, source_target_pairs={{0,1},{1,0},{2,3},{3,2},{4,5},{5,4},{6,7},{7,6},{8,9},{9,8},{10,11... | collective-permute-start | bytes 442376 | tf_op jit(solution)/shard_map/ppermute | solution.py:206
  39.3 1.6 %collective-permute-start.8 = (bf16[96,768]{1,0:T(8,128)(2,1)S(1)}, bf16[96,768]{1,0:T(8,128)(2,1)S(1)}, u32[]{:S(2)}, u32[]{:S(2)}) collective-permute-start(bf16[96,768]{1,0:T(8,128)(2,1)S(1)} %collective-permute-done.7.refs_6_), channel_id=1, source_target_pairs={{0,1},{1,0},{2,3},{3,2},{4,5},{5,4},{6,7},{7,6},{8,9},{9,8},{10,11... | collective-permute-start | bytes 442376 | tf_op jit(solution)/shard_map/ppermute | solution.py:206
  40.7 6.6 %collective-permute-start.15 = (bf16[96,1536]{1,0:T(8,128)(2,1)S(1)}, bf16[96,1536]{1,0:T(8,128)(2,1)S(1)}, u32[]{:S(2)}, u32[]{:S(2)}) collective-permute-start(bf16[96,1536]{1,0:T(8,128)(2,1)S(1)} %get-tuple-element.45.refs_0_), channel_id=1, source_target_pairs={{0,1},{1,0},{2,3},{3,2},{4,5},{5,4},{6,7},{7,6},{8,9},{9,8},{10,11... | collective-permute-start | bytes 884744 | tf_op jit(solution)/shard_map/ppermute | solution.py:206
  42.5 17.0 %copy-start.7 = (f32[3072]{0:T(1024)S(1)}, f32[3072]{0:T(1024)}, u32[]{:S(2)}) copy-start(f32[3072]{0:T(1024)} %param.15) | copy-start | bytes 36868
  42.5 4.8 %collective-permute-start.17 = (bf16[96,1536]{1,0:T(8,128)(2,1)S(1)}, bf16[96,1536]{1,0:T(8,128)(2,1)S(1)}, u32[]{:S(2)}, u32[]{:S(2)}) collective-permute-start(bf16[96,1536]{1,0:T(8,128)(2,1)S(1)} %collective-permute-done.16.refs_2_), channel_id=1, source_target_pairs={{0,1},{1,0},{2,3},{3,2},{4,5},{5,4},{6,7},{7,6},{8,9},{9,8},{10,11... | collective-permute-start | bytes 884744 | tf_op jit(solution)/shard_map/ppermute | solution.py:206
  42.9 9.2 %collective-permute-start.12 = (bf16[24,1536]{1,0:T(8,128)(2,1)S(1)}, bf16[24,1536]{1,0:T(8,128)(2,1)S(1)}, u32[]{:S(2)}, u32[]{:S(2)}) collective-permute-start(bf16[24,1536]{1,0:T(8,128)(2,1)S(1)} %get-tuple-element.41), channel_id=1, source_target_pairs={{0,4},{1,5},{2,6},{3,7},{4,0},{5,1},{6,2},{7,3},{8,12},{9,13},{10,... | collective-permute-start | bytes 221192 | tf_op jit(solution)/shard_map/ppermute | solution.py:203
  44.1 8.3 %collective-permute-start.13 = (bf16[24,1536]{1,0:T(8,128)(2,1)S(1)}, bf16[24,1536]{1,0:T(8,128)(2,1)S(1)}, u32[]{:S(2)}, u32[]{:S(2)}) collective-permute-start(bf16[24,1536]{1,0:T(8,128)(2,1)S(1)} %get-tuple-element.42), channel_id=1, source_target_pairs={{0,8},{1,9},{2,10},{3,11},{4,12},{5,13},{6,14},{7,15},{8,0},{9,1},... | collective-permute-start | bytes 221192 | tf_op jit(solution)/shard_map/ppermute | solution.py:203
  47.0 7.1 %collective-permute-start.14 = (bf16[24,1536]{1,0:T(8,128)(2,1)S(1)}, bf16[24,1536]{1,0:T(8,128)(2,1)S(1)}, u32[]{:S(2)}, u32[]{:S(2)}) collective-permute-start(bf16[24,1536]{1,0:T(8,128)(2,1)S(1)} %get-tuple-element.43), channel_id=1, source_target_pairs={{0,12},{1,13},{2,14},{3,15},{4,8},{5,9},{6,10},{7,11},{8,4},{9,5},... | collective-permute-start | bytes 221192 | tf_op jit(solution)/shard_map/ppermute | solution.py:203
  47.9 6.2 %collective-permute-start.18 = (bf16[24,1536]{1,0:T(8,128)(2,1)S(1)}, bf16[24,1536]{1,0:T(8,128)(2,1)S(1)}, u32[]{:S(2)}, u32[]{:S(2)}) collective-permute-start(bf16[24,1536]{1,0:T(8,128)(2,1)S(1)} %get-tuple-element.48), channel_id=1, source_target_pairs={{0,4},{1,5},{2,6},{3,7},{4,0},{5,1},{6,2},{7,3},{8,12},{9,13},{10,... | collective-permute-start | bytes 221192 | tf_op jit(solution)/shard_map/ppermute | solution.py:203
  48.3 11.1 %collective-permute-start.19 = (bf16[24,1536]{1,0:T(8,128)(2,1)S(1)}, bf16[24,1536]{1,0:T(8,128)(2,1)S(1)}, u32[]{:S(2)}, u32[]{:S(2)}) collective-permute-start(bf16[24,1536]{1,0:T(8,128)(2,1)S(1)} %get-tuple-element.49), channel_id=1, source_target_pairs={{0,8},{1,9},{2,10},{3,11},{4,12},{5,13},{6,14},{7,15},{8,0},{9,1},... | collective-permute-start | bytes 221192 | tf_op jit(solution)/shard_map/ppermute | solution.py:203
  52.1 7.3 %collective-permute-start.20 = (bf16[24,1536]{1,0:T(8,128)(2,1)S(1)}, bf16[24,1536]{1,0:T(8,128)(2,1)S(1)}, u32[]{:S(2)}, u32[]{:S(2)}) collective-permute-start(bf16[24,1536]{1,0:T(8,128)(2,1)S(1)} %get-tuple-element.50), channel_id=1, source_target_pairs={{0,12},{1,13},{2,14},{3,15},{4,8},{5,9},{6,10},{7,11},{8,4},{9,5},... | collective-permute-start | bytes 221192 | tf_op jit(solution)/shard_map/ppermute | solution.py:203

commit v4 on v3

--- a/solution.py
+++ b/solution.py
@@ -15,9 +15,10 @@
 
 
 def prepare_kernel(groups, members, chunks, *refs):
-    sources, (w_ref,) = refs[:6], refs[6:7]
-    qouts, kvouts, wouts = refs[7 : 7 + groups], refs[7 + groups : 7 + 2 * groups], refs[7 + 2 * groups :][:chunks]
-    query, key_new, value_new, kst, vst, est, packed, sems = refs[7 + 2 * groups + chunks :]
+    sources, w_ref = refs[:6], refs[6]
+    outs = refs[7:]
+    qout, fulls, kvouts, wouts = outs[0], outs[:groups], outs[groups : 2 * groups], outs[2 * groups : 2 * groups + chunks]
+    query, key_new, value_new, kst, vst, est, packed, sems = outs[2 * groups + chunks :]
     rows, width = query.shape
     me = lax.axis_index("patch")
     first = pl.multiple_of((me // 2) * (2 * rows), 2 * rows)
@@ -68,7 +69,12 @@
     for k in range(groups):
         target = (me // members) ^ k
         kvouts[k][...] = packed[target]
-        qouts[k][...] = query[:, pl.ds(pl.multiple_of(target * share, share), share)]
+        wanted = query[:, pl.ds(pl.multiple_of(target * share, share), share)]
+        if k == 0:
+            qout[...] = wanted
+        else:
+            fulls[k][:, :share] = wanted
+            fulls[k][:, share:] = packed[target]
     for m in moves:
         m.wait()
 
@@ -78,10 +84,12 @@
     share = width // groups
     depth, model = w_out.shape
     outs = (
-        [((rows, share), jnp.bfloat16)] * groups
+        [((rows, share), jnp.bfloat16)]
+        + [((rows, 3 * share), jnp.bfloat16)] * (groups - 1)
         + [((rows, 2 * share), jnp.bfloat16)] * groups
         + [((depth, model // chunks), jnp.bfloat16)] * chunks
     )
+    sources = (query, key_new, value_new, key_stale, value_stale, powers, w_out)
     result = pl.pallas_call(
         functools.partial(prepare_kernel, groups, members, chunks),
         out_shape=[jax.ShapeDtypeStruct(*o) for o in outs],
@@ -98,19 +106,19 @@
         cost_estimate=pl.CostEstimate(
             flops=10 * rows * width, bytes_accessed=14 * rows * width + 4 * depth * model, transcendentals=0
         ),
-    )(query, key_new, value_new, key_stale, value_stale, powers, w_out)
+    )(*(pltpu.with_memory_space_constraint(x, pltpu.HBM) for x in sources))
     return result[:groups], result[groups : 2 * groups], result[2 * groups :]
 
 
-def attend_kernel(groups, members, dim, *refs):
+def attend_kernel(groups, dim, *refs):
     queries = refs[:groups]
-    kvs = refs[groups : groups + members]
-    att, kv = refs[groups + members :]
+    kvs = refs[groups:-2]
+    att, kv = refs[-2:]
     share = att.shape[1]
     block = kvs[0].shape[0]
-    for j in range(members):
+    for j in range(len(kvs)):
         kv[j * block : (j + 1) * block] = kvs[j][...]
-    query = jnp.concatenate([q[...].astype(jnp.float32) for q in queries], axis=0).astype(jnp.bfloat16)
+    query = jnp.concatenate([q[:, :share].astype(jnp.float32) for q in queries], axis=0).astype(jnp.bfloat16)
     inverse = 1.0 / dim**0.5
     for h in range(share // dim):
         cols = slice(h * dim, (h + 1) * dim)
@@ -129,20 +137,21 @@
         att[:, cols] = (numer / total).astype(jnp.bfloat16)
 
 
-def attend(groups, members, dim, queries, kvs):
+def attend(groups, dim, queries, kvs):
     rows, share = queries[0].shape
     block = kvs[0].shape[0]
+    pieces = len(kvs)
     return pl.pallas_call(
-        functools.partial(attend_kernel, groups, members, dim),
+        functools.partial(attend_kernel, groups, dim),
         out_shape=jax.ShapeDtypeStruct((groups * rows, share), jnp.bfloat16),
-        in_specs=[VMEM] * (groups + members),
+        in_specs=[VMEM] * (groups + pieces),
         out_specs=VMEM,
-        scratch_shapes=[pltpu.VMEM((members * block, 2 * share), jnp.bfloat16)],
+        scratch_shapes=[pltpu.VMEM((pieces * block, 2 * share), jnp.bfloat16)],
         compiler_params=pltpu.CompilerParams(vmem_limit_bytes=24 * 1024 * 1024),
         cost_estimate=pl.CostEstimate(
-            flops=4 * groups * rows * members * block * share,
-            bytes_accessed=4 * members * block * share,
-            transcendentals=groups * rows * members * block * share // dim,
+            flops=4 * groups * rows * pieces * block * share,
+            bytes_accessed=4 * pieces * block * share,
+            transcendentals=groups * rows * pieces * block * share // dim,
         ),
     )(*queries, *kvs)
 
@@ -199,35 +208,45 @@
     members = patch // groups
     chunks = 2
 
-    def across(x, k):
-        return lax.ppermute(x, "patch", [(p, ((p // members) ^ k) * members + p % members) for p in range(patch)])
-
-    def within(x, j):
-        return lax.ppermute(x, "patch", [(p, p ^ j) for p in range(patch)])
+    def send(x, k, j):
+        return lax.ppermute(x, "patch", [(p, ((p // members) ^ k) * members + (p % members) ^ j) for p in range(patch)])
 
     def spread(pieces, bit):
         while bit:
             for j in list(pieces):
-                pieces[j ^ bit] = within(pieces[j], bit)
+                pieces[j ^ bit] = send(pieces[j], 0, bit)
             bit //= 2
         return [pieces[j] for j in range(members)]
 
     far = members // 2
-    queries, fresh, ws = prepare(
-        groups, members, chunks, query, key_new, value_new, key_stale, value_stale, exponents.T, w_out
-    )
-    fresh = [fresh[0]] + [across(fresh[k], k) for k in range(1, groups)]
-    both = jnp.concatenate(fresh, axis=0)
-    kvs = spread({0: both}, far)
-    queries = [queries[0]] + [across(after(queries[k], both), k) for k in range(1, groups)]
-    att = attend(groups, members, dim, queries, kvs)
+    rows = query.shape[0]
+    share = query.shape[1] // groups
+    result = prepare(groups, members, chunks, query, key_new, value_new, key_stale, value_stale, exponents.T, w_out)
+    queries, fresh, ws = result
+    others = [send(ws[0], 0, far)]
+    queries = list(queries)
+    halves = []
+    for ks in (range(groups - 1, groups // 2 - 1, -1), range(groups // 2 - 1, -1, -1)):
+        half = []
+        for k in ks:
+            for j in range(members - 2, -1, -2):
+                if j:
+                    half.append(send(fresh[k], k, j))
+                elif k:
+                    queries[k] = send(queries[k], k, 0)
+                    half.append(queries[k][:, share:])
+                else:
+                    half.append(fresh[0])
+        halves.append(jnp.concatenate(half, axis=0))
+    kvs = halves + [send(h, 0, 1) for h in halves]
+    for c in range(1, chunks):
+        others.append(send(after(ws[c], halves[0]), 0, far))
+    att = attend(groups, dim, queries, kvs)
     sums = []
     done = None
     for c in range(chunks):
-        own = ws[c] if c == 0 else after(ws[c], both)
-        other = within(own, far)
-        if done is not None:
-            other = after(other, *done)
+        other = others[c]
+        other = after(other, *(done if c else halves))
         pieces = spread({0: ws[c], far: other}, far // 2)
         if w_out.shape[0] % 16:
             order = (lax.axis_index("patch") % members) ^ jnp.arange(members)
@@ -235,7 +254,7 @@
         done = project(groups, members, att, pieces)
         total = done[0]
         for k in range(1, groups):
-            total = total + across(done[k], k).astype(jnp.float32)
+            total = total + send(done[k], k, 0).astype(jnp.float32)
         sums.append(total)
     return (jnp.concatenate(sums, axis=1) * gate[None, :]).astype(jnp.bfloat16)
 

time: 60.6 us -> 49.5 us (0.82)
  local copies, waits for them, and re-layouts: 7.04 us -> 0.02 us
  waiting for transfers between devices: 23.5 us -> 19.6 us
    unnamed x19 -> x2, local copies, waits for them, and re-layouts: 7.04 us -> 0.01 us
    ppermute x21, waiting for transfers between devices: 23.5 us -> 19.6 us  [send(): lax.ppermute(x, 'patch', [(p, (p // members ^ k) * members + p % members...]
  transfers between devices with their start and end apart: 21 -> 21, of which waited for: 10 -> 7; matrix products, arithmetic and copies ran while one was open for 0% -> 0% of each run, Pallas kernels for 4% -> 4%
where the time goes in v4:
time: 49.5 us; the launch traced here: 49.4 us
  starting transfers between devices  25.1 us (51%)
  waiting for transfers between devices  19.6 us (40%)
  Pallas kernels  3.63 us (7%)
  other arithmetic  0.78 us (2%)
    ppermute x21, starting transfers between devices, send(): lax.ppermute(x, 'patch', [(p, (p // members ^ k) * members + p % members...  25.1 us
    ppermute x21, waiting for transfers between devices, send(): lax.ppermute(x, 'patch', [(p, (p // members ^ k) * members + p % members...  19.6 us
    pallas_call x1, Pallas kernels, prepare(): pl.pallas_call(functools.partial(prepare_kernel, groups, members, chunks)...  1.42 us
    pallas_call x2, Pallas kernels, project(): pl.pallas_call(functools.partial(project_kernel, groups, members, len(ws)...  1.29 us
  transfers between devices with their start and end apart: 21, of which 7 were waited for; matrix products, arithmetic and copies ran while one was open for 0% of the time, Pallas kernels for 4%

profile of v4, /device:TPU:0, one launch (start us, length us, event | category | flops | bytes accessed | tf_op | source)
XLA Modules:
  0.0 49.4 jit_solution(5710506215168438152)
XLA Ops:
  0.0 1.4 %shard_map.82 = (bf16[24,384]{1,0:T(8,128)(2,1)S(1)}, bf16[24,1152]{1,0:T(8,128)(2,1)S(1)}, bf16[24,1152]{1,0:T(8,128)(2,1)S(1)}, bf16[24,1152]{1,0:T(8,128)(2,1...) custom-call(bf16[24,1536]{1,0:T(8,128)(2,1)} %refs_0_.1, ...), custom_call_target="tpu_custom_call" | custom-call | flops 368640 | bytes 1695744 | tf_op jit(solution)/shard_map/pallas_call | solution.py:93
  1.4 3.0 %collective-permute-start.10 = (bf16[96,1536]{1,0:T(8,128)(2,1)S(1)}, bf16[96,1536]{1,0:T(8,128)(2,1)S(1)}, u32[]{:S(2)}, u32[]{:S(2)}) collective-permute-start(bf16[96,1536]{1,0:T(8,128)(2,1)S(1)} %get-tuple-element.34.refs_0_), channel_id=1, source_target_pairs={{0,2},{1,3},{2,0},{3,1},{4,6},{5,7},{6,4},{7,5},{8,10},{9,11},{10,... | collective-permute-start | bytes 884744 | tf_op jit(solution)/shard_map/ppermute | solution.py:212
  4.5 1.6 %collective-permute-start = (bf16[24,1152]{1,0:T(8,128)(2,1)S(1)}, bf16[24,1152]{1,0:T(8,128)(2,1)S(1)}, u32[]{:S(2)}, u32[]{:S(2)}) collective-permute-start(bf16[24,1152]{1,0:T(8,128)(2,1)S(1)} %get-tuple-element.27), channel_id=1, source_target_pairs={{0,4},{1,5},{2,6},{3,7},{4,0},{5,1},{6,2},{7,3},{8,12},{9,13},{10,... | collective-permute-start | bytes 165896 | tf_op jit(solution)/shard_map/ppermute | solution.py:212
  6.0 0.5 %collective-permute-start.6 = (bf16[24,768]{1,0:T(8,128)(2,1)S(1)}, bf16[24,768]{1,0:T(8,128)(2,1)S(1)}, u32[]{:S(2)}, u32[]{:S(2)}) collective-permute-start(bf16[24,768]{1,0:T(8,128)(2,1)S(1)} %get-tuple-element.33), channel_id=1, source_target_pairs={{0,2},{1,3},{2,0},{3,1},{4,6},{5,7},{6,4},{7,5},{8,10},{9,11},{10,... | collective-permute-start | bytes 110600 | tf_op jit(solution)/shard_map/ppermute | solution.py:212
  6.5 1.4 %collective-permute-start.5 = (bf16[24,768]{1,0:T(8,128)(2,1)S(1)}, bf16[24,768]{1,0:T(8,128)(2,1)S(1)}, u32[]{:S(2)}, u32[]{:S(2)}) collective-permute-start(bf16[24,768]{1,0:T(8,128)(2,1)S(1)} %get-tuple-element.32), channel_id=1, source_target_pairs={{0,6},{1,7},{2,4},{3,5},{4,2},{5,3},{6,0},{7,1},{8,14},{9,15},{10,... | collective-permute-start | bytes 110600 | tf_op jit(solution)/shard_map/ppermute | solution.py:212
  7.9 3.6 %collective-permute-start.2 = (bf16[24,1152]{1,0:T(8,128)(2,1)S(1)}, bf16[24,1152]{1,0:T(8,128)(2,1)S(1)}, u32[]{:S(2)}, u32[]{:S(2)}) collective-permute-start(bf16[24,1152]{1,0:T(8,128)(2,1)S(1)} %get-tuple-element.29), channel_id=1, source_target_pairs={{0,12},{1,13},{2,14},{3,15},{4,8},{5,9},{6,10},{7,11},{8,4},{9,5},... | collective-permute-start | bytes 165896 | tf_op jit(solution)/shard_map/ppermute | solution.py:212
  11.6 0.0 collective-permute-done.refs_1_
  11.6 0.0 collective-permute-start.1
  11.6 1.5 %collective-permute-done.6 = bf16[24,768]{1,0:T(8,128)(2,1)S(1)} collective-permute-done((bf16[24,768]{1,0:T(8,128)(2,1)S(1)}, bf16[24,768]{1,0:T(8,128)(2,1)S(1)}, u32[]{:S(2)}, u32[]{:S(2)}) %collective-permute-start.6) | collective-permute-done | bytes 36896 | tf_op jit(solution)/shard_map/ppermute | solution.py:212
  13.0 4.8 %collective-permute-start.3 = (bf16[24,768]{1,0:T(8,128)(2,1)S(1)}, bf16[24,768]{1,0:T(8,128)(2,1)S(1)}, u32[]{:S(2)}, u32[]{:S(2)}) collective-permute-start(bf16[24,768]{1,0:T(8,128)(2,1)S(1)} %get-tuple-element.30), channel_id=1, source_target_pairs={{0,14},{1,15},{2,12},{3,13},{4,10},{5,11},{6,8},{7,9},{8,6},{9,7},... | collective-permute-start | bytes 110600 | tf_op jit(solution)/shard_map/ppermute | solution.py:212
  17.8 0.0 collective-permute-done.5
  17.8 0.0 collective-permute-start.4
  17.8 0.0 collective-permute-done.2.refs_3_
  17.9 0.1 collective-permute-start.9
  17.9 0.0 collective-permute-done.1.refs_2_
  18.0 1.8 %collective-permute-done.3 = bf16[24,768]{1,0:T(8,128)(2,1)S(1)} collective-permute-done((bf16[24,768]{1,0:T(8,128)(2,1)S(1)}, bf16[24,768]{1,0:T(8,128)(2,1)S(1)}, u32[]{:S(2)}, u32[]{:S(2)}) %collective-permute-start.3) | collective-permute-done | bytes 36896 | tf_op jit(solution)/shard_map/ppermute | solution.py:212
  19.8 3.8 %collective-permute-done.4 = bf16[24,768]{1,0:T(8,128)(2,1)S(1)} collective-permute-done((bf16[24,768]{1,0:T(8,128)(2,1)S(1)}, bf16[24,768]{1,0:T(8,128)(2,1)S(1)}, u32[]{:S(2)}, u32[]{:S(2)}) %collective-permute-start.4) | collective-permute-done | bytes 36896 | tf_op jit(solution)/shard_map/ppermute | solution.py:212
  23.6 0.0 collective-permute-done.10.refs_2_
  23.6 0.1 collective-permute-start.11
  23.7 0.6 %collective-permute-start.16 = (bf16[96,1536]{1,0:T(8,128)(2,1)S(1)}, bf16[96,1536]{1,0:T(8,128)(2,1)S(1)}, u32[]{:S(2)}, u32[]{:S(2)}) collective-permute-start(bf16[96,1536]{1,0:T(8,128)(2,1)S(1)} %get-tuple-element.41.refs_0_), channel_id=1, source_target_pairs={{0,2},{1,3},{2,0},{3,1},{4,6},{5,7},{6,4},{7,5},{8,10},{9,11},{10,... | collective-permute-start | bytes 884744 | tf_op jit(solution)/shard_map/ppermute | solution.py:212
  24.3 0.2 collective-permute-start.8
  24.4 0.3 collective-permute-start.7
  24.8 0.9 %collective-permute-done.8.refs_7_ = bf16[96,768]{1,0:T(8,128)(2,1)S(1)} collective-permute-done((bf16[96,768]{1,0:T(8,128)(2,1)S(1)}, bf16[96,768]{1,0:T(8,128)(2,1)S(1)}, u32[]{:S(2)}, u32[]{:S(2)}) %collective-permute-start.8) | collective-permute-done | bytes 147488 | tf_op jit(solution)/shard_map/ppermute | solution.py:212
  25.6 0.2 collective-permute-start.15
  25.8 0.0 collective-permute-done.7.refs_6_
  25.8 0.9 %shard_map.83.att = bf16[96,384]{1,0:T(8,128)(2,1)S(1)} custom-call(bf16[24,384]{1,0:T(8,128)(2,1)S(1)} %get-tuple-element.26.refs_0_, bf16[24,1152]{1,0:T(8,128)(2,1)S(1)} %collective-permute-done.refs_1_, bf16[24,1152]{1,0:T(8,128)(2,1)S(1)} %collective-permute-done.1.refs_2_, bf16[24,1152]{1,0:T(8,128)(2,1)S(1)} %collective-permute-done.2.refs_3_, ...), custom_call_target="tpu_custom_call" | custom-call | flops 56623104 | bytes 589824 | tf_op jit(solution)/shard_map/pallas_call | solution.py:144
  26.8 0.0 collective-permute-done.9.refs_1_
  26.8 0.0 collective-permute-done.11.refs_3_
  26.8 0.7 %shard_map.84 = (f32[24,1536]{1,0:T(8,128)S(1)}, bf16[24,1536]{1,0:T(8,128)(2,1)S(1)}, bf16[24,1536]{1,0:T(8,128)(2,1)S(1)}, bf16[24,1536]{1,0:T(8,128)(2,1)S(1)}) custom-call(bf16[96,384]{1,0:T(8,128)(2,1)S(1)} %shard_map.83.att, bf16[96,1536]{1,0:T(8,128)(2,1)S(1)} %get-tuple-element.34.refs_0_, bf16[96,1536]{1,0:T(8,128)(2,1)S(1)} %collective-permute-done.9.refs_1_, ...), custom_call_target="tpu_custom_call" | custom-call | flops 113246208 | bytes 1179648 | tf_op jit(solution)/shard_map/pallas_call | solution.py:186
  27.5 0.0 copy-start
  27.5 5.6 %collective-permute-done.16.refs_2_ = bf16[96,1536]{1,0:T(8,128)(2,1)S(1)} collective-permute-done((bf16[96,1536]{1,0:T(8,128)(2,1)S(1)}, bf16[96,1536]{1,0:T(8,128)(2,1)S(1)}, u32[]{:S(2)}, u32[]{:S(2)}) %collective-permute-start.16) | collective-permute-done | bytes 294944 | tf_op jit(solution)/shard_map/ppermute | solution.py:212
  33.1 0.0 collective-permute-start.17
  33.1 0.0 collective-permute-start.12
  33.1 1.3 %collective-permute-start.13 = (bf16[24,1536]{1,0:T(8,128)(2,1)S(1)}, bf16[24,1536]{1,0:T(8,128)(2,1)S(1)}, u32[]{:S(2)}, u32[]{:S(2)}) collective-permute-start(bf16[24,1536]{1,0:T(8,128)(2,1)S(1)} %get-tuple-element.38), channel_id=1, source_target_pairs={{0,8},{1,9},{2,10},{3,11},{4,12},{5,13},{6,14},{7,15},{8,0},{9,1},... | collective-permute-start | bytes 221192 | tf_op jit(solution)/shard_map/ppermute | solution.py:212
  34.4 3.1 %collective-permute-start.14 = (bf16[24,1536]{1,0:T(8,128)(2,1)S(1)}, bf16[24,1536]{1,0:T(8,128)(2,1)S(1)}, u32[]{:S(2)}, u32[]{:S(2)}) collective-permute-start(bf16[24,1536]{1,0:T(8,128)(2,1)S(1)} %get-tuple-element.39), channel_id=1, source_target_pairs={{0,12},{1,13},{2,14},{3,15},{4,8},{5,9},{6,10},{7,11},{8,4},{9,5},... | collective-permute-start | bytes 221192 | tf_op jit(solution)/shard_map/ppermute | solution.py:212
  37.5 0.0 collective-permute-done.15.refs_1_
  37.5 0.0 collective-permute-done.17.refs_3_
  37.5 0.6 %shard_map.85 = (f32[24,1536]{1,0:T(8,128)S(1)}, bf16[24,1536]{1,0:T(8,128)(2,1)S(1)}, bf16[24,1536]{1,0:T(8,128)(2,1)S(1)}, bf16[24,1536]{1,0:T(8,128)(2,1)S(1)}) custom-call(bf16[96,384]{1,0:T(8,128)(2,1)S(1)} %shard_map.83.att, bf16[96,1536]{1,0:T(8,128)(2,1)S(1)} %get-tuple-element.41.refs_0_, bf16[96,1536]{1,0:T(8,128)(2,1)S(1)} %collective-permute-done.15.refs_1_, ...), custom_call_target="tpu_custom_call" | custom-call | flops 113246208 | bytes 1179648 | tf_op jit(solution)/shard_map/pallas_call | solution.py:186
  38.2 0.1 collective-permute-start.18
  38.2 1.3 %collective-permute-start.19 = (bf16[24,1536]{1,0:T(8,128)(2,1)S(1)}, bf16[24,1536]{1,0:T(8,128)(2,1)S(1)}, u32[]{:S(2)}, u32[]{:S(2)}) collective-permute-start(bf16[24,1536]{1,0:T(8,128)(2,1)S(1)} %get-tuple-element.45), channel_id=1, source_target_pairs={{0,8},{1,9},{2,10},{3,11},{4,12},{5,13},{6,14},{7,15},{8,0},{9,1},... | collective-permute-start | bytes 221192 | tf_op jit(solution)/shard_map/ppermute | solution.py:212
  39.5 0.0 collective-permute-done.12
  39.5 3.1 %collective-permute-start.20 = (bf16[24,1536]{1,0:T(8,128)(2,1)S(1)}, bf16[24,1536]{1,0:T(8,128)(2,1)S(1)}, u32[]{:S(2)}, u32[]{:S(2)}) collective-permute-start(bf16[24,1536]{1,0:T(8,128)(2,1)S(1)} %get-tuple-element.46), channel_id=1, source_target_pairs={{0,12},{1,13},{2,14},{3,15},{4,8},{5,9},{6,10},{7,11},{8,4},{9,5},... | collective-permute-start | bytes 221192 | tf_op jit(solution)/shard_map/ppermute | solution.py:212
  42.6 0.0 collective-permute-done.13
  42.6 0.0 collective-permute-done.14
  42.7 0.7 %collective-permute-done.18 = bf16[24,1536]{1,0:T(8,128)(2,1)S(1)} collective-permute-done((bf16[24,1536]{1,0:T(8,128)(2,1)S(1)}, bf16[24,1536]{1,0:T(8,128)(2,1)S(1)}, u32[]{:S(2)}, u32[]{:S(2)}) %collective-permute-start.18) | collective-permute-done | bytes 73760 | tf_op jit(solution)/shard_map/ppermute | solution.py:212
  43.4 5.2 %collective-permute-done.19 = bf16[24,1536]{1,0:T(8,128)(2,1)S(1)} collective-permute-done((bf16[24,1536]{1,0:T(8,128)(2,1)S(1)}, bf16[24,1536]{1,0:T(8,128)(2,1)S(1)}, u32[]{:S(2)}, u32[]{:S(2)}) %collective-permute-start.19) | collective-permute-done | bytes 73760 | tf_op jit(solution)/shard_map/ppermute | solution.py:212
  48.6 0.0 collective-permute-done.20
  48.7 0.7 %fusion = bf16[24,3072]{1,0:T(8,128)(2,1)} fusion(f32[24,1536]{1,0:T(8,128)S(1)} %convert_add_fusion, f32[24,1536]{1,0:T(8,128)S(1)} %convert_add_fusion.1, f32[3072]{0:T(1024)S(1)} %copy-done), kind=kLoop, calls=%fused_computation.1 | loop fusion | flops 221184 | bytes 454656 | tf_op jit(solution)/shard_map/convert_element_type | solution.py:259
  (8 shorter events, 0.1 us)
Async XLA Ops:
  1.4 22.2 %collective-permute-start.10 = (bf16[96,1536]{1,0:T(8,128)(2,1)S(1)}, bf16[96,1536]{1,0:T(8,128)(2,1)S(1)}, u32[]{:S(2)}, u32[]{:S(2)}) collective-permute-start(bf16[96,1536]{1,0:T(8,128)(2,1)S(1)} %get-tuple-element.34.refs_0_), channel_id=1, source_target_pairs={{0,2},{1,3},{2,0},{3,1},{4,6},{5,7},{6,4},{7,5},{8,10},{9,11},{10,... | collective-permute-start | bytes 884744 | tf_op jit(solution)/shard_map/ppermute | solution.py:212
  4.5 7.1 %collective-permute-start = (bf16[24,1152]{1,0:T(8,128)(2,1)S(1)}, bf16[24,1152]{1,0:T(8,128)(2,1)S(1)}, u32[]{:S(2)}, u32[]{:S(2)}) collective-permute-start(bf16[24,1152]{1,0:T(8,128)(2,1)S(1)} %get-tuple-element.27), channel_id=1, source_target_pairs={{0,4},{1,5},{2,6},{3,7},{4,0},{5,1},{6,2},{7,3},{8,12},{9,13},{10,... | collective-permute-start | bytes 165896 | tf_op jit(solution)/shard_map/ppermute | solution.py:212
  6.0 7.0 %collective-permute-start.6 = (bf16[24,768]{1,0:T(8,128)(2,1)S(1)}, bf16[24,768]{1,0:T(8,128)(2,1)S(1)}, u32[]{:S(2)}, u32[]{:S(2)}) collective-permute-start(bf16[24,768]{1,0:T(8,128)(2,1)S(1)} %get-tuple-element.33), channel_id=1, source_target_pairs={{0,2},{1,3},{2,0},{3,1},{4,6},{5,7},{6,4},{7,5},{8,10},{9,11},{10,... | collective-permute-start | bytes 110600 | tf_op jit(solution)/shard_map/ppermute | solution.py:212
  6.5 11.3 %collective-permute-start.5 = (bf16[24,768]{1,0:T(8,128)(2,1)S(1)}, bf16[24,768]{1,0:T(8,128)(2,1)S(1)}, u32[]{:S(2)}, u32[]{:S(2)}) collective-permute-start(bf16[24,768]{1,0:T(8,128)(2,1)S(1)} %get-tuple-element.32), channel_id=1, source_target_pairs={{0,6},{1,7},{2,4},{3,5},{4,2},{5,3},{6,0},{7,1},{8,14},{9,15},{10,... | collective-permute-start | bytes 110600 | tf_op jit(solution)/shard_map/ppermute | solution.py:212
  7.9 9.9 %collective-permute-start.2 = (bf16[24,1152]{1,0:T(8,128)(2,1)S(1)}, bf16[24,1152]{1,0:T(8,128)(2,1)S(1)}, u32[]{:S(2)}, u32[]{:S(2)}) collective-permute-start(bf16[24,1152]{1,0:T(8,128)(2,1)S(1)} %get-tuple-element.29), channel_id=1, source_target_pairs={{0,12},{1,13},{2,14},{3,15},{4,8},{5,9},{6,10},{7,11},{8,4},{9,5},... | collective-permute-start | bytes 165896 | tf_op jit(solution)/shard_map/ppermute | solution.py:212
  11.6 6.4 %collective-permute-start.1 = (bf16[24,1152]{1,0:T(8,128)(2,1)S(1)}, bf16[24,1152]{1,0:T(8,128)(2,1)S(1)}, u32[]{:S(2)}, u32[]{:S(2)}) collective-permute-start(bf16[24,1152]{1,0:T(8,128)(2,1)S(1)} %get-tuple-element.28), channel_id=1, source_target_pairs={{0,8},{1,9},{2,10},{3,11},{4,12},{5,13},{6,14},{7,15},{8,0},{9,1},... | collective-permute-start | bytes 165896 | tf_op jit(solution)/shard_map/ppermute | solution.py:212
  13.0 6.7 %collective-permute-start.3 = (bf16[24,768]{1,0:T(8,128)(2,1)S(1)}, bf16[24,768]{1,0:T(8,128)(2,1)S(1)}, u32[]{:S(2)}, u32[]{:S(2)}) collective-permute-start(bf16[24,768]{1,0:T(8,128)(2,1)S(1)} %get-tuple-element.30), channel_id=1, source_target_pairs={{0,14},{1,15},{2,12},{3,13},{4,10},{5,11},{6,8},{7,9},{8,6},{9,7},... | collective-permute-start | bytes 110600 | tf_op jit(solution)/shard_map/ppermute | solution.py:212
  17.8 5.8 %collective-permute-start.4 = (bf16[24,768]{1,0:T(8,128)(2,1)S(1)}, bf16[24,768]{1,0:T(8,128)(2,1)S(1)}, u32[]{:S(2)}, u32[]{:S(2)}) collective-permute-start(bf16[24,768]{1,0:T(8,128)(2,1)S(1)} %get-tuple-element.31), channel_id=1, source_target_pairs={{0,10},{1,11},{2,8},{3,9},{4,14},{5,15},{6,12},{7,13},{8,2},{9,3},... | collective-permute-start | bytes 110600 | tf_op jit(solution)/shard_map/ppermute | solution.py:212
  17.9 8.9 %collective-permute-start.9 = (bf16[96,1536]{1,0:T(8,128)(2,1)S(1)}, bf16[96,1536]{1,0:T(8,128)(2,1)S(1)}, u32[]{:S(2)}, u32[]{:S(2)}) collective-permute-start(bf16[96,1536]{1,0:T(8,128)(2,1)S(1)} %get-tuple-element.34.refs_0_), channel_id=1, source_target_pairs={{0,1},{1,0},{2,3},{3,2},{4,5},{5,4},{6,7},{7,6},{8,9},{9,8},{10,11... | collective-permute-start | bytes 884744 | tf_op jit(solution)/shard_map/ppermute | solution.py:212
  23.6 3.2 %collective-permute-start.11 = (bf16[96,1536]{1,0:T(8,128)(2,1)S(1)}, bf16[96,1536]{1,0:T(8,128)(2,1)S(1)}, u32[]{:S(2)}, u32[]{:S(2)}) collective-permute-start(bf16[96,1536]{1,0:T(8,128)(2,1)S(1)} %collective-permute-done.10.refs_2_), channel_id=1, source_target_pairs={{0,1},{1,0},{2,3},{3,2},{4,5},{5,4},{6,7},{7,6},{8,9},{9,8},{10,11... | collective-permute-start | bytes 884744 | tf_op jit(solution)/shard_map/ppermute | solution.py:212
  23.7 9.4 %collective-permute-start.16 = (bf16[96,1536]{1,0:T(8,128)(2,1)S(1)}, bf16[96,1536]{1,0:T(8,128)(2,1)S(1)}, u32[]{:S(2)}, u32[]{:S(2)}) collective-permute-start(bf16[96,1536]{1,0:T(8,128)(2,1)S(1)} %get-tuple-element.41.refs_0_), channel_id=1, source_target_pairs={{0,2},{1,3},{2,0},{3,1},{4,6},{5,7},{6,4},{7,5},{8,10},{9,11},{10,... | collective-permute-start | bytes 884744 | tf_op jit(solution)/shard_map/ppermute | solution.py:212
  24.3 1.4 %collective-permute-start.8 = (bf16[96,768]{1,0:T(8,128)(2,1)S(1)}, bf16[96,768]{1,0:T(8,128)(2,1)S(1)}, u32[]{:S(2)}, u32[]{:S(2)}) collective-permute-start(bf16[96,768]{1,0:T(8,128)(2,1)S(1)} %pad_maximum_fusion.1.refs_5_), channel_id=1, source_target_pairs={{0,1},{1,0},{2,3},{3,2},{4,5},{5,4},{6,7},{7,6},{8,9},{9,8},{10,11... | collective-permute-start | bytes 442376 | tf_op jit(solution)/shard_map/ppermute | solution.py:212
  24.4 1.4 %collective-permute-start.7 = (bf16[96,768]{1,0:T(8,128)(2,1)S(1)}, bf16[96,768]{1,0:T(8,128)(2,1)S(1)}, u32[]{:S(2)}, u32[]{:S(2)}) collective-permute-start(bf16[96,768]{1,0:T(8,128)(2,1)S(1)} %pad_maximum_fusion.refs_4_), channel_id=1, source_target_pairs={{0,1},{1,0},{2,3},{3,2},{4,5},{5,4},{6,7},{7,6},{8,9},{9,8},{10,11... | collective-permute-start | bytes 442376 | tf_op jit(solution)/shard_map/ppermute | solution.py:212
  25.6 11.9 %collective-permute-start.15 = (bf16[96,1536]{1,0:T(8,128)(2,1)S(1)}, bf16[96,1536]{1,0:T(8,128)(2,1)S(1)}, u32[]{:S(2)}, u32[]{:S(2)}) collective-permute-start(bf16[96,1536]{1,0:T(8,128)(2,1)S(1)} %get-tuple-element.41.refs_0_), channel_id=1, source_target_pairs={{0,1},{1,0},{2,3},{3,2},{4,5},{5,4},{6,7},{7,6},{8,9},{9,8},{10,11... | collective-permute-start | bytes 884744 | tf_op jit(solution)/shard_map/ppermute | solution.py:212
  27.5 21.2 %copy-start = (f32[3072]{0:T(1024)S(1)}, f32[3072]{0:T(1024)}, u32[]{:S(2)}) copy-start(f32[3072]{0:T(1024)} %param.15) | copy-start | bytes 36868
  33.1 4.4 %collective-permute-start.17 = (bf16[96,1536]{1,0:T(8,128)(2,1)S(1)}, bf16[96,1536]{1,0:T(8,128)(2,1)S(1)}, u32[]{:S(2)}, u32[]{:S(2)}) collective-permute-start(bf16[96,1536]{1,0:T(8,128)(2,1)S(1)} %collective-permute-done.16.refs_2_), channel_id=1, source_target_pairs={{0,1},{1,0},{2,3},{3,2},{4,5},{5,4},{6,7},{7,6},{8,9},{9,8},{10,11... | collective-permute-start | bytes 884744 | tf_op jit(solution)/shard_map/ppermute | solution.py:212
  33.1 6.4 %collective-permute-start.12 = (bf16[24,1536]{1,0:T(8,128)(2,1)S(1)}, bf16[24,1536]{1,0:T(8,128)(2,1)S(1)}, u32[]{:S(2)}, u32[]{:S(2)}) collective-permute-start(bf16[24,1536]{1,0:T(8,128)(2,1)S(1)} %get-tuple-element.37), channel_id=1, source_target_pairs={{0,4},{1,5},{2,6},{3,7},{4,0},{5,1},{6,2},{7,3},{8,12},{9,13},{10,... | collective-permute-start | bytes 221192 | tf_op jit(solution)/shard_map/ppermute | solution.py:212
  33.1 9.5 %collective-permute-start.13 = (bf16[24,1536]{1,0:T(8,128)(2,1)S(1)}, bf16[24,1536]{1,0:T(8,128)(2,1)S(1)}, u32[]{:S(2)}, u32[]{:S(2)}) collective-permute-start(bf16[24,1536]{1,0:T(8,128)(2,1)S(1)} %get-tuple-element.38), channel_id=1, source_target_pairs={{0,8},{1,9},{2,10},{3,11},{4,12},{5,13},{6,14},{7,15},{8,0},{9,1},... | collective-permute-start | bytes 221192 | tf_op jit(solution)/shard_map/ppermute | solution.py:212
  34.4 8.2 %collective-permute-start.14 = (bf16[24,1536]{1,0:T(8,128)(2,1)S(1)}, bf16[24,1536]{1,0:T(8,128)(2,1)S(1)}, u32[]{:S(2)}, u32[]{:S(2)}) collective-permute-start(bf16[24,1536]{1,0:T(8,128)(2,1)S(1)} %get-tuple-element.39), channel_id=1, source_target_pairs={{0,12},{1,13},{2,14},{3,15},{4,8},{5,9},{6,10},{7,11},{8,4},{9,5},... | collective-permute-start | bytes 221192 | tf_op jit(solution)/shard_map/ppermute | solution.py:212
  38.2 5.3 %collective-permute-start.18 = (bf16[24,1536]{1,0:T(8,128)(2,1)S(1)}, bf16[24,1536]{1,0:T(8,128)(2,1)S(1)}, u32[]{:S(2)}, u32[]{:S(2)}) collective-permute-start(bf16[24,1536]{1,0:T(8,128)(2,1)S(1)} %get-tuple-element.44), channel_id=1, source_target_pairs={{0,4},{1,5},{2,6},{3,7},{4,0},{5,1},{6,2},{7,3},{8,12},{9,13},{10,... | collective-permute-start | bytes 221192 | tf_op jit(solution)/shard_map/ppermute | solution.py:212
  38.2 10.4 %collective-permute-start.19 = (bf16[24,1536]{1,0:T(8,128)(2,1)S(1)}, bf16[24,1536]{1,0:T(8,128)(2,1)S(1)}, u32[]{:S(2)}, u32[]{:S(2)}) collective-permute-start(bf16[24,1536]{1,0:T(8,128)(2,1)S(1)} %get-tuple-element.45), channel_id=1, source_target_pairs={{0,8},{1,9},{2,10},{3,11},{4,12},{5,13},{6,14},{7,15},{8,0},{9,1},... | collective-permute-start | bytes 221192 | tf_op jit(solution)/shard_map/ppermute | solution.py:212
  39.5 9.1 %collective-permute-start.20 = (bf16[24,1536]{1,0:T(8,128)(2,1)S(1)}, bf16[24,1536]{1,0:T(8,128)(2,1)S(1)}, u32[]{:S(2)}, u32[]{:S(2)}) collective-permute-start(bf16[24,1536]{1,0:T(8,128)(2,1)S(1)} %get-tuple-element.46), channel_id=1, source_target_pairs={{0,12},{1,13},{2,14},{3,15},{4,8},{5,9},{6,10},{7,11},{8,4},{9,5},... | collective-permute-start | bytes 221192 | tf_op jit(solution)/shard_map/ppermute | solution.py:212

commit v5 on v4

--- a/solution.py
+++ b/solution.py
@@ -17,8 +17,9 @@
 def prepare_kernel(groups, members, chunks, *refs):
     sources, w_ref = refs[:6], refs[6]
     outs = refs[7:]
-    qout, fulls, kvouts, wouts = outs[0], outs[:groups], outs[groups : 2 * groups], outs[2 * groups : 2 * groups + chunks]
-    query, key_new, value_new, kst, vst, est, packed, sems = outs[2 * groups + chunks :]
+    qout, kvout, fulls = outs[0], outs[1], outs[1 : 1 + groups]
+    wout, wparts = outs[1 + groups], outs[2 + groups : 2 + groups + chunks]
+    query, key_new, value_new, kst, vst, est, packed, sems = outs[2 + groups + chunks :]
     rows, width = query.shape
     me = lax.axis_index("patch")
     first = pl.multiple_of((me // 2) * (2 * rows), 2 * rows)
@@ -30,10 +31,13 @@
     }
     for i in order:
         copies[i].start()
-    part = w_ref.shape[1] // chunks
-    moves = [
-        pltpu.make_async_copy(w_ref.at[:, pl.ds(i * part, part)], wouts[i], sems.at[6 + i]) for i in range(chunks)
-    ]
+    moves = [pltpu.make_async_copy(w_ref, wout, sems.at[6])]
+    for i in range(chunks):
+        size, part = wparts[i].shape
+        left = sum(w.shape[1] for w in wparts[:i])
+        top = pl.multiple_of((lax.axis_index("groups") % 2) * size, size) if size < w_ref.shape[0] else 0
+        view = w_ref.at[pl.ds(top, size), pl.ds(left, part)]
+        moves.append(pltpu.make_async_copy(view, wparts[i], sems.at[7 + i]))
     for m in moves:
         m.start()
     heads = est.shape[0] // 2
@@ -68,10 +72,10 @@
     copies[0].wait()
     for k in range(groups):
         target = (me // members) ^ k
-        kvouts[k][...] = packed[target]
         wanted = query[:, pl.ds(pl.multiple_of(target * share, share), share)]
         if k == 0:
             qout[...] = wanted
+            kvout[...] = packed[target]
         else:
             fulls[k][:, :share] = wanted
             fulls[k][:, share:] = packed[target]
@@ -79,19 +83,19 @@
         m.wait()
 
 
-def prepare(groups, members, chunks, query, key_new, value_new, key_stale, value_stale, powers, w_out):
+def prepare(groups, members, chunks, split, query, key_new, value_new, key_stale, value_stale, powers, w_out):
     rows, width = query.shape
     share = width // groups
     depth, model = w_out.shape
     outs = (
-        [((rows, share), jnp.bfloat16)]
+        [((rows, share), jnp.bfloat16), ((rows, 2 * share), jnp.bfloat16)]
         + [((rows, 3 * share), jnp.bfloat16)] * (groups - 1)
-        + [((rows, 2 * share), jnp.bfloat16)] * groups
-        + [((depth, model // chunks), jnp.bfloat16)] * chunks
+        + [((depth, model), jnp.bfloat16)]
+        + [((depth // split, c), jnp.bfloat16) for c in chunks]
     )
     sources = (query, key_new, value_new, key_stale, value_stale, powers, w_out)
     result = pl.pallas_call(
-        functools.partial(prepare_kernel, groups, members, chunks),
+        functools.partial(prepare_kernel, groups, members, len(chunks)),
         out_shape=[jax.ShapeDtypeStruct(*o) for o in outs],
         in_specs=[HBM] * 7,
         out_specs=[VMEM] * len(outs),
@@ -100,14 +104,14 @@
         + [
             pltpu.VMEM(powers.shape, jnp.int32),
             pltpu.VMEM((groups, rows, 2 * share), jnp.bfloat16),
-            pltpu.SemaphoreType.DMA((6 + chunks,)),
+            pltpu.SemaphoreType.DMA((7 + len(chunks),)),
         ],
         compiler_params=pltpu.CompilerParams(vmem_limit_bytes=24 * 1024 * 1024),
         cost_estimate=pl.CostEstimate(
             flops=10 * rows * width, bytes_accessed=14 * rows * width + 4 * depth * model, transcendentals=0
         ),
     )(*(pltpu.with_memory_space_constraint(x, pltpu.HBM) for x in sources))
-    return result[:groups], result[groups : 2 * groups], result[2 * groups :]
+    return result[0], result[1 : 1 + groups], result[1 + groups], result[2 + groups :]
 
 
 def attend_kernel(groups, dim, *refs):
@@ -156,16 +160,23 @@
     )(*queries, *kvs)
 
 
-def project_kernel(groups, members, pieces, att, *refs):
-    ws = refs[:pieces]
-    outs = refs[pieces : pieces + groups]
-    wide, sems = refs[pieces + groups :]
-    depth = ws[0].shape[0]
+def project_kernel(groups, members, places, att, *refs):
+    ws = refs[: len(places)]
+    outs = refs[len(places) : len(places) + groups]
+    wide, sems = refs[len(places) + groups :]
     q = lax.axis_index("patch") % members
+    side = lax.axis_index("groups") % 2
     copies = []
-    for j in range(pieces):
-        at = pl.multiple_of((q ^ j) * depth, depth) if pieces > 1 else 0
-        copies.append(pltpu.make_async_copy(ws[j], wide.at[pl.ds(at, depth)], sems.at[j]))
+    for i, (piece, (j, flip, col)) in enumerate(zip(ws, places)):
+        size, part = piece.shape
+        row = 0
+        if j is not None:
+            row = (q ^ j) * (size if flip is None else 2 * size)
+            if flip is not None:
+                row = row + (side ^ flip) * size
+            row = pl.multiple_of(row, size)
+        view = wide.at[pl.ds(row, size), pl.ds(col, part)]
+        copies.append(pltpu.make_async_copy(piece, view, sems.at[i]))
     for c in copies:
         c.start()
     for c in copies:
@@ -179,37 +190,46 @@
             outs[k][:, cols] = part[k * rows : (k + 1) * rows].astype(outs[k].dtype)
 
 
-def project(groups, members, att, ws):
+def project(groups, members, att, model, pieces, places):
     rows = att.shape[0] // groups
     share = att.shape[1]
-    model = ws[0].shape[1]
     return pl.pallas_call(
-        functools.partial(project_kernel, groups, members, len(ws)),
+        functools.partial(project_kernel, groups, members, places),
         out_shape=[jax.ShapeDtypeStruct((rows, model), jnp.float32)]
         + [jax.ShapeDtypeStruct((rows, model), jnp.bfloat16)] * (groups - 1),
-        in_specs=[VMEM] + [ANY] * len(ws),
+        in_specs=[VMEM] + [ANY] * len(pieces),
         out_specs=[VMEM] * groups,
-        scratch_shapes=[pltpu.VMEM((share, model), jnp.bfloat16), pltpu.SemaphoreType.DMA((len(ws),))],
+        scratch_shapes=[pltpu.VMEM((share, model), jnp.bfloat16), pltpu.SemaphoreType.DMA((len(pieces),))],
         compiler_params=pltpu.CompilerParams(vmem_limit_bytes=24 * 1024 * 1024),
         cost_estimate=pl.CostEstimate(
             flops=2 * groups * rows * share * model, bytes_accessed=2 * share * model, transcendentals=0
         ),
-    )(att, *ws)
+    )(att, *pieces)
 
 
 def after(x, *others):
+    if not others:
+        return x
     return lax.optimization_barrier((x, *others))[0]
 
 
-def per_device(patch, query, key_new, value_new, key_stale, value_stale, exponents, w_out, gate):
+def per_device(parts, patch, query, key_new, value_new, key_stale, value_stale, exponents, w_out, gate):
     heads = exponents.shape[1] // 2
-    dim = query.shape[1] // heads
+    rows, width = query.shape
+    dim = width // heads
     groups = math.gcd(patch, heads)
     members = patch // groups
-    chunks = 2
+    share = width // groups
+    depth, model = w_out.shape
+    far = members // 2
+    shared = parts % 2 == 0 and depth % 32 == 0
+    chunks = [2 * model // 3, model // 3] if shared and model % 384 == 0 else [model]
 
     def send(x, k, j):
         return lax.ppermute(x, "patch", [(p, ((p // members) ^ k) * members + (p % members) ^ j) for p in range(patch)])
+
+    def swap(x):
+        return lax.ppermute(x, "groups", [(g, g ^ 1) for g in range(parts)])
 
     def spread(pieces, bit):
         while bit:
@@ -218,50 +238,46 @@
             bit //= 2
         return [pieces[j] for j in range(members)]
 
-    far = members // 2
-    rows = query.shape[0]
-    share = query.shape[1] // groups
-    result = prepare(groups, members, chunks, query, key_new, value_new, key_stale, value_stale, exponents.T, w_out)
-    queries, fresh, ws = result
-    others = [send(ws[0], 0, far)]
-    queries = list(queries)
-    halves = []
-    for ks in (range(groups - 1, groups // 2 - 1, -1), range(groups // 2 - 1, -1, -1)):
-        half = []
-        for k in ks:
-            for j in range(members - 2, -1, -2):
-                if j:
-                    half.append(send(fresh[k], k, j))
-                elif k:
-                    queries[k] = send(queries[k], k, 0)
-                    half.append(queries[k][:, share:])
-                else:
-                    half.append(fresh[0])
-        halves.append(jnp.concatenate(half, axis=0))
-    kvs = halves + [send(h, 0, 1) for h in halves]
-    for c in range(1, chunks):
-        others.append(send(after(ws[c], halves[0]), 0, far))
-    att = attend(groups, dim, queries, kvs)
-    sums = []
-    done = None
-    for c in range(chunks):
-        other = others[c]
-        other = after(other, *(done if c else halves))
-        pieces = spread({0: ws[c], far: other}, far // 2)
-        if w_out.shape[0] % 16:
-            order = (lax.axis_index("patch") % members) ^ jnp.arange(members)
-            pieces = [jnp.stack(pieces)[order].reshape(-1, pieces[0].shape[1])]
-        done = project(groups, members, att, pieces)
-        total = done[0]
-        for k in range(1, groups):
-            total = total + send(done[k], k, 0).astype(jnp.float32)
-        sums.append(total)
-    return (jnp.concatenate(sums, axis=1) * gate[None, :]).astype(jnp.bfloat16)
+    own_query, fresh, w_own, w_parts = prepare(
+        groups, members, chunks, 2 if shared else 1, query, key_new, value_new, key_stale, value_stale, exponents.T, w_out
+    )
+    arrived = [send(fresh[k], k, 0) for k in range(1, groups)]
+    both = jnp.concatenate([fresh[0]] + [x[:, share:] for x in arrived], axis=0)
+    mine = [send(w, 0, far) for w in w_parts] if shared else []
+    both = after(both, *mine)
+    kvs = spread({0: both}, far)
+    att = attend(groups, dim, [own_query] + arrived, kvs)
+
+    if shared:
+        pieces, places = [w_own], [(0, None, 0)]
+        others = []
+        for c, w in enumerate(mine):
+            left = sum(chunks[:c])
+            others += [(w, (far, 0, left)), (swap(w), (far, 1, left))]
+        bit = 1
+        while bit < far:
+            pieces, places = (
+                pieces + [send(after(x, both), 0, bit) for x in pieces],
+                places + [(p[0] ^ bit, p[1], p[2]) for p in places],
+            )
+            others = others + [(send(after(x, *(kvs if p[1] else [both])), 0, bit), (p[0] ^ bit, p[1], p[2])) for x, p in others]
+            bit *= 2
+        pieces = pieces + [x for x, _ in others]
+        places = places + [p for _, p in others]
+    else:
+        order = (lax.axis_index("patch") % members) ^ jnp.arange(members)
+        pieces = [jnp.stack(spread({0: w_parts[0]}, far))[order].reshape(-1, model)]
+        places = [(None, None, 0)]
+    sums = project(groups, members, att, model, pieces, places)
+    total = sums[0]
+    for k in range(1, groups):
+        total = total + send(sums[k], k, 0).astype(jnp.float32)
+    return (total * gate[None, :]).astype(jnp.bfloat16)
 
 
 def solution(mesh):
     return jax.shard_map(
-        functools.partial(per_device, mesh.shape["patch"]),
+        functools.partial(per_device, mesh.shape["groups"], mesh.shape["patch"]),
         mesh=mesh,
         in_specs=(
             P(("groups", "patch"), None),

time: 49.5 us -> 43.7 us (0.88)
  starting transfers between devices: 25.1 us -> 16.5 us
  waiting for transfers between devices: 19.6 us -> 22.6 us
    ppermute x21 -> x16, starting transfers between devices: 25.1 us -> 13.5 us  [send(): lax.ppermute(x, 'patch', [(p, (p // members ^ k) * members + p % members...]
    ppermute x0 -> x2, starting transfers between devices: none -> 2.98 us  [swap(): return lax.ppermute(x, 'groups', [(g, g ^ 1) for g in range(parts)])]
    ppermute x0 -> x2, waiting for transfers between devices: none -> 2.97 us  [swap(): return lax.ppermute(x, 'groups', [(g, g ^ 1) for g in range(parts)])]
    pallas_call x3 -> x2, Pallas kernels: 2.71 us -> 2.67 us  [the longest x1 1.48 us: prepare(): pl.pallas_call(functools.partial(prepare_kernel, groups, members, len(chu...]
    ppermute x21 -> x16, waiting for transfers between devices: 19.6 us -> 19.6 us  [send(): lax.ppermute(x, 'patch', [(p, (p // members ^ k) * members + p % members...]
  transfers between devices with their start and end apart: 21 -> 18, of which waited for: 7 -> 7; matrix products, arithmetic and copies ran while one was open for 0% -> 0% of each run, Pallas kernels for 4% -> 2%
where the time goes in v5:
time: 43.7 us; the launch traced here: 43.6 us
  waiting for transfers between devices  22.6 us (52%)
  starting transfers between devices  16.5 us (38%)
  Pallas kernels  3.6 us (8%)
  other arithmetic  0.76 us (2%)
    ppermute x16, waiting for transfers between devices, send(): lax.ppermute(x, 'patch', [(p, (p // members ^ k) * members + p % members...  19.6 us
    ppermute x16, starting transfers between devices, send(): lax.ppermute(x, 'patch', [(p, (p // members ^ k) * members + p % members...  13.5 us
    ppermute x2, starting transfers between devices, swap(): return lax.ppermute(x, 'groups', [(g, g ^ 1) for g in range(parts)])  2.98 us
    ppermute x2, waiting for transfers between devices, swap(): return lax.ppermute(x, 'groups', [(g, g ^ 1) for g in range(parts)])  2.97 us
    pallas_call x1, Pallas kernels, prepare(): pl.pallas_call(functools.partial(prepare_kernel, groups, members, len(chu...  1.48 us
    pallas_call x1, Pallas kernels, project(): pl.pallas_call(functools.partial(project_kernel, groups, members, places)...  1.19 us
    pallas_call x1, Pallas kernels, attend(): pl.pallas_call(functools.partial(attend_kernel, groups, dim), out_shape=j...  0.93 us
  transfers between devices with their start and end apart: 18, of which 7 were waited for; matrix products, arithmetic and copies ran while one was open for 0% of the time, Pallas kernels for 2%

profile of v5, /device:TPU:0, one launch (start us, length us, event | category | flops | bytes accessed | tf_op | source)
XLA Modules:
  0.0 43.6 jit_solution(10890516185937829395)
XLA Ops:
  0.0 1.5 %shard_map.82 = (bf16[24,384]{1,0:T(8,128)(2,1)S(1)}, bf16[24,768]{1,0:T(8,128)(2,1)S(1)}, bf16[24,1152]{1,0:T(8,128)(2,1)S(1)}, bf16[24,1152]{1,0:T(8,128)(2,1)...) custom-call(bf16[24,1536]{1,0:T(8,128)(2,1)} %refs_0_.1, ...), custom_call_target="tpu_custom_call" | custom-call | flops 368640 | bytes 1695744 | tf_op jit(solution)/shard_map/pallas_call | solution.py:97
  1.5 3.0 %collective-permute-start.3 = (bf16[48,2048]{1,0:T(8,128)(2,1)S(1)}, bf16[48,2048]{1,0:T(8,128)(2,1)S(1)}, u32[]{:S(2)}, u32[]{:S(2)}) collective-permute-start(bf16[48,2048]{1,0:T(8,128)(2,1)S(1)} %get-tuple-element.28), channel_id=1, source_target_pairs={{0,2},{1,3},{2,0},{3,1},{4,6},{5,7},{6,4},{7,5},{8,10},{9,11},{10,... | collective-permute-start | bytes 589832 | tf_op jit(solution)/shard_map/ppermute | solution.py:229
  4.5 1.6 %collective-permute-start = (bf16[24,1152]{1,0:T(8,128)(2,1)S(1)}, bf16[24,1152]{1,0:T(8,128)(2,1)S(1)}, u32[]{:S(2)}, u32[]{:S(2)}) collective-permute-start(bf16[24,1152]{1,0:T(8,128)(2,1)S(1)} %get-tuple-element.24), channel_id=1, source_target_pairs={{0,4},{1,5},{2,6},{3,7},{4,0},{5,1},{6,2},{7,3},{8,12},{9,13},{10,... | collective-permute-start | bytes 165896 | tf_op jit(solution)/shard_map/ppermute | solution.py:229
  6.1 2.6 %collective-permute-start.1 = (bf16[24,1152]{1,0:T(8,128)(2,1)S(1)}, bf16[24,1152]{1,0:T(8,128)(2,1)S(1)}, u32[]{:S(2)}, u32[]{:S(2)}) collective-permute-start(bf16[24,1152]{1,0:T(8,128)(2,1)S(1)} %get-tuple-element.25), channel_id=1, source_target_pairs={{0,8},{1,9},{2,10},{3,11},{4,12},{5,13},{6,14},{7,15},{8,0},{9,1},... | collective-permute-start | bytes 165896 | tf_op jit(solution)/shard_map/ppermute | solution.py:229
  8.7 0.2 collective-permute-start.2
  8.9 0.3 collective-permute-start.4
  9.2 0.0 collective-permute-done.refs_1_
  9.2 2.7 %collective-permute-done.1.refs_2_ = bf16[24,1152]{1,0:T(8,128)(2,1)S(1)} collective-permute-done((bf16[24,1152]{1,0:T(8,128)(2,1)S(1)}, bf16[24,1152]{1,0:T(8,128)(2,1)S(1)}, u32[]{:S(2)}, u32[]{:S(2)}) %collective-permute-start.1) | collective-permute-done | bytes 55328 | tf_op jit(solution)/shard_map/ppermute | solution.py:229
  11.9 2.7 %collective-permute-done.2.refs_3_ = bf16[24,1152]{1,0:T(8,128)(2,1)S(1)} collective-permute-done((bf16[24,1152]{1,0:T(8,128)(2,1)S(1)}, bf16[24,1152]{1,0:T(8,128)(2,1)S(1)}, u32[]{:S(2)}, u32[]{:S(2)}) %collective-permute-start.2) | collective-permute-done | bytes 55328 | tf_op jit(solution)/shard_map/ppermute | solution.py:229
  14.7 0.0 collective-permute-done.4.refs_4_
  14.7 0.0 collective-permute-done.3.refs_2_
  14.7 0.1 collective-permute-start.8
  14.8 0.6 %collective-permute-start.6 = (bf16[96,768]{1,0:T(8,128)(2,1)S(1)}, bf16[96,768]{1,0:T(8,128)(2,1)S(1)}, u32[]{:S(2)}, u32[]{:S(2)}) collective-permute-start(bf16[96,768]{1,0:T(8,128)(2,1)S(1)} %pad_maximum_fusion.refs_4_), channel_id=1, source_target_pairs={{0,2},{1,3},{2,0},{3,1},{4,6},{5,7},{6,4},{7,5},{8,10},{9,11},{10,... | collective-permute-start | bytes 442376 | tf_op jit(solution)/shard_map/ppermute | solution.py:229
  15.3 1.5 %collective-permute-start.9 = (bf16[48,2048]{1,0:T(8,128)(2,1)S(1)}, bf16[48,2048]{1,0:T(8,128)(2,1)S(1)}, u32[]{:S(2)}, u32[]{:S(2)}) collective-permute-start(bf16[48,2048]{1,0:T(8,128)(2,1)S(1)} %collective-permute-done.3.refs_2_), channel_id=1, source_target_pairs={{0,16},{16,0},{1,17},{17,1},{2,18},{18,2},{3,19},{19,3},{4,20},{20... | collective-permute-start | bytes 589832 | tf_op jit(solution)/shard_map/ppermute | solution.py:232
  16.8 0.0 collective-permute-start.5
  16.8 4.2 %collective-permute-done.6.refs_6_ = bf16[96,768]{1,0:T(8,128)(2,1)S(1)} collective-permute-done((bf16[96,768]{1,0:T(8,128)(2,1)S(1)}, bf16[96,768]{1,0:T(8,128)(2,1)S(1)}, u32[]{:S(2)}, u32[]{:S(2)}) %collective-permute-start.6) | collective-permute-done | bytes 147488 | tf_op jit(solution)/shard_map/ppermute | solution.py:229
  21.0 0.0 collective-permute-start.7
  21.0 1.5 %collective-permute-start.10 = (bf16[48,1024]{1,0:T(8,128)(2,1)S(1)}, bf16[48,1024]{1,0:T(8,128)(2,1)S(1)}, u32[]{:S(2)}, u32[]{:S(2)}) collective-permute-start(bf16[48,1024]{1,0:T(8,128)(2,1)S(1)} %collective-permute-done.4.refs_4_), channel_id=1, source_target_pairs={{0,16},{16,0},{1,17},{17,1},{2,18},{18,2},{3,19},{19,3},{4,20},{20... | collective-permute-start | bytes 294920 | tf_op jit(solution)/shard_map/ppermute | solution.py:232
  22.5 0.0 collective-permute-done.5.refs_5_
  22.5 0.2 collective-permute-start.11
  22.7 0.0 collective-permute-done.9.refs_3_
  22.8 0.0 collective-permute-done.7.refs_7_
  22.8 0.3 collective-permute-start.12
  23.0 0.2 collective-permute-start.13
  23.3 3.0 %collective-permute-done.10.refs_5_ = bf16[48,1024]{1,0:T(8,128)(2,1)S(1)} collective-permute-done((bf16[48,1024]{1,0:T(8,128)(2,1)S(1)}, bf16[48,1024]{1,0:T(8,128)(2,1)S(1)}, u32[]{:S(2)}, u32[]{:S(2)}) %collective-permute-start.10) | collective-permute-done | bytes 98336 | tf_op jit(solution)/shard_map/ppermute | solution.py:232
  26.2 0.0 collective-permute-start.14
  26.2 0.9 %shard_map.83.att = bf16[96,384]{1,0:T(8,128)(2,1)S(1)} custom-call(bf16[24,384]{1,0:T(8,128)(2,1)S(1)} %get-tuple-element.23.refs_0_, bf16[24,1152]{1,0:T(8,128)(2,1)S(1)} %collective-permute-done.refs_1_, bf16[24,1152]{1,0:T(8,128)(2,1)S(1)} %collective-permute-done.1.refs_2_, bf16[24,1152]{1,0:T(8,128)(2,1)S(1)} %collective-permute-done.2.refs_3_, ...), custom_call_target="tpu_custom_call" | custom-call | flops 56623104 | bytes 589824 | tf_op jit(solution)/shard_map/pallas_call | solution.py:148
  27.2 0.0 copy-start
  27.2 0.0 collective-permute-done.13.refs_8_
  27.2 0.0 collective-permute-done.11.refs_6_
  27.2 0.3 collective-permute-done.14.refs_9_
  27.5 0.0 collective-permute-done.12.refs_7_
  27.5 0.0 collective-permute-done.8.refs_1_
  27.5 1.2 %shard_map.84 = (f32[24,3072]{1,0:T(8,128)S(1)}, bf16[24,3072]{1,0:T(8,128)(2,1)S(1)}, bf16[24,3072]{1,0:T(8,128)(2,1)S(1)}, bf16[24,3072]{1,0:T(8,128)(2,1)S(1)}) custom-call(bf16[96,384]{1,0:T(8,128)(2,1)S(1)} %shard_map.83.att, bf16[96,3072]{1,0:T(8,128)(2,1)S(1)} %get-tuple-element.32.refs_0_, bf16[96,3072]{1,0:T(8,128)(2,1)S(1)} %collective-permute-done.8.refs_1_, ...), custom_call_target="tpu_custom_call" | custom-call | flops 226492416 | bytes 2359296 | tf_op jit(solution)/shard_map/pallas_call | solution.py:196
  28.7 0.1 collective-permute-start.15
  28.8 2.9 %collective-permute-start.16 = (bf16[24,3072]{1,0:T(8,128)(2,1)S(1)}, bf16[24,3072]{1,0:T(8,128)(2,1)S(1)}, u32[]{:S(2)}, u32[]{:S(2)}) collective-permute-start(bf16[24,3072]{1,0:T(8,128)(2,1)S(1)} %get-tuple-element.39), channel_id=1, source_target_pairs={{0,8},{1,9},{2,10},{3,11},{4,12},{5,13},{6,14},{7,15},{8,0},{9,1},... | collective-permute-start | bytes 442376 | tf_op jit(solution)/shard_map/ppermute | solution.py:229
  31.7 1.5 %collective-permute-start.17 = (bf16[24,3072]{1,0:T(8,128)(2,1)S(1)}, bf16[24,3072]{1,0:T(8,128)(2,1)S(1)}, u32[]{:S(2)}, u32[]{:S(2)}) collective-permute-start(bf16[24,3072]{1,0:T(8,128)(2,1)S(1)} %get-tuple-element.40), channel_id=1, source_target_pairs={{0,12},{1,13},{2,14},{3,15},{4,8},{5,9},{6,10},{7,11},{8,4},{9,5},... | collective-permute-start | bytes 442376 | tf_op jit(solution)/shard_map/ppermute | solution.py:229
  33.2 4.2 %collective-permute-done.15 = bf16[24,3072]{1,0:T(8,128)(2,1)S(1)} collective-permute-done((bf16[24,3072]{1,0:T(8,128)(2,1)S(1)}, bf16[24,3072]{1,0:T(8,128)(2,1)S(1)}, u32[]{:S(2)}, u32[]{:S(2)}) %collective-permute-start.15) | collective-permute-done | bytes 147488 | tf_op jit(solution)/shard_map/ppermute | solution.py:229
  37.4 5.4 %collective-permute-done.16 = bf16[24,3072]{1,0:T(8,128)(2,1)S(1)} collective-permute-done((bf16[24,3072]{1,0:T(8,128)(2,1)S(1)}, bf16[24,3072]{1,0:T(8,128)(2,1)S(1)}, u32[]{:S(2)}, u32[]{:S(2)}) %collective-permute-start.16) | collective-permute-done | bytes 147488 | tf_op jit(solution)/shard_map/ppermute | solution.py:229
  42.8 0.0 collective-permute-done.17
  42.8 0.0 copy-done
  42.8 0.8 %multiply_convert_fusion = bf16[24,3072]{1,0:T(8,128)(2,1)} fusion(bf16[24,3072]{1,0:T(8,128)(2,1)S(1)} %collective-permute-done.17, bf16[24,3072]{1,0:T(8,128)(2,1)S(1)} %collective-permute-done.16, f32[24,3072]{1,0:T(8,128)S(1)} %get-tuple-element.37, bf16[24,3072]{1,0:T(8,128)(2,1)S(1)} %collective-permute-done.15, f32[3072]{0:T(1024)S(1)} %copy-done), kind=kLoop, calls=%fused_computation | loop fusion | flops 589824 | bytes 897024 | tf_op jit(solution)/shard_map/convert_element_type | solution.py:275
  (4 shorter events, 0.0 us)
Async XLA Ops:
  1.5 13.2 %collective-permute-start.3 = (bf16[48,2048]{1,0:T(8,128)(2,1)S(1)}, bf16[48,2048]{1,0:T(8,128)(2,1)S(1)}, u32[]{:S(2)}, u32[]{:S(2)}) collective-permute-start(bf16[48,2048]{1,0:T(8,128)(2,1)S(1)} %get-tuple-element.28), channel_id=1, source_target_pairs={{0,2},{1,3},{2,0},{3,1},{4,6},{5,7},{6,4},{7,5},{8,10},{9,11},{10,... | collective-permute-start | bytes 589832 | tf_op jit(solution)/shard_map/ppermute | solution.py:229
  4.5 4.7 %collective-permute-start = (bf16[24,1152]{1,0:T(8,128)(2,1)S(1)}, bf16[24,1152]{1,0:T(8,128)(2,1)S(1)}, u32[]{:S(2)}, u32[]{:S(2)}) collective-permute-start(bf16[24,1152]{1,0:T(8,128)(2,1)S(1)} %get-tuple-element.24), channel_id=1, source_target_pairs={{0,4},{1,5},{2,6},{3,7},{4,0},{5,1},{6,2},{7,3},{8,12},{9,13},{10,... | collective-permute-start | bytes 165896 | tf_op jit(solution)/shard_map/ppermute | solution.py:229
  6.1 5.8 %collective-permute-start.1 = (bf16[24,1152]{1,0:T(8,128)(2,1)S(1)}, bf16[24,1152]{1,0:T(8,128)(2,1)S(1)}, u32[]{:S(2)}, u32[]{:S(2)}) collective-permute-start(bf16[24,1152]{1,0:T(8,128)(2,1)S(1)} %get-tuple-element.25), channel_id=1, source_target_pairs={{0,8},{1,9},{2,10},{3,11},{4,12},{5,13},{6,14},{7,15},{8,0},{9,1},... | collective-permute-start | bytes 165896 | tf_op jit(solution)/shard_map/ppermute | solution.py:229
  8.7 6.0 %collective-permute-start.2 = (bf16[24,1152]{1,0:T(8,128)(2,1)S(1)}, bf16[24,1152]{1,0:T(8,128)(2,1)S(1)}, u32[]{:S(2)}, u32[]{:S(2)}) collective-permute-start(bf16[24,1152]{1,0:T(8,128)(2,1)S(1)} %get-tuple-element.26), channel_id=1, source_target_pairs={{0,12},{1,13},{2,14},{3,15},{4,8},{5,9},{6,10},{7,11},{8,4},{9,5},... | collective-permute-start | bytes 165896 | tf_op jit(solution)/shard_map/ppermute | solution.py:229
  8.9 5.8 %collective-permute-start.4 = (bf16[48,1024]{1,0:T(8,128)(2,1)S(1)}, bf16[48,1024]{1,0:T(8,128)(2,1)S(1)}, u32[]{:S(2)}, u32[]{:S(2)}) collective-permute-start(bf16[48,1024]{1,0:T(8,128)(2,1)S(1)} %get-tuple-element.29), channel_id=1, source_target_pairs={{0,2},{1,3},{2,0},{3,1},{4,6},{5,7},{6,4},{7,5},{8,10},{9,11},{10,... | collective-permute-start | bytes 294920 | tf_op jit(solution)/shard_map/ppermute | solution.py:229
  14.7 12.9 %collective-permute-start.8 = (bf16[96,3072]{1,0:T(8,128)(2,1)S(1)}, bf16[96,3072]{1,0:T(8,128)(2,1)S(1)}, u32[]{:S(2)}, u32[]{:S(2)}) collective-permute-start(bf16[96,3072]{1,0:T(8,128)(2,1)S(1)} %get-tuple-element.32.refs_0_), channel_id=1, source_target_pairs={{0,1},{1,0},{2,3},{3,2},{4,5},{5,4},{6,7},{7,6},{8,9},{9,8},{10,11... | collective-permute-start | bytes 1769480 | tf_op jit(solution)/shard_map/ppermute | solution.py:229
  14.8 6.3 %collective-permute-start.6 = (bf16[96,768]{1,0:T(8,128)(2,1)S(1)}, bf16[96,768]{1,0:T(8,128)(2,1)S(1)}, u32[]{:S(2)}, u32[]{:S(2)}) collective-permute-start(bf16[96,768]{1,0:T(8,128)(2,1)S(1)} %pad_maximum_fusion.refs_4_), channel_id=1, source_target_pairs={{0,2},{1,3},{2,0},{3,1},{4,6},{5,7},{6,4},{7,5},{8,10},{9,11},{10,... | collective-permute-start | bytes 442376 | tf_op jit(solution)/shard_map/ppermute | solution.py:229
  15.3 7.4 %collective-permute-start.9 = (bf16[48,2048]{1,0:T(8,128)(2,1)S(1)}, bf16[48,2048]{1,0:T(8,128)(2,1)S(1)}, u32[]{:S(2)}, u32[]{:S(2)}) collective-permute-start(bf16[48,2048]{1,0:T(8,128)(2,1)S(1)} %collective-permute-done.3.refs_2_), channel_id=1, source_target_pairs={{0,16},{16,0},{1,17},{17,1},{2,18},{18,2},{3,19},{19,3},{4,20},{20... | collective-permute-start | bytes 589832 | tf_op jit(solution)/shard_map/ppermute | solution.py:232
  16.8 5.7 %collective-permute-start.5 = (bf16[96,768]{1,0:T(8,128)(2,1)S(1)}, bf16[96,768]{1,0:T(8,128)(2,1)S(1)}, u32[]{:S(2)}, u32[]{:S(2)}) collective-permute-start(bf16[96,768]{1,0:T(8,128)(2,1)S(1)} %pad_maximum_fusion.refs_4_), channel_id=1, source_target_pairs={{0,1},{1,0},{2,3},{3,2},{4,5},{5,4},{6,7},{7,6},{8,9},{9,8},{10,11... | collective-permute-start | bytes 442376 | tf_op jit(solution)/shard_map/ppermute | solution.py:229
  21.0 1.7 %collective-permute-start.7 = (bf16[96,768]{1,0:T(8,128)(2,1)S(1)}, bf16[96,768]{1,0:T(8,128)(2,1)S(1)}, u32[]{:S(2)}, u32[]{:S(2)}) collective-permute-start(bf16[96,768]{1,0:T(8,128)(2,1)S(1)} %collective-permute-done.6.refs_6_), channel_id=1, source_target_pairs={{0,1},{1,0},{2,3},{3,2},{4,5},{5,4},{6,7},{7,6},{8,9},{9,8},{10,11... | collective-permute-start | bytes 442376 | tf_op jit(solution)/shard_map/ppermute | solution.py:229
  21.0 5.2 %collective-permute-start.10 = (bf16[48,1024]{1,0:T(8,128)(2,1)S(1)}, bf16[48,1024]{1,0:T(8,128)(2,1)S(1)}, u32[]{:S(2)}, u32[]{:S(2)}) collective-permute-start(bf16[48,1024]{1,0:T(8,128)(2,1)S(1)} %collective-permute-done.4.refs_4_), channel_id=1, source_target_pairs={{0,16},{16,0},{1,17},{17,1},{2,18},{18,2},{3,19},{19,3},{4,20},{20... | collective-permute-start | bytes 294920 | tf_op jit(solution)/shard_map/ppermute | solution.py:232
  22.5 4.7 %collective-permute-start.11 = (bf16[48,2048]{1,0:T(8,128)(2,1)S(1)}, bf16[48,2048]{1,0:T(8,128)(2,1)S(1)}, u32[]{:S(2)}, u32[]{:S(2)}) collective-permute-start(bf16[48,2048]{1,0:T(8,128)(2,1)S(1)} %collective-permute-done.3.refs_2_), channel_id=1, source_target_pairs={{0,1},{1,0},{2,3},{3,2},{4,5},{5,4},{6,7},{7,6},{8,9},{9,8},{10,11... | collective-permute-start | bytes 589832 | tf_op jit(solution)/shard_map/ppermute | solution.py:229
  22.8 4.8 %collective-permute-start.12 = (bf16[48,2048]{1,0:T(8,128)(2,1)S(1)}, bf16[48,2048]{1,0:T(8,128)(2,1)S(1)}, u32[]{:S(2)}, u32[]{:S(2)}) collective-permute-start(bf16[48,2048]{1,0:T(8,128)(2,1)S(1)} %collective-permute-done.9.refs_3_), channel_id=1, source_target_pairs={{0,1},{1,0},{2,3},{3,2},{4,5},{5,4},{6,7},{7,6},{8,9},{9,8},{10,11... | collective-permute-start | bytes 589832 | tf_op jit(solution)/shard_map/ppermute | solution.py:229
  23.0 4.1 %collective-permute-start.13 = (bf16[48,1024]{1,0:T(8,128)(2,1)S(1)}, bf16[48,1024]{1,0:T(8,128)(2,1)S(1)}, u32[]{:S(2)}, u32[]{:S(2)}) collective-permute-start(bf16[48,1024]{1,0:T(8,128)(2,1)S(1)} %collective-permute-done.4.refs_4_), channel_id=1, source_target_pairs={{0,1},{1,0},{2,3},{3,2},{4,5},{5,4},{6,7},{7,6},{8,9},{9,8},{10,11... | collective-permute-start | bytes 294920 | tf_op jit(solution)/shard_map/ppermute | solution.py:229
  26.2 1.3 %collective-permute-start.14 = (bf16[48,1024]{1,0:T(8,128)(2,1)S(1)}, bf16[48,1024]{1,0:T(8,128)(2,1)S(1)}, u32[]{:S(2)}, u32[]{:S(2)}) collective-permute-start(bf16[48,1024]{1,0:T(8,128)(2,1)S(1)} %collective-permute-done.10.refs_5_), channel_id=1, source_target_pairs={{0,1},{1,0},{2,3},{3,2},{4,5},{5,4},{6,7},{7,6},{8,9},{9,8},{10,11... | collective-permute-start | bytes 294920 | tf_op jit(solution)/shard_map/ppermute | solution.py:229
  27.2 15.7 %copy-start = (f32[3072]{0:T(1024)S(1)}, f32[3072]{0:T(1024)}, u32[]{:S(2)}) copy-start(f32[3072]{0:T(1024)} %param.15) | copy-start | bytes 36868
  28.7 8.7 %collective-permute-start.15 = (bf16[24,3072]{1,0:T(8,128)(2,1)S(1)}, bf16[24,3072]{1,0:T(8,128)(2,1)S(1)}, u32[]{:S(2)}, u32[]{:S(2)}) collective-permute-start(bf16[24,3072]{1,0:T(8,128)(2,1)S(1)} %get-tuple-element.38), channel_id=1, source_target_pairs={{0,4},{1,5},{2,6},{3,7},{4,0},{5,1},{6,2},{7,3},{8,12},{9,13},{10,... | collective-permute-start | bytes 442376 | tf_op jit(solution)/shard_map/ppermute | solution.py:229
  28.8 14.0 %collective-permute-start.16 = (bf16[24,3072]{1,0:T(8,128)(2,1)S(1)}, bf16[24,3072]{1,0:T(8,128)(2,1)S(1)}, u32[]{:S(2)}, u32[]{:S(2)}) collective-permute-start(bf16[24,3072]{1,0:T(8,128)(2,1)S(1)} %get-tuple-element.39), channel_id=1, source_target_pairs={{0,8},{1,9},{2,10},{3,11},{4,12},{5,13},{6,14},{7,15},{8,0},{9,1},... | collective-permute-start | bytes 442376 | tf_op jit(solution)/shard_map/ppermute | solution.py:229
  31.7 11.1 %collective-permute-start.17 = (bf16[24,3072]{1,0:T(8,128)(2,1)S(1)}, bf16[24,3072]{1,0:T(8,128)(2,1)S(1)}, u32[]{:S(2)}, u32[]{:S(2)}) collective-permute-start(bf16[24,3072]{1,0:T(8,128)(2,1)S(1)} %get-tuple-element.40), channel_id=1, source_target_pairs={{0,12},{1,13},{2,14},{3,15},{4,8},{5,9},{6,10},{7,11},{8,4},{9,5},... | collective-permute-start | bytes 442376 | tf_op jit(solution)/shard_map/ppermute | solution.py:229

commit v6 on v5

--- a/solution.py
+++ b/solution.py
@@ -142,7 +142,7 @@
 
 
 def attend(groups, dim, queries, kvs):
-    rows, share = queries[0].shape
+    rows, share = queries[-1].shape
     block = kvs[0].shape[0]
     pieces = len(kvs)
     return pl.pallas_call(
@@ -186,8 +186,8 @@
     for t in range(width // tile):
         cols = slice(t * tile, (t + 1) * tile)
         part = jnp.dot(att[...], wide[:, cols], preferred_element_type=jnp.float32)
-        for k in range(groups):
-            outs[k][:, cols] = part[k * rows : (k + 1) * rows].astype(outs[k].dtype)
+        for i in range(groups):
+            outs[i][:, cols] = part[i * rows : (i + 1) * rows].astype(outs[i].dtype)
 
 
 def project(groups, members, att, model, pieces, places):
@@ -195,8 +195,8 @@
     share = att.shape[1]
     return pl.pallas_call(
         functools.partial(project_kernel, groups, members, places),
-        out_shape=[jax.ShapeDtypeStruct((rows, model), jnp.float32)]
-        + [jax.ShapeDtypeStruct((rows, model), jnp.bfloat16)] * (groups - 1),
+        out_shape=[jax.ShapeDtypeStruct((rows, model), jnp.bfloat16)] * (groups - 1)
+        + [jax.ShapeDtypeStruct((rows, model), jnp.float32)],
         in_specs=[VMEM] + [ANY] * len(pieces),
         out_specs=[VMEM] * groups,
         scratch_shapes=[pltpu.VMEM((share, model), jnp.bfloat16), pltpu.SemaphoreType.DMA((len(pieces),))],
@@ -241,37 +241,47 @@
     own_query, fresh, w_own, w_parts = prepare(
         groups, members, chunks, 2 if shared else 1, query, key_new, value_new, key_stale, value_stale, exponents.T, w_out
     )
-    arrived = [send(fresh[k], k, 0) for k in range(1, groups)]
-    both = jnp.concatenate([fresh[0]] + [x[:, share:] for x in arrived], axis=0)
+    order = range(groups - 1, 0, -1)
+    arrived = [send(fresh[k], k, 0) for k in order]
+    both = jnp.concatenate([x[:, share:] for x in arrived] + [fresh[0]], axis=0)
     mine = [send(w, 0, far) for w in w_parts] if shared else []
     both = after(both, *mine)
-    kvs = spread({0: both}, far)
-    att = attend(groups, dim, [own_query] + arrived, kvs)
+    swapped = [swap(w) for w in mine]
+    pieces = {0: both}
+    bit = far
+    while bit:
+        for j in list(pieces):
+            relay = after(pieces[j], *swapped[:1]) if j else both
+            pieces[j ^ bit] = send(relay, 0, bit)
+        bit //= 2
+    kvs = [pieces[j] for j in range(members)]
+    kvs[-1] = after(kvs[-1], *swapped)
+    att = attend(groups, dim, arrived + [own_query], kvs)
 
     if shared:
         pieces, places = [w_own], [(0, None, 0)]
         others = []
         for c, w in enumerate(mine):
             left = sum(chunks[:c])
-            others += [(w, (far, 0, left)), (swap(w), (far, 1, left))]
+            others += [(w, (far, 0, left)), (swapped[c], (far, 1, left))]
         bit = 1
         while bit < far:
             pieces, places = (
                 pieces + [send(after(x, both), 0, bit) for x in pieces],
                 places + [(p[0] ^ bit, p[1], p[2]) for p in places],
             )
-            others = others + [(send(after(x, *(kvs if p[1] else [both])), 0, bit), (p[0] ^ bit, p[1], p[2])) for x, p in others]
+            others = others + [(send(after(x, both), 0, bit), (p[0] ^ bit, p[1], p[2])) for x, p in others]
             bit *= 2
         pieces = pieces + [x for x, _ in others]
         places = places + [p for _, p in others]
     else:
-        order = (lax.axis_index("patch") % members) ^ jnp.arange(members)
-        pieces = [jnp.stack(spread({0: w_parts[0]}, far))[order].reshape(-1, model)]
+        spots = (lax.axis_index("patch") % members) ^ jnp.arange(members)
+        pieces = [jnp.stack(spread({0: w_parts[0]}, far))[spots].reshape(-1, model)]
         places = [(None, None, 0)]
     sums = project(groups, members, att, model, pieces, places)
-    total = sums[0]
-    for k in range(1, groups):
-        total = total + send(sums[k], k, 0).astype(jnp.float32)
+    total = sums[-1]
+    for k, part in zip(order, sums):
+        total = total + send(part, k, 0).astype(jnp.float32)
     return (total * gate[None, :]).astype(jnp.bfloat16)
 
 

time: 43.7 us -> 43.1 us (0.986)
  starting transfers between devices: 16.5 us -> 15.6 us
    ppermute x16, waiting for transfers between devices: 19.6 us -> 21.4 us  [send(): lax.ppermute(x, 'patch', [(p, (p // members ^ k) * members + p % members...]
    ppermute x2, waiting for transfers between devices: 2.97 us -> 1.44 us  [swap(): return lax.ppermute(x, 'groups', [(g, g ^ 1) for g in range(parts)])]
    ppermute x2, starting transfers between devices: 2.98 us -> 1.87 us  [swap(): return lax.ppermute(x, 'groups', [(g, g ^ 1) for g in range(parts)])]
  transfers between devices with their start and end apart: 18 -> 18, of which waited for: 7 -> 10; matrix products, arithmetic and copies ran while one was open for 0% -> 0% of each run, Pallas kernels for 2% -> 2%
where the time goes in v6:
time: 43.1 us; the launch traced here: 42.9 us
  waiting for transfers between devices  22.8 us (53%)
  starting transfers between devices  15.6 us (36%)
  Pallas kernels  3.63 us (8%)
  other arithmetic  0.76 us (2%)
    ppermute x16, waiting for transfers between devices, send(): lax.ppermute(x, 'patch', [(p, (p // members ^ k) * members + p % members...  21.4 us
    ppermute x16, starting transfers between devices, send(): lax.ppermute(x, 'patch', [(p, (p // members ^ k) * members + p % members...  13.8 us
    ppermute x2, starting transfers between devices, swap(): return lax.ppermute(x, 'groups', [(g, g ^ 1) for g in range(parts)])  1.87 us
    pallas_call x1, Pallas kernels, prepare(): pl.pallas_call(functools.partial(prepare_kernel, groups, members, len(chu...  1.48 us
    ppermute x2, waiting for transfers between devices, swap(): return lax.ppermute(x, 'groups', [(g, g ^ 1) for g in range(parts)])  1.44 us
    pallas_call x1, Pallas kernels, project(): pl.pallas_call(functools.partial(project_kernel, groups, members, places)...  1.22 us
    pallas_call x1, Pallas kernels, attend(): pl.pallas_call(functools.partial(attend_kernel, groups, dim), out_shape=j...  0.93 us
  transfers between devices with their start and end apart: 18, of which 10 were waited for; matrix products, arithmetic and copies ran while one was open for 0% of the time, Pallas kernels for 2%

profile of v6, /device:TPU:0, one launch (start us, length us, event | category | flops | bytes accessed | tf_op | source)
XLA Modules:
  0.0 42.9 jit_solution(16217733417958722781)
XLA Ops:
  0.0 1.5 %shard_map.82 = (bf16[24,384]{1,0:T(8,128)(2,1)S(1)}, bf16[24,768]{1,0:T(8,128)(2,1)S(1)}, bf16[24,1152]{1,0:T(8,128)(2,1)S(1)}, bf16[24,1152]{1,0:T(8,128)(2,1)...) custom-call(bf16[24,1536]{1,0:T(8,128)(2,1)} %refs_0_.1, ...), custom_call_target="tpu_custom_call" | custom-call | flops 368640 | bytes 1695744 | tf_op jit(solution)/shard_map/pallas_call | solution.py:97
  1.5 3.0 %collective-permute-start.3 = (bf16[48,2048]{1,0:T(8,128)(2,1)S(1)}, bf16[48,2048]{1,0:T(8,128)(2,1)S(1)}, u32[]{:S(2)}, u32[]{:S(2)}) collective-permute-start(bf16[48,2048]{1,0:T(8,128)(2,1)S(1)} %get-tuple-element.30), channel_id=1, source_target_pairs={{0,2},{1,3},{2,0},{3,1},{4,6},{5,7},{6,4},{7,5},{8,10},{9,11},{10,... | collective-permute-start | bytes 589832 | tf_op jit(solution)/shard_map/ppermute | solution.py:229
  4.5 3.6 %collective-permute-start = (bf16[24,1152]{1,0:T(8,128)(2,1)S(1)}, bf16[24,1152]{1,0:T(8,128)(2,1)S(1)}, u32[]{:S(2)}, u32[]{:S(2)}) collective-permute-start(bf16[24,1152]{1,0:T(8,128)(2,1)S(1)} %get-tuple-element.25), channel_id=1, source_target_pairs={{0,12},{1,13},{2,14},{3,15},{4,8},{5,9},{6,10},{7,11},{8,4},{9,5},... | collective-permute-start | bytes 165896 | tf_op jit(solution)/shard_map/ppermute | solution.py:229
  8.1 0.0 collective-permute-start.1
  8.1 0.8 %collective-permute-start.2 = (bf16[24,1152]{1,0:T(8,128)(2,1)S(1)}, bf16[24,1152]{1,0:T(8,128)(2,1)S(1)}, u32[]{:S(2)}, u32[]{:S(2)}) collective-permute-start(bf16[24,1152]{1,0:T(8,128)(2,1)S(1)} %get-tuple-element.27), channel_id=1, source_target_pairs={{0,4},{1,5},{2,6},{3,7},{4,0},{5,1},{6,2},{7,3},{8,12},{9,13},{10,... | collective-permute-start | bytes 165896 | tf_op jit(solution)/shard_map/ppermute | solution.py:229
  8.9 0.3 collective-permute-start.4
  9.2 1.9 %collective-permute-done.refs_0_ = bf16[24,1152]{1,0:T(8,128)(2,1)S(1)} collective-permute-done((bf16[24,1152]{1,0:T(8,128)(2,1)S(1)}, bf16[24,1152]{1,0:T(8,128)(2,1)S(1)}, u32[]{:S(2)}, u32[]{:S(2)}) %collective-permute-start) | collective-permute-done | bytes 55328 | tf_op jit(solution)/shard_map/ppermute | solution.py:229
  11.1 2.0 %collective-permute-done.1.refs_1_ = bf16[24,1152]{1,0:T(8,128)(2,1)S(1)} collective-permute-done((bf16[24,1152]{1,0:T(8,128)(2,1)S(1)}, bf16[24,1152]{1,0:T(8,128)(2,1)S(1)}, u32[]{:S(2)}, u32[]{:S(2)}) %collective-permute-start.1) | collective-permute-done | bytes 55328 | tf_op jit(solution)/shard_map/ppermute | solution.py:229
  13.2 0.0 collective-permute-done.2.refs_2_
  13.2 0.3 collective-permute-done.4.refs_4_
  13.5 0.0 collective-permute-done.3.refs_2_
  13.5 0.0 collective-permute-start.10
  13.5 1.5 %collective-permute-start.7 = (bf16[48,2048]{1,0:T(8,128)(2,1)S(1)}, bf16[48,2048]{1,0:T(8,128)(2,1)S(1)}, u32[]{:S(2)}, u32[]{:S(2)}) collective-permute-start(bf16[48,2048]{1,0:T(8,128)(2,1)S(1)} %collective-permute-done.3.refs_2_), channel_id=1, source_target_pairs={{0,16},{16,0},{1,17},{17,1},{2,18},{18,2},{3,19},{19,3},{4,20},{20... | collective-permute-start | bytes 589832 | tf_op jit(solution)/shard_map/ppermute | solution.py:232
  15.0 0.5 %collective-permute-start.6 = (bf16[96,768]{1,0:T(8,128)(2,1)S(1)}, bf16[96,768]{1,0:T(8,128)(2,1)S(1)}, u32[]{:S(2)}, u32[]{:S(2)}) collective-permute-start(bf16[96,768]{1,0:T(8,128)(2,1)S(1)} %pad_maximum_fusion.refs_4_), channel_id=1, source_target_pairs={{0,2},{1,3},{2,0},{3,1},{4,6},{5,7},{6,4},{7,5},{8,10},{9,11},{10,... | collective-permute-start | bytes 442376 | tf_op jit(solution)/shard_map/ppermute | solution.py:229
  15.5 0.4 collective-permute-start.9
  15.9 0.0 collective-permute-start.5
  15.9 5.1 %collective-permute-done.6.refs_6_ = bf16[96,768]{1,0:T(8,128)(2,1)S(1)} collective-permute-done((bf16[96,768]{1,0:T(8,128)(2,1)S(1)}, bf16[96,768]{1,0:T(8,128)(2,1)S(1)}, u32[]{:S(2)}, u32[]{:S(2)}) %collective-permute-start.6) | collective-permute-done | bytes 147488 | tf_op jit(solution)/shard_map/ppermute | solution.py:229
  21.0 0.2 collective-permute-done.7.refs_3_
  21.2 0.0 collective-permute-start.8
  21.2 0.5 %collective-permute-start.11 = (bf16[48,2048]{1,0:T(8,128)(2,1)S(1)}, bf16[48,2048]{1,0:T(8,128)(2,1)S(1)}, u32[]{:S(2)}, u32[]{:S(2)}) collective-permute-start(bf16[48,2048]{1,0:T(8,128)(2,1)S(1)} %collective-permute-done.3.refs_2_), channel_id=1, source_target_pairs={{0,1},{1,0},{2,3},{3,2},{4,5},{5,4},{6,7},{7,6},{8,9},{9,8},{10,11... | collective-permute-start | bytes 589832 | tf_op jit(solution)/shard_map/ppermute | solution.py:229
  21.7 1.2 %collective-permute-done.9.refs_5_ = bf16[48,1024]{1,0:T(8,128)(2,1)S(1)} collective-permute-done((bf16[48,1024]{1,0:T(8,128)(2,1)S(1)}, bf16[48,1024]{1,0:T(8,128)(2,1)S(1)}, u32[]{:S(2)}, u32[]{:S(2)}) %collective-permute-start.9) | collective-permute-done | bytes 98336 | tf_op jit(solution)/shard_map/ppermute | solution.py:232
  23.0 0.0 collective-permute-start.12
  23.0 0.0 collective-permute-done.5.refs_5_
  23.0 0.5 %collective-permute-start.13 = (bf16[48,1024]{1,0:T(8,128)(2,1)S(1)}, bf16[48,1024]{1,0:T(8,128)(2,1)S(1)}, u32[]{:S(2)}, u32[]{:S(2)}) collective-permute-start(bf16[48,1024]{1,0:T(8,128)(2,1)S(1)} %collective-permute-done.4.refs_4_), channel_id=1, source_target_pairs={{0,1},{1,0},{2,3},{3,2},{4,5},{5,4},{6,7},{7,6},{8,9},{9,8},{10,11... | collective-permute-start | bytes 294920 | tf_op jit(solution)/shard_map/ppermute | solution.py:229
  23.5 0.0 collective-permute-done.8.refs_7_
  23.5 0.1 collective-permute-start.14
  23.5 0.9 %shard_map.83.att = bf16[96,384]{1,0:T(8,128)(2,1)S(1)} custom-call(bf16[24,1152]{1,0:T(8,128)(2,1)S(1)} %collective-permute-done.refs_0_, bf16[24,1152]{1,0:T(8,128)(2,1)S(1)} %collective-permute-done.1.refs_1_, bf16[24,1152]{1,0:T(8,128)(2,1)S(1)} %collective-permute-done.2.refs_2_, bf16[24,384]{1,0:T(8,128)(2,1)S(1)} %get-tuple-element.28.refs_3_, ...), custom_call_target="tpu_custom_call" | custom-call | flops 56623104 | bytes 589824 | tf_op jit(solution)/shard_map/pallas_call | solution.py:148
  24.5 0.0 copy-start
  24.5 0.1 collective-permute-done.13.refs_8_
  24.5 0.2 collective-permute-done.14.refs_9_
  24.8 0.0 collective-permute-done.11.refs_6_
  24.8 0.0 collective-permute-done.12.refs_7_
  24.8 0.0 collective-permute-done.10.refs_1_
  24.8 1.2 %shard_map.84 = (bf16[24,3072]{1,0:T(8,128)(2,1)S(1)}, bf16[24,3072]{1,0:T(8,128)(2,1)S(1)}, bf16[24,3072]{1,0:T(8,128)(2,1)S(1)}, f32[24,3072]{1,0:T(8,128)S(1)}) custom-call(bf16[96,384]{1,0:T(8,128)(2,1)S(1)} %shard_map.83.att, bf16[96,3072]{1,0:T(8,128)(2,1)S(1)} %get-tuple-element.36.refs_0_, bf16[96,3072]{1,0:T(8,128)(2,1)S(1)} %collective-permute-done.10.refs_1_, ...), custom_call_target="tpu_custom_call" | custom-call | flops 226492416 | bytes 2359296 | tf_op jit(solution)/shard_map/pallas_call | solution.py:196
  26.0 3.7 %collective-permute-start.15 = (bf16[24,3072]{1,0:T(8,128)(2,1)S(1)}, bf16[24,3072]{1,0:T(8,128)(2,1)S(1)}, u32[]{:S(2)}, u32[]{:S(2)}) collective-permute-start(bf16[24,3072]{1,0:T(8,128)(2,1)S(1)} %get-tuple-element.42), channel_id=1, source_target_pairs={{0,12},{1,13},{2,14},{3,15},{4,8},{5,9},{6,10},{7,11},{8,4},{9,5},... | collective-permute-start | bytes 442376 | tf_op jit(solution)/shard_map/ppermute | solution.py:229
  29.7 0.0 collective-permute-start.16
  29.7 0.8 %collective-permute-start.17 = (bf16[24,3072]{1,0:T(8,128)(2,1)S(1)}, bf16[24,3072]{1,0:T(8,128)(2,1)S(1)}, u32[]{:S(2)}, u32[]{:S(2)}) collective-permute-start(bf16[24,3072]{1,0:T(8,128)(2,1)S(1)} %get-tuple-element.44), channel_id=1, source_target_pairs={{0,4},{1,5},{2,6},{3,7},{4,0},{5,1},{6,2},{7,3},{8,12},{9,13},{10,... | collective-permute-start | bytes 442376 | tf_op jit(solution)/shard_map/ppermute | solution.py:229
  30.5 4.2 %collective-permute-done.15 = bf16[24,3072]{1,0:T(8,128)(2,1)S(1)} collective-permute-done((bf16[24,3072]{1,0:T(8,128)(2,1)S(1)}, bf16[24,3072]{1,0:T(8,128)(2,1)S(1)}, u32[]{:S(2)}, u32[]{:S(2)}) %collective-permute-start.15) | collective-permute-done | bytes 147488 | tf_op jit(solution)/shard_map/ppermute | solution.py:229
  34.7 7.5 %collective-permute-done.16 = bf16[24,3072]{1,0:T(8,128)(2,1)S(1)} collective-permute-done((bf16[24,3072]{1,0:T(8,128)(2,1)S(1)}, bf16[24,3072]{1,0:T(8,128)(2,1)S(1)}, u32[]{:S(2)}, u32[]{:S(2)}) %collective-permute-start.16) | collective-permute-done | bytes 147488 | tf_op jit(solution)/shard_map/ppermute | solution.py:229
  42.2 0.0 collective-permute-done.17
  42.2 0.0 copy-done
  42.2 0.7 %multiply_convert_fusion = bf16[24,3072]{1,0:T(8,128)(2,1)} fusion(bf16[24,3072]{1,0:T(8,128)(2,1)S(1)} %collective-permute-done.17, bf16[24,3072]{1,0:T(8,128)(2,1)S(1)} %collective-permute-done.16, f32[24,3072]{1,0:T(8,128)S(1)} %get-tuple-element.41, bf16[24,3072]{1,0:T(8,128)(2,1)S(1)} %collective-permute-done.15, f32[3072]{0:T(1024)S(1)} %copy-done), kind=kLoop, calls=%fused_computation | loop fusion | flops 589824 | bytes 897024 | tf_op jit(solution)/shard_map/convert_element_type | solution.py:285
  (4 shorter events, 0.0 us)
Async XLA Ops:
  1.5 12.0 %collective-permute-start.3 = (bf16[48,2048]{1,0:T(8,128)(2,1)S(1)}, bf16[48,2048]{1,0:T(8,128)(2,1)S(1)}, u32[]{:S(2)}, u32[]{:S(2)}) collective-permute-start(bf16[48,2048]{1,0:T(8,128)(2,1)S(1)} %get-tuple-element.30), channel_id=1, source_target_pairs={{0,2},{1,3},{2,0},{3,1},{4,6},{5,7},{6,4},{7,5},{8,10},{9,11},{10,... | collective-permute-start | bytes 589832 | tf_op jit(solution)/shard_map/ppermute | solution.py:229
  4.5 6.6 %collective-permute-start = (bf16[24,1152]{1,0:T(8,128)(2,1)S(1)}, bf16[24,1152]{1,0:T(8,128)(2,1)S(1)}, u32[]{:S(2)}, u32[]{:S(2)}) collective-permute-start(bf16[24,1152]{1,0:T(8,128)(2,1)S(1)} %get-tuple-element.25), channel_id=1, source_target_pairs={{0,12},{1,13},{2,14},{3,15},{4,8},{5,9},{6,10},{7,11},{8,4},{9,5},... | collective-permute-start | bytes 165896 | tf_op jit(solution)/shard_map/ppermute | solution.py:229
  8.1 5.1 %collective-permute-start.1 = (bf16[24,1152]{1,0:T(8,128)(2,1)S(1)}, bf16[24,1152]{1,0:T(8,128)(2,1)S(1)}, u32[]{:S(2)}, u32[]{:S(2)}) collective-permute-start(bf16[24,1152]{1,0:T(8,128)(2,1)S(1)} %get-tuple-element.26), channel_id=1, source_target_pairs={{0,8},{1,9},{2,10},{3,11},{4,12},{5,13},{6,14},{7,15},{8,0},{9,1},... | collective-permute-start | bytes 165896 | tf_op jit(solution)/shard_map/ppermute | solution.py:229
  8.1 5.1 %collective-permute-start.2 = (bf16[24,1152]{1,0:T(8,128)(2,1)S(1)}, bf16[24,1152]{1,0:T(8,128)(2,1)S(1)}, u32[]{:S(2)}, u32[]{:S(2)}) collective-permute-start(bf16[24,1152]{1,0:T(8,128)(2,1)S(1)} %get-tuple-element.27), channel_id=1, source_target_pairs={{0,4},{1,5},{2,6},{3,7},{4,0},{5,1},{6,2},{7,3},{8,12},{9,13},{10,... | collective-permute-start | bytes 165896 | tf_op jit(solution)/shard_map/ppermute | solution.py:229
  8.9 4.6 %collective-permute-start.4 = (bf16[48,1024]{1,0:T(8,128)(2,1)S(1)}, bf16[48,1024]{1,0:T(8,128)(2,1)S(1)}, u32[]{:S(2)}, u32[]{:S(2)}) collective-permute-start(bf16[48,1024]{1,0:T(8,128)(2,1)S(1)} %get-tuple-element.31), channel_id=1, source_target_pairs={{0,2},{1,3},{2,0},{3,1},{4,6},{5,7},{6,4},{7,5},{8,10},{9,11},{10,... | collective-permute-start | bytes 294920 | tf_op jit(solution)/shard_map/ppermute | solution.py:229
  13.5 11.3 %collective-permute-start.10 = (bf16[96,3072]{1,0:T(8,128)(2,1)S(1)}, bf16[96,3072]{1,0:T(8,128)(2,1)S(1)}, u32[]{:S(2)}, u32[]{:S(2)}) collective-permute-start(bf16[96,3072]{1,0:T(8,128)(2,1)S(1)} %get-tuple-element.36.refs_0_), channel_id=1, source_target_pairs={{0,1},{1,0},{2,3},{3,2},{4,5},{5,4},{6,7},{7,6},{8,9},{9,8},{10,11... | collective-permute-start | bytes 1769480 | tf_op jit(solution)/shard_map/ppermute | solution.py:229
  13.5 7.7 %collective-permute-start.7 = (bf16[48,2048]{1,0:T(8,128)(2,1)S(1)}, bf16[48,2048]{1,0:T(8,128)(2,1)S(1)}, u32[]{:S(2)}, u32[]{:S(2)}) collective-permute-start(bf16[48,2048]{1,0:T(8,128)(2,1)S(1)} %collective-permute-done.3.refs_2_), channel_id=1, source_target_pairs={{0,16},{16,0},{1,17},{17,1},{2,18},{18,2},{3,19},{19,3},{4,20},{20... | collective-permute-start | bytes 589832 | tf_op jit(solution)/shard_map/ppermute | solution.py:232
  15.0 6.0 %collective-permute-start.6 = (bf16[96,768]{1,0:T(8,128)(2,1)S(1)}, bf16[96,768]{1,0:T(8,128)(2,1)S(1)}, u32[]{:S(2)}, u32[]{:S(2)}) collective-permute-start(bf16[96,768]{1,0:T(8,128)(2,1)S(1)} %pad_maximum_fusion.refs_4_), channel_id=1, source_target_pairs={{0,2},{1,3},{2,0},{3,1},{4,6},{5,7},{6,4},{7,5},{8,10},{9,11},{10,... | collective-permute-start | bytes 442376 | tf_op jit(solution)/shard_map/ppermute | solution.py:229
  15.5 7.4 %collective-permute-start.9 = (bf16[48,1024]{1,0:T(8,128)(2,1)S(1)}, bf16[48,1024]{1,0:T(8,128)(2,1)S(1)}, u32[]{:S(2)}, u32[]{:S(2)}) collective-permute-start(bf16[48,1024]{1,0:T(8,128)(2,1)S(1)} %collective-permute-done.4.refs_4_), channel_id=1, source_target_pairs={{0,16},{16,0},{1,17},{17,1},{2,18},{18,2},{3,19},{19,3},{4,20},{20... | collective-permute-start | bytes 294920 | tf_op jit(solution)/shard_map/ppermute | solution.py:232
  15.9 7.0 %collective-permute-start.5 = (bf16[96,768]{1,0:T(8,128)(2,1)S(1)}, bf16[96,768]{1,0:T(8,128)(2,1)S(1)}, u32[]{:S(2)}, u32[]{:S(2)}) collective-permute-start(bf16[96,768]{1,0:T(8,128)(2,1)S(1)} %pad_maximum_fusion.refs_4_), channel_id=1, source_target_pairs={{0,1},{1,0},{2,3},{3,2},{4,5},{5,4},{6,7},{7,6},{8,9},{9,8},{10,11... | collective-permute-start | bytes 442376 | tf_op jit(solution)/shard_map/ppermute | solution.py:229
  21.2 2.2 %collective-permute-start.8 = (bf16[96,768]{1,0:T(8,128)(2,1)S(1)}, bf16[96,768]{1,0:T(8,128)(2,1)S(1)}, u32[]{:S(2)}, u32[]{:S(2)}) collective-permute-start(bf16[96,768]{1,0:T(8,128)(2,1)S(1)} %collective-permute-done.6.refs_6_), channel_id=1, source_target_pairs={{0,1},{1,0},{2,3},{3,2},{4,5},{5,4},{6,7},{7,6},{8,9},{9,8},{10,11... | collective-permute-start | bytes 442376 | tf_op jit(solution)/shard_map/ppermute | solution.py:229
  21.2 3.5 %collective-permute-start.11 = (bf16[48,2048]{1,0:T(8,128)(2,1)S(1)}, bf16[48,2048]{1,0:T(8,128)(2,1)S(1)}, u32[]{:S(2)}, u32[]{:S(2)}) collective-permute-start(bf16[48,2048]{1,0:T(8,128)(2,1)S(1)} %collective-permute-done.3.refs_2_), channel_id=1, source_target_pairs={{0,1},{1,0},{2,3},{3,2},{4,5},{5,4},{6,7},{7,6},{8,9},{9,8},{10,11... | collective-permute-start | bytes 589832 | tf_op jit(solution)/shard_map/ppermute | solution.py:229
  23.0 1.8 %collective-permute-start.12 = (bf16[48,2048]{1,0:T(8,128)(2,1)S(1)}, bf16[48,2048]{1,0:T(8,128)(2,1)S(1)}, u32[]{:S(2)}, u32[]{:S(2)}) collective-permute-start(bf16[48,2048]{1,0:T(8,128)(2,1)S(1)} %collective-permute-done.7.refs_3_), channel_id=1, source_target_pairs={{0,1},{1,0},{2,3},{3,2},{4,5},{5,4},{6,7},{7,6},{8,9},{9,8},{10,11... | collective-permute-start | bytes 589832 | tf_op jit(solution)/shard_map/ppermute | solution.py:229
  23.0 1.6 %collective-permute-start.13 = (bf16[48,1024]{1,0:T(8,128)(2,1)S(1)}, bf16[48,1024]{1,0:T(8,128)(2,1)S(1)}, u32[]{:S(2)}, u32[]{:S(2)}) collective-permute-start(bf16[48,1024]{1,0:T(8,128)(2,1)S(1)} %collective-permute-done.4.refs_4_), channel_id=1, source_target_pairs={{0,1},{1,0},{2,3},{3,2},{4,5},{5,4},{6,7},{7,6},{8,9},{9,8},{10,11... | collective-permute-start | bytes 294920 | tf_op jit(solution)/shard_map/ppermute | solution.py:229
  23.5 1.3 %collective-permute-start.14 = (bf16[48,1024]{1,0:T(8,128)(2,1)S(1)}, bf16[48,1024]{1,0:T(8,128)(2,1)S(1)}, u32[]{:S(2)}, u32[]{:S(2)}) collective-permute-start(bf16[48,1024]{1,0:T(8,128)(2,1)S(1)} %collective-permute-done.9.refs_5_), channel_id=1, source_target_pairs={{0,1},{1,0},{2,3},{3,2},{4,5},{5,4},{6,7},{7,6},{8,9},{9,8},{10,11... | collective-permute-start | bytes 294920 | tf_op jit(solution)/shard_map/ppermute | solution.py:229
  24.5 17.7 %copy-start = (f32[3072]{0:T(1024)S(1)}, f32[3072]{0:T(1024)}, u32[]{:S(2)}) copy-start(f32[3072]{0:T(1024)} %param.15) | copy-start | bytes 36868
  26.0 8.6 %collective-permute-start.15 = (bf16[24,3072]{1,0:T(8,128)(2,1)S(1)}, bf16[24,3072]{1,0:T(8,128)(2,1)S(1)}, u32[]{:S(2)}, u32[]{:S(2)}) collective-permute-start(bf16[24,3072]{1,0:T(8,128)(2,1)S(1)} %get-tuple-element.42), channel_id=1, source_target_pairs={{0,12},{1,13},{2,14},{3,15},{4,8},{5,9},{6,10},{7,11},{8,4},{9,5},... | collective-permute-start | bytes 442376 | tf_op jit(solution)/shard_map/ppermute | solution.py:229
  29.7 12.5 %collective-permute-start.16 = (bf16[24,3072]{1,0:T(8,128)(2,1)S(1)}, bf16[24,3072]{1,0:T(8,128)(2,1)S(1)}, u32[]{:S(2)}, u32[]{:S(2)}) collective-permute-start(bf16[24,3072]{1,0:T(8,128)(2,1)S(1)} %get-tuple-element.43), channel_id=1, source_target_pairs={{0,8},{1,9},{2,10},{3,11},{4,12},{5,13},{6,14},{7,15},{8,0},{9,1},... | collective-permute-start | bytes 442376 | tf_op jit(solution)/shard_map/ppermute | solution.py:229
  29.7 12.5 %collective-permute-start.17 = (bf16[24,3072]{1,0:T(8,128)(2,1)S(1)}, bf16[24,3072]{1,0:T(8,128)(2,1)S(1)}, u32[]{:S(2)}, u32[]{:S(2)}) collective-permute-start(bf16[24,3072]{1,0:T(8,128)(2,1)S(1)} %get-tuple-element.44), channel_id=1, source_target_pairs={{0,4},{1,5},{2,6},{3,7},{4,0},{5,1},{6,2},{7,3},{8,12},{9,13},{10,... | collective-permute-start | bytes 442376 | tf_op jit(solution)/shard_map/ppermute | solution.py:229

commit v7 on v6

--- a/solution.py
+++ b/solution.py
@@ -17,9 +17,9 @@
 def prepare_kernel(groups, members, chunks, *refs):
     sources, w_ref = refs[:6], refs[6]
     outs = refs[7:]
-    qout, kvout, fulls = outs[0], outs[1], outs[1 : 1 + groups]
-    wout, wparts = outs[1 + groups], outs[2 + groups : 2 + groups + chunks]
-    query, key_new, value_new, kst, vst, est, packed, sems = outs[2 + groups + chunks :]
+    qout, fulls, kvouts, wout = outs[0], outs[:groups], outs[groups : 2 * groups], outs[2 * groups]
+    wparts = outs[2 * groups + 1 : 2 * groups + 1 + chunks]
+    query, key_new, value_new, kst, vst, est, packed, sems = outs[2 * groups + 1 + chunks :]
     rows, width = query.shape
     me = lax.axis_index("patch")
     first = pl.multiple_of((me // 2) * (2 * rows), 2 * rows)
@@ -73,9 +73,9 @@
     for k in range(groups):
         target = (me // members) ^ k
         wanted = query[:, pl.ds(pl.multiple_of(target * share, share), share)]
+        kvouts[k][...] = packed[target]
         if k == 0:
             qout[...] = wanted
-            kvout[...] = packed[target]
         else:
             fulls[k][:, :share] = wanted
             fulls[k][:, share:] = packed[target]
@@ -88,10 +88,11 @@
     share = width // groups
     depth, model = w_out.shape
     outs = (
-        [((rows, share), jnp.bfloat16), ((rows, 2 * share), jnp.bfloat16)]
+        [((rows, share), jnp.bfloat16)]
         + [((rows, 3 * share), jnp.bfloat16)] * (groups - 1)
+        + [((rows, 2 * share), jnp.bfloat16)] * groups
         + [((depth, model), jnp.bfloat16)]
-        + [((depth // split, c), jnp.bfloat16) for c in chunks]
+        + [((depth // (split if i == 0 else 1), c), jnp.bfloat16) for i, c in enumerate(chunks)]
     )
     sources = (query, key_new, value_new, key_stale, value_stale, powers, w_out)
     result = pl.pallas_call(
@@ -111,7 +112,7 @@
             flops=10 * rows * width, bytes_accessed=14 * rows * width + 4 * depth * model, transcendentals=0
         ),
     )(*(pltpu.with_memory_space_constraint(x, pltpu.HBM) for x in sources))
-    return result[0], result[1 : 1 + groups], result[1 + groups], result[2 + groups :]
+    return result[:groups], result[groups : 2 * groups], result[2 * groups], result[2 * groups + 1 :]
 
 
 def attend_kernel(groups, dim, *refs):
@@ -238,32 +239,26 @@
             bit //= 2
         return [pieces[j] for j in range(members)]
 
-    own_query, fresh, w_own, w_parts = prepare(
+    full, fresh, w_own, w_parts = prepare(
         groups, members, chunks, 2 if shared else 1, query, key_new, value_new, key_stale, value_stale, exponents.T, w_out
     )
     order = range(groups - 1, 0, -1)
-    arrived = [send(fresh[k], k, 0) for k in order]
-    both = jnp.concatenate([x[:, share:] for x in arrived] + [fresh[0]], axis=0)
+    arrived = [send(full[k], k, 0) for k in order]
     mine = [send(w, 0, far) for w in w_parts] if shared else []
+    arrived[0] = after(arrived[0], *mine[:1])
+    swapped = swap(mine[0]) if shared else fresh[0]
+    fresh = [after(x, arrived[0]) for x in fresh]
+    side = [send(fresh[k], k, j) for j in range(2, members, 2) for k in [*order, 0]]
+    side[0] = after(side[0], swapped)
+    both = jnp.concatenate([x[:, share:] for x in arrived] + [fresh[0]] + side, axis=0)
     both = after(both, *mine)
-    swapped = [swap(w) for w in mine]
-    pieces = {0: both}
-    bit = far
-    while bit:
-        for j in list(pieces):
-            relay = after(pieces[j], *swapped[:1]) if j else both
-            pieces[j ^ bit] = send(relay, 0, bit)
-        bit //= 2
-    kvs = [pieces[j] for j in range(members)]
-    kvs[-1] = after(kvs[-1], *swapped)
-    att = attend(groups, dim, arrived + [own_query], kvs)
+    theirs = after(send(both, 0, 1), swapped)
+    att = attend(groups, dim, arrived + [full[0]], [both, theirs])
 
     if shared:
         pieces, places = [w_own], [(0, None, 0)]
         others = []
-        for c, w in enumerate(mine):
-            left = sum(chunks[:c])
-            others += [(w, (far, 0, left)), (swapped[c], (far, 1, left))]
+        others += [(mine[0], (far, 0, 0)), (swapped, (far, 1, 0)), (mine[1], (far, None, chunks[0]))]
         bit = 1
         while bit < far:
             pieces, places = (

time: 43.1 us -> 44.7 us (1.037)
  starting transfers between devices: 15.6 us -> 21.3 us
  waiting for transfers between devices: 22.8 us -> 18.8 us
    ppermute x16 -> x17, starting transfers between devices: 13.8 us -> 19.7 us  [send(): lax.ppermute(x, 'patch', [(p, (p // members ^ k) * members + p % members...]
    ppermute x16 -> x17, waiting for transfers between devices: 21.4 us -> 16.5 us  [send(): lax.ppermute(x, 'patch', [(p, (p // members ^ k) * members + p % members...]
    ppermute x2 -> x1, waiting for transfers between devices: 1.44 us -> 2.28 us  [swap(): return lax.ppermute(x, 'groups', [(g, g ^ 1) for g in range(parts)])]
    ppermute x2 -> x1, starting transfers between devices: 1.87 us -> 1.56 us  [swap(): return lax.ppermute(x, 'groups', [(g, g ^ 1) for g in range(parts)])]
  transfers between devices with their start and end apart: 18 -> 18, of which waited for: 10 -> 7; matrix products, arithmetic and copies ran while one was open for 0% -> 0% of each run, Pallas kernels for 2% -> 2%
where the time goes in v7:
time: 44.7 us; the launch traced here: 44.6 us
  starting transfers between devices  21.3 us (48%)
  waiting for transfers between devices  18.8 us (42%)
  Pallas kernels  3.6 us (8%)
  other arithmetic  0.75 us (2%)
    ppermute x17, starting transfers between devices, send(): lax.ppermute(x, 'patch', [(p, (p // members ^ k) * members + p % members...  19.7 us
    ppermute x17, waiting for transfers between devices, send(): lax.ppermute(x, 'patch', [(p, (p // members ^ k) * members + p % members...  16.5 us
    ppermute x1, waiting for transfers between devices, swap(): return lax.ppermute(x, 'groups', [(g, g ^ 1) for g in range(parts)])  2.28 us
    ppermute x1, starting transfers between devices, swap(): return lax.ppermute(x, 'groups', [(g, g ^ 1) for g in range(parts)])  1.56 us
    pallas_call x1, Pallas kernels, prepare(): pl.pallas_call(functools.partial(prepare_kernel, groups, members, len(chu...  1.51 us
    pallas_call x1, Pallas kernels, project(): pl.pallas_call(functools.partial(project_kernel, groups, members, places)...  1.16 us
    pallas_call x1, Pallas kernels, attend(): pl.pallas_call(functools.partial(attend_kernel, groups, dim), out_shape=j...  0.92 us
  transfers between devices with their start and end apart: 18, of which 7 were waited for; matrix products, arithmetic and copies ran while one was open for 0% of the time, Pallas kernels for 2%

profile of v7, /device:TPU:0, one launch (start us, length us, event | category | flops | bytes accessed | tf_op | source)
XLA Modules:
  0.0 44.6 jit_solution(2080657706947572703)
XLA Ops:
  0.0 1.5 %shard_map.82 = (bf16[24,384]{1,0:T(8,128)(2,1)S(1)}, bf16[24,1152]{1,0:T(8,128)(2,1)S(1)}, bf16[24,1152]{1,0:T(8,128)(2,1)S(1)}, bf16[24,1152]{1,0:T(8,128)(2,1...) custom-call(bf16[24,1536]{1,0:T(8,128)(2,1)} %refs_0_.1, ...), custom_call_target="tpu_custom_call" | custom-call | flops 368640 | bytes 1695744 | tf_op jit(solution)/shard_map/pallas_call | solution.py:98
  1.5 3.0 %collective-permute-start.1 = (bf16[48,2048]{1,0:T(8,128)(2,1)S(1)}, bf16[48,2048]{1,0:T(8,128)(2,1)S(1)}, u32[]{:S(2)}, u32[]{:S(2)}) collective-permute-start(bf16[48,2048]{1,0:T(8,128)(2,1)S(1)} %get-tuple-element.33), channel_id=1, source_target_pairs={{0,2},{1,3},{2,0},{3,1},{4,6},{5,7},{6,4},{7,5},{8,10},{9,11},{10,... | collective-permute-start | bytes 589832 | tf_op jit(solution)/shard_map/ppermute | solution.py:230
  4.6 3.6 %collective-permute-start = (bf16[24,1152]{1,0:T(8,128)(2,1)S(1)}, bf16[24,1152]{1,0:T(8,128)(2,1)S(1)}, u32[]{:S(2)}, u32[]{:S(2)}) collective-permute-start(bf16[24,1152]{1,0:T(8,128)(2,1)S(1)} %get-tuple-element.32), channel_id=1, source_target_pairs={{0,12},{1,13},{2,14},{3,15},{4,8},{5,9},{6,10},{7,11},{8,4},{9,5},... | collective-permute-start | bytes 165896 | tf_op jit(solution)/shard_map/ppermute | solution.py:230
  8.2 0.0 collective-permute-start.2
  8.2 0.8 %collective-permute-start.3 = (bf16[24,1152]{1,0:T(8,128)(2,1)S(1)}, bf16[24,1152]{1,0:T(8,128)(2,1)S(1)}, u32[]{:S(2)}, u32[]{:S(2)}) collective-permute-start(bf16[24,1152]{1,0:T(8,128)(2,1)S(1)} %get-tuple-element.36), channel_id=1, source_target_pairs={{0,4},{1,5},{2,6},{3,7},{4,0},{5,1},{6,2},{7,3},{8,12},{9,13},{10,... | collective-permute-start | bytes 165896 | tf_op jit(solution)/shard_map/ppermute | solution.py:230
  8.9 0.3 collective-permute-start.9
  9.2 1.9 %collective-permute-done.refs_0_ = bf16[24,1152]{1,0:T(8,128)(2,1)S(1)} collective-permute-done((bf16[24,1152]{1,0:T(8,128)(2,1)S(1)}, bf16[24,1152]{1,0:T(8,128)(2,1)S(1)}, u32[]{:S(2)}, u32[]{:S(2)}) %collective-permute-start) | collective-permute-done | bytes 55328 | tf_op jit(solution)/shard_map/ppermute | solution.py:230
  11.2 0.0 collective-permute-done.1.refs_2_
  11.2 0.3 collective-permute-start.8
  11.5 4.6 %collective-permute-start.4 = (bf16[24,768]{1,0:T(8,128)(2,1)S(1)}, bf16[24,768]{1,0:T(8,128)(2,1)S(1)}, u32[]{:S(2)}, u32[]{:S(2)}) collective-permute-start(bf16[24,768]{1,0:T(8,128)(2,1)S(1)} %get-tuple-element.41), channel_id=1, source_target_pairs={{0,14},{1,15},{2,12},{3,13},{4,10},{5,11},{6,8},{7,9},{8,6},{9,7},... | collective-permute-start | bytes 110600 | tf_op jit(solution)/shard_map/ppermute | solution.py:230
  16.1 0.0 collective-permute-done.2.refs_1_
  16.1 0.0 collective-permute-start.6
  16.1 0.0 collective-permute-done.3.refs_2_
  16.1 1.6 %collective-permute-start.5 = (bf16[48,2048]{1,0:T(8,128)(2,1)S(1)}, bf16[48,2048]{1,0:T(8,128)(2,1)S(1)}, u32[]{:S(2)}, u32[]{:S(2)}) collective-permute-start(bf16[48,2048]{1,0:T(8,128)(2,1)S(1)} %collective-permute-done.1.refs_2_), channel_id=1, source_target_pairs={{0,16},{16,0},{1,17},{17,1},{2,18},{18,2},{3,19},{19,3},{4,20},{20... | collective-permute-start | bytes 589832 | tf_op jit(solution)/shard_map/ppermute | solution.py:233
  17.7 0.5 %collective-permute-done.4 = bf16[24,768]{1,0:T(8,128)(2,1)S(1)} collective-permute-done((bf16[24,768]{1,0:T(8,128)(2,1)S(1)}, bf16[24,768]{1,0:T(8,128)(2,1)S(1)}, u32[]{:S(2)}, u32[]{:S(2)}) %collective-permute-start.4) | collective-permute-done | bytes 36896 | tf_op jit(solution)/shard_map/ppermute | solution.py:230
  18.2 1.4 %collective-permute-start.7 = (bf16[24,768]{1,0:T(8,128)(2,1)S(1)}, bf16[24,768]{1,0:T(8,128)(2,1)S(1)}, u32[]{:S(2)}, u32[]{:S(2)}) collective-permute-start(bf16[24,768]{1,0:T(8,128)(2,1)S(1)} %get-tuple-element.46), channel_id=1, source_target_pairs={{0,6},{1,7},{2,4},{3,5},{4,2},{5,3},{6,0},{7,1},{8,14},{9,15},{10,... | collective-permute-start | bytes 110600 | tf_op jit(solution)/shard_map/ppermute | solution.py:230
  19.6 2.3 %collective-permute-done.5.refs_3_ = bf16[48,2048]{1,0:T(8,128)(2,1)S(1)} collective-permute-done((bf16[48,2048]{1,0:T(8,128)(2,1)S(1)}, bf16[48,2048]{1,0:T(8,128)(2,1)S(1)}, u32[]{:S(2)}, u32[]{:S(2)}) %collective-permute-start.5) | collective-permute-done | bytes 196640 | tf_op jit(solution)/shard_map/ppermute | solution.py:233
  21.9 0.0 collective-permute-done.6
  21.9 1.2 %collective-permute-done.7 = bf16[24,768]{1,0:T(8,128)(2,1)S(1)} collective-permute-done((bf16[24,768]{1,0:T(8,128)(2,1)S(1)}, bf16[24,768]{1,0:T(8,128)(2,1)S(1)}, u32[]{:S(2)}, u32[]{:S(2)}) %collective-permute-start.7) | collective-permute-done | bytes 36896 | tf_op jit(solution)/shard_map/ppermute | solution.py:230
  23.0 0.0 collective-permute-done.8
  23.0 0.0 collective-permute-done.9.refs_4_
  23.1 0.1 collective-permute-start.11
  23.1 0.5 %collective-permute-start.10 = (bf16[192,768]{1,0:T(8,128)(2,1)S(1)}, bf16[192,768]{1,0:T(8,128)(2,1)S(1)}, u32[]{:S(2)}, u32[]{:S(2)}) collective-permute-start(bf16[192,768]{1,0:T(8,128)(2,1)S(1)} %constant_dynamic-update-slice_fusion.refs_4_), channel_id=1, source_target_pairs={{0,1},{1,0},{2,3},{3,2},{4,5},{5,4},{6,7},{7,6},{8,9},{9,8},{10,11... | collective-permute-start | bytes 884744 | tf_op jit(solution)/shard_map/ppermute | solution.py:230
  23.6 0.1 collective-permute-start.12
  23.7 0.4 collective-permute-start.13
  24.1 0.1 collective-permute-start.14
  24.2 1.3 %collective-permute-done.10.refs_5_ = bf16[192,768]{1,0:T(8,128)(2,1)S(1)} collective-permute-done((bf16[192,768]{1,0:T(8,128)(2,1)S(1)}, bf16[192,768]{1,0:T(8,128)(2,1)S(1)}, u32[]{:S(2)}, u32[]{:S(2)}) %collective-permute-start.10) | collective-permute-done | bytes 294944 | tf_op jit(solution)/shard_map/ppermute | solution.py:230
  25.6 0.9 %shard_map.83.att = bf16[96,384]{1,0:T(8,128)(2,1)S(1)} custom-call(bf16[24,1152]{1,0:T(8,128)(2,1)S(1)} %collective-permute-done.refs_0_, bf16[24,1152]{1,0:T(8,128)(2,1)S(1)} %collective-permute-done.2.refs_1_, bf16[24,1152]{1,0:T(8,128)(2,1)S(1)} %collective-permute-done.3.refs_2_, bf16[24,384]{1,0:T(8,128)(2,1)S(1)} %get-tuple-element.37.refs_3_, ...), custom_call_target="tpu_custom_call" | custom-call | flops 56623104 | bytes 589824 | tf_op jit(solution)/shard_map/pallas_call | solution.py:149
  26.5 0.0 copy-start
  26.5 0.0 collective-permute-done.12.refs_5_
  26.5 0.0 collective-permute-done.13.refs_6_
  26.5 0.0 collective-permute-done.14.refs_7_
  26.5 0.0 collective-permute-done.11.refs_1_
  26.5 1.2 %shard_map.84 = (bf16[24,3072]{1,0:T(8,128)(2,1)S(1)}, bf16[24,3072]{1,0:T(8,128)(2,1)S(1)}, bf16[24,3072]{1,0:T(8,128)(2,1)S(1)}, f32[24,3072]{1,0:T(8,128)S(1)}) custom-call(bf16[96,384]{1,0:T(8,128)(2,1)S(1)} %shard_map.83.att, bf16[96,3072]{1,0:T(8,128)(2,1)S(1)} %get-tuple-element.51.refs_0_, bf16[96,3072]{1,0:T(8,128)(2,1)S(1)} %collective-permute-done.11.refs_1_, ...), custom_call_target="tpu_custom_call" | custom-call | flops 226492416 | bytes 2359296 | tf_op jit(solution)/shard_map/pallas_call | solution.py:197
  27.7 3.9 %collective-permute-start.15 = (bf16[24,3072]{1,0:T(8,128)(2,1)S(1)}, bf16[24,3072]{1,0:T(8,128)(2,1)S(1)}, u32[]{:S(2)}, u32[]{:S(2)}) collective-permute-start(bf16[24,3072]{1,0:T(8,128)(2,1)S(1)} %get-tuple-element.56), channel_id=1, source_target_pairs={{0,12},{1,13},{2,14},{3,15},{4,8},{5,9},{6,10},{7,11},{8,4},{9,5},... | collective-permute-start | bytes 442376 | tf_op jit(solution)/shard_map/ppermute | solution.py:230
  31.6 0.0 collective-permute-start.16
  31.6 0.6 %collective-permute-start.17 = (bf16[24,3072]{1,0:T(8,128)(2,1)S(1)}, bf16[24,3072]{1,0:T(8,128)(2,1)S(1)}, u32[]{:S(2)}, u32[]{:S(2)}) collective-permute-start(bf16[24,3072]{1,0:T(8,128)(2,1)S(1)} %get-tuple-element.58), channel_id=1, source_target_pairs={{0,4},{1,5},{2,6},{3,7},{4,0},{5,1},{6,2},{7,3},{8,12},{9,13},{10,... | collective-permute-start | bytes 442376 | tf_op jit(solution)/shard_map/ppermute | solution.py:230
  32.3 4.1 %collective-permute-done.15 = bf16[24,3072]{1,0:T(8,128)(2,1)S(1)} collective-permute-done((bf16[24,3072]{1,0:T(8,128)(2,1)S(1)}, bf16[24,3072]{1,0:T(8,128)(2,1)S(1)}, u32[]{:S(2)}, u32[]{:S(2)}) %collective-permute-start.15) | collective-permute-done | bytes 147488 | tf_op jit(solution)/shard_map/ppermute | solution.py:230
  36.3 7.5 %collective-permute-done.16 = bf16[24,3072]{1,0:T(8,128)(2,1)S(1)} collective-permute-done((bf16[24,3072]{1,0:T(8,128)(2,1)S(1)}, bf16[24,3072]{1,0:T(8,128)(2,1)S(1)}, u32[]{:S(2)}, u32[]{:S(2)}) %collective-permute-start.16) | collective-permute-done | bytes 147488 | tf_op jit(solution)/shard_map/ppermute | solution.py:230
  43.8 0.0 collective-permute-done.17
  43.8 0.0 copy-done
  43.8 0.8 %multiply_convert_fusion = bf16[24,3072]{1,0:T(8,128)(2,1)} fusion(bf16[24,3072]{1,0:T(8,128)(2,1)S(1)} %collective-permute-done.17, bf16[24,3072]{1,0:T(8,128)(2,1)S(1)} %collective-permute-done.16, f32[24,3072]{1,0:T(8,128)S(1)} %get-tuple-element.55, bf16[24,3072]{1,0:T(8,128)(2,1)S(1)} %collective-permute-done.15, f32[3072]{0:T(1024)S(1)} %copy-done), kind=kLoop, calls=%fused_computation | loop fusion | flops 589824 | bytes 897024 | tf_op jit(solution)/shard_map/convert_element_type | solution.py:280
  (8 shorter events, 0.0 us)
Async XLA Ops:
  1.5 9.6 %collective-permute-start.1 = (bf16[48,2048]{1,0:T(8,128)(2,1)S(1)}, bf16[48,2048]{1,0:T(8,128)(2,1)S(1)}, u32[]{:S(2)}, u32[]{:S(2)}) collective-permute-start(bf16[48,2048]{1,0:T(8,128)(2,1)S(1)} %get-tuple-element.33), channel_id=1, source_target_pairs={{0,2},{1,3},{2,0},{3,1},{4,6},{5,7},{6,4},{7,5},{8,10},{9,11},{10,... | collective-permute-start | bytes 589832 | tf_op jit(solution)/shard_map/ppermute | solution.py:230
  4.6 6.6 %collective-permute-start = (bf16[24,1152]{1,0:T(8,128)(2,1)S(1)}, bf16[24,1152]{1,0:T(8,128)(2,1)S(1)}, u32[]{:S(2)}, u32[]{:S(2)}) collective-permute-start(bf16[24,1152]{1,0:T(8,128)(2,1)S(1)} %get-tuple-element.32), channel_id=1, source_target_pairs={{0,12},{1,13},{2,14},{3,15},{4,8},{5,9},{6,10},{7,11},{8,4},{9,5},... | collective-permute-start | bytes 165896 | tf_op jit(solution)/shard_map/ppermute | solution.py:230
  8.2 7.9 %collective-permute-start.2 = (bf16[24,1152]{1,0:T(8,128)(2,1)S(1)}, bf16[24,1152]{1,0:T(8,128)(2,1)S(1)}, u32[]{:S(2)}, u32[]{:S(2)}) collective-permute-start(bf16[24,1152]{1,0:T(8,128)(2,1)S(1)} %get-tuple-element.35), channel_id=1, source_target_pairs={{0,8},{1,9},{2,10},{3,11},{4,12},{5,13},{6,14},{7,15},{8,0},{9,1},... | collective-permute-start | bytes 165896 | tf_op jit(solution)/shard_map/ppermute | solution.py:230
  8.2 8.0 %collective-permute-start.3 = (bf16[24,1152]{1,0:T(8,128)(2,1)S(1)}, bf16[24,1152]{1,0:T(8,128)(2,1)S(1)}, u32[]{:S(2)}, u32[]{:S(2)}) collective-permute-start(bf16[24,1152]{1,0:T(8,128)(2,1)S(1)} %get-tuple-element.36), channel_id=1, source_target_pairs={{0,4},{1,5},{2,6},{3,7},{4,0},{5,1},{6,2},{7,3},{8,12},{9,13},{10,... | collective-permute-start | bytes 165896 | tf_op jit(solution)/shard_map/ppermute | solution.py:230
  8.9 14.1 %collective-permute-start.9 = (bf16[96,1024]{1,0:T(8,128)(2,1)S(1)}, bf16[96,1024]{1,0:T(8,128)(2,1)S(1)}, u32[]{:S(2)}, u32[]{:S(2)}) collective-permute-start(bf16[96,1024]{1,0:T(8,128)(2,1)S(1)} %get-tuple-element.47), channel_id=1, source_target_pairs={{0,2},{1,3},{2,0},{3,1},{4,6},{5,7},{6,4},{7,5},{8,10},{9,11},{10,... | collective-permute-start | bytes 589832 | tf_op jit(solution)/shard_map/ppermute | solution.py:230
  11.2 11.9 %collective-permute-start.8 = (bf16[24,768]{1,0:T(8,128)(2,1)S(1)}, bf16[24,768]{1,0:T(8,128)(2,1)S(1)}, u32[]{:S(2)}, u32[]{:S(2)}) collective-permute-start(bf16[24,768]{1,0:T(8,128)(2,1)S(1)} %get-tuple-element.39), channel_id=1, source_target_pairs={{0,2},{1,3},{2,0},{3,1},{4,6},{5,7},{6,4},{7,5},{8,10},{9,11},{10,... | collective-permute-start | bytes 110600 | tf_op jit(solution)/shard_map/ppermute | solution.py:230
  11.5 6.7 %collective-permute-start.4 = (bf16[24,768]{1,0:T(8,128)(2,1)S(1)}, bf16[24,768]{1,0:T(8,128)(2,1)S(1)}, u32[]{:S(2)}, u32[]{:S(2)}) collective-permute-start(bf16[24,768]{1,0:T(8,128)(2,1)S(1)} %get-tuple-element.41), channel_id=1, source_target_pairs={{0,14},{1,15},{2,12},{3,13},{4,10},{5,11},{6,8},{7,9},{8,6},{9,7},... | collective-permute-start | bytes 110600 | tf_op jit(solution)/shard_map/ppermute | solution.py:230
  16.1 5.8 %collective-permute-start.6 = (bf16[24,768]{1,0:T(8,128)(2,1)S(1)}, bf16[24,768]{1,0:T(8,128)(2,1)S(1)}, u32[]{:S(2)}, u32[]{:S(2)}) collective-permute-start(bf16[24,768]{1,0:T(8,128)(2,1)S(1)} %get-tuple-element.44), channel_id=1, source_target_pairs={{0,10},{1,11},{2,8},{3,9},{4,14},{5,15},{6,12},{7,13},{8,2},{9,3},... | collective-permute-start | bytes 110600 | tf_op jit(solution)/shard_map/ppermute | solution.py:230
  16.1 5.7 %collective-permute-start.5 = (bf16[48,2048]{1,0:T(8,128)(2,1)S(1)}, bf16[48,2048]{1,0:T(8,128)(2,1)S(1)}, u32[]{:S(2)}, u32[]{:S(2)}) collective-permute-start(bf16[48,2048]{1,0:T(8,128)(2,1)S(1)} %collective-permute-done.1.refs_2_), channel_id=1, source_target_pairs={{0,16},{16,0},{1,17},{17,1},{2,18},{18,2},{3,19},{19,3},{4,20},{20... | collective-permute-start | bytes 589832 | tf_op jit(solution)/shard_map/ppermute | solution.py:233
  18.2 4.9 %collective-permute-start.7 = (bf16[24,768]{1,0:T(8,128)(2,1)S(1)}, bf16[24,768]{1,0:T(8,128)(2,1)S(1)}, u32[]{:S(2)}, u32[]{:S(2)}) collective-permute-start(bf16[24,768]{1,0:T(8,128)(2,1)S(1)} %get-tuple-element.46), channel_id=1, source_target_pairs={{0,6},{1,7},{2,4},{3,5},{4,2},{5,3},{6,0},{7,1},{8,14},{9,15},{10,... | collective-permute-start | bytes 110600 | tf_op jit(solution)/shard_map/ppermute | solution.py:230
  23.1 3.5 %collective-permute-start.11 = (bf16[96,3072]{1,0:T(8,128)(2,1)S(1)}, bf16[96,3072]{1,0:T(8,128)(2,1)S(1)}, u32[]{:S(2)}, u32[]{:S(2)}) collective-permute-start(bf16[96,3072]{1,0:T(8,128)(2,1)S(1)} %get-tuple-element.51.refs_0_), channel_id=1, source_target_pairs={{0,1},{1,0},{2,3},{3,2},{4,5},{5,4},{6,7},{7,6},{8,9},{9,8},{10,11... | collective-permute-start | bytes 1769480 | tf_op jit(solution)/shard_map/ppermute | solution.py:230
  23.1 2.4 %collective-permute-start.10 = (bf16[192,768]{1,0:T(8,128)(2,1)S(1)}, bf16[192,768]{1,0:T(8,128)(2,1)S(1)}, u32[]{:S(2)}, u32[]{:S(2)}) collective-permute-start(bf16[192,768]{1,0:T(8,128)(2,1)S(1)} %constant_dynamic-update-slice_fusion.refs_4_), channel_id=1, source_target_pairs={{0,1},{1,0},{2,3},{3,2},{4,5},{5,4},{6,7},{7,6},{8,9},{9,8},{10,11... | collective-permute-start | bytes 884744 | tf_op jit(solution)/shard_map/ppermute | solution.py:230
  23.6 2.9 %collective-permute-start.12 = (bf16[48,2048]{1,0:T(8,128)(2,1)S(1)}, bf16[48,2048]{1,0:T(8,128)(2,1)S(1)}, u32[]{:S(2)}, u32[]{:S(2)}) collective-permute-start(bf16[48,2048]{1,0:T(8,128)(2,1)S(1)} %collective-permute-done.1.refs_2_), channel_id=1, source_target_pairs={{0,1},{1,0},{2,3},{3,2},{4,5},{5,4},{6,7},{7,6},{8,9},{9,8},{10,11... | collective-permute-start | bytes 589832 | tf_op jit(solution)/shard_map/ppermute | solution.py:230
  23.7 2.8 %collective-permute-start.13 = (bf16[48,2048]{1,0:T(8,128)(2,1)S(1)}, bf16[48,2048]{1,0:T(8,128)(2,1)S(1)}, u32[]{:S(2)}, u32[]{:S(2)}) collective-permute-start(bf16[48,2048]{1,0:T(8,128)(2,1)S(1)} %collective-permute-done.5.refs_3_), channel_id=1, source_target_pairs={{0,1},{1,0},{2,3},{3,2},{4,5},{5,4},{6,7},{7,6},{8,9},{9,8},{10,11... | collective-permute-start | bytes 589832 | tf_op jit(solution)/shard_map/ppermute | solution.py:230
  24.1 2.4 %collective-permute-start.14 = (bf16[96,1024]{1,0:T(8,128)(2,1)S(1)}, bf16[96,1024]{1,0:T(8,128)(2,1)S(1)}, u32[]{:S(2)}, u32[]{:S(2)}) collective-permute-start(bf16[96,1024]{1,0:T(8,128)(2,1)S(1)} %collective-permute-done.9.refs_4_), channel_id=1, source_target_pairs={{0,1},{1,0},{2,3},{3,2},{4,5},{5,4},{6,7},{7,6},{8,9},{9,8},{10,11... | collective-permute-start | bytes 589832 | tf_op jit(solution)/shard_map/ppermute | solution.py:230
  26.5 17.3 %copy-start = (f32[3072]{0:T(1024)S(1)}, f32[3072]{0:T(1024)}, u32[]{:S(2)}) copy-start(f32[3072]{0:T(1024)} %param.15) | copy-start | bytes 36868
  27.7 8.6 %collective-permute-start.15 = (bf16[24,3072]{1,0:T(8,128)(2,1)S(1)}, bf16[24,3072]{1,0:T(8,128)(2,1)S(1)}, u32[]{:S(2)}, u32[]{:S(2)}) collective-permute-start(bf16[24,3072]{1,0:T(8,128)(2,1)S(1)} %get-tuple-element.56), channel_id=1, source_target_pairs={{0,12},{1,13},{2,14},{3,15},{4,8},{5,9},{6,10},{7,11},{8,4},{9,5},... | collective-permute-start | bytes 442376 | tf_op jit(solution)/shard_map/ppermute | solution.py:230
  31.6 12.2 %collective-permute-start.16 = (bf16[24,3072]{1,0:T(8,128)(2,1)S(1)}, bf16[24,3072]{1,0:T(8,128)(2,1)S(1)}, u32[]{:S(2)}, u32[]{:S(2)}) collective-permute-start(bf16[24,3072]{1,0:T(8,128)(2,1)S(1)} %get-tuple-element.57), channel_id=1, source_target_pairs={{0,8},{1,9},{2,10},{3,11},{4,12},{5,13},{6,14},{7,15},{8,0},{9,1},... | collective-permute-start | bytes 442376 | tf_op jit(solution)/shard_map/ppermute | solution.py:230
  31.6 12.2 %collective-permute-start.17 = (bf16[24,3072]{1,0:T(8,128)(2,1)S(1)}, bf16[24,3072]{1,0:T(8,128)(2,1)S(1)}, u32[]{:S(2)}, u32[]{:S(2)}) collective-permute-start(bf16[24,3072]{1,0:T(8,128)(2,1)S(1)} %get-tuple-element.58), channel_id=1, source_target_pairs={{0,4},{1,5},{2,6},{3,7},{4,0},{5,1},{6,2},{7,3},{8,12},{9,13},{10,... | collective-permute-start | bytes 442376 | tf_op jit(solution)/shard_map/ppermute | solution.py:230

commit v8 on v6

--- a/solution.py
+++ b/solution.py
@@ -223,7 +223,7 @@
     depth, model = w_out.shape
     far = members // 2
     shared = parts % 2 == 0 and depth % 32 == 0
-    chunks = [2 * model // 3, model // 3] if shared and model % 384 == 0 else [model]
+    chunks = [model]
 
     def send(x, k, j):
         return lax.ppermute(x, "patch", [(p, ((p // members) ^ k) * members + (p % members) ^ j) for p in range(patch)])
@@ -251,11 +251,9 @@
     bit = far
     while bit:
         for j in list(pieces):
-            relay = after(pieces[j], *swapped[:1]) if j else both
-            pieces[j ^ bit] = send(relay, 0, bit)
+            pieces[j ^ bit] = send(pieces[j], 0, bit)
         bit //= 2
     kvs = [pieces[j] for j in range(members)]
-    kvs[-1] = after(kvs[-1], *swapped)
     att = attend(groups, dim, arrived + [own_query], kvs)
 
     if shared:
@@ -270,7 +268,7 @@
                 pieces + [send(after(x, both), 0, bit) for x in pieces],
                 places + [(p[0] ^ bit, p[1], p[2]) for p in places],
             )
-            others = others + [(send(after(x, both), 0, bit), (p[0] ^ bit, p[1], p[2])) for x, p in others]
+            others = others + [(send(after(x, *(kvs if p[1] else [both])), 0, bit), (p[0] ^ bit, p[1], p[2])) for x, p in others]
             bit *= 2
         pieces = pieces + [x for x, _ in others]
         places = places + [p for _, p in others]

time: 43.1 us -> 40.9 us (0.949)
  waiting for transfers between devices: 22.8 us -> 21.5 us
  starting transfers between devices: 15.6 us -> 15 us
    ppermute x16 -> x13, waiting for transfers between devices: 21.4 us -> 20.4 us  [send(): lax.ppermute(x, 'patch', [(p, (p // members ^ k) * members + p % members...]
    ppermute x2 -> x1, starting transfers between devices: 1.87 us -> 1.49 us  [swap(): return lax.ppermute(x, 'groups', [(g, g ^ 1) for g in range(parts)])]
    ppermute x2 -> x1, waiting for transfers between devices: 1.44 us -> 1.06 us  [swap(): return lax.ppermute(x, 'groups', [(g, g ^ 1) for g in range(parts)])]
    ppermute x16 -> x13, starting transfers between devices: 13.8 us -> 13.5 us  [send(): lax.ppermute(x, 'patch', [(p, (p // members ^ k) * members + p % members...]
  transfers between devices with their start and end apart: 18 -> 14, of which waited for: 10 -> 8; matrix products, arithmetic and copies ran while one was open for 0% -> 0% of each run, Pallas kernels for 2% -> 2%
where the time goes in v8:
time: 40.9 us; the launch traced here: 40.8 us
  waiting for transfers between devices  21.5 us (53%)
  starting transfers between devices  15 us (37%)
  Pallas kernels  3.54 us (9%)
  other arithmetic  0.76 us (2%)
    ppermute x13, waiting for transfers between devices, send(): lax.ppermute(x, 'patch', [(p, (p // members ^ k) * members + p % members...  20.4 us
    ppermute x13, starting transfers between devices, send(): lax.ppermute(x, 'patch', [(p, (p // members ^ k) * members + p % members...  13.5 us
    ppermute x1, starting transfers between devices, swap(): return lax.ppermute(x, 'groups', [(g, g ^ 1) for g in range(parts)])  1.49 us
    pallas_call x1, Pallas kernels, prepare(): pl.pallas_call(functools.partial(prepare_kernel, groups, members, len(chu...  1.48 us
    pallas_call x1, Pallas kernels, project(): pl.pallas_call(functools.partial(project_kernel, groups, members, places)...  1.13 us
    ppermute x1, waiting for transfers between devices, swap(): return lax.ppermute(x, 'groups', [(g, g ^ 1) for g in range(parts)])  1.06 us
    pallas_call x1, Pallas kernels, attend(): pl.pallas_call(functools.partial(attend_kernel, groups, dim), out_shape=j...  0.93 us
  transfers between devices with their start and end apart: 14, of which 8 were waited for; matrix products, arithmetic and copies ran while one was open for 0% of the time, Pallas kernels for 2%

profile of v8, /device:TPU:0, one launch (start us, length us, event | category | flops | bytes accessed | tf_op | source)
XLA Modules:
  0.0 40.8 jit_solution(6003042803021102932)
XLA Ops:
  0.0 1.5 %shard_map.82 = (bf16[24,384]{1,0:T(8,128)(2,1)S(1)}, bf16[24,768]{1,0:T(8,128)(2,1)S(1)}, bf16[24,1152]{1,0:T(8,128)(2,1)S(1)}, bf16[24,1152]{1,0:T(8,128)(2,1)...) custom-call(bf16[24,1536]{1,0:T(8,128)(2,1)} %refs_0_.1, ...), custom_call_target="tpu_custom_call" | custom-call | flops 368640 | bytes 1695744 | tf_op jit(solution)/shard_map/pallas_call | solution.py:97
  1.5 3.0 %collective-permute-start.3 = (bf16[48,3072]{1,0:T(8,128)(2,1)S(1)}, bf16[48,3072]{1,0:T(8,128)(2,1)S(1)}, u32[]{:S(2)}, u32[]{:S(2)}) collective-permute-start(bf16[48,3072]{1,0:T(8,128)(2,1)S(1)} %get-tuple-element.25), channel_id=1, source_target_pairs={{0,2},{1,3},{2,0},{3,1},{4,6},{5,7},{6,4},{7,5},{8,10},{9,11},{10,... | collective-permute-start | bytes 884744 | tf_op jit(solution)/shard_map/ppermute | solution.py:229
  4.5 3.6 %collective-permute-start = (bf16[24,1152]{1,0:T(8,128)(2,1)S(1)}, bf16[24,1152]{1,0:T(8,128)(2,1)S(1)}, u32[]{:S(2)}, u32[]{:S(2)}) collective-permute-start(bf16[24,1152]{1,0:T(8,128)(2,1)S(1)} %get-tuple-element.20), channel_id=1, source_target_pairs={{0,12},{1,13},{2,14},{3,15},{4,8},{5,9},{6,10},{7,11},{8,4},{9,5},... | collective-permute-start | bytes 165896 | tf_op jit(solution)/shard_map/ppermute | solution.py:229
  8.1 0.0 collective-permute-start.1
  8.1 0.8 %collective-permute-start.2 = (bf16[24,1152]{1,0:T(8,128)(2,1)S(1)}, bf16[24,1152]{1,0:T(8,128)(2,1)S(1)}, u32[]{:S(2)}, u32[]{:S(2)}) collective-permute-start(bf16[24,1152]{1,0:T(8,128)(2,1)S(1)} %get-tuple-element.22), channel_id=1, source_target_pairs={{0,4},{1,5},{2,6},{3,7},{4,0},{5,1},{6,2},{7,3},{8,12},{9,13},{10,... | collective-permute-start | bytes 165896 | tf_op jit(solution)/shard_map/ppermute | solution.py:229
  8.9 2.2 %collective-permute-done.refs_0_ = bf16[24,1152]{1,0:T(8,128)(2,1)S(1)} collective-permute-done((bf16[24,1152]{1,0:T(8,128)(2,1)S(1)}, bf16[24,1152]{1,0:T(8,128)(2,1)S(1)}, u32[]{:S(2)}, u32[]{:S(2)}) %collective-permute-start) | collective-permute-done | bytes 55328 | tf_op jit(solution)/shard_map/ppermute | solution.py:229
  11.1 2.0 %collective-permute-done.1.refs_1_ = bf16[24,1152]{1,0:T(8,128)(2,1)S(1)} collective-permute-done((bf16[24,1152]{1,0:T(8,128)(2,1)S(1)}, bf16[24,1152]{1,0:T(8,128)(2,1)S(1)}, u32[]{:S(2)}, u32[]{:S(2)}) %collective-permute-start.1) | collective-permute-done | bytes 55328 | tf_op jit(solution)/shard_map/ppermute | solution.py:229
  13.2 0.0 collective-permute-done.2.refs_2_
  13.2 0.0 collective-permute-done.3.refs_2_
  13.2 0.6 %collective-permute-start.5 = (bf16[96,768]{1,0:T(8,128)(2,1)S(1)}, bf16[96,768]{1,0:T(8,128)(2,1)S(1)}, u32[]{:S(2)}, u32[]{:S(2)}) collective-permute-start(bf16[96,768]{1,0:T(8,128)(2,1)S(1)} %pad_maximum_fusion.refs_4_), channel_id=1, source_target_pairs={{0,2},{1,3},{2,0},{3,1},{4,6},{5,7},{6,4},{7,5},{8,10},{9,11},{10,... | collective-permute-start | bytes 442376 | tf_op jit(solution)/shard_map/ppermute | solution.py:229
  13.8 1.5 %collective-permute-start.8 = (bf16[48,3072]{1,0:T(8,128)(2,1)S(1)}, bf16[48,3072]{1,0:T(8,128)(2,1)S(1)}, u32[]{:S(2)}, u32[]{:S(2)}) collective-permute-start(bf16[48,3072]{1,0:T(8,128)(2,1)S(1)} %collective-permute-done.3.refs_2_), channel_id=1, source_target_pairs={{0,16},{16,0},{1,17},{17,1},{2,18},{18,2},{3,19},{19,3},{4,20},{20... | collective-permute-start | bytes 884744 | tf_op jit(solution)/shard_map/ppermute | solution.py:232
  15.3 0.0 collective-permute-start.7
  15.3 0.5 %collective-permute-start.4 = (bf16[96,768]{1,0:T(8,128)(2,1)S(1)}, bf16[96,768]{1,0:T(8,128)(2,1)S(1)}, u32[]{:S(2)}, u32[]{:S(2)}) collective-permute-start(bf16[96,768]{1,0:T(8,128)(2,1)S(1)} %pad_maximum_fusion.refs_4_), channel_id=1, source_target_pairs={{0,1},{1,0},{2,3},{3,2},{4,5},{5,4},{6,7},{7,6},{8,9},{9,8},{10,11... | collective-permute-start | bytes 442376 | tf_op jit(solution)/shard_map/ppermute | solution.py:229
  15.8 2.6 %collective-permute-done.5.refs_6_ = bf16[96,768]{1,0:T(8,128)(2,1)S(1)} collective-permute-done((bf16[96,768]{1,0:T(8,128)(2,1)S(1)}, bf16[96,768]{1,0:T(8,128)(2,1)S(1)}, u32[]{:S(2)}, u32[]{:S(2)}) %collective-permute-start.5) | collective-permute-done | bytes 147488 | tf_op jit(solution)/shard_map/ppermute | solution.py:229
  18.4 0.0 collective-permute-start.6
  18.4 0.5 %collective-permute-start.9 = (bf16[48,3072]{1,0:T(8,128)(2,1)S(1)}, bf16[48,3072]{1,0:T(8,128)(2,1)S(1)}, u32[]{:S(2)}, u32[]{:S(2)}) collective-permute-start(bf16[48,3072]{1,0:T(8,128)(2,1)S(1)} %collective-permute-done.3.refs_2_), channel_id=1, source_target_pairs={{0,1},{1,0},{2,3},{3,2},{4,5},{5,4},{6,7},{7,6},{8,9},{9,8},{10,11... | collective-permute-start | bytes 884744 | tf_op jit(solution)/shard_map/ppermute | solution.py:229
  18.9 0.0 collective-permute-done.4.refs_5_
  18.9 0.9 %collective-permute-done.6.refs_7_ = bf16[96,768]{1,0:T(8,128)(2,1)S(1)} collective-permute-done((bf16[96,768]{1,0:T(8,128)(2,1)S(1)}, bf16[96,768]{1,0:T(8,128)(2,1)S(1)}, u32[]{:S(2)}, u32[]{:S(2)}) %collective-permute-start.6) | collective-permute-done | bytes 147488 | tf_op jit(solution)/shard_map/ppermute | solution.py:229
  19.8 1.1 %collective-permute-done.8.refs_3_ = bf16[48,3072]{1,0:T(8,128)(2,1)S(1)} collective-permute-done((bf16[48,3072]{1,0:T(8,128)(2,1)S(1)}, bf16[48,3072]{1,0:T(8,128)(2,1)S(1)}, u32[]{:S(2)}, u32[]{:S(2)}) %collective-permute-start.8) | collective-permute-done | bytes 294944 | tf_op jit(solution)/shard_map/ppermute | solution.py:232
  20.9 0.0 collective-permute-start.10
  20.9 0.9 %shard_map.83.att = bf16[96,384]{1,0:T(8,128)(2,1)S(1)} custom-call(bf16[24,1152]{1,0:T(8,128)(2,1)S(1)} %collective-permute-done.refs_0_, bf16[24,1152]{1,0:T(8,128)(2,1)S(1)} %collective-permute-done.1.refs_1_, bf16[24,1152]{1,0:T(8,128)(2,1)S(1)} %collective-permute-done.2.refs_2_, bf16[24,384]{1,0:T(8,128)(2,1)S(1)} %get-tuple-element.23.refs_3_, ...), custom_call_target="tpu_custom_call" | custom-call | flops 56623104 | bytes 589824 | tf_op jit(solution)/shard_map/pallas_call | solution.py:148
  21.8 0.0 copy-start
  21.8 0.0 collective-permute-done.9.refs_4_
  21.8 0.6 %collective-permute-done.10.refs_5_ = bf16[48,3072]{1,0:T(8,128)(2,1)S(1)} collective-permute-done((bf16[48,3072]{1,0:T(8,128)(2,1)S(1)}, bf16[48,3072]{1,0:T(8,128)(2,1)S(1)}, u32[]{:S(2)}, u32[]{:S(2)}) %collective-permute-start.10) | collective-permute-done | bytes 294944 | tf_op jit(solution)/shard_map/ppermute | solution.py:229
  22.5 0.0 collective-permute-done.7.refs_1_
  22.5 1.1 %shard_map.84 = (bf16[24,3072]{1,0:T(8,128)(2,1)S(1)}, bf16[24,3072]{1,0:T(8,128)(2,1)S(1)}, bf16[24,3072]{1,0:T(8,128)(2,1)S(1)}, f32[24,3072]{1,0:T(8,128)S(1)}) custom-call(bf16[96,384]{1,0:T(8,128)(2,1)S(1)} %shard_map.83.att, bf16[96,3072]{1,0:T(8,128)(2,1)S(1)} %get-tuple-element.28.refs_0_, bf16[96,3072]{1,0:T(8,128)(2,1)S(1)} %collective-permute-done.7.refs_1_, ...), custom_call_target="tpu_custom_call" | custom-call | flops 226492416 | bytes 2359296 | tf_op jit(solution)/shard_map/pallas_call | solution.py:196
  23.6 3.7 %collective-permute-start.11 = (bf16[24,3072]{1,0:T(8,128)(2,1)S(1)}, bf16[24,3072]{1,0:T(8,128)(2,1)S(1)}, u32[]{:S(2)}, u32[]{:S(2)}) collective-permute-start(bf16[24,3072]{1,0:T(8,128)(2,1)S(1)} %get-tuple-element.32), channel_id=1, source_target_pairs={{0,12},{1,13},{2,14},{3,15},{4,8},{5,9},{6,10},{7,11},{8,4},{9,5},... | collective-permute-start | bytes 442376 | tf_op jit(solution)/shard_map/ppermute | solution.py:229
  27.3 0.0 collective-permute-start.12
  27.3 0.8 %collective-permute-start.13 = (bf16[24,3072]{1,0:T(8,128)(2,1)S(1)}, bf16[24,3072]{1,0:T(8,128)(2,1)S(1)}, u32[]{:S(2)}, u32[]{:S(2)}) collective-permute-start(bf16[24,3072]{1,0:T(8,128)(2,1)S(1)} %get-tuple-element.34), channel_id=1, source_target_pairs={{0,4},{1,5},{2,6},{3,7},{4,0},{5,1},{6,2},{7,3},{8,12},{9,13},{10,... | collective-permute-start | bytes 442376 | tf_op jit(solution)/shard_map/ppermute | solution.py:229
  28.0 4.2 %collective-permute-done.11 = bf16[24,3072]{1,0:T(8,128)(2,1)S(1)} collective-permute-done((bf16[24,3072]{1,0:T(8,128)(2,1)S(1)}, bf16[24,3072]{1,0:T(8,128)(2,1)S(1)}, u32[]{:S(2)}, u32[]{:S(2)}) %collective-permute-start.11) | collective-permute-done | bytes 147488 | tf_op jit(solution)/shard_map/ppermute | solution.py:229
  32.2 7.8 %collective-permute-done.12 = bf16[24,3072]{1,0:T(8,128)(2,1)S(1)} collective-permute-done((bf16[24,3072]{1,0:T(8,128)(2,1)S(1)}, bf16[24,3072]{1,0:T(8,128)(2,1)S(1)}, u32[]{:S(2)}, u32[]{:S(2)}) %collective-permute-start.12) | collective-permute-done | bytes 147488 | tf_op jit(solution)/shard_map/ppermute | solution.py:229
  40.0 0.0 collective-permute-done.13
  40.0 0.0 copy-done
  40.0 0.8 %multiply_convert_fusion = bf16[24,3072]{1,0:T(8,128)(2,1)} fusion(bf16[24,3072]{1,0:T(8,128)(2,1)S(1)} %collective-permute-done.13, bf16[24,3072]{1,0:T(8,128)(2,1)S(1)} %collective-permute-done.12, f32[24,3072]{1,0:T(8,128)S(1)} %get-tuple-element.31, bf16[24,3072]{1,0:T(8,128)(2,1)S(1)} %collective-permute-done.11, f32[3072]{0:T(1024)S(1)} %copy-done), kind=kLoop, calls=%fused_computation | loop fusion | flops 589824 | bytes 897024 | tf_op jit(solution)/shard_map/convert_element_type | solution.py:283
  (4 shorter events, 0.0 us)
Async XLA Ops:
  1.5 11.7 %collective-permute-start.3 = (bf16[48,3072]{1,0:T(8,128)(2,1)S(1)}, bf16[48,3072]{1,0:T(8,128)(2,1)S(1)}, u32[]{:S(2)}, u32[]{:S(2)}) collective-permute-start(bf16[48,3072]{1,0:T(8,128)(2,1)S(1)} %get-tuple-element.25), channel_id=1, source_target_pairs={{0,2},{1,3},{2,0},{3,1},{4,6},{5,7},{6,4},{7,5},{8,10},{9,11},{10,... | collective-permute-start | bytes 884744 | tf_op jit(solution)/shard_map/ppermute | solution.py:229
  4.5 6.6 %collective-permute-start = (bf16[24,1152]{1,0:T(8,128)(2,1)S(1)}, bf16[24,1152]{1,0:T(8,128)(2,1)S(1)}, u32[]{:S(2)}, u32[]{:S(2)}) collective-permute-start(bf16[24,1152]{1,0:T(8,128)(2,1)S(1)} %get-tuple-element.20), channel_id=1, source_target_pairs={{0,12},{1,13},{2,14},{3,15},{4,8},{5,9},{6,10},{7,11},{8,4},{9,5},... | collective-permute-start | bytes 165896 | tf_op jit(solution)/shard_map/ppermute | solution.py:229
  8.1 5.1 %collective-permute-start.1 = (bf16[24,1152]{1,0:T(8,128)(2,1)S(1)}, bf16[24,1152]{1,0:T(8,128)(2,1)S(1)}, u32[]{:S(2)}, u32[]{:S(2)}) collective-permute-start(bf16[24,1152]{1,0:T(8,128)(2,1)S(1)} %get-tuple-element.21), channel_id=1, source_target_pairs={{0,8},{1,9},{2,10},{3,11},{4,12},{5,13},{6,14},{7,15},{8,0},{9,1},... | collective-permute-start | bytes 165896 | tf_op jit(solution)/shard_map/ppermute | solution.py:229
  8.1 5.1 %collective-permute-start.2 = (bf16[24,1152]{1,0:T(8,128)(2,1)S(1)}, bf16[24,1152]{1,0:T(8,128)(2,1)S(1)}, u32[]{:S(2)}, u32[]{:S(2)}) collective-permute-start(bf16[24,1152]{1,0:T(8,128)(2,1)S(1)} %get-tuple-element.22), channel_id=1, source_target_pairs={{0,4},{1,5},{2,6},{3,7},{4,0},{5,1},{6,2},{7,3},{8,12},{9,13},{10,... | collective-permute-start | bytes 165896 | tf_op jit(solution)/shard_map/ppermute | solution.py:229
  13.2 5.2 %collective-permute-start.5 = (bf16[96,768]{1,0:T(8,128)(2,1)S(1)}, bf16[96,768]{1,0:T(8,128)(2,1)S(1)}, u32[]{:S(2)}, u32[]{:S(2)}) collective-permute-start(bf16[96,768]{1,0:T(8,128)(2,1)S(1)} %pad_maximum_fusion.refs_4_), channel_id=1, source_target_pairs={{0,2},{1,3},{2,0},{3,1},{4,6},{5,7},{6,4},{7,5},{8,10},{9,11},{10,... | collective-permute-start | bytes 442376 | tf_op jit(solution)/shard_map/ppermute | solution.py:229
  13.8 7.1 %collective-permute-start.8 = (bf16[48,3072]{1,0:T(8,128)(2,1)S(1)}, bf16[48,3072]{1,0:T(8,128)(2,1)S(1)}, u32[]{:S(2)}, u32[]{:S(2)}) collective-permute-start(bf16[48,3072]{1,0:T(8,128)(2,1)S(1)} %collective-permute-done.3.refs_2_), channel_id=1, source_target_pairs={{0,16},{16,0},{1,17},{17,1},{2,18},{18,2},{3,19},{19,3},{4,20},{20... | collective-permute-start | bytes 884744 | tf_op jit(solution)/shard_map/ppermute | solution.py:232
  15.3 7.2 %collective-permute-start.7 = (bf16[96,3072]{1,0:T(8,128)(2,1)S(1)}, bf16[96,3072]{1,0:T(8,128)(2,1)S(1)}, u32[]{:S(2)}, u32[]{:S(2)}) collective-permute-start(bf16[96,3072]{1,0:T(8,128)(2,1)S(1)} %get-tuple-element.28.refs_0_), channel_id=1, source_target_pairs={{0,1},{1,0},{2,3},{3,2},{4,5},{5,4},{6,7},{7,6},{8,9},{9,8},{10,11... | collective-permute-start | bytes 1769480 | tf_op jit(solution)/shard_map/ppermute | solution.py:229
  15.3 3.7 %collective-permute-start.4 = (bf16[96,768]{1,0:T(8,128)(2,1)S(1)}, bf16[96,768]{1,0:T(8,128)(2,1)S(1)}, u32[]{:S(2)}, u32[]{:S(2)}) collective-permute-start(bf16[96,768]{1,0:T(8,128)(2,1)S(1)} %pad_maximum_fusion.refs_4_), channel_id=1, source_target_pairs={{0,1},{1,0},{2,3},{3,2},{4,5},{5,4},{6,7},{7,6},{8,9},{9,8},{10,11... | collective-permute-start | bytes 442376 | tf_op jit(solution)/shard_map/ppermute | solution.py:229
  18.4 1.4 %collective-permute-start.6 = (bf16[96,768]{1,0:T(8,128)(2,1)S(1)}, bf16[96,768]{1,0:T(8,128)(2,1)S(1)}, u32[]{:S(2)}, u32[]{:S(2)}) collective-permute-start(bf16[96,768]{1,0:T(8,128)(2,1)S(1)} %collective-permute-done.5.refs_6_), channel_id=1, source_target_pairs={{0,1},{1,0},{2,3},{3,2},{4,5},{5,4},{6,7},{7,6},{8,9},{9,8},{10,11... | collective-permute-start | bytes 442376 | tf_op jit(solution)/shard_map/ppermute | solution.py:229
  18.4 3.4 %collective-permute-start.9 = (bf16[48,3072]{1,0:T(8,128)(2,1)S(1)}, bf16[48,3072]{1,0:T(8,128)(2,1)S(1)}, u32[]{:S(2)}, u32[]{:S(2)}) collective-permute-start(bf16[48,3072]{1,0:T(8,128)(2,1)S(1)} %collective-permute-done.3.refs_2_), channel_id=1, source_target_pairs={{0,1},{1,0},{2,3},{3,2},{4,5},{5,4},{6,7},{7,6},{8,9},{9,8},{10,11... | collective-permute-start | bytes 884744 | tf_op jit(solution)/shard_map/ppermute | solution.py:229
  20.9 1.6 %collective-permute-start.10 = (bf16[48,3072]{1,0:T(8,128)(2,1)S(1)}, bf16[48,3072]{1,0:T(8,128)(2,1)S(1)}, u32[]{:S(2)}, u32[]{:S(2)}) collective-permute-start(bf16[48,3072]{1,0:T(8,128)(2,1)S(1)} %collective-permute-done.8.refs_3_), channel_id=1, source_target_pairs={{0,1},{1,0},{2,3},{3,2},{4,5},{5,4},{6,7},{7,6},{8,9},{9,8},{10,11... | collective-permute-start | bytes 884744 | tf_op jit(solution)/shard_map/ppermute | solution.py:229
  21.8 18.2 %copy-start = (f32[3072]{0:T(1024)S(1)}, f32[3072]{0:T(1024)}, u32[]{:S(2)}) copy-start(f32[3072]{0:T(1024)} %param.15) | copy-start | bytes 36868
  23.6 8.6 %collective-permute-start.11 = (bf16[24,3072]{1,0:T(8,128)(2,1)S(1)}, bf16[24,3072]{1,0:T(8,128)(2,1)S(1)}, u32[]{:S(2)}, u32[]{:S(2)}) collective-permute-start(bf16[24,3072]{1,0:T(8,128)(2,1)S(1)} %get-tuple-element.32), channel_id=1, source_target_pairs={{0,12},{1,13},{2,14},{3,15},{4,8},{5,9},{6,10},{7,11},{8,4},{9,5},... | collective-permute-start | bytes 442376 | tf_op jit(solution)/shard_map/ppermute | solution.py:229
  27.3 12.8 %collective-permute-start.12 = (bf16[24,3072]{1,0:T(8,128)(2,1)S(1)}, bf16[24,3072]{1,0:T(8,128)(2,1)S(1)}, u32[]{:S(2)}, u32[]{:S(2)}) collective-permute-start(bf16[24,3072]{1,0:T(8,128)(2,1)S(1)} %get-tuple-element.33), channel_id=1, source_target_pairs={{0,8},{1,9},{2,10},{3,11},{4,12},{5,13},{6,14},{7,15},{8,0},{9,1},... | collective-permute-start | bytes 442376 | tf_op jit(solution)/shard_map/ppermute | solution.py:229
  27.3 12.8 %collective-permute-start.13 = (bf16[24,3072]{1,0:T(8,128)(2,1)S(1)}, bf16[24,3072]{1,0:T(8,128)(2,1)S(1)}, u32[]{:S(2)}, u32[]{:S(2)}) collective-permute-start(bf16[24,3072]{1,0:T(8,128)(2,1)S(1)} %get-tuple-element.34), channel_id=1, source_target_pairs={{0,4},{1,5},{2,6},{3,7},{4,0},{5,1},{6,2},{7,3},{8,12},{9,13},{10,... | collective-permute-start | bytes 442376 | tf_op jit(solution)/shard_map/ppermute | solution.py:229

commit v9 on v8

--- a/solution.py
+++ b/solution.py
@@ -14,12 +14,12 @@
 HBM = pl.BlockSpec(memory_space=pltpu.HBM)
 
 
-def prepare_kernel(groups, members, chunks, *refs):
+def prepare_kernel(groups, members, *refs):
     sources, w_ref = refs[:6], refs[6]
     outs = refs[7:]
     qout, kvout, fulls = outs[0], outs[1], outs[1 : 1 + groups]
-    wout, wparts = outs[1 + groups], outs[2 + groups : 2 + groups + chunks]
-    query, key_new, value_new, kst, vst, est, packed, sems = outs[2 + groups + chunks :]
+    wout, wpart = outs[1 + groups], outs[2 + groups]
+    query, key_new, value_new, kst, vst, est, packed, sems = outs[3 + groups :]
     rows, width = query.shape
     me = lax.axis_index("patch")
     first = pl.multiple_of((me // 2) * (2 * rows), 2 * rows)
@@ -31,13 +31,12 @@
     }
     for i in order:
         copies[i].start()
-    moves = [pltpu.make_async_copy(w_ref, wout, sems.at[6])]
-    for i in range(chunks):
-        size, part = wparts[i].shape
-        left = sum(w.shape[1] for w in wparts[:i])
-        top = pl.multiple_of((lax.axis_index("groups") % 2) * size, size) if size < w_ref.shape[0] else 0
-        view = w_ref.at[pl.ds(top, size), pl.ds(left, part)]
-        moves.append(pltpu.make_async_copy(view, wparts[i], sems.at[7 + i]))
+    size = wpart.shape[0]
+    top = pl.multiple_of((lax.axis_index("groups") % 2) * size, size) if size < w_ref.shape[0] else 0
+    moves = [
+        pltpu.make_async_copy(w_ref.at[pl.ds(top, size)], wpart, sems.at[7]),
+        pltpu.make_async_copy(w_ref, wout, sems.at[6]),
+    ]
     for m in moves:
         m.start()
     heads = est.shape[0] // 2
@@ -83,19 +82,18 @@
         m.wait()
 
 
-def prepare(groups, members, chunks, split, query, key_new, value_new, key_stale, value_stale, powers, w_out):
+def prepare(groups, members, split, query, key_new, value_new, key_stale, value_stale, powers, w_out):
     rows, width = query.shape
     share = width // groups
     depth, model = w_out.shape
     outs = (
         [((rows, share), jnp.bfloat16), ((rows, 2 * share), jnp.bfloat16)]
         + [((rows, 3 * share), jnp.bfloat16)] * (groups - 1)
-        + [((depth, model), jnp.bfloat16)]
-        + [((depth // split, c), jnp.bfloat16) for c in chunks]
+        + [((depth, model), jnp.bfloat16), ((depth // split, model), jnp.bfloat16)]
     )
     sources = (query, key_new, value_new, key_stale, value_stale, powers, w_out)
     result = pl.pallas_call(
-        functools.partial(prepare_kernel, groups, members, len(chunks)),
+        functools.partial(prepare_kernel, groups, members),
         out_shape=[jax.ShapeDtypeStruct(*o) for o in outs],
         in_specs=[HBM] * 7,
         out_specs=[VMEM] * len(outs),
@@ -104,14 +102,14 @@
         + [
             pltpu.VMEM(powers.shape, jnp.int32),
             pltpu.VMEM((groups, rows, 2 * share), jnp.bfloat16),
-            pltpu.SemaphoreType.DMA((7 + len(chunks),)),
+            pltpu.SemaphoreType.DMA((8,)),
         ],
         compiler_params=pltpu.CompilerParams(vmem_limit_bytes=24 * 1024 * 1024),
         cost_estimate=pl.CostEstimate(
             flops=10 * rows * width, bytes_accessed=14 * rows * width + 4 * depth * model, transcendentals=0
         ),
     )(*(pltpu.with_memory_space_constraint(x, pltpu.HBM) for x in sources))
-    return result[0], result[1 : 1 + groups], result[1 + groups], result[2 + groups :]
+    return result[0], result[1 : 1 + groups], result[-2], result[-1]
 
 
 def attend_kernel(groups, dim, *refs):
@@ -164,24 +162,23 @@
     ws = refs[: len(places)]
     outs = refs[len(places) : len(places) + groups]
     wide, sems = refs[len(places) + groups :]
+    rows, width = outs[0].shape
     q = lax.axis_index("patch") % members
     side = lax.axis_index("groups") % 2
     copies = []
-    for i, (piece, (j, flip, col)) in enumerate(zip(ws, places)):
-        size, part = piece.shape
+    for i, (piece, (j, flip, left)) in enumerate(zip(ws, places)):
+        size = piece.shape[0]
         row = 0
         if j is not None:
             row = (q ^ j) * (size if flip is None else 2 * size)
             if flip is not None:
                 row = row + (side ^ flip) * size
             row = pl.multiple_of(row, size)
-        view = wide.at[pl.ds(row, size), pl.ds(col, part)]
-        copies.append(pltpu.make_async_copy(piece, view, sems.at[i]))
+        copies.append(pltpu.make_async_copy(piece.at[:, pl.ds(left, width)], wide.at[pl.ds(row, size)], sems.at[i]))
     for c in copies:
         c.start()
     for c in copies:
         c.wait()
-    rows, width = outs[0].shape
     tile = 512 if width % 512 == 0 else width
     for t in range(width // tile):
         cols = slice(t * tile, (t + 1) * tile)
@@ -190,19 +187,19 @@
             outs[i][:, cols] = part[i * rows : (i + 1) * rows].astype(outs[i].dtype)
 
 
-def project(groups, members, att, model, pieces, places):
+def project(groups, members, att, width, pieces, places):
     rows = att.shape[0] // groups
     share = att.shape[1]
     return pl.pallas_call(
         functools.partial(project_kernel, groups, members, places),
-        out_shape=[jax.ShapeDtypeStruct((rows, model), jnp.bfloat16)] * (groups - 1)
-        + [jax.ShapeDtypeStruct((rows, model), jnp.float32)],
+        out_shape=[jax.ShapeDtypeStruct((rows, width), jnp.bfloat16)] * (groups - 1)
+        + [jax.ShapeDtypeStruct((rows, width), jnp.float32)],
         in_specs=[VMEM] + [ANY] * len(pieces),
         out_specs=[VMEM] * groups,
-        scratch_shapes=[pltpu.VMEM((share, model), jnp.bfloat16), pltpu.SemaphoreType.DMA((len(pieces),))],
+        scratch_shapes=[pltpu.VMEM((share, width), jnp.bfloat16), pltpu.SemaphoreType.DMA((len(pieces),))],
         compiler_params=pltpu.CompilerParams(vmem_limit_bytes=24 * 1024 * 1024),
         cost_estimate=pl.CostEstimate(
-            flops=2 * groups * rows * share * model, bytes_accessed=2 * share * model, transcendentals=0
+            flops=2 * groups * rows * share * width, bytes_accessed=2 * share * width, transcendentals=0
         ),
     )(att, *pieces)
 
@@ -222,8 +219,8 @@
     share = width // groups
     depth, model = w_out.shape
     far = members // 2
-    shared = parts % 2 == 0 and depth % 32 == 0
-    chunks = [model]
+    shared = parts % 2 == 0 and members == 4 and depth % 32 == 0
+    half = model // 2
 
     def send(x, k, j):
         return lax.ppermute(x, "patch", [(p, ((p // members) ^ k) * members + (p % members) ^ j) for p in range(patch)])
@@ -238,49 +235,40 @@
             bit //= 2
         return [pieces[j] for j in range(members)]
 
-    own_query, fresh, w_own, w_parts = prepare(
-        groups, members, chunks, 2 if shared else 1, query, key_new, value_new, key_stale, value_stale, exponents.T, w_out
+    own_query, fresh, w_own, w_part = prepare(
+        groups, members, 2 if shared else 1, query, key_new, value_new, key_stale, value_stale, exponents.T, w_out
     )
     order = range(groups - 1, 0, -1)
     arrived = [send(fresh[k], k, 0) for k in order]
     both = jnp.concatenate([x[:, share:] for x in arrived] + [fresh[0]], axis=0)
-    mine = [send(w, 0, far) for w in w_parts] if shared else []
-    both = after(both, *mine)
-    swapped = [swap(w) for w in mine]
-    pieces = {0: both}
-    bit = far
-    while bit:
-        for j in list(pieces):
-            pieces[j ^ bit] = send(pieces[j], 0, bit)
-        bit //= 2
-    kvs = [pieces[j] for j in range(members)]
+    if shared:
+        y_part = send(w_part, 0, 2)
+        both = after(both, y_part)
+    kvs = spread({0: both}, far)
     att = attend(groups, dim, arrived + [own_query], kvs)
 
+    jobs = []
     if shared:
-        pieces, places = [w_own], [(0, None, 0)]
-        others = []
-        for c, w in enumerate(mine):
-            left = sum(chunks[:c])
-            others += [(w, (far, 0, left)), (swapped[c], (far, 1, left))]
-        bit = 1
-        while bit < far:
-            pieces, places = (
-                pieces + [send(after(x, both), 0, bit) for x in pieces],
-                places + [(p[0] ^ bit, p[1], p[2]) for p in places],
-            )
-            others = others + [(send(after(x, *(kvs if p[1] else [both])), 0, bit), (p[0] ^ bit, p[1], p[2])) for x, p in others]
-            bit *= 2
-        pieces = pieces + [x for x, _ in others]
-        places = places + [p for _, p in others]
+        w_core = send(after(w_own, both), 0, 1)
+        y_core = send(after(y_part, both), 0, 1)
+        x_part = swap(y_part)
+        edges = (0, half, model)
+        for left, right in zip(edges, edges[1:]):
+            x_core = send(after(x_part, att)[:, left:right], 0, 1)
+            pieces = [w_own, w_core, y_part, x_part, y_core, x_core]
+            places = [(0, None, left), (1, None, left), (2, 0, left), (2, 1, left), (3, 0, left), (3, 1, 0)]
+            jobs.append((right - left, pieces, places))
     else:
         spots = (lax.axis_index("patch") % members) ^ jnp.arange(members)
-        pieces = [jnp.stack(spread({0: w_parts[0]}, far))[spots].reshape(-1, model)]
-        places = [(None, None, 0)]
-    sums = project(groups, members, att, model, pieces, places)
-    total = sums[-1]
-    for k, part in zip(order, sums):
-        total = total + send(part, k, 0).astype(jnp.float32)
-    return (total * gate[None, :]).astype(jnp.bfloat16)
+        jobs.append((model, [jnp.stack(spread({0: w_own}, far))[spots].reshape(-1, model)], [(None, None, 0)]))
+    totals = []
+    for width, pieces, places in jobs:
+        sums = project(groups, members, att, width, pieces, places)
+        total = sums[-1]
+        for k, part in zip(order, sums):
+            total = total + send(part, k, 0).astype(jnp.float32)
+        totals.append(total)
+    return (jnp.concatenate(totals, axis=1) * gate[None, :]).astype(jnp.bfloat16)
 
 
 def solution(mesh):

time: 40.9 us -> 40.5 us (level)
  waiting for transfers between devices: 21.5 us -> 15.4 us
  starting transfers between devices: 15 us -> 20.1 us
  Pallas kernels: 3.54 us -> 4 us
    ppermute x13 -> x17, waiting for transfers between devices: 20.4 us -> 15.3 us  [send(): lax.ppermute(x, 'patch', [(p, (p // members ^ k) * members + p % members...]
    ppermute x13 -> x17, starting transfers between devices: 13.5 us -> 18.6 us  [send(): lax.ppermute(x, 'patch', [(p, (p // members ^ k) * members + p % members...]
    ppermute x1, waiting for transfers between devices: 1.06 us -> 0.13 us  [swap(): return lax.ppermute(x, 'groups', [(g, g ^ 1) for g in range(parts)])]
    pallas_call x1 -> x2, Pallas kernels: 1.13 us -> 1.58 us  [project(): pl.pallas_call(functools.partial(project_kernel, groups, members, places)...]
  transfers between devices with their start and end apart: 14 -> 18, of which waited for: 8 -> 8; matrix products, arithmetic and copies ran while one was open for 0% -> 0% of each run, Pallas kernels for 2% -> 6%
where the time goes in v9:
time: 40.5 us; the launch traced here: 40.4 us
  starting transfers between devices  20.1 us (50%)
  waiting for transfers between devices  15.4 us (38%)
  Pallas kernels  4 us (10%)
  other arithmetic  0.78 us (2%)
    ppermute x17, starting transfers between devices, send(): lax.ppermute(x, 'patch', [(p, (p // members ^ k) * members + p % members...  18.6 us
    ppermute x17, waiting for transfers between devices, send(): lax.ppermute(x, 'patch', [(p, (p // members ^ k) * members + p % members...  15.3 us
    pallas_call x2, Pallas kernels, project(): pl.pallas_call(functools.partial(project_kernel, groups, members, places)...  1.58 us
    pallas_call x1, Pallas kernels, prepare(): pl.pallas_call(functools.partial(prepare_kernel, groups, members), out_sh...  1.5 us
    ppermute x1, starting transfers between devices, swap(): return lax.ppermute(x, 'groups', [(g, g ^ 1) for g in range(parts)])  1.49 us
    pallas_call x1, Pallas kernels, attend(): pl.pallas_call(functools.partial(attend_kernel, groups, dim), out_shape=j...  0.92 us
  transfers between devices with their start and end apart: 18, of which 8 were waited for; matrix products, arithmetic and copies ran while one was open for 0% of the time, Pallas kernels for 6%

profile of v9, /device:TPU:0, one launch (start us, length us, event | category | flops | bytes accessed | tf_op | source)
XLA Modules:
  0.0 40.4 jit_solution(17889414370497506878)
XLA Ops:
  0.0 1.5 %shard_map.82 = (bf16[24,384]{1,0:T(8,128)(2,1)S(1)}, bf16[24,768]{1,0:T(8,128)(2,1)S(1)}, bf16[24,1152]{1,0:T(8,128)(2,1)S(1)}, bf16[24,1152]{1,0:T(8,128)(2,1)...) custom-call(bf16[24,1536]{1,0:T(8,128)(2,1)} %refs_0_.1, ...), custom_call_target="tpu_custom_call" | custom-call | flops 368640 | bytes 1695744 | tf_op jit(solution)/shard_map/pallas_call | solution.py:95
  1.5 3.0 %collective-permute-start.3 = (bf16[48,3072]{1,0:T(8,128)(2,1)S(1)}, bf16[48,3072]{1,0:T(8,128)(2,1)S(1)}, u32[]{:S(2)}, u32[]{:S(2)}) collective-permute-start(bf16[48,3072]{1,0:T(8,128)(2,1)S(1)} %get-tuple-element.29), channel_id=1, source_target_pairs={{0,2},{1,3},{2,0},{3,1},{4,6},{5,7},{6,4},{7,5},{8,10},{9,11},{10,... | collective-permute-start | bytes 884744 | tf_op jit(solution)/shard_map/ppermute | solution.py:226
  4.5 3.6 %collective-permute-start = (bf16[24,1152]{1,0:T(8,128)(2,1)S(1)}, bf16[24,1152]{1,0:T(8,128)(2,1)S(1)}, u32[]{:S(2)}, u32[]{:S(2)}) collective-permute-start(bf16[24,1152]{1,0:T(8,128)(2,1)S(1)} %get-tuple-element.24), channel_id=1, source_target_pairs={{0,12},{1,13},{2,14},{3,15},{4,8},{5,9},{6,10},{7,11},{8,4},{9,5},... | collective-permute-start | bytes 165896 | tf_op jit(solution)/shard_map/ppermute | solution.py:226
  8.1 0.0 collective-permute-start.1
  8.1 0.8 %collective-permute-start.2 = (bf16[24,1152]{1,0:T(8,128)(2,1)S(1)}, bf16[24,1152]{1,0:T(8,128)(2,1)S(1)}, u32[]{:S(2)}, u32[]{:S(2)}) collective-permute-start(bf16[24,1152]{1,0:T(8,128)(2,1)S(1)} %get-tuple-element.26), channel_id=1, source_target_pairs={{0,4},{1,5},{2,6},{3,7},{4,0},{5,1},{6,2},{7,3},{8,12},{9,13},{10,... | collective-permute-start | bytes 165896 | tf_op jit(solution)/shard_map/ppermute | solution.py:226
  8.9 2.2 %collective-permute-done.refs_0_ = bf16[24,1152]{1,0:T(8,128)(2,1)S(1)} collective-permute-done((bf16[24,1152]{1,0:T(8,128)(2,1)S(1)}, bf16[24,1152]{1,0:T(8,128)(2,1)S(1)}, u32[]{:S(2)}, u32[]{:S(2)}) %collective-permute-start) | collective-permute-done | bytes 55328 | tf_op jit(solution)/shard_map/ppermute | solution.py:226
  11.2 2.0 %collective-permute-done.1.refs_1_ = bf16[24,1152]{1,0:T(8,128)(2,1)S(1)} collective-permute-done((bf16[24,1152]{1,0:T(8,128)(2,1)S(1)}, bf16[24,1152]{1,0:T(8,128)(2,1)S(1)}, u32[]{:S(2)}, u32[]{:S(2)}) %collective-permute-start.1) | collective-permute-done | bytes 55328 | tf_op jit(solution)/shard_map/ppermute | solution.py:226
  13.2 0.0 collective-permute-done.2.refs_2_
  13.2 0.0 collective-permute-done.3.refs_2_
  13.2 0.6 %collective-permute-start.5 = (bf16[96,768]{1,0:T(8,128)(2,1)S(1)}, bf16[96,768]{1,0:T(8,128)(2,1)S(1)}, u32[]{:S(2)}, u32[]{:S(2)}) collective-permute-start(bf16[96,768]{1,0:T(8,128)(2,1)S(1)} %pad_maximum_fusion.refs_4_), channel_id=1, source_target_pairs={{0,2},{1,3},{2,0},{3,1},{4,6},{5,7},{6,4},{7,5},{8,10},{9,11},{10,... | collective-permute-start | bytes 442376 | tf_op jit(solution)/shard_map/ppermute | solution.py:226
  13.8 1.5 %collective-permute-start.8 = (bf16[48,3072]{1,0:T(8,128)(2,1)S(1)}, bf16[48,3072]{1,0:T(8,128)(2,1)S(1)}, u32[]{:S(2)}, u32[]{:S(2)}) collective-permute-start(bf16[48,3072]{1,0:T(8,128)(2,1)S(1)} %collective-permute-done.3.refs_2_), channel_id=1, source_target_pairs={{0,16},{16,0},{1,17},{17,1},{2,18},{18,2},{3,19},{19,3},{4,20},{20... | collective-permute-start | bytes 884744 | tf_op jit(solution)/shard_map/ppermute | solution.py:229
  15.3 0.0 collective-permute-start.4
  15.3 3.1 %collective-permute-done.5.refs_6_ = bf16[96,768]{1,0:T(8,128)(2,1)S(1)} collective-permute-done((bf16[96,768]{1,0:T(8,128)(2,1)S(1)}, bf16[96,768]{1,0:T(8,128)(2,1)S(1)}, u32[]{:S(2)}, u32[]{:S(2)}) %collective-permute-start.5) | collective-permute-done | bytes 147488 | tf_op jit(solution)/shard_map/ppermute | solution.py:226
  18.5 0.0 collective-permute-start.6
  18.5 0.5 %collective-permute-start.9 = (bf16[48,3072]{1,0:T(8,128)(2,1)S(1)}, bf16[48,3072]{1,0:T(8,128)(2,1)S(1)}, u32[]{:S(2)}, u32[]{:S(2)}) collective-permute-start(bf16[48,3072]{1,0:T(8,128)(2,1)S(1)} %collective-permute-done.3.refs_2_), channel_id=1, source_target_pairs={{0,1},{1,0},{2,3},{3,2},{4,5},{5,4},{6,7},{7,6},{8,9},{9,8},{10,11... | collective-permute-start | bytes 884744 | tf_op jit(solution)/shard_map/ppermute | solution.py:226
  19.0 0.0 collective-permute-start.7
  19.0 0.0 collective-permute-done.4.refs_5_
  19.0 0.9 %collective-permute-done.6.refs_7_ = bf16[96,768]{1,0:T(8,128)(2,1)S(1)} collective-permute-done((bf16[96,768]{1,0:T(8,128)(2,1)S(1)}, bf16[96,768]{1,0:T(8,128)(2,1)S(1)}, u32[]{:S(2)}, u32[]{:S(2)}) %collective-permute-start.6) | collective-permute-done | bytes 147488 | tf_op jit(solution)/shard_map/ppermute | solution.py:226
  19.8 0.9 %shard_map.83.att = bf16[96,384]{1,0:T(8,128)(2,1)S(1)} custom-call(bf16[24,1152]{1,0:T(8,128)(2,1)S(1)} %collective-permute-done.refs_0_, bf16[24,1152]{1,0:T(8,128)(2,1)S(1)} %collective-permute-done.1.refs_1_, bf16[24,1152]{1,0:T(8,128)(2,1)S(1)} %collective-permute-done.2.refs_2_, bf16[24,384]{1,0:T(8,128)(2,1)S(1)} %get-tuple-element.27.refs_3_, ...), custom_call_target="tpu_custom_call" | custom-call | flops 56623104 | bytes 589824 | tf_op jit(solution)/shard_map/pallas_call | solution.py:146
  20.8 0.1 collective-permute-done.8.refs_3_
  20.9 0.1 collective-permute-start.10
  21.0 0.5 %collective-permute-start.14 = (bf16[48,1536]{1,0:T(8,128)(2,1)S(1)}, bf16[48,1536]{1,0:T(8,128)(2,1)S(1)}, u32[]{:S(2)}, u32[]{:S(2)}) collective-permute-start(bf16[48,1536]{1,0:T(8,128)(2,1)S(1)} %get-tuple-element.44), channel_id=1, source_target_pairs={{0,1},{1,0},{2,3},{3,2},{4,5},{5,4},{6,7},{7,6},{8,9},{9,8},{10,11... | collective-permute-start | bytes 442376 | tf_op jit(solution)/shard_map/ppermute | solution.py:226
  21.5 0.0 collective-permute-done.9.refs_4_
  21.5 0.9 %collective-permute-done.10.refs_5_ = bf16[48,1536]{1,0:T(8,128)(2,1)S(1)} collective-permute-done((bf16[48,1536]{1,0:T(8,128)(2,1)S(1)}, bf16[48,1536]{1,0:T(8,128)(2,1)S(1)}, u32[]{:S(2)}, u32[]{:S(2)}) %collective-permute-start.10) | collective-permute-done | bytes 147488 | tf_op jit(solution)/shard_map/ppermute | solution.py:226
  22.3 0.0 collective-permute-done.7.refs_1_
  22.3 0.8 %shard_map.84 = (bf16[24,1536]{1,0:T(8,128)(2,1)S(1)}, bf16[24,1536]{1,0:T(8,128)(2,1)S(1)}, bf16[24,1536]{1,0:T(8,128)(2,1)S(1)}, f32[24,1536]{1,0:T(8,128)S(1)}) custom-call(bf16[96,384]{1,0:T(8,128)(2,1)S(1)} %shard_map.83.att, bf16[96,3072]{1,0:T(8,128)(2,1)S(1)} %get-tuple-element.32.refs_0_, bf16[96,3072]{1,0:T(8,128)(2,1)S(1)} %collective-permute-done.7.refs_1_, ...), custom_call_target="tpu_custom_call" | custom-call | flops 113246208 | bytes 1179648 | tf_op jit(solution)/shard_map/pallas_call | solution.py:193
  23.1 3.7 %collective-permute-start.11 = (bf16[24,1536]{1,0:T(8,128)(2,1)S(1)}, bf16[24,1536]{1,0:T(8,128)(2,1)S(1)}, u32[]{:S(2)}, u32[]{:S(2)}) collective-permute-start(bf16[24,1536]{1,0:T(8,128)(2,1)S(1)} %get-tuple-element.36), channel_id=1, source_target_pairs={{0,12},{1,13},{2,14},{3,15},{4,8},{5,9},{6,10},{7,11},{8,4},{9,5},... | collective-permute-start | bytes 221192 | tf_op jit(solution)/shard_map/ppermute | solution.py:226
  26.8 0.0 collective-permute-start.12
  26.8 0.0 copy-start
  26.8 0.8 %collective-permute-start.13 = (bf16[24,1536]{1,0:T(8,128)(2,1)S(1)}, bf16[24,1536]{1,0:T(8,128)(2,1)S(1)}, u32[]{:S(2)}, u32[]{:S(2)}) collective-permute-start(bf16[24,1536]{1,0:T(8,128)(2,1)S(1)} %get-tuple-element.38), channel_id=1, source_target_pairs={{0,4},{1,5},{2,6},{3,7},{4,0},{5,1},{6,2},{7,3},{8,12},{9,13},{10,... | collective-permute-start | bytes 221192 | tf_op jit(solution)/shard_map/ppermute | solution.py:226
  27.6 0.0 collective-permute-done.14.refs_5_
  27.6 0.8 %shard_map.85 = (bf16[24,1536]{1,0:T(8,128)(2,1)S(1)}, bf16[24,1536]{1,0:T(8,128)(2,1)S(1)}, bf16[24,1536]{1,0:T(8,128)(2,1)S(1)}, f32[24,1536]{1,0:T(8,128)S(1)}) custom-call(bf16[96,384]{1,0:T(8,128)(2,1)S(1)} %shard_map.83.att, bf16[96,3072]{1,0:T(8,128)(2,1)S(1)} %get-tuple-element.32.refs_0_, bf16[96,3072]{1,0:T(8,128)(2,1)S(1)} %collective-permute-done.7.refs_1_, ...), custom_call_target="tpu_custom_call" | custom-call | flops 113246208 | bytes 1179648 | tf_op jit(solution)/shard_map/pallas_call | solution.py:193
  28.4 3.7 %collective-permute-start.15 = (bf16[24,1536]{1,0:T(8,128)(2,1)S(1)}, bf16[24,1536]{1,0:T(8,128)(2,1)S(1)}, u32[]{:S(2)}, u32[]{:S(2)}) collective-permute-start(bf16[24,1536]{1,0:T(8,128)(2,1)S(1)} %get-tuple-element.40), channel_id=1, source_target_pairs={{0,12},{1,13},{2,14},{3,15},{4,8},{5,9},{6,10},{7,11},{8,4},{9,5},... | collective-permute-start | bytes 221192 | tf_op jit(solution)/shard_map/ppermute | solution.py:226
  32.1 0.0 collective-permute-start.16
  32.1 0.0 collective-permute-done.11
  32.1 1.4 %collective-permute-start.17 = (bf16[24,1536]{1,0:T(8,128)(2,1)S(1)}, bf16[24,1536]{1,0:T(8,128)(2,1)S(1)}, u32[]{:S(2)}, u32[]{:S(2)}) collective-permute-start(bf16[24,1536]{1,0:T(8,128)(2,1)S(1)} %get-tuple-element.42), channel_id=1, source_target_pairs={{0,4},{1,5},{2,6},{3,7},{4,0},{5,1},{6,2},{7,3},{8,12},{9,13},{10,... | collective-permute-start | bytes 221192 | tf_op jit(solution)/shard_map/ppermute | solution.py:226
  33.4 3.7 %collective-permute-done.12 = bf16[24,1536]{1,0:T(8,128)(2,1)S(1)} collective-permute-done((bf16[24,1536]{1,0:T(8,128)(2,1)S(1)}, bf16[24,1536]{1,0:T(8,128)(2,1)S(1)}, u32[]{:S(2)}, u32[]{:S(2)}) %collective-permute-start.12) | collective-permute-done | bytes 73760 | tf_op jit(solution)/shard_map/ppermute | solution.py:226
  37.2 0.0 collective-permute-done.13
  37.2 0.0 collective-permute-done.15
  37.2 2.4 %collective-permute-done.16 = bf16[24,1536]{1,0:T(8,128)(2,1)S(1)} collective-permute-done((bf16[24,1536]{1,0:T(8,128)(2,1)S(1)}, bf16[24,1536]{1,0:T(8,128)(2,1)S(1)}, u32[]{:S(2)}, u32[]{:S(2)}) %collective-permute-start.16) | collective-permute-done | bytes 73760 | tf_op jit(solution)/shard_map/ppermute | solution.py:226
  39.6 0.0 collective-permute-done.17
  39.7 0.0 copy-done
  39.7 0.7 %fusion = bf16[24,3072]{1,0:T(8,128)(2,1)} fusion(f32[24,1536]{1,0:T(8,128)S(1)} %convert_add_fusion, f32[24,1536]{1,0:T(8,128)S(1)} %convert_add_fusion.1, f32[3072]{0:T(1024)S(1)} %copy-done), kind=kLoop, calls=%fused_computation.1 | loop fusion | flops 221184 | bytes 454656 | tf_op jit(solution)/shard_map/convert_element_type | solution.py:271
  (7 shorter events, 0.1 us)
Async XLA Ops:
  1.5 11.7 %collective-permute-start.3 = (bf16[48,3072]{1,0:T(8,128)(2,1)S(1)}, bf16[48,3072]{1,0:T(8,128)(2,1)S(1)}, u32[]{:S(2)}, u32[]{:S(2)}) collective-permute-start(bf16[48,3072]{1,0:T(8,128)(2,1)S(1)} %get-tuple-element.29), channel_id=1, source_target_pairs={{0,2},{1,3},{2,0},{3,1},{4,6},{5,7},{6,4},{7,5},{8,10},{9,11},{10,... | collective-permute-start | bytes 884744 | tf_op jit(solution)/shard_map/ppermute | solution.py:226
  4.5 6.6 %collective-permute-start = (bf16[24,1152]{1,0:T(8,128)(2,1)S(1)}, bf16[24,1152]{1,0:T(8,128)(2,1)S(1)}, u32[]{:S(2)}, u32[]{:S(2)}) collective-permute-start(bf16[24,1152]{1,0:T(8,128)(2,1)S(1)} %get-tuple-element.24), channel_id=1, source_target_pairs={{0,12},{1,13},{2,14},{3,15},{4,8},{5,9},{6,10},{7,11},{8,4},{9,5},... | collective-permute-start | bytes 165896 | tf_op jit(solution)/shard_map/ppermute | solution.py:226
  8.1 5.1 %collective-permute-start.1 = (bf16[24,1152]{1,0:T(8,128)(2,1)S(1)}, bf16[24,1152]{1,0:T(8,128)(2,1)S(1)}, u32[]{:S(2)}, u32[]{:S(2)}) collective-permute-start(bf16[24,1152]{1,0:T(8,128)(2,1)S(1)} %get-tuple-element.25), channel_id=1, source_target_pairs={{0,8},{1,9},{2,10},{3,11},{4,12},{5,13},{6,14},{7,15},{8,0},{9,1},... | collective-permute-start | bytes 165896 | tf_op jit(solution)/shard_map/ppermute | solution.py:226
  8.1 5.1 %collective-permute-start.2 = (bf16[24,1152]{1,0:T(8,128)(2,1)S(1)}, bf16[24,1152]{1,0:T(8,128)(2,1)S(1)}, u32[]{:S(2)}, u32[]{:S(2)}) collective-permute-start(bf16[24,1152]{1,0:T(8,128)(2,1)S(1)} %get-tuple-element.26), channel_id=1, source_target_pairs={{0,4},{1,5},{2,6},{3,7},{4,0},{5,1},{6,2},{7,3},{8,12},{9,13},{10,... | collective-permute-start | bytes 165896 | tf_op jit(solution)/shard_map/ppermute | solution.py:226
  13.2 5.2 %collective-permute-start.5 = (bf16[96,768]{1,0:T(8,128)(2,1)S(1)}, bf16[96,768]{1,0:T(8,128)(2,1)S(1)}, u32[]{:S(2)}, u32[]{:S(2)}) collective-permute-start(bf16[96,768]{1,0:T(8,128)(2,1)S(1)} %pad_maximum_fusion.refs_4_), channel_id=1, source_target_pairs={{0,2},{1,3},{2,0},{3,1},{4,6},{5,7},{6,4},{7,5},{8,10},{9,11},{10,... | collective-permute-start | bytes 442376 | tf_op jit(solution)/shard_map/ppermute | solution.py:226
  13.8 7.1 %collective-permute-start.8 = (bf16[48,3072]{1,0:T(8,128)(2,1)S(1)}, bf16[48,3072]{1,0:T(8,128)(2,1)S(1)}, u32[]{:S(2)}, u32[]{:S(2)}) collective-permute-start(bf16[48,3072]{1,0:T(8,128)(2,1)S(1)} %collective-permute-done.3.refs_2_), channel_id=1, source_target_pairs={{0,16},{16,0},{1,17},{17,1},{2,18},{18,2},{3,19},{19,3},{4,20},{20... | collective-permute-start | bytes 884744 | tf_op jit(solution)/shard_map/ppermute | solution.py:229
  15.3 3.7 %collective-permute-start.4 = (bf16[96,768]{1,0:T(8,128)(2,1)S(1)}, bf16[96,768]{1,0:T(8,128)(2,1)S(1)}, u32[]{:S(2)}, u32[]{:S(2)}) collective-permute-start(bf16[96,768]{1,0:T(8,128)(2,1)S(1)} %pad_maximum_fusion.refs_4_), channel_id=1, source_target_pairs={{0,1},{1,0},{2,3},{3,2},{4,5},{5,4},{6,7},{7,6},{8,9},{9,8},{10,11... | collective-permute-start | bytes 442376 | tf_op jit(solution)/shard_map/ppermute | solution.py:226
  18.5 1.4 %collective-permute-start.6 = (bf16[96,768]{1,0:T(8,128)(2,1)S(1)}, bf16[96,768]{1,0:T(8,128)(2,1)S(1)}, u32[]{:S(2)}, u32[]{:S(2)}) collective-permute-start(bf16[96,768]{1,0:T(8,128)(2,1)S(1)} %collective-permute-done.5.refs_6_), channel_id=1, source_target_pairs={{0,1},{1,0},{2,3},{3,2},{4,5},{5,4},{6,7},{7,6},{8,9},{9,8},{10,11... | collective-permute-start | bytes 442376 | tf_op jit(solution)/shard_map/ppermute | solution.py:226
  18.5 3.0 %collective-permute-start.9 = (bf16[48,3072]{1,0:T(8,128)(2,1)S(1)}, bf16[48,3072]{1,0:T(8,128)(2,1)S(1)}, u32[]{:S(2)}, u32[]{:S(2)}) collective-permute-start(bf16[48,3072]{1,0:T(8,128)(2,1)S(1)} %collective-permute-done.3.refs_2_), channel_id=1, source_target_pairs={{0,1},{1,0},{2,3},{3,2},{4,5},{5,4},{6,7},{7,6},{8,9},{9,8},{10,11... | collective-permute-start | bytes 884744 | tf_op jit(solution)/shard_map/ppermute | solution.py:226
  19.0 3.4 %collective-permute-start.7 = (bf16[96,3072]{1,0:T(8,128)(2,1)S(1)}, bf16[96,3072]{1,0:T(8,128)(2,1)S(1)}, u32[]{:S(2)}, u32[]{:S(2)}) collective-permute-start(bf16[96,3072]{1,0:T(8,128)(2,1)S(1)} %get-tuple-element.32.refs_0_), channel_id=1, source_target_pairs={{0,1},{1,0},{2,3},{3,2},{4,5},{5,4},{6,7},{7,6},{8,9},{9,8},{10,11... | collective-permute-start | bytes 1769480 | tf_op jit(solution)/shard_map/ppermute | solution.py:226
  20.9 1.4 %collective-permute-start.10 = (bf16[48,1536]{1,0:T(8,128)(2,1)S(1)}, bf16[48,1536]{1,0:T(8,128)(2,1)S(1)}, u32[]{:S(2)}, u32[]{:S(2)}) collective-permute-start(bf16[48,1536]{1,0:T(8,128)(2,1)S(1)} %get-tuple-element.43), channel_id=1, source_target_pairs={{0,1},{1,0},{2,3},{3,2},{4,5},{5,4},{6,7},{7,6},{8,9},{9,8},{10,11... | collective-permute-start | bytes 442376 | tf_op jit(solution)/shard_map/ppermute | solution.py:226
  21.0 6.6 %collective-permute-start.14 = (bf16[48,1536]{1,0:T(8,128)(2,1)S(1)}, bf16[48,1536]{1,0:T(8,128)(2,1)S(1)}, u32[]{:S(2)}, u32[]{:S(2)}) collective-permute-start(bf16[48,1536]{1,0:T(8,128)(2,1)S(1)} %get-tuple-element.44), channel_id=1, source_target_pairs={{0,1},{1,0},{2,3},{3,2},{4,5},{5,4},{6,7},{7,6},{8,9},{9,8},{10,11... | collective-permute-start | bytes 442376 | tf_op jit(solution)/shard_map/ppermute | solution.py:226
  23.1 8.9 %collective-permute-start.11 = (bf16[24,1536]{1,0:T(8,128)(2,1)S(1)}, bf16[24,1536]{1,0:T(8,128)(2,1)S(1)}, u32[]{:S(2)}, u32[]{:S(2)}) collective-permute-start(bf16[24,1536]{1,0:T(8,128)(2,1)S(1)} %get-tuple-element.36), channel_id=1, source_target_pairs={{0,12},{1,13},{2,14},{3,15},{4,8},{5,9},{6,10},{7,11},{8,4},{9,5},... | collective-permute-start | bytes 221192 | tf_op jit(solution)/shard_map/ppermute | solution.py:226
  26.8 10.3 %collective-permute-start.12 = (bf16[24,1536]{1,0:T(8,128)(2,1)S(1)}, bf16[24,1536]{1,0:T(8,128)(2,1)S(1)}, u32[]{:S(2)}, u32[]{:S(2)}) collective-permute-start(bf16[24,1536]{1,0:T(8,128)(2,1)S(1)} %get-tuple-element.37), channel_id=1, source_target_pairs={{0,8},{1,9},{2,10},{3,11},{4,12},{5,13},{6,14},{7,15},{8,0},{9,1},... | collective-permute-start | bytes 221192 | tf_op jit(solution)/shard_map/ppermute | solution.py:226
  26.8 12.9 %copy-start = (f32[3072]{0:T(1024)S(1)}, f32[3072]{0:T(1024)}, u32[]{:S(2)}) copy-start(f32[3072]{0:T(1024)} %param.15) | copy-start | bytes 36868
  26.8 10.3 %collective-permute-start.13 = (bf16[24,1536]{1,0:T(8,128)(2,1)S(1)}, bf16[24,1536]{1,0:T(8,128)(2,1)S(1)}, u32[]{:S(2)}, u32[]{:S(2)}) collective-permute-start(bf16[24,1536]{1,0:T(8,128)(2,1)S(1)} %get-tuple-element.38), channel_id=1, source_target_pairs={{0,4},{1,5},{2,6},{3,7},{4,0},{5,1},{6,2},{7,3},{8,12},{9,13},{10,... | collective-permute-start | bytes 221192 | tf_op jit(solution)/shard_map/ppermute | solution.py:226
  28.4 8.8 %collective-permute-start.15 = (bf16[24,1536]{1,0:T(8,128)(2,1)S(1)}, bf16[24,1536]{1,0:T(8,128)(2,1)S(1)}, u32[]{:S(2)}, u32[]{:S(2)}) collective-permute-start(bf16[24,1536]{1,0:T(8,128)(2,1)S(1)} %get-tuple-element.40), channel_id=1, source_target_pairs={{0,12},{1,13},{2,14},{3,15},{4,8},{5,9},{6,10},{7,11},{8,4},{9,5},... | collective-permute-start | bytes 221192 | tf_op jit(solution)/shard_map/ppermute | solution.py:226
  32.1 7.6 %collective-permute-start.16 = (bf16[24,1536]{1,0:T(8,128)(2,1)S(1)}, bf16[24,1536]{1,0:T(8,128)(2,1)S(1)}, u32[]{:S(2)}, u32[]{:S(2)}) collective-permute-start(bf16[24,1536]{1,0:T(8,128)(2,1)S(1)} %get-tuple-element.41), channel_id=1, source_target_pairs={{0,8},{1,9},{2,10},{3,11},{4,12},{5,13},{6,14},{7,15},{8,0},{9,1},... | collective-permute-start | bytes 221192 | tf_op jit(solution)/shard_map/ppermute | solution.py:226
  32.1 7.6 %collective-permute-start.17 = (bf16[24,1536]{1,0:T(8,128)(2,1)S(1)}, bf16[24,1536]{1,0:T(8,128)(2,1)S(1)}, u32[]{:S(2)}, u32[]{:S(2)}) collective-permute-start(bf16[24,1536]{1,0:T(8,128)(2,1)S(1)} %get-tuple-element.42), channel_id=1, source_target_pairs={{0,4},{1,5},{2,6},{3,7},{4,0},{5,1},{6,2},{7,3},{8,12},{9,13},{10,... | collective-permute-start | bytes 221192 | tf_op jit(solution)/shard_map/ppermute | solution.py:226

commit v10 on v9

--- a/solution.py
+++ b/solution.py
@@ -254,7 +254,7 @@
         x_part = swap(y_part)
         edges = (0, half, model)
         for left, right in zip(edges, edges[1:]):
-            x_core = send(after(x_part, att)[:, left:right], 0, 1)
+            x_core = send(after(x_part, kvs[far])[:, left:right], 0, 1)
             pieces = [w_own, w_core, y_part, x_part, y_core, x_core]
             places = [(0, None, left), (1, None, left), (2, 0, left), (2, 1, left), (3, 0, left), (3, 1, 0)]
             jobs.append((right - left, pieces, places))
@@ -264,6 +264,7 @@
     totals = []
     for width, pieces, places in jobs:
         sums = project(groups, members, att, width, pieces, places)
+        att = after(att, *sums)
         total = sums[-1]
         for k, part in zip(order, sums):
             total = total + send(part, k, 0).astype(jnp.float32)

time: 40.5 us -> 39.4 us (0.973)
  waiting for transfers between devices: 15.4 us -> 13 us
  starting transfers between devices: 20.1 us -> 21.2 us
    ppermute x17, waiting for transfers between devices: 15.3 us -> 11.8 us  [send(): lax.ppermute(x, 'patch', [(p, (p // members ^ k) * members + p % members...]
    ppermute x1, waiting for transfers between devices: 0.13 us -> 1.2 us  [swap(): return lax.ppermute(x, 'groups', [(g, g ^ 1) for g in range(parts)])]
    ppermute x17, starting transfers between devices: 18.6 us -> 19.5 us  [send(): lax.ppermute(x, 'patch', [(p, (p // members ^ k) * members + p % members...]
  transfers between devices with their start and end apart: 18 -> 18, of which waited for: 8 -> 5; matrix products, arithmetic and copies ran while one was open for 0% -> 0% of each run, Pallas kernels for 6% -> 6%
where the time goes in v10:
time: 39.4 us; the launch traced here: 39.3 us
  starting transfers between devices  21.2 us (54%)
  waiting for transfers between devices  13 us (33%)
  Pallas kernels  4.03 us (10%)
  other arithmetic  0.78 us (2%)
    ppermute x17, starting transfers between devices, send(): lax.ppermute(x, 'patch', [(p, (p // members ^ k) * members + p % members...  19.5 us
    ppermute x17, waiting for transfers between devices, send(): lax.ppermute(x, 'patch', [(p, (p // members ^ k) * members + p % members...  11.8 us
    ppermute x1, starting transfers between devices, swap(): return lax.ppermute(x, 'groups', [(g, g ^ 1) for g in range(parts)])  1.71 us
    pallas_call x2, Pallas kernels, project(): pl.pallas_call(functools.partial(project_kernel, groups, members, places)...  1.6 us
    pallas_call x1, Pallas kernels, prepare(): pl.pallas_call(functools.partial(prepare_kernel, groups, members), out_sh...  1.5 us
    ppermute x1, waiting for transfers between devices, swap(): return lax.ppermute(x, 'groups', [(g, g ^ 1) for g in range(parts)])  1.2 us
    pallas_call x1, Pallas kernels, attend(): pl.pallas_call(functools.partial(attend_kernel, groups, dim), out_shape=j...  0.93 us
  transfers between devices with their start and end apart: 18, of which 5 were waited for; matrix products, arithmetic and copies ran while one was open for 0% of the time, Pallas kernels for 6%

profile of v10, /device:TPU:0, one launch (start us, length us, event | category | flops | bytes accessed | tf_op | source)
XLA Modules:
  0.0 39.3 jit_solution(7000165931356080241)
XLA Ops:
  0.0 1.5 %shard_map.82 = (bf16[24,384]{1,0:T(8,128)(2,1)S(1)}, bf16[24,768]{1,0:T(8,128)(2,1)S(1)}, bf16[24,1152]{1,0:T(8,128)(2,1)S(1)}, bf16[24,1152]{1,0:T(8,128)(2,1)...) custom-call(bf16[24,1536]{1,0:T(8,128)(2,1)} %refs_0_.1, ...), custom_call_target="tpu_custom_call" | custom-call | flops 368640 | bytes 1695744 | tf_op jit(solution)/shard_map/pallas_call | solution.py:95
  1.5 3.0 %collective-permute-start.3 = (bf16[48,3072]{1,0:T(8,128)(2,1)S(1)}, bf16[48,3072]{1,0:T(8,128)(2,1)S(1)}, u32[]{:S(2)}, u32[]{:S(2)}) collective-permute-start(bf16[48,3072]{1,0:T(8,128)(2,1)S(1)} %get-tuple-element.30), channel_id=1, source_target_pairs={{0,2},{1,3},{2,0},{3,1},{4,6},{5,7},{6,4},{7,5},{8,10},{9,11},{10,... | collective-permute-start | bytes 884744 | tf_op jit(solution)/shard_map/ppermute | solution.py:226
  4.5 3.6 %collective-permute-start = (bf16[24,1152]{1,0:T(8,128)(2,1)S(1)}, bf16[24,1152]{1,0:T(8,128)(2,1)S(1)}, u32[]{:S(2)}, u32[]{:S(2)}) collective-permute-start(bf16[24,1152]{1,0:T(8,128)(2,1)S(1)} %get-tuple-element.25), channel_id=1, source_target_pairs={{0,12},{1,13},{2,14},{3,15},{4,8},{5,9},{6,10},{7,11},{8,4},{9,5},... | collective-permute-start | bytes 165896 | tf_op jit(solution)/shard_map/ppermute | solution.py:226
  8.1 0.0 collective-permute-start.1
  8.1 0.8 %collective-permute-start.2 = (bf16[24,1152]{1,0:T(8,128)(2,1)S(1)}, bf16[24,1152]{1,0:T(8,128)(2,1)S(1)}, u32[]{:S(2)}, u32[]{:S(2)}) collective-permute-start(bf16[24,1152]{1,0:T(8,128)(2,1)S(1)} %get-tuple-element.27), channel_id=1, source_target_pairs={{0,4},{1,5},{2,6},{3,7},{4,0},{5,1},{6,2},{7,3},{8,12},{9,13},{10,... | collective-permute-start | bytes 165896 | tf_op jit(solution)/shard_map/ppermute | solution.py:226
  8.9 2.6 %collective-permute-done.3.refs_2_ = bf16[48,3072]{1,0:T(8,128)(2,1)S(1)} collective-permute-done((bf16[48,3072]{1,0:T(8,128)(2,1)S(1)}, bf16[48,3072]{1,0:T(8,128)(2,1)S(1)}, u32[]{:S(2)}, u32[]{:S(2)}) %collective-permute-start.3) | collective-permute-done | bytes 294944 | tf_op jit(solution)/shard_map/ppermute | solution.py:226
  11.5 1.7 %collective-permute-start.8 = (bf16[48,3072]{1,0:T(8,128)(2,1)S(1)}, bf16[48,3072]{1,0:T(8,128)(2,1)S(1)}, u32[]{:S(2)}, u32[]{:S(2)}) collective-permute-start(bf16[48,3072]{1,0:T(8,128)(2,1)S(1)} %collective-permute-done.3.refs_2_), channel_id=1, source_target_pairs={{0,16},{16,0},{1,17},{17,1},{2,18},{18,2},{3,19},{19,3},{4,20},{20... | collective-permute-start | bytes 884744 | tf_op jit(solution)/shard_map/ppermute | solution.py:229
  13.3 0.0 collective-permute-done.refs_0_
  13.3 0.0 collective-permute-done.1.refs_1_
  13.3 0.0 collective-permute-done.2.refs_2_
  13.3 1.6 %collective-permute-start.5 = (bf16[96,768]{1,0:T(8,128)(2,1)S(1)}, bf16[96,768]{1,0:T(8,128)(2,1)S(1)}, u32[]{:S(2)}, u32[]{:S(2)}) collective-permute-start(bf16[96,768]{1,0:T(8,128)(2,1)S(1)} %pad_maximum_fusion.refs_4_), channel_id=1, source_target_pairs={{0,2},{1,3},{2,0},{3,1},{4,6},{5,7},{6,4},{7,5},{8,10},{9,11},{10,... | collective-permute-start | bytes 442376 | tf_op jit(solution)/shard_map/ppermute | solution.py:226
  14.9 0.0 collective-permute-start.4
  14.9 0.5 %collective-permute-start.9 = (bf16[48,3072]{1,0:T(8,128)(2,1)S(1)}, bf16[48,3072]{1,0:T(8,128)(2,1)S(1)}, u32[]{:S(2)}, u32[]{:S(2)}) collective-permute-start(bf16[48,3072]{1,0:T(8,128)(2,1)S(1)} %collective-permute-done.3.refs_2_), channel_id=1, source_target_pairs={{0,1},{1,0},{2,3},{3,2},{4,5},{5,4},{6,7},{7,6},{8,9},{9,8},{10,11... | collective-permute-start | bytes 884744 | tf_op jit(solution)/shard_map/ppermute | solution.py:226
  15.4 0.0 collective-permute-start.7
  15.4 3.1 %collective-permute-done.5.refs_6_ = bf16[96,768]{1,0:T(8,128)(2,1)S(1)} collective-permute-done((bf16[96,768]{1,0:T(8,128)(2,1)S(1)}, bf16[96,768]{1,0:T(8,128)(2,1)S(1)}, u32[]{:S(2)}, u32[]{:S(2)}) %collective-permute-start.5) | collective-permute-done | bytes 147488 | tf_op jit(solution)/shard_map/ppermute | solution.py:226
  18.5 0.0 collective-permute-start.6
  18.5 1.2 %collective-permute-done.8.refs_3_ = bf16[48,3072]{1,0:T(8,128)(2,1)S(1)} collective-permute-done((bf16[48,3072]{1,0:T(8,128)(2,1)S(1)}, bf16[48,3072]{1,0:T(8,128)(2,1)S(1)}, u32[]{:S(2)}, u32[]{:S(2)}) %collective-permute-start.8) | collective-permute-done | bytes 294944 | tf_op jit(solution)/shard_map/ppermute | solution.py:229
  19.8 0.1 collective-permute-start.10
  19.8 0.0 collective-permute-done.4.refs_5_
  19.9 0.5 %collective-permute-start.14 = (bf16[48,1536]{1,0:T(8,128)(2,1)S(1)}, bf16[48,1536]{1,0:T(8,128)(2,1)S(1)}, u32[]{:S(2)}, u32[]{:S(2)}) collective-permute-start(bf16[48,1536]{1,0:T(8,128)(2,1)S(1)} %get-tuple-element.45), channel_id=1, source_target_pairs={{0,1},{1,0},{2,3},{3,2},{4,5},{5,4},{6,7},{7,6},{8,9},{9,8},{10,11... | collective-permute-start | bytes 442376 | tf_op jit(solution)/shard_map/ppermute | solution.py:226
  20.3 0.0 collective-permute-done.6.refs_7_
  20.3 0.9 %shard_map.83.att = bf16[96,384]{1,0:T(8,128)(2,1)S(1)} custom-call(bf16[24,1152]{1,0:T(8,128)(2,1)S(1)} %collective-permute-done.refs_0_, bf16[24,1152]{1,0:T(8,128)(2,1)S(1)} %collective-permute-done.1.refs_1_, bf16[24,1152]{1,0:T(8,128)(2,1)S(1)} %collective-permute-done.2.refs_2_, bf16[24,384]{1,0:T(8,128)(2,1)S(1)} %get-tuple-element.28.refs_3_, ...), custom_call_target="tpu_custom_call" | custom-call | flops 56623104 | bytes 589824 | tf_op jit(solution)/shard_map/pallas_call | solution.py:146
  21.3 0.0 collective-permute-done.9.refs_4_
  21.3 0.0 collective-permute-done.10.refs_5_
  21.3 0.0 collective-permute-done.7.refs_1_
  21.3 0.8 %shard_map.84 = (bf16[24,1536]{1,0:T(8,128)(2,1)S(1)}, bf16[24,1536]{1,0:T(8,128)(2,1)S(1)}, bf16[24,1536]{1,0:T(8,128)(2,1)S(1)}, f32[24,1536]{1,0:T(8,128)S(1)}) custom-call(bf16[96,384]{1,0:T(8,128)(2,1)S(1)} %shard_map.83.att, bf16[96,3072]{1,0:T(8,128)(2,1)S(1)} %get-tuple-element.33.refs_0_, bf16[96,3072]{1,0:T(8,128)(2,1)S(1)} %collective-permute-done.7.refs_1_, ...), custom_call_target="tpu_custom_call" | custom-call | flops 113246208 | bytes 1179648 | tf_op jit(solution)/shard_map/pallas_call | solution.py:193
  22.1 3.6 %collective-permute-start.11 = (bf16[24,1536]{1,0:T(8,128)(2,1)S(1)}, bf16[24,1536]{1,0:T(8,128)(2,1)S(1)}, u32[]{:S(2)}, u32[]{:S(2)}) collective-permute-start(bf16[24,1536]{1,0:T(8,128)(2,1)S(1)} %get-tuple-element.37), channel_id=1, source_target_pairs={{0,12},{1,13},{2,14},{3,15},{4,8},{5,9},{6,10},{7,11},{8,4},{9,5},... | collective-permute-start | bytes 221192 | tf_op jit(solution)/shard_map/ppermute | solution.py:226
  25.7 0.0 collective-permute-start.12
  25.7 0.9 %collective-permute-start.13 = (bf16[24,1536]{1,0:T(8,128)(2,1)S(1)}, bf16[24,1536]{1,0:T(8,128)(2,1)S(1)}, u32[]{:S(2)}, u32[]{:S(2)}) collective-permute-start(bf16[24,1536]{1,0:T(8,128)(2,1)S(1)} %get-tuple-element.39), channel_id=1, source_target_pairs={{0,4},{1,5},{2,6},{3,7},{4,0},{5,1},{6,2},{7,3},{8,12},{9,13},{10,... | collective-permute-start | bytes 221192 | tf_op jit(solution)/shard_map/ppermute | solution.py:226
  26.6 0.0 copy-start
  26.6 0.0 collective-permute-done.14.refs_5_
  26.6 0.8 %shard_map.85 = (bf16[24,1536]{1,0:T(8,128)(2,1)S(1)}, bf16[24,1536]{1,0:T(8,128)(2,1)S(1)}, bf16[24,1536]{1,0:T(8,128)(2,1)S(1)}, f32[24,1536]{1,0:T(8,128)S(1)}) custom-call(bf16[96,384]{1,0:T(8,128)(2,1)S(1)} %shard_map.83.att, bf16[96,3072]{1,0:T(8,128)(2,1)S(1)} %get-tuple-element.33.refs_0_, bf16[96,3072]{1,0:T(8,128)(2,1)S(1)} %collective-permute-done.7.refs_1_, ...), custom_call_target="tpu_custom_call" | custom-call | flops 113246208 | bytes 1179648 | tf_op jit(solution)/shard_map/pallas_call | solution.py:193
  27.4 3.6 %collective-permute-start.15 = (bf16[24,1536]{1,0:T(8,128)(2,1)S(1)}, bf16[24,1536]{1,0:T(8,128)(2,1)S(1)}, u32[]{:S(2)}, u32[]{:S(2)}) collective-permute-start(bf16[24,1536]{1,0:T(8,128)(2,1)S(1)} %get-tuple-element.42), channel_id=1, source_target_pairs={{0,12},{1,13},{2,14},{3,15},{4,8},{5,9},{6,10},{7,11},{8,4},{9,5},... | collective-permute-start | bytes 221192 | tf_op jit(solution)/shard_map/ppermute | solution.py:226
  31.0 0.0 collective-permute-start.16
  31.0 0.0 collective-permute-done.11
  31.0 1.4 %collective-permute-start.17 = (bf16[24,1536]{1,0:T(8,128)(2,1)S(1)}, bf16[24,1536]{1,0:T(8,128)(2,1)S(1)}, u32[]{:S(2)}, u32[]{:S(2)}) collective-permute-start(bf16[24,1536]{1,0:T(8,128)(2,1)S(1)} %get-tuple-element.44), channel_id=1, source_target_pairs={{0,4},{1,5},{2,6},{3,7},{4,0},{5,1},{6,2},{7,3},{8,12},{9,13},{10,... | collective-permute-start | bytes 221192 | tf_op jit(solution)/shard_map/ppermute | solution.py:226
  32.4 3.6 %collective-permute-done.12 = bf16[24,1536]{1,0:T(8,128)(2,1)S(1)} collective-permute-done((bf16[24,1536]{1,0:T(8,128)(2,1)S(1)}, bf16[24,1536]{1,0:T(8,128)(2,1)S(1)}, u32[]{:S(2)}, u32[]{:S(2)}) %collective-permute-start.12) | collective-permute-done | bytes 73760 | tf_op jit(solution)/shard_map/ppermute | solution.py:226
  36.0 0.0 collective-permute-done.13
  36.0 0.0 collective-permute-done.15
  36.1 2.5 %collective-permute-done.16 = bf16[24,1536]{1,0:T(8,128)(2,1)S(1)} collective-permute-done((bf16[24,1536]{1,0:T(8,128)(2,1)S(1)}, bf16[24,1536]{1,0:T(8,128)(2,1)S(1)}, u32[]{:S(2)}, u32[]{:S(2)}) %collective-permute-start.16) | collective-permute-done | bytes 73760 | tf_op jit(solution)/shard_map/ppermute | solution.py:226
  38.5 0.0 collective-permute-done.17
  38.6 0.0 copy-done
  38.6 0.7 %fusion = bf16[24,3072]{1,0:T(8,128)(2,1)} fusion(f32[24,1536]{1,0:T(8,128)S(1)} %convert_add_fusion, f32[24,1536]{1,0:T(8,128)S(1)} %convert_add_fusion.1, f32[3072]{0:T(1024)S(1)} %copy-done), kind=kLoop, calls=%fused_computation.1 | loop fusion | flops 221184 | bytes 454656 | tf_op jit(solution)/shard_map/convert_element_type | solution.py:272
  (7 shorter events, 0.1 us)
Async XLA Ops:
  1.5 10.0 %collective-permute-start.3 = (bf16[48,3072]{1,0:T(8,128)(2,1)S(1)}, bf16[48,3072]{1,0:T(8,128)(2,1)S(1)}, u32[]{:S(2)}, u32[]{:S(2)}) collective-permute-start(bf16[48,3072]{1,0:T(8,128)(2,1)S(1)} %get-tuple-element.30), channel_id=1, source_target_pairs={{0,2},{1,3},{2,0},{3,1},{4,6},{5,7},{6,4},{7,5},{8,10},{9,11},{10,... | collective-permute-start | bytes 884744 | tf_op jit(solution)/shard_map/ppermute | solution.py:226
  4.5 8.7 %collective-permute-start = (bf16[24,1152]{1,0:T(8,128)(2,1)S(1)}, bf16[24,1152]{1,0:T(8,128)(2,1)S(1)}, u32[]{:S(2)}, u32[]{:S(2)}) collective-permute-start(bf16[24,1152]{1,0:T(8,128)(2,1)S(1)} %get-tuple-element.25), channel_id=1, source_target_pairs={{0,12},{1,13},{2,14},{3,15},{4,8},{5,9},{6,10},{7,11},{8,4},{9,5},... | collective-permute-start | bytes 165896 | tf_op jit(solution)/shard_map/ppermute | solution.py:226
  8.1 5.1 %collective-permute-start.1 = (bf16[24,1152]{1,0:T(8,128)(2,1)S(1)}, bf16[24,1152]{1,0:T(8,128)(2,1)S(1)}, u32[]{:S(2)}, u32[]{:S(2)}) collective-permute-start(bf16[24,1152]{1,0:T(8,128)(2,1)S(1)} %get-tuple-element.26), channel_id=1, source_target_pairs={{0,8},{1,9},{2,10},{3,11},{4,12},{5,13},{6,14},{7,15},{8,0},{9,1},... | collective-permute-start | bytes 165896 | tf_op jit(solution)/shard_map/ppermute | solution.py:226
  8.1 5.1 %collective-permute-start.2 = (bf16[24,1152]{1,0:T(8,128)(2,1)S(1)}, bf16[24,1152]{1,0:T(8,128)(2,1)S(1)}, u32[]{:S(2)}, u32[]{:S(2)}) collective-permute-start(bf16[24,1152]{1,0:T(8,128)(2,1)S(1)} %get-tuple-element.27), channel_id=1, source_target_pairs={{0,4},{1,5},{2,6},{3,7},{4,0},{5,1},{6,2},{7,3},{8,12},{9,13},{10,... | collective-permute-start | bytes 165896 | tf_op jit(solution)/shard_map/ppermute | solution.py:226
  11.5 8.2 %collective-permute-start.8 = (bf16[48,3072]{1,0:T(8,128)(2,1)S(1)}, bf16[48,3072]{1,0:T(8,128)(2,1)S(1)}, u32[]{:S(2)}, u32[]{:S(2)}) collective-permute-start(bf16[48,3072]{1,0:T(8,128)(2,1)S(1)} %collective-permute-done.3.refs_2_), channel_id=1, source_target_pairs={{0,16},{16,0},{1,17},{17,1},{2,18},{18,2},{3,19},{19,3},{4,20},{20... | collective-permute-start | bytes 884744 | tf_op jit(solution)/shard_map/ppermute | solution.py:229
  13.3 5.2 %collective-permute-start.5 = (bf16[96,768]{1,0:T(8,128)(2,1)S(1)}, bf16[96,768]{1,0:T(8,128)(2,1)S(1)}, u32[]{:S(2)}, u32[]{:S(2)}) collective-permute-start(bf16[96,768]{1,0:T(8,128)(2,1)S(1)} %pad_maximum_fusion.refs_4_), channel_id=1, source_target_pairs={{0,2},{1,3},{2,0},{3,1},{4,6},{5,7},{6,4},{7,5},{8,10},{9,11},{10,... | collective-permute-start | bytes 442376 | tf_op jit(solution)/shard_map/ppermute | solution.py:226
  14.9 4.9 %collective-permute-start.4 = (bf16[96,768]{1,0:T(8,128)(2,1)S(1)}, bf16[96,768]{1,0:T(8,128)(2,1)S(1)}, u32[]{:S(2)}, u32[]{:S(2)}) collective-permute-start(bf16[96,768]{1,0:T(8,128)(2,1)S(1)} %pad_maximum_fusion.refs_4_), channel_id=1, source_target_pairs={{0,1},{1,0},{2,3},{3,2},{4,5},{5,4},{6,7},{7,6},{8,9},{9,8},{10,11... | collective-permute-start | bytes 442376 | tf_op jit(solution)/shard_map/ppermute | solution.py:226
  14.9 6.4 %collective-permute-start.9 = (bf16[48,3072]{1,0:T(8,128)(2,1)S(1)}, bf16[48,3072]{1,0:T(8,128)(2,1)S(1)}, u32[]{:S(2)}, u32[]{:S(2)}) collective-permute-start(bf16[48,3072]{1,0:T(8,128)(2,1)S(1)} %collective-permute-done.3.refs_2_), channel_id=1, source_target_pairs={{0,1},{1,0},{2,3},{3,2},{4,5},{5,4},{6,7},{7,6},{8,9},{9,8},{10,11... | collective-permute-start | bytes 884744 | tf_op jit(solution)/shard_map/ppermute | solution.py:226
  15.4 5.9 %collective-permute-start.7 = (bf16[96,3072]{1,0:T(8,128)(2,1)S(1)}, bf16[96,3072]{1,0:T(8,128)(2,1)S(1)}, u32[]{:S(2)}, u32[]{:S(2)}) collective-permute-start(bf16[96,3072]{1,0:T(8,128)(2,1)S(1)} %get-tuple-element.33.refs_0_), channel_id=1, source_target_pairs={{0,1},{1,0},{2,3},{3,2},{4,5},{5,4},{6,7},{7,6},{8,9},{9,8},{10,11... | collective-permute-start | bytes 1769480 | tf_op jit(solution)/shard_map/ppermute | solution.py:226
  18.5 1.8 %collective-permute-start.6 = (bf16[96,768]{1,0:T(8,128)(2,1)S(1)}, bf16[96,768]{1,0:T(8,128)(2,1)S(1)}, u32[]{:S(2)}, u32[]{:S(2)}) collective-permute-start(bf16[96,768]{1,0:T(8,128)(2,1)S(1)} %collective-permute-done.5.refs_6_), channel_id=1, source_target_pairs={{0,1},{1,0},{2,3},{3,2},{4,5},{5,4},{6,7},{7,6},{8,9},{9,8},{10,11... | collective-permute-start | bytes 442376 | tf_op jit(solution)/shard_map/ppermute | solution.py:226
  19.8 1.5 %collective-permute-start.10 = (bf16[48,1536]{1,0:T(8,128)(2,1)S(1)}, bf16[48,1536]{1,0:T(8,128)(2,1)S(1)}, u32[]{:S(2)}, u32[]{:S(2)}) collective-permute-start(bf16[48,1536]{1,0:T(8,128)(2,1)S(1)} %get-tuple-element.46), channel_id=1, source_target_pairs={{0,1},{1,0},{2,3},{3,2},{4,5},{5,4},{6,7},{7,6},{8,9},{9,8},{10,11... | collective-permute-start | bytes 442376 | tf_op jit(solution)/shard_map/ppermute | solution.py:226
  19.9 6.7 %collective-permute-start.14 = (bf16[48,1536]{1,0:T(8,128)(2,1)S(1)}, bf16[48,1536]{1,0:T(8,128)(2,1)S(1)}, u32[]{:S(2)}, u32[]{:S(2)}) collective-permute-start(bf16[48,1536]{1,0:T(8,128)(2,1)S(1)} %get-tuple-element.45), channel_id=1, source_target_pairs={{0,1},{1,0},{2,3},{3,2},{4,5},{5,4},{6,7},{7,6},{8,9},{9,8},{10,11... | collective-permute-start | bytes 442376 | tf_op jit(solution)/shard_map/ppermute | solution.py:226
  22.1 8.8 %collective-permute-start.11 = (bf16[24,1536]{1,0:T(8,128)(2,1)S(1)}, bf16[24,1536]{1,0:T(8,128)(2,1)S(1)}, u32[]{:S(2)}, u32[]{:S(2)}) collective-permute-start(bf16[24,1536]{1,0:T(8,128)(2,1)S(1)} %get-tuple-element.37), channel_id=1, source_target_pairs={{0,12},{1,13},{2,14},{3,15},{4,8},{5,9},{6,10},{7,11},{8,4},{9,5},... | collective-permute-start | bytes 221192 | tf_op jit(solution)/shard_map/ppermute | solution.py:226
  25.7 10.3 %collective-permute-start.12 = (bf16[24,1536]{1,0:T(8,128)(2,1)S(1)}, bf16[24,1536]{1,0:T(8,128)(2,1)S(1)}, u32[]{:S(2)}, u32[]{:S(2)}) collective-permute-start(bf16[24,1536]{1,0:T(8,128)(2,1)S(1)} %get-tuple-element.38), channel_id=1, source_target_pairs={{0,8},{1,9},{2,10},{3,11},{4,12},{5,13},{6,14},{7,15},{8,0},{9,1},... | collective-permute-start | bytes 221192 | tf_op jit(solution)/shard_map/ppermute | solution.py:226
  25.7 10.3 %collective-permute-start.13 = (bf16[24,1536]{1,0:T(8,128)(2,1)S(1)}, bf16[24,1536]{1,0:T(8,128)(2,1)S(1)}, u32[]{:S(2)}, u32[]{:S(2)}) collective-permute-start(bf16[24,1536]{1,0:T(8,128)(2,1)S(1)} %get-tuple-element.39), channel_id=1, source_target_pairs={{0,4},{1,5},{2,6},{3,7},{4,0},{5,1},{6,2},{7,3},{8,12},{9,13},{10,... | collective-permute-start | bytes 221192 | tf_op jit(solution)/shard_map/ppermute | solution.py:226
  26.6 12.0 %copy-start = (f32[3072]{0:T(1024)S(1)}, f32[3072]{0:T(1024)}, u32[]{:S(2)}) copy-start(f32[3072]{0:T(1024)} %param.15) | copy-start | bytes 36868
  27.4 8.7 %collective-permute-start.15 = (bf16[24,1536]{1,0:T(8,128)(2,1)S(1)}, bf16[24,1536]{1,0:T(8,128)(2,1)S(1)}, u32[]{:S(2)}, u32[]{:S(2)}) collective-permute-start(bf16[24,1536]{1,0:T(8,128)(2,1)S(1)} %get-tuple-element.42), channel_id=1, source_target_pairs={{0,12},{1,13},{2,14},{3,15},{4,8},{5,9},{6,10},{7,11},{8,4},{9,5},... | collective-permute-start | bytes 221192 | tf_op jit(solution)/shard_map/ppermute | solution.py:226
  31.0 7.6 %collective-permute-start.16 = (bf16[24,1536]{1,0:T(8,128)(2,1)S(1)}, bf16[24,1536]{1,0:T(8,128)(2,1)S(1)}, u32[]{:S(2)}, u32[]{:S(2)}) collective-permute-start(bf16[24,1536]{1,0:T(8,128)(2,1)S(1)} %get-tuple-element.43), channel_id=1, source_target_pairs={{0,8},{1,9},{2,10},{3,11},{4,12},{5,13},{6,14},{7,15},{8,0},{9,1},... | collective-permute-start | bytes 221192 | tf_op jit(solution)/shard_map/ppermute | solution.py:226
  31.0 7.6 %collective-permute-start.17 = (bf16[24,1536]{1,0:T(8,128)(2,1)S(1)}, bf16[24,1536]{1,0:T(8,128)(2,1)S(1)}, u32[]{:S(2)}, u32[]{:S(2)}) collective-permute-start(bf16[24,1536]{1,0:T(8,128)(2,1)S(1)} %get-tuple-element.44), channel_id=1, source_target_pairs={{0,4},{1,5},{2,6},{3,7},{4,0},{5,1},{6,2},{7,3},{8,12},{9,13},{10,... | collective-permute-start | bytes 221192 | tf_op jit(solution)/shard_map/ppermute | solution.py:226

commit v11 on v10

--- a/solution.py
+++ b/solution.py
@@ -18,8 +18,8 @@
     sources, w_ref = refs[:6], refs[6]
     outs = refs[7:]
     qout, kvout, fulls = outs[0], outs[1], outs[1 : 1 + groups]
-    wout, wpart = outs[1 + groups], outs[2 + groups]
-    query, key_new, value_new, kst, vst, est, packed, sems = outs[3 + groups :]
+    wout = outs[1 + groups]
+    query, key_new, value_new, kst, vst, est, packed, sems = outs[2 + groups :]
     rows, width = query.shape
     me = lax.axis_index("patch")
     first = pl.multiple_of((me // 2) * (2 * rows), 2 * rows)
@@ -31,14 +31,8 @@
     }
     for i in order:
         copies[i].start()
-    size = wpart.shape[0]
-    top = pl.multiple_of((lax.axis_index("groups") % 2) * size, size) if size < w_ref.shape[0] else 0
-    moves = [
-        pltpu.make_async_copy(w_ref.at[pl.ds(top, size)], wpart, sems.at[7]),
-        pltpu.make_async_copy(w_ref, wout, sems.at[6]),
-    ]
-    for m in moves:
-        m.start()
+    move = pltpu.make_async_copy(w_ref, wout, sems.at[6])
+    move.start()
     heads = est.shape[0] // 2
     dim = width // heads
     share = width // groups
@@ -78,18 +72,17 @@
         else:
             fulls[k][:, :share] = wanted
             fulls[k][:, share:] = packed[target]
-    for m in moves:
-        m.wait()
-
-
-def prepare(groups, members, split, query, key_new, value_new, key_stale, value_stale, powers, w_out):
+    move.wait()
+
+
+def prepare(groups, members, query, key_new, value_new, key_stale, value_stale, powers, w_out):
     rows, width = query.shape
     share = width // groups
     depth, model = w_out.shape
     outs = (
         [((rows, share), jnp.bfloat16), ((rows, 2 * share), jnp.bfloat16)]
         + [((rows, 3 * share), jnp.bfloat16)] * (groups - 1)
-        + [((depth, model), jnp.bfloat16), ((depth // split, model), jnp.bfloat16)]
+        + [((depth, model), jnp.bfloat16)]
     )
     sources = (query, key_new, value_new, key_stale, value_stale, powers, w_out)
     result = pl.pallas_call(
@@ -102,14 +95,14 @@
         + [
             pltpu.VMEM(powers.shape, jnp.int32),
             pltpu.VMEM((groups, rows, 2 * share), jnp.bfloat16),
-            pltpu.SemaphoreType.DMA((8,)),
+            pltpu.SemaphoreType.DMA((7,)),
         ],
         compiler_params=pltpu.CompilerParams(vmem_limit_bytes=24 * 1024 * 1024),
         cost_estimate=pl.CostEstimate(
             flops=10 * rows * width, bytes_accessed=14 * rows * width + 4 * depth * model, transcendentals=0
         ),
     )(*(pltpu.with_memory_space_constraint(x, pltpu.HBM) for x in sources))
-    return result[0], result[1 : 1 + groups], result[-2], result[-1]
+    return result[0], result[1 : 1 + groups], result[-1]
 
 
 def attend_kernel(groups, dim, *refs):
@@ -235,14 +228,17 @@
             bit //= 2
         return [pieces[j] for j in range(members)]
 
-    own_query, fresh, w_own, w_part = prepare(
-        groups, members, 2 if shared else 1, query, key_new, value_new, key_stale, value_stale, exponents.T, w_out
+    if shared:
+        side = lax.axis_index("groups") & 1
+        w_part = lax.dynamic_slice_in_dim(w_out, side * (depth // 2), depth // 2, 0)
+        y_part = send(w_part, 0, far)
+    own_query, fresh, w_own = prepare(
+        groups, members, query, key_new, value_new, key_stale, value_stale, exponents.T, w_out
     )
     order = range(groups - 1, 0, -1)
     arrived = [send(fresh[k], k, 0) for k in order]
     both = jnp.concatenate([x[:, share:] for x in arrived] + [fresh[0]], axis=0)
     if shared:
-        y_part = send(w_part, 0, 2)
         both = after(both, y_part)
     kvs = spread({0: both}, far)
     att = attend(groups, dim, arrived + [own_query], kvs)

time: 39.4 us -> 39.2 us (level)
  starting transfers between devices: 21.2 us -> 19.8 us
  local copies, waits for them, and re-layouts: 0.04 us -> 1.02 us
    ppermute x17, waiting for transfers between devices: 11.8 us -> 13.3 us  [send(): lax.ppermute(x, 'patch', [(p, (p // members ^ k) * members + p % members...]
    ppermute x17, starting transfers between devices: 19.5 us -> 18.1 us  [send(): lax.ppermute(x, 'patch', [(p, (p // members ^ k) * members + p % members...]
    ppermute x1, waiting for transfers between devices: 1.2 us -> 0.01 us  [swap(): return lax.ppermute(x, 'groups', [(g, g ^ 1) for g in range(parts)])]
    dynamic_slice x0 -> x1, local copies, waits for them, and re-layouts: none -> 0.98 us  [per_device(): w_part = lax.dynamic_slice_in_dim(w_out, side * (depth // 2), depth // 2, 0)]
  transfers between devices with their start and end apart: 18 -> 18, of which waited for: 5 -> 7; matrix products, arithmetic and copies ran while one was open for 0% -> 0% of each run, Pallas kernels for 6% -> 10%
where the time goes in v11:
time: 39.2 us; the launch traced here: 39 us
  starting transfers between devices  19.8 us (51%)
  waiting for transfers between devices  13.3 us (34%)
  Pallas kernels  3.93 us (10%)
  local copies, waits for them, and re-layouts  1.02 us (3%)
  other arithmetic  0.78 us (2%)
    ppermute x17, starting transfers between devices, send(): lax.ppermute(x, 'patch', [(p, (p // members ^ k) * members + p % members...  18.1 us
    ppermute x17, waiting for transfers between devices, send(): lax.ppermute(x, 'patch', [(p, (p // members ^ k) * members + p % members...  13.3 us
    ppermute x1, starting transfers between devices, swap(): return lax.ppermute(x, 'groups', [(g, g ^ 1) for g in range(parts)])  1.71 us
    pallas_call x2, Pallas kernels, project(): pl.pallas_call(functools.partial(project_kernel, groups, members, places)...  1.6 us
    pallas_call x1, Pallas kernels, prepare(): pl.pallas_call(functools.partial(prepare_kernel, groups, members), out_sh...  1.4 us
    dynamic_slice x1, local copies, waits for them, and re-layouts, per_device(): w_part = lax.dynamic_slice_in_dim(w_out, side * (depth // 2), depth // 2, 0)  0.98 us
    pallas_call x1, Pallas kernels, attend(): pl.pallas_call(functools.partial(attend_kernel, groups, dim), out_shape=j...  0.93 us
  transfers between devices with their start and end apart: 18, of which 7 were waited for; matrix products, arithmetic and copies ran while one was open for 0% of the time, Pallas kernels for 10%

profile of v11, /device:TPU:0, one launch (start us, length us, event | category | flops | bytes accessed | tf_op | source)
XLA Modules:
  0.0 39.0 jit_solution(11798982013108574274)
XLA Ops:
  0.0 1.0 %constant_dynamic-slice_fusion = bf16[48,3072]{1,0:T(8,128)(2,1)S(1)} fusion(bf16[96,3072]{1,0:T(8,128)(2,1)} %refs_6_.1, s32[]{:T(128)S(6)} %select_n.3), kind=kLoop, calls=%fused_computation.5 | loop fusion | bytes 589828 | tf_op jit(solution)/shard_map/dynamic_slice | solution.py:233
  1.0 3.0 %collective-permute-start.3 = (bf16[48,3072]{1,0:T(8,128)(2,1)S(1)}, bf16[48,3072]{1,0:T(8,128)(2,1)S(1)}, u32[]{:S(2)}, u32[]{:S(2)}) collective-permute-start(bf16[48,3072]{1,0:T(8,128)(2,1)S(1)} %constant_dynamic-slice_fusion), channel_id=1, source_target_pairs={{0,2},{1,3},{2,0},{3,1},{4,6},{5,7},{6,4},{7,5},{8,10},{9,11},{10,... | collective-permute-start | bytes 884744 | tf_op jit(solution)/shard_map/ppermute | solution.py:219
  4.0 1.4 %shard_map.82 = (bf16[24,384]{1,0:T(8,128)(2,1)S(1)}, bf16[24,768]{1,0:T(8,128)(2,1)S(1)}, bf16[24,1152]{1,0:T(8,128)(2,1)S(1)}, bf16[24,1152]{1,0:T(8,128)(2,1)...) custom-call(bf16[24,1536]{1,0:T(8,128)(2,1)} %refs_0_.1, bf16[24,1536]{1,0:T(8,128)(2,1)} %refs_1_.1, ...), custom_call_target="tpu_custom_call" | custom-call | flops 368640 | bytes 1695744 | tf_op jit(solution)/shard_map/pallas_call | solution.py:88
  5.4 3.7 %collective-permute-start = (bf16[24,1152]{1,0:T(8,128)(2,1)S(1)}, bf16[24,1152]{1,0:T(8,128)(2,1)S(1)}, u32[]{:S(2)}, u32[]{:S(2)}) collective-permute-start(bf16[24,1152]{1,0:T(8,128)(2,1)S(1)} %get-tuple-element.24), channel_id=1, source_target_pairs={{0,12},{1,13},{2,14},{3,15},{4,8},{5,9},{6,10},{7,11},{8,4},{9,5},... | collective-permute-start | bytes 165896 | tf_op jit(solution)/shard_map/ppermute | solution.py:219
  9.1 0.0 collective-permute-start.1
  9.1 0.8 %collective-permute-start.2 = (bf16[24,1152]{1,0:T(8,128)(2,1)S(1)}, bf16[24,1152]{1,0:T(8,128)(2,1)S(1)}, u32[]{:S(2)}, u32[]{:S(2)}) collective-permute-start(bf16[24,1152]{1,0:T(8,128)(2,1)S(1)} %get-tuple-element.26), channel_id=1, source_target_pairs={{0,4},{1,5},{2,6},{3,7},{4,0},{5,1},{6,2},{7,3},{8,12},{9,13},{10,... | collective-permute-start | bytes 165896 | tf_op jit(solution)/shard_map/ppermute | solution.py:219
  9.9 1.1 %collective-permute-done.3.refs_2_ = bf16[48,3072]{1,0:T(8,128)(2,1)S(1)} collective-permute-done((bf16[48,3072]{1,0:T(8,128)(2,1)S(1)}, bf16[48,3072]{1,0:T(8,128)(2,1)S(1)}, u32[]{:S(2)}, u32[]{:S(2)}) %collective-permute-start.3) | collective-permute-done | bytes 294944 | tf_op jit(solution)/shard_map/ppermute | solution.py:219
  11.0 1.7 %collective-permute-start.8 = (bf16[48,3072]{1,0:T(8,128)(2,1)S(1)}, bf16[48,3072]{1,0:T(8,128)(2,1)S(1)}, u32[]{:S(2)}, u32[]{:S(2)}) collective-permute-start(bf16[48,3072]{1,0:T(8,128)(2,1)S(1)} %collective-permute-done.3.refs_2_), channel_id=1, source_target_pairs={{0,16},{16,0},{1,17},{17,1},{2,18},{18,2},{3,19},{19,3},{4,20},{20... | collective-permute-start | bytes 884744 | tf_op jit(solution)/shard_map/ppermute | solution.py:222
  12.7 0.0 collective-permute-done.refs_0_
  12.7 1.4 %collective-permute-done.1.refs_1_ = bf16[24,1152]{1,0:T(8,128)(2,1)S(1)} collective-permute-done((bf16[24,1152]{1,0:T(8,128)(2,1)S(1)}, bf16[24,1152]{1,0:T(8,128)(2,1)S(1)}, u32[]{:S(2)}, u32[]{:S(2)}) %collective-permute-start.1) | collective-permute-done | bytes 55328 | tf_op jit(solution)/shard_map/ppermute | solution.py:219
  14.2 0.0 collective-permute-done.2.refs_2_
  14.2 0.6 %collective-permute-start.5 = (bf16[96,768]{1,0:T(8,128)(2,1)S(1)}, bf16[96,768]{1,0:T(8,128)(2,1)S(1)}, u32[]{:S(2)}, u32[]{:S(2)}) collective-permute-start(bf16[96,768]{1,0:T(8,128)(2,1)S(1)} %pad_maximum_fusion.refs_4_), channel_id=1, source_target_pairs={{0,2},{1,3},{2,0},{3,1},{4,6},{5,7},{6,4},{7,5},{8,10},{9,11},{10,... | collective-permute-start | bytes 442376 | tf_op jit(solution)/shard_map/ppermute | solution.py:219
  14.8 0.0 collective-permute-start.4
  14.8 0.5 %collective-permute-start.9 = (bf16[48,3072]{1,0:T(8,128)(2,1)S(1)}, bf16[48,3072]{1,0:T(8,128)(2,1)S(1)}, u32[]{:S(2)}, u32[]{:S(2)}) collective-permute-start(bf16[48,3072]{1,0:T(8,128)(2,1)S(1)} %collective-permute-done.3.refs_2_), channel_id=1, source_target_pairs={{0,1},{1,0},{2,3},{3,2},{4,5},{5,4},{6,7},{7,6},{8,9},{9,8},{10,11... | collective-permute-start | bytes 884744 | tf_op jit(solution)/shard_map/ppermute | solution.py:219
  15.3 0.0 collective-permute-start.7
  15.3 4.1 %collective-permute-done.5.refs_6_ = bf16[96,768]{1,0:T(8,128)(2,1)S(1)} collective-permute-done((bf16[96,768]{1,0:T(8,128)(2,1)S(1)}, bf16[96,768]{1,0:T(8,128)(2,1)S(1)}, u32[]{:S(2)}, u32[]{:S(2)}) %collective-permute-start.5) | collective-permute-done | bytes 147488 | tf_op jit(solution)/shard_map/ppermute | solution.py:219
  19.4 0.0 collective-permute-start.6
  19.4 0.0 collective-permute-done.8.refs_3_
  19.4 0.6 %collective-permute-start.10 = (bf16[48,1536]{1,0:T(8,128)(2,1)S(1)}, bf16[48,1536]{1,0:T(8,128)(2,1)S(1)}, u32[]{:S(2)}, u32[]{:S(2)}) collective-permute-start(bf16[48,1536]{1,0:T(8,128)(2,1)S(1)} %get-tuple-element.44), channel_id=1, source_target_pairs={{0,1},{1,0},{2,3},{3,2},{4,5},{5,4},{6,7},{7,6},{8,9},{9,8},{10,11... | collective-permute-start | bytes 442376 | tf_op jit(solution)/shard_map/ppermute | solution.py:219
  20.0 0.0 collective-permute-done.4.refs_5_
  20.0 0.1 collective-permute-start.14
  20.1 0.7 %collective-permute-done.6.refs_7_ = bf16[96,768]{1,0:T(8,128)(2,1)S(1)} collective-permute-done((bf16[96,768]{1,0:T(8,128)(2,1)S(1)}, bf16[96,768]{1,0:T(8,128)(2,1)S(1)}, u32[]{:S(2)}, u32[]{:S(2)}) %collective-permute-start.6) | collective-permute-done | bytes 147488 | tf_op jit(solution)/shard_map/ppermute | solution.py:219
  20.8 0.9 %shard_map.83.att = bf16[96,384]{1,0:T(8,128)(2,1)S(1)} custom-call(bf16[24,1152]{1,0:T(8,128)(2,1)S(1)} %collective-permute-done.refs_0_, bf16[24,1152]{1,0:T(8,128)(2,1)S(1)} %collective-permute-done.1.refs_1_, bf16[24,1152]{1,0:T(8,128)(2,1)S(1)} %collective-permute-done.2.refs_2_, bf16[24,384]{1,0:T(8,128)(2,1)S(1)} %get-tuple-element.27.refs_3_, ...), custom_call_target="tpu_custom_call" | custom-call | flops 56623104 | bytes 589824 | tf_op jit(solution)/shard_map/pallas_call | solution.py:139
  21.7 0.0 collective-permute-done.9.refs_4_
  21.7 0.0 collective-permute-done.10.refs_5_
  21.7 0.0 collective-permute-done.7.refs_1_
  21.7 0.8 %shard_map.84 = (bf16[24,1536]{1,0:T(8,128)(2,1)S(1)}, bf16[24,1536]{1,0:T(8,128)(2,1)S(1)}, bf16[24,1536]{1,0:T(8,128)(2,1)S(1)}, f32[24,1536]{1,0:T(8,128)S(1)}) custom-call(bf16[96,384]{1,0:T(8,128)(2,1)S(1)} %shard_map.83.att, bf16[96,3072]{1,0:T(8,128)(2,1)S(1)} %get-tuple-element.31.refs_0_, bf16[96,3072]{1,0:T(8,128)(2,1)S(1)} %collective-permute-done.7.refs_1_, ...), custom_call_target="tpu_custom_call" | custom-call | flops 113246208 | bytes 1179648 | tf_op jit(solution)/shard_map/pallas_call | solution.py:186
  22.5 2.6 %collective-permute-start.11 = (bf16[24,1536]{1,0:T(8,128)(2,1)S(1)}, bf16[24,1536]{1,0:T(8,128)(2,1)S(1)}, u32[]{:S(2)}, u32[]{:S(2)}) collective-permute-start(bf16[24,1536]{1,0:T(8,128)(2,1)S(1)} %get-tuple-element.35), channel_id=1, source_target_pairs={{0,12},{1,13},{2,14},{3,15},{4,8},{5,9},{6,10},{7,11},{8,4},{9,5},... | collective-permute-start | bytes 221192 | tf_op jit(solution)/shard_map/ppermute | solution.py:219
  25.2 0.0 collective-permute-start.12
  25.2 1.8 %collective-permute-start.13 = (bf16[24,1536]{1,0:T(8,128)(2,1)S(1)}, bf16[24,1536]{1,0:T(8,128)(2,1)S(1)}, u32[]{:S(2)}, u32[]{:S(2)}) collective-permute-start(bf16[24,1536]{1,0:T(8,128)(2,1)S(1)} %get-tuple-element.37), channel_id=1, source_target_pairs={{0,4},{1,5},{2,6},{3,7},{4,0},{5,1},{6,2},{7,3},{8,12},{9,13},{10,... | collective-permute-start | bytes 221192 | tf_op jit(solution)/shard_map/ppermute | solution.py:219
  27.0 0.0 copy-start
  27.0 0.0 collective-permute-done.14.refs_5_
  27.0 0.8 %shard_map.85 = (bf16[24,1536]{1,0:T(8,128)(2,1)S(1)}, bf16[24,1536]{1,0:T(8,128)(2,1)S(1)}, bf16[24,1536]{1,0:T(8,128)(2,1)S(1)}, f32[24,1536]{1,0:T(8,128)S(1)}) custom-call(bf16[96,384]{1,0:T(8,128)(2,1)S(1)} %shard_map.83.att, bf16[96,3072]{1,0:T(8,128)(2,1)S(1)} %get-tuple-element.31.refs_0_, bf16[96,3072]{1,0:T(8,128)(2,1)S(1)} %collective-permute-done.7.refs_1_, ...), custom_call_target="tpu_custom_call" | custom-call | flops 113246208 | bytes 1179648 | tf_op jit(solution)/shard_map/pallas_call | solution.py:186
  27.8 2.6 %collective-permute-start.15 = (bf16[24,1536]{1,0:T(8,128)(2,1)S(1)}, bf16[24,1536]{1,0:T(8,128)(2,1)S(1)}, u32[]{:S(2)}, u32[]{:S(2)}) collective-permute-start(bf16[24,1536]{1,0:T(8,128)(2,1)S(1)} %get-tuple-element.40), channel_id=1, source_target_pairs={{0,12},{1,13},{2,14},{3,15},{4,8},{5,9},{6,10},{7,11},{8,4},{9,5},... | collective-permute-start | bytes 221192 | tf_op jit(solution)/shard_map/ppermute | solution.py:219
  30.4 0.0 collective-permute-start.16
  30.4 0.0 collective-permute-done.11
  30.4 1.8 %collective-permute-start.17 = (bf16[24,1536]{1,0:T(8,128)(2,1)S(1)}, bf16[24,1536]{1,0:T(8,128)(2,1)S(1)}, u32[]{:S(2)}, u32[]{:S(2)}) collective-permute-start(bf16[24,1536]{1,0:T(8,128)(2,1)S(1)} %get-tuple-element.42), channel_id=1, source_target_pairs={{0,4},{1,5},{2,6},{3,7},{4,0},{5,1},{6,2},{7,3},{8,12},{9,13},{10,... | collective-permute-start | bytes 221192 | tf_op jit(solution)/shard_map/ppermute | solution.py:219
  32.3 1.9 %collective-permute-done.12 = bf16[24,1536]{1,0:T(8,128)(2,1)S(1)} collective-permute-done((bf16[24,1536]{1,0:T(8,128)(2,1)S(1)}, bf16[24,1536]{1,0:T(8,128)(2,1)S(1)}, u32[]{:S(2)}, u32[]{:S(2)}) %collective-permute-start.12) | collective-permute-done | bytes 73760 | tf_op jit(solution)/shard_map/ppermute | solution.py:219
  34.2 0.0 collective-permute-done.13
  34.2 0.3 collective-permute-done.15
  34.5 3.7 %collective-permute-done.16 = bf16[24,1536]{1,0:T(8,128)(2,1)S(1)} collective-permute-done((bf16[24,1536]{1,0:T(8,128)(2,1)S(1)}, bf16[24,1536]{1,0:T(8,128)(2,1)S(1)}, u32[]{:S(2)}, u32[]{:S(2)}) %collective-permute-start.16) | collective-permute-done | bytes 73760 | tf_op jit(solution)/shard_map/ppermute | solution.py:219
  38.3 0.0 collective-permute-done.17
  38.3 0.0 copy-done
  38.3 0.7 %fusion = bf16[24,3072]{1,0:T(8,128)(2,1)} fusion(f32[24,1536]{1,0:T(8,128)S(1)} %convert_add_fusion, f32[24,1536]{1,0:T(8,128)S(1)} %convert_add_fusion.1, f32[3072]{0:T(1024)S(1)} %copy-done), kind=kLoop, calls=%fused_computation.1 | loop fusion | flops 221184 | bytes 454656 | tf_op jit(solution)/shard_map/convert_element_type | solution.py:268
  (7 shorter events, 0.1 us)
Async XLA Ops:
  1.0 10.0 %collective-permute-start.3 = (bf16[48,3072]{1,0:T(8,128)(2,1)S(1)}, bf16[48,3072]{1,0:T(8,128)(2,1)S(1)}, u32[]{:S(2)}, u32[]{:S(2)}) collective-permute-start(bf16[48,3072]{1,0:T(8,128)(2,1)S(1)} %constant_dynamic-slice_fusion), channel_id=1, source_target_pairs={{0,2},{1,3},{2,0},{3,1},{4,6},{5,7},{6,4},{7,5},{8,10},{9,11},{10,... | collective-permute-start | bytes 884744 | tf_op jit(solution)/shard_map/ppermute | solution.py:219
  5.4 7.3 %collective-permute-start = (bf16[24,1152]{1,0:T(8,128)(2,1)S(1)}, bf16[24,1152]{1,0:T(8,128)(2,1)S(1)}, u32[]{:S(2)}, u32[]{:S(2)}) collective-permute-start(bf16[24,1152]{1,0:T(8,128)(2,1)S(1)} %get-tuple-element.24), channel_id=1, source_target_pairs={{0,12},{1,13},{2,14},{3,15},{4,8},{5,9},{6,10},{7,11},{8,4},{9,5},... | collective-permute-start | bytes 165896 | tf_op jit(solution)/shard_map/ppermute | solution.py:219
  9.1 5.1 %collective-permute-start.1 = (bf16[24,1152]{1,0:T(8,128)(2,1)S(1)}, bf16[24,1152]{1,0:T(8,128)(2,1)S(1)}, u32[]{:S(2)}, u32[]{:S(2)}) collective-permute-start(bf16[24,1152]{1,0:T(8,128)(2,1)S(1)} %get-tuple-element.25), channel_id=1, source_target_pairs={{0,8},{1,9},{2,10},{3,11},{4,12},{5,13},{6,14},{7,15},{8,0},{9,1},... | collective-permute-start | bytes 165896 | tf_op jit(solution)/shard_map/ppermute | solution.py:219
  9.1 5.1 %collective-permute-start.2 = (bf16[24,1152]{1,0:T(8,128)(2,1)S(1)}, bf16[24,1152]{1,0:T(8,128)(2,1)S(1)}, u32[]{:S(2)}, u32[]{:S(2)}) collective-permute-start(bf16[24,1152]{1,0:T(8,128)(2,1)S(1)} %get-tuple-element.26), channel_id=1, source_target_pairs={{0,4},{1,5},{2,6},{3,7},{4,0},{5,1},{6,2},{7,3},{8,12},{9,13},{10,... | collective-permute-start | bytes 165896 | tf_op jit(solution)/shard_map/ppermute | solution.py:219
  11.0 8.4 %collective-permute-start.8 = (bf16[48,3072]{1,0:T(8,128)(2,1)S(1)}, bf16[48,3072]{1,0:T(8,128)(2,1)S(1)}, u32[]{:S(2)}, u32[]{:S(2)}) collective-permute-start(bf16[48,3072]{1,0:T(8,128)(2,1)S(1)} %collective-permute-done.3.refs_2_), channel_id=1, source_target_pairs={{0,16},{16,0},{1,17},{17,1},{2,18},{18,2},{3,19},{19,3},{4,20},{20... | collective-permute-start | bytes 884744 | tf_op jit(solution)/shard_map/ppermute | solution.py:222
  14.2 5.2 %collective-permute-start.5 = (bf16[96,768]{1,0:T(8,128)(2,1)S(1)}, bf16[96,768]{1,0:T(8,128)(2,1)S(1)}, u32[]{:S(2)}, u32[]{:S(2)}) collective-permute-start(bf16[96,768]{1,0:T(8,128)(2,1)S(1)} %pad_maximum_fusion.refs_4_), channel_id=1, source_target_pairs={{0,2},{1,3},{2,0},{3,1},{4,6},{5,7},{6,4},{7,5},{8,10},{9,11},{10,... | collective-permute-start | bytes 442376 | tf_op jit(solution)/shard_map/ppermute | solution.py:219
  14.8 5.2 %collective-permute-start.4 = (bf16[96,768]{1,0:T(8,128)(2,1)S(1)}, bf16[96,768]{1,0:T(8,128)(2,1)S(1)}, u32[]{:S(2)}, u32[]{:S(2)}) collective-permute-start(bf16[96,768]{1,0:T(8,128)(2,1)S(1)} %pad_maximum_fusion.refs_4_), channel_id=1, source_target_pairs={{0,1},{1,0},{2,3},{3,2},{4,5},{5,4},{6,7},{7,6},{8,9},{9,8},{10,11... | collective-permute-start | bytes 442376 | tf_op jit(solution)/shard_map/ppermute | solution.py:219
  14.8 6.9 %collective-permute-start.9 = (bf16[48,3072]{1,0:T(8,128)(2,1)S(1)}, bf16[48,3072]{1,0:T(8,128)(2,1)S(1)}, u32[]{:S(2)}, u32[]{:S(2)}) collective-permute-start(bf16[48,3072]{1,0:T(8,128)(2,1)S(1)} %collective-permute-done.3.refs_2_), channel_id=1, source_target_pairs={{0,1},{1,0},{2,3},{3,2},{4,5},{5,4},{6,7},{7,6},{8,9},{9,8},{10,11... | collective-permute-start | bytes 884744 | tf_op jit(solution)/shard_map/ppermute | solution.py:219
  15.3 6.5 %collective-permute-start.7 = (bf16[96,3072]{1,0:T(8,128)(2,1)S(1)}, bf16[96,3072]{1,0:T(8,128)(2,1)S(1)}, u32[]{:S(2)}, u32[]{:S(2)}) collective-permute-start(bf16[96,3072]{1,0:T(8,128)(2,1)S(1)} %get-tuple-element.31.refs_0_), channel_id=1, source_target_pairs={{0,1},{1,0},{2,3},{3,2},{4,5},{5,4},{6,7},{7,6},{8,9},{9,8},{10,11... | collective-permute-start | bytes 1769480 | tf_op jit(solution)/shard_map/ppermute | solution.py:219
  19.4 1.4 %collective-permute-start.6 = (bf16[96,768]{1,0:T(8,128)(2,1)S(1)}, bf16[96,768]{1,0:T(8,128)(2,1)S(1)}, u32[]{:S(2)}, u32[]{:S(2)}) collective-permute-start(bf16[96,768]{1,0:T(8,128)(2,1)S(1)} %collective-permute-done.5.refs_6_), channel_id=1, source_target_pairs={{0,1},{1,0},{2,3},{3,2},{4,5},{5,4},{6,7},{7,6},{8,9},{9,8},{10,11... | collective-permute-start | bytes 442376 | tf_op jit(solution)/shard_map/ppermute | solution.py:219
  19.4 2.3 %collective-permute-start.10 = (bf16[48,1536]{1,0:T(8,128)(2,1)S(1)}, bf16[48,1536]{1,0:T(8,128)(2,1)S(1)}, u32[]{:S(2)}, u32[]{:S(2)}) collective-permute-start(bf16[48,1536]{1,0:T(8,128)(2,1)S(1)} %get-tuple-element.44), channel_id=1, source_target_pairs={{0,1},{1,0},{2,3},{3,2},{4,5},{5,4},{6,7},{7,6},{8,9},{9,8},{10,11... | collective-permute-start | bytes 442376 | tf_op jit(solution)/shard_map/ppermute | solution.py:219
  20.0 7.0 %collective-permute-start.14 = (bf16[48,1536]{1,0:T(8,128)(2,1)S(1)}, bf16[48,1536]{1,0:T(8,128)(2,1)S(1)}, u32[]{:S(2)}, u32[]{:S(2)}) collective-permute-start(bf16[48,1536]{1,0:T(8,128)(2,1)S(1)} %get-tuple-element.43), channel_id=1, source_target_pairs={{0,1},{1,0},{2,3},{3,2},{4,5},{5,4},{6,7},{7,6},{8,9},{9,8},{10,11... | collective-permute-start | bytes 442376 | tf_op jit(solution)/shard_map/ppermute | solution.py:219
  22.5 7.9 %collective-permute-start.11 = (bf16[24,1536]{1,0:T(8,128)(2,1)S(1)}, bf16[24,1536]{1,0:T(8,128)(2,1)S(1)}, u32[]{:S(2)}, u32[]{:S(2)}) collective-permute-start(bf16[24,1536]{1,0:T(8,128)(2,1)S(1)} %get-tuple-element.35), channel_id=1, source_target_pairs={{0,12},{1,13},{2,14},{3,15},{4,8},{5,9},{6,10},{7,11},{8,4},{9,5},... | collective-permute-start | bytes 221192 | tf_op jit(solution)/shard_map/ppermute | solution.py:219
  25.2 9.0 %collective-permute-start.12 = (bf16[24,1536]{1,0:T(8,128)(2,1)S(1)}, bf16[24,1536]{1,0:T(8,128)(2,1)S(1)}, u32[]{:S(2)}, u32[]{:S(2)}) collective-permute-start(bf16[24,1536]{1,0:T(8,128)(2,1)S(1)} %get-tuple-element.36), channel_id=1, source_target_pairs={{0,8},{1,9},{2,10},{3,11},{4,12},{5,13},{6,14},{7,15},{8,0},{9,1},... | collective-permute-start | bytes 221192 | tf_op jit(solution)/shard_map/ppermute | solution.py:219
  25.2 9.0 %collective-permute-start.13 = (bf16[24,1536]{1,0:T(8,128)(2,1)S(1)}, bf16[24,1536]{1,0:T(8,128)(2,1)S(1)}, u32[]{:S(2)}, u32[]{:S(2)}) collective-permute-start(bf16[24,1536]{1,0:T(8,128)(2,1)S(1)} %get-tuple-element.37), channel_id=1, source_target_pairs={{0,4},{1,5},{2,6},{3,7},{4,0},{5,1},{6,2},{7,3},{8,12},{9,13},{10,... | collective-permute-start | bytes 221192 | tf_op jit(solution)/shard_map/ppermute | solution.py:219
  27.0 11.3 %copy-start = (f32[3072]{0:T(1024)S(1)}, f32[3072]{0:T(1024)}, u32[]{:S(2)}) copy-start(f32[3072]{0:T(1024)} %param.15) | copy-start | bytes 36868
  27.8 6.7 %collective-permute-start.15 = (bf16[24,1536]{1,0:T(8,128)(2,1)S(1)}, bf16[24,1536]{1,0:T(8,128)(2,1)S(1)}, u32[]{:S(2)}, u32[]{:S(2)}) collective-permute-start(bf16[24,1536]{1,0:T(8,128)(2,1)S(1)} %get-tuple-element.40), channel_id=1, source_target_pairs={{0,12},{1,13},{2,14},{3,15},{4,8},{5,9},{6,10},{7,11},{8,4},{9,5},... | collective-permute-start | bytes 221192 | tf_op jit(solution)/shard_map/ppermute | solution.py:219
  30.4 7.8 %collective-permute-start.16 = (bf16[24,1536]{1,0:T(8,128)(2,1)S(1)}, bf16[24,1536]{1,0:T(8,128)(2,1)S(1)}, u32[]{:S(2)}, u32[]{:S(2)}) collective-permute-start(bf16[24,1536]{1,0:T(8,128)(2,1)S(1)} %get-tuple-element.41), channel_id=1, source_target_pairs={{0,8},{1,9},{2,10},{3,11},{4,12},{5,13},{6,14},{7,15},{8,0},{9,1},... | collective-permute-start | bytes 221192 | tf_op jit(solution)/shard_map/ppermute | solution.py:219
  30.4 7.8 %collective-permute-start.17 = (bf16[24,1536]{1,0:T(8,128)(2,1)S(1)}, bf16[24,1536]{1,0:T(8,128)(2,1)S(1)}, u32[]{:S(2)}, u32[]{:S(2)}) collective-permute-start(bf16[24,1536]{1,0:T(8,128)(2,1)S(1)} %get-tuple-element.42), channel_id=1, source_target_pairs={{0,4},{1,5},{2,6},{3,7},{4,0},{5,1},{6,2},{7,3},{8,12},{9,13},{10,... | collective-permute-start | bytes 221192 | tf_op jit(solution)/shard_map/ppermute | solution.py:219

commit v12 on v11

--- a/solution.py
+++ b/solution.py
@@ -151,26 +151,23 @@
     )(*queries, *kvs)
 
 
-def project_kernel(groups, members, places, att, *refs):
-    ws = refs[: len(places)]
-    outs = refs[len(places) : len(places) + groups]
-    wide, sems = refs[len(places) + groups :]
+def project_kernel(groups, members, left, places, att, *refs):
+    ws = refs[: 2 * len(places)]
+    outs = refs[2 * len(places) : 2 * len(places) + groups]
+    wide, sems = refs[2 * len(places) + groups :]
     rows, width = outs[0].shape
-    q = lax.axis_index("patch") % members
-    side = lax.axis_index("groups") % 2
-    copies = []
-    for i, (piece, (j, flip, left)) in enumerate(zip(ws, places)):
-        size = piece.shape[0]
-        row = 0
-        if j is not None:
-            row = (q ^ j) * (size if flip is None else 2 * size)
-            if flip is not None:
-                row = row + (side ^ flip) * size
-            row = pl.multiple_of(row, size)
-        copies.append(pltpu.make_async_copy(piece.at[:, pl.ds(left, width)], wide.at[pl.ds(row, size)], sems.at[i]))
-    for c in copies:
-        c.start()
-    for c in copies:
+    me = lax.axis_index("patch")
+    direct = ((me ^ lax.axis_index("groups")) & 1) == 0
+    waits = []
+    for i, j in enumerate(places):
+        depth = ws[2 * i].shape[0]
+        row = 0 if j is None else pl.multiple_of(((me % members) ^ j) * depth, depth)
+        views = [w if w.shape[1] == width else w.at[:, pl.ds(left, width)] for w in ws[2 * i : 2 * i + 2]]
+        copies = [pltpu.make_async_copy(v, wide.at[pl.ds(row, depth)], sems.at[i]) for v in views]
+        pl.when(direct)(copies[0].start)
+        pl.when(jnp.logical_not(direct))(copies[1].start)
+        waits.append(copies[0])
+    for c in waits:
         c.wait()
     tile = 512 if width % 512 == 0 else width
     for t in range(width // tile):
@@ -180,21 +177,23 @@
             outs[i][:, cols] = part[i * rows : (i + 1) * rows].astype(outs[i].dtype)
 
 
-def project(groups, members, att, width, pieces, places):
+def project(groups, members, att, width, left, pieces):
     rows = att.shape[0] // groups
     share = att.shape[1]
+    places = [p[0] for p in pieces]
+    ws = [w for p in pieces for w in p[1:]]
     return pl.pallas_call(
-        functools.partial(project_kernel, groups, members, places),
+        functools.partial(project_kernel, groups, members, left, places),
         out_shape=[jax.ShapeDtypeStruct((rows, width), jnp.bfloat16)] * (groups - 1)
         + [jax.ShapeDtypeStruct((rows, width), jnp.float32)],
-        in_specs=[VMEM] + [ANY] * len(pieces),
+        in_specs=[VMEM] + [ANY] * len(ws),
         out_specs=[VMEM] * groups,
-        scratch_shapes=[pltpu.VMEM((share, width), jnp.bfloat16), pltpu.SemaphoreType.DMA((len(pieces),))],
+        scratch_shapes=[pltpu.VMEM((share, width), jnp.bfloat16), pltpu.SemaphoreType.DMA((len(places),))],
         compiler_params=pltpu.CompilerParams(vmem_limit_bytes=24 * 1024 * 1024),
         cost_estimate=pl.CostEstimate(
             flops=2 * groups * rows * share * width, bytes_accessed=2 * share * width, transcendentals=0
         ),
-    )(att, *pieces)
+    )(att, *ws)
 
 
 def after(x, *others):
@@ -228,10 +227,13 @@
             bit //= 2
         return [pieces[j] for j in range(members)]
 
+    def relay(x, direct, move):
+        everyone = [(g, p) for g in range(parts) for p in range(patch) if ((g ^ p) & 1 == 0) == direct]
+        pairs = [(g * patch + p, move(g, p)[0] * patch + move(g, p)[1]) for g, p in everyone]
+        return lax.ppermute(x, ("groups", "patch"), pairs)
+
     if shared:
-        side = lax.axis_index("groups") & 1
-        w_part = lax.dynamic_slice_in_dim(w_out, side * (depth // 2), depth // 2, 0)
-        y_part = send(w_part, 0, far)
+        w_far = relay(w_out, True, lambda g, p: (g, p ^ 2))
     own_query, fresh, w_own = prepare(
         groups, members, query, key_new, value_new, key_stale, value_stale, exponents.T, w_out
     )
@@ -239,27 +241,26 @@
     arrived = [send(fresh[k], k, 0) for k in order]
     both = jnp.concatenate([x[:, share:] for x in arrived] + [fresh[0]], axis=0)
     if shared:
-        both = after(both, y_part)
+        both = after(both, w_far)
     kvs = spread({0: both}, far)
     att = attend(groups, dim, arrived + [own_query], kvs)
 
     jobs = []
     if shared:
         w_core = send(after(w_own, both), 0, 1)
-        y_core = send(after(y_part, both), 0, 1)
-        x_part = swap(y_part)
-        edges = (0, half, model)
-        for left, right in zip(edges, edges[1:]):
-            x_core = send(after(x_part, kvs[far])[:, left:right], 0, 1)
-            pieces = [w_own, w_core, y_part, x_part, y_core, x_core]
-            places = [(0, None, left), (1, None, left), (2, 0, left), (2, 1, left), (3, 0, left), (3, 1, 0)]
-            jobs.append((right - left, pieces, places))
+        w_diagonal = relay(after(w_far, both), True, lambda g, p: (g, p ^ 1))
+        w_swapped = relay(after(w_far, *arrived), True, lambda g, p: (g ^ 1, p))
+        for left in (0, half):
+            crossed = relay(after(w_swapped, *kvs)[:, left : left + half], False, lambda g, p: (g, p ^ 1))
+            pieces = [(0, w_own, w_own), (1, w_core, w_core), (2, w_far, w_swapped), (3, crossed, w_diagonal)]
+            jobs.append((half, left, pieces))
     else:
         spots = (lax.axis_index("patch") % members) ^ jnp.arange(members)
-        jobs.append((model, [jnp.stack(spread({0: w_own}, far))[spots].reshape(-1, model)], [(None, None, 0)]))
+        whole = jnp.stack(spread({0: w_own}, far))[spots].reshape(-1, model)
+        jobs.append((model, 0, [(None, whole, whole)]))
     totals = []
-    for width, pieces, places in jobs:
-        sums = project(groups, members, att, width, pieces, places)
+    for width, left, pieces in jobs:
+        sums = project(groups, members, att, width, left, pieces)
         att = after(att, *sums)
         total = sums[-1]
         for k, part in zip(order, sums):

time: 39.2 us -> 45.9 us (1.17)
  starting transfers between devices: 19.8 us -> 26.4 us
  waiting for transfers between devices: 13.3 us -> 14.7 us
  local copies, waits for them, and re-layouts: 1.02 us -> 0.06 us
    ppermute x1 -> x5, starting transfers between devices: 1.71 us -> 10.8 us  [relay(): return lax.ppermute(x, ('groups', 'patch'), pairs)]
    ppermute x17 -> x13, starting transfers between devices: 18.1 us -> 15.6 us  [send(): lax.ppermute(x, 'patch', [(p, (p // members ^ k) * members + p % members...]
    ppermute x17 -> x13, waiting for transfers between devices: 13.3 us -> 14.7 us  [send(): lax.ppermute(x, 'patch', [(p, (p // members ^ k) * members + p % members...]
    dynamic_slice x1 -> x0, local copies, waits for them, and re-layouts: 0.98 us -> none  [per_device(): w_part = lax.dynamic_slice_in_dim(w_out, side * (depth // 2), depth // 2, 0)]
  transfers between devices with their start and end apart: 18 -> 18, of which waited for: 7 -> 6; matrix products, arithmetic and copies ran while one was open for 0% -> 0% of each run, Pallas kernels for 10% -> 8%
where the time goes in v12:
time: 45.9 us; the launch traced here: 45.7 us
  starting transfers between devices  26.4 us (58%)
  waiting for transfers between devices  14.7 us (32%)
  Pallas kernels  3.58 us (8%)
  other arithmetic  0.77 us (2%)
    ppermute x13, starting transfers between devices, send(): lax.ppermute(x, 'patch', [(p, (p // members ^ k) * members + p % members...  15.6 us
    ppermute x13, waiting for transfers between devices, send(): lax.ppermute(x, 'patch', [(p, (p // members ^ k) * members + p % members...  14.7 us
    ppermute x5, starting transfers between devices, relay(): return lax.ppermute(x, ('groups', 'patch'), pairs)  10.8 us
    pallas_call x1, Pallas kernels, prepare(): pl.pallas_call(functools.partial(prepare_kernel, groups, members), out_sh...  1.41 us
    pallas_call x2, Pallas kernels, project(): pl.pallas_call(functools.partial(project_kernel, groups, members, left, p...  1.24 us
    pallas_call x1, Pallas kernels, attend(): pl.pallas_call(functools.partial(attend_kernel, groups, dim), out_shape=j...  0.93 us
  transfers between devices with their start and end apart: 18, of which 6 were waited for; matrix products, arithmetic and copies ran while one was open for 0% of the time, Pallas kernels for 8%

profile of v12, /device:TPU:0, one launch (start us, length us, event | category | flops | bytes accessed | tf_op | source)
XLA Modules:
  0.0 45.7 jit_solution(10155371983217902207)
XLA Ops:
  0.0 4.9 %collective-permute-start.3 = (bf16[96,3072]{1,0:T(8,128)(2,1)}, bf16[96,3072]{1,0:T(8,128)(2,1)S(1)}, u32[]{:S(2)}, u32[]{:S(2)}) collective-permute-start(bf16[96,3072]{1,0:T(8,128)(2,1)} %refs_6_.1), channel_id=1, source_target_pairs={{0,2},{2,0},{4,6},{6,4},{8,10},{10,8},{12,14},{14,12},{17,19},{19,... | collective-permute-start | bytes 1769480 | tf_op jit(solution)/shard_map/ppermute | solution.py:233
  4.9 1.4 %shard_map.82 = (bf16[24,384]{1,0:T(8,128)(2,1)S(1)}, bf16[24,768]{1,0:T(8,128)(2,1)S(1)}, bf16[24,1152]{1,0:T(8,128)(2,1)S(1)}, bf16[24,1152]{1,0:T(8,128)(2,1)...) custom-call(bf16[24,1536]{1,0:T(8,128)(2,1)} %refs_0_.1, bf16[24,1536]{1,0:T(8,128)(2,1)} %refs_1_.1, ...), custom_call_target="tpu_custom_call" | custom-call | flops 368640 | bytes 1695744 | tf_op jit(solution)/shard_map/pallas_call | solution.py:88
  6.3 3.7 %collective-permute-start = (bf16[24,1152]{1,0:T(8,128)(2,1)S(1)}, bf16[24,1152]{1,0:T(8,128)(2,1)S(1)}, u32[]{:S(2)}, u32[]{:S(2)}) collective-permute-start(bf16[24,1152]{1,0:T(8,128)(2,1)S(1)} %get-tuple-element.25), channel_id=1, source_target_pairs={{0,12},{1,13},{2,14},{3,15},{4,8},{5,9},{6,10},{7,11},{8,4},{9,5},... | collective-permute-start | bytes 165896 | tf_op jit(solution)/shard_map/ppermute | solution.py:218
  10.0 0.0 collective-permute-start.1
  10.0 0.8 %collective-permute-start.2 = (bf16[24,1152]{1,0:T(8,128)(2,1)S(1)}, bf16[24,1152]{1,0:T(8,128)(2,1)S(1)}, u32[]{:S(2)}, u32[]{:S(2)}) collective-permute-start(bf16[24,1152]{1,0:T(8,128)(2,1)S(1)} %get-tuple-element.27), channel_id=1, source_target_pairs={{0,4},{1,5},{2,6},{3,7},{4,0},{5,1},{6,2},{7,3},{8,12},{9,13},{10,... | collective-permute-start | bytes 165896 | tf_op jit(solution)/shard_map/ppermute | solution.py:218
  10.7 1.9 %collective-permute-done.refs_0_ = bf16[24,1152]{1,0:T(8,128)(2,1)S(1)} collective-permute-done((bf16[24,1152]{1,0:T(8,128)(2,1)S(1)}, bf16[24,1152]{1,0:T(8,128)(2,1)S(1)}, u32[]{:S(2)}, u32[]{:S(2)}) %collective-permute-start) | collective-permute-done | bytes 55328 | tf_op jit(solution)/shard_map/ppermute | solution.py:218
  12.6 2.4 %collective-permute-done.1.refs_1_ = bf16[24,1152]{1,0:T(8,128)(2,1)S(1)} collective-permute-done((bf16[24,1152]{1,0:T(8,128)(2,1)S(1)}, bf16[24,1152]{1,0:T(8,128)(2,1)S(1)}, u32[]{:S(2)}, u32[]{:S(2)}) %collective-permute-start.1) | collective-permute-done | bytes 55328 | tf_op jit(solution)/shard_map/ppermute | solution.py:218
  15.0 0.0 collective-permute-done.2.refs_2_
  15.0 0.0 collective-permute-done.3.refs_4_
  15.0 1.5 %collective-permute-start.8 = (bf16[96,3072]{1,0:T(8,128)(2,1)S(1)}, bf16[96,3072]{1,0:T(8,128)(2,1)S(1)}, u32[]{:S(2)}, u32[]{:S(2)}) collective-permute-start(bf16[96,3072]{1,0:T(8,128)(2,1)S(1)} %collective-permute-done.3.refs_4_), channel_id=1, source_target_pairs={{0,16},{2,18},{4,20},{6,22},{8,24},{10,26},{12,28},{14,30},{17,1},... | collective-permute-start | bytes 1769480 | tf_op jit(solution)/shard_map/ppermute | solution.py:233
  16.5 1.7 %collective-permute-start.5 = (bf16[96,768]{1,0:T(8,128)(2,1)S(1)}, bf16[96,768]{1,0:T(8,128)(2,1)S(1)}, u32[]{:S(2)}, u32[]{:S(2)}) collective-permute-start(bf16[96,768]{1,0:T(8,128)(2,1)S(1)} %pad_maximum_fusion.refs_4_), channel_id=1, source_target_pairs={{0,2},{1,3},{2,0},{3,1},{4,6},{5,7},{6,4},{7,5},{8,10},{9,11},{10,... | collective-permute-start | bytes 442376 | tf_op jit(solution)/shard_map/ppermute | solution.py:218
  18.2 0.0 collective-permute-start.4
  18.2 3.5 %collective-permute-done.5.refs_6_ = bf16[96,768]{1,0:T(8,128)(2,1)S(1)} collective-permute-done((bf16[96,768]{1,0:T(8,128)(2,1)S(1)}, bf16[96,768]{1,0:T(8,128)(2,1)S(1)}, u32[]{:S(2)}, u32[]{:S(2)}) %collective-permute-start.5) | collective-permute-done | bytes 147488 | tf_op jit(solution)/shard_map/ppermute | solution.py:218
  21.7 0.0 collective-permute-start.6
  21.7 0.5 %collective-permute-start.7 = (bf16[96,3072]{1,0:T(8,128)(2,1)S(1)}, bf16[96,3072]{1,0:T(8,128)(2,1)S(1)}, u32[]{:S(2)}, u32[]{:S(2)}) collective-permute-start(bf16[96,3072]{1,0:T(8,128)(2,1)S(1)} %get-tuple-element.32.refs_0_.refs_1_), channel_id=1, source_target_pairs={{0,1},{1,0},{2,3},{3,2},{4,5},{5,4},{6,7},{7,6},{8,9},{9,8},{10,11... | collective-permute-start | bytes 1769480 | tf_op jit(solution)/shard_map/ppermute | solution.py:218
  22.3 1.9 %collective-permute-start.10 = (bf16[96,3072]{1,0:T(8,128)(2,1)S(1)}, bf16[96,3072]{1,0:T(8,128)(2,1)S(1)}, u32[]{:S(2)}, u32[]{:S(2)}) collective-permute-start(bf16[96,3072]{1,0:T(8,128)(2,1)S(1)} %collective-permute-done.3.refs_4_), channel_id=1, source_target_pairs={{0,1},{2,3},{4,5},{6,7},{8,9},{10,11},{12,13},{14,15},{17,16},{19,... | collective-permute-start | bytes 1769480 | tf_op jit(solution)/shard_map/ppermute | solution.py:233
  24.2 0.0 collective-permute-done.4.refs_5_
  24.2 0.0 collective-permute-done.6.refs_7_
  24.2 0.0 collective-permute-done.8.refs_5_
  24.3 1.3 %collective-permute-start.9 = (bf16[96,1536]{1,0:T(8,128)(2,1)S(1)}, bf16[96,1536]{1,0:T(8,128)(2,1)S(1)}, u32[]{:S(2)}, u32[]{:S(2)}) collective-permute-start(bf16[96,1536]{1,0:T(8,128)(2,1)S(1)} %get-tuple-element.46), channel_id=1, source_target_pairs={{1,0},{3,2},{5,4},{7,6},{9,8},{11,10},{13,12},{15,14},{16,17},{18,... | collective-permute-start | bytes 884744 | tf_op jit(solution)/shard_map/ppermute | solution.py:233
  25.6 1.3 %collective-permute-start.14 = (bf16[96,1536]{1,0:T(8,128)(2,1)S(1)}, bf16[96,1536]{1,0:T(8,128)(2,1)S(1)}, u32[]{:S(2)}, u32[]{:S(2)}) collective-permute-start(bf16[96,1536]{1,0:T(8,128)(2,1)S(1)} %get-tuple-element.45), channel_id=1, source_target_pairs={{1,0},{3,2},{5,4},{7,6},{9,8},{11,10},{13,12},{15,14},{16,17},{18,... | collective-permute-start | bytes 884744 | tf_op jit(solution)/shard_map/ppermute | solution.py:233
  26.9 0.9 %shard_map.83.att = bf16[96,384]{1,0:T(8,128)(2,1)S(1)} custom-call(bf16[24,1152]{1,0:T(8,128)(2,1)S(1)} %collective-permute-done.refs_0_, bf16[24,1152]{1,0:T(8,128)(2,1)S(1)} %collective-permute-done.1.refs_1_, bf16[24,1152]{1,0:T(8,128)(2,1)S(1)} %collective-permute-done.2.refs_2_, bf16[24,384]{1,0:T(8,128)(2,1)S(1)} %get-tuple-element.28.refs_3_, ...), custom_call_target="tpu_custom_call" | custom-call | flops 56623104 | bytes 589824 | tf_op jit(solution)/shard_map/pallas_call | solution.py:139
  27.8 0.0 collective-permute-done.7.refs_2_.refs_3_
  27.8 0.0 collective-permute-done.10.refs_7_
  27.8 0.0 collective-permute-done.9.refs_6_
  27.8 0.6 %shard_map.84 = (bf16[24,1536]{1,0:T(8,128)(2,1)S(1)}, bf16[24,1536]{1,0:T(8,128)(2,1)S(1)}, bf16[24,1536]{1,0:T(8,128)(2,1)S(1)}, f32[24,1536]{1,0:T(8,128)S(1)}) custom-call(bf16[96,384]{1,0:T(8,128)(2,1)S(1)} %shard_map.83.att, bf16[96,3072]{1,0:T(8,128)(2,1)S(1)} %get-tuple-element.32.refs_0_.refs_1_, ...), custom_call_target="tpu_custom_call" | custom-call | flops 113246208 | bytes 1179648 | tf_op jit(solution)/shard_map/pallas_call | solution.py:185
  28.5 2.1 %collective-permute-start.11 = (bf16[24,1536]{1,0:T(8,128)(2,1)S(1)}, bf16[24,1536]{1,0:T(8,128)(2,1)S(1)}, u32[]{:S(2)}, u32[]{:S(2)}) collective-permute-start(bf16[24,1536]{1,0:T(8,128)(2,1)S(1)} %get-tuple-element.37), channel_id=1, source_target_pairs={{0,12},{1,13},{2,14},{3,15},{4,8},{5,9},{6,10},{7,11},{8,4},{9,5},... | collective-permute-start | bytes 221192 | tf_op jit(solution)/shard_map/ppermute | solution.py:218
  30.6 0.0 collective-permute-start.12
  30.6 2.3 %collective-permute-start.13 = (bf16[24,1536]{1,0:T(8,128)(2,1)S(1)}, bf16[24,1536]{1,0:T(8,128)(2,1)S(1)}, u32[]{:S(2)}, u32[]{:S(2)}) collective-permute-start(bf16[24,1536]{1,0:T(8,128)(2,1)S(1)} %get-tuple-element.39), channel_id=1, source_target_pairs={{0,4},{1,5},{2,6},{3,7},{4,0},{5,1},{6,2},{7,3},{8,12},{9,13},{10,... | collective-permute-start | bytes 221192 | tf_op jit(solution)/shard_map/ppermute | solution.py:218
  32.9 0.0 copy-start
  32.9 0.0 collective-permute-done.14.refs_6_
  32.9 0.6 %shard_map.85 = (bf16[24,1536]{1,0:T(8,128)(2,1)S(1)}, bf16[24,1536]{1,0:T(8,128)(2,1)S(1)}, bf16[24,1536]{1,0:T(8,128)(2,1)S(1)}, f32[24,1536]{1,0:T(8,128)S(1)}) custom-call(bf16[96,384]{1,0:T(8,128)(2,1)S(1)} %shard_map.83.att, bf16[96,3072]{1,0:T(8,128)(2,1)S(1)} %get-tuple-element.32.refs_0_.refs_1_, ...), custom_call_target="tpu_custom_call" | custom-call | flops 113246208 | bytes 1179648 | tf_op jit(solution)/shard_map/pallas_call | solution.py:185
  33.6 2.1 %collective-permute-start.15 = (bf16[24,1536]{1,0:T(8,128)(2,1)S(1)}, bf16[24,1536]{1,0:T(8,128)(2,1)S(1)}, u32[]{:S(2)}, u32[]{:S(2)}) collective-permute-start(bf16[24,1536]{1,0:T(8,128)(2,1)S(1)} %get-tuple-element.42), channel_id=1, source_target_pairs={{0,12},{1,13},{2,14},{3,15},{4,8},{5,9},{6,10},{7,11},{8,4},{9,5},... | collective-permute-start | bytes 221192 | tf_op jit(solution)/shard_map/ppermute | solution.py:218
  35.7 0.0 collective-permute-start.16
  35.7 0.0 collective-permute-done.11
  35.7 2.3 %collective-permute-start.17 = (bf16[24,1536]{1,0:T(8,128)(2,1)S(1)}, bf16[24,1536]{1,0:T(8,128)(2,1)S(1)}, u32[]{:S(2)}, u32[]{:S(2)}) collective-permute-start(bf16[24,1536]{1,0:T(8,128)(2,1)S(1)} %get-tuple-element.44), channel_id=1, source_target_pairs={{0,4},{1,5},{2,6},{3,7},{4,0},{5,1},{6,2},{7,3},{8,12},{9,13},{10,... | collective-permute-start | bytes 221192 | tf_op jit(solution)/shard_map/ppermute | solution.py:218
  38.0 0.6 %collective-permute-done.12 = bf16[24,1536]{1,0:T(8,128)(2,1)S(1)} collective-permute-done((bf16[24,1536]{1,0:T(8,128)(2,1)S(1)}, bf16[24,1536]{1,0:T(8,128)(2,1)S(1)}, u32[]{:S(2)}, u32[]{:S(2)}) %collective-permute-start.12) | collective-permute-done | bytes 73760 | tf_op jit(solution)/shard_map/ppermute | solution.py:218
  38.7 0.0 collective-permute-done.13
  38.7 2.0 %collective-permute-done.15 = bf16[24,1536]{1,0:T(8,128)(2,1)S(1)} collective-permute-done((bf16[24,1536]{1,0:T(8,128)(2,1)S(1)}, bf16[24,1536]{1,0:T(8,128)(2,1)S(1)}, u32[]{:S(2)}, u32[]{:S(2)}) %collective-permute-start.15) | collective-permute-done | bytes 73760 | tf_op jit(solution)/shard_map/ppermute | solution.py:218
  40.7 4.2 %collective-permute-done.16 = bf16[24,1536]{1,0:T(8,128)(2,1)S(1)} collective-permute-done((bf16[24,1536]{1,0:T(8,128)(2,1)S(1)}, bf16[24,1536]{1,0:T(8,128)(2,1)S(1)}, u32[]{:S(2)}, u32[]{:S(2)}) %collective-permute-start.16) | collective-permute-done | bytes 73760 | tf_op jit(solution)/shard_map/ppermute | solution.py:218
  45.0 0.0 collective-permute-done.17
  45.0 0.0 copy-done
  45.0 0.7 %fusion = bf16[24,3072]{1,0:T(8,128)(2,1)} fusion(f32[24,1536]{1,0:T(8,128)S(1)} %convert_add_fusion, f32[24,1536]{1,0:T(8,128)S(1)} %convert_add_fusion.1, f32[3072]{0:T(1024)S(1)} %copy-done), kind=kLoop, calls=%fused_computation.1 | loop fusion | flops 221184 | bytes 454656 | tf_op jit(solution)/shard_map/convert_element_type | solution.py:269
  (7 shorter events, 0.1 us)
Async XLA Ops:
  0.0 15.0 %collective-permute-start.3 = (bf16[96,3072]{1,0:T(8,128)(2,1)}, bf16[96,3072]{1,0:T(8,128)(2,1)S(1)}, u32[]{:S(2)}, u32[]{:S(2)}) collective-permute-start(bf16[96,3072]{1,0:T(8,128)(2,1)} %refs_6_.1), channel_id=1, source_target_pairs={{0,2},{2,0},{4,6},{6,4},{8,10},{10,8},{12,14},{14,12},{17,19},{19,... | collective-permute-start | bytes 1769480 | tf_op jit(solution)/shard_map/ppermute | solution.py:233
  6.3 6.4 %collective-permute-start = (bf16[24,1152]{1,0:T(8,128)(2,1)S(1)}, bf16[24,1152]{1,0:T(8,128)(2,1)S(1)}, u32[]{:S(2)}, u32[]{:S(2)}) collective-permute-start(bf16[24,1152]{1,0:T(8,128)(2,1)S(1)} %get-tuple-element.25), channel_id=1, source_target_pairs={{0,12},{1,13},{2,14},{3,15},{4,8},{5,9},{6,10},{7,11},{8,4},{9,5},... | collective-permute-start | bytes 165896 | tf_op jit(solution)/shard_map/ppermute | solution.py:218
  10.0 5.1 %collective-permute-start.1 = (bf16[24,1152]{1,0:T(8,128)(2,1)S(1)}, bf16[24,1152]{1,0:T(8,128)(2,1)S(1)}, u32[]{:S(2)}, u32[]{:S(2)}) collective-permute-start(bf16[24,1152]{1,0:T(8,128)(2,1)S(1)} %get-tuple-element.26), channel_id=1, source_target_pairs={{0,8},{1,9},{2,10},{3,11},{4,12},{5,13},{6,14},{7,15},{8,0},{9,1},... | collective-permute-start | bytes 165896 | tf_op jit(solution)/shard_map/ppermute | solution.py:218
  10.0 5.1 %collective-permute-start.2 = (bf16[24,1152]{1,0:T(8,128)(2,1)S(1)}, bf16[24,1152]{1,0:T(8,128)(2,1)S(1)}, u32[]{:S(2)}, u32[]{:S(2)}) collective-permute-start(bf16[24,1152]{1,0:T(8,128)(2,1)S(1)} %get-tuple-element.27), channel_id=1, source_target_pairs={{0,4},{1,5},{2,6},{3,7},{4,0},{5,1},{6,2},{7,3},{8,12},{9,13},{10,... | collective-permute-start | bytes 165896 | tf_op jit(solution)/shard_map/ppermute | solution.py:218
  15.0 9.2 %collective-permute-start.8 = (bf16[96,3072]{1,0:T(8,128)(2,1)S(1)}, bf16[96,3072]{1,0:T(8,128)(2,1)S(1)}, u32[]{:S(2)}, u32[]{:S(2)}) collective-permute-start(bf16[96,3072]{1,0:T(8,128)(2,1)S(1)} %collective-permute-done.3.refs_4_), channel_id=1, source_target_pairs={{0,16},{2,18},{4,20},{6,22},{8,24},{10,26},{12,28},{14,30},{17,1},... | collective-permute-start | bytes 1769480 | tf_op jit(solution)/shard_map/ppermute | solution.py:233
  16.5 5.2 %collective-permute-start.5 = (bf16[96,768]{1,0:T(8,128)(2,1)S(1)}, bf16[96,768]{1,0:T(8,128)(2,1)S(1)}, u32[]{:S(2)}, u32[]{:S(2)}) collective-permute-start(bf16[96,768]{1,0:T(8,128)(2,1)S(1)} %pad_maximum_fusion.refs_4_), channel_id=1, source_target_pairs={{0,2},{1,3},{2,0},{3,1},{4,6},{5,7},{6,4},{7,5},{8,10},{9,11},{10,... | collective-permute-start | bytes 442376 | tf_op jit(solution)/shard_map/ppermute | solution.py:218
  18.2 6.0 %collective-permute-start.4 = (bf16[96,768]{1,0:T(8,128)(2,1)S(1)}, bf16[96,768]{1,0:T(8,128)(2,1)S(1)}, u32[]{:S(2)}, u32[]{:S(2)}) collective-permute-start(bf16[96,768]{1,0:T(8,128)(2,1)S(1)} %pad_maximum_fusion.refs_4_), channel_id=1, source_target_pairs={{0,1},{1,0},{2,3},{3,2},{4,5},{5,4},{6,7},{7,6},{8,9},{9,8},{10,11... | collective-permute-start | bytes 442376 | tf_op jit(solution)/shard_map/ppermute | solution.py:218
  21.7 2.5 %collective-permute-start.6 = (bf16[96,768]{1,0:T(8,128)(2,1)S(1)}, bf16[96,768]{1,0:T(8,128)(2,1)S(1)}, u32[]{:S(2)}, u32[]{:S(2)}) collective-permute-start(bf16[96,768]{1,0:T(8,128)(2,1)S(1)} %collective-permute-done.5.refs_6_), channel_id=1, source_target_pairs={{0,1},{1,0},{2,3},{3,2},{4,5},{5,4},{6,7},{7,6},{8,9},{9,8},{10,11... | collective-permute-start | bytes 442376 | tf_op jit(solution)/shard_map/ppermute | solution.py:218
  21.7 6.1 %collective-permute-start.7 = (bf16[96,3072]{1,0:T(8,128)(2,1)S(1)}, bf16[96,3072]{1,0:T(8,128)(2,1)S(1)}, u32[]{:S(2)}, u32[]{:S(2)}) collective-permute-start(bf16[96,3072]{1,0:T(8,128)(2,1)S(1)} %get-tuple-element.32.refs_0_.refs_1_), channel_id=1, source_target_pairs={{0,1},{1,0},{2,3},{3,2},{4,5},{5,4},{6,7},{7,6},{8,9},{9,8},{10,11... | collective-permute-start | bytes 1769480 | tf_op jit(solution)/shard_map/ppermute | solution.py:218
  22.3 5.6 %collective-permute-start.10 = (bf16[96,3072]{1,0:T(8,128)(2,1)S(1)}, bf16[96,3072]{1,0:T(8,128)(2,1)S(1)}, u32[]{:S(2)}, u32[]{:S(2)}) collective-permute-start(bf16[96,3072]{1,0:T(8,128)(2,1)S(1)} %collective-permute-done.3.refs_4_), channel_id=1, source_target_pairs={{0,1},{2,3},{4,5},{6,7},{8,9},{10,11},{12,13},{14,15},{17,16},{19,... | collective-permute-start | bytes 1769480 | tf_op jit(solution)/shard_map/ppermute | solution.py:233
  24.3 3.6 %collective-permute-start.9 = (bf16[96,1536]{1,0:T(8,128)(2,1)S(1)}, bf16[96,1536]{1,0:T(8,128)(2,1)S(1)}, u32[]{:S(2)}, u32[]{:S(2)}) collective-permute-start(bf16[96,1536]{1,0:T(8,128)(2,1)S(1)} %get-tuple-element.46), channel_id=1, source_target_pairs={{1,0},{3,2},{5,4},{7,6},{9,8},{11,10},{13,12},{15,14},{16,17},{18,... | collective-permute-start | bytes 884744 | tf_op jit(solution)/shard_map/ppermute | solution.py:233
  25.6 7.4 %collective-permute-start.14 = (bf16[96,1536]{1,0:T(8,128)(2,1)S(1)}, bf16[96,1536]{1,0:T(8,128)(2,1)S(1)}, u32[]{:S(2)}, u32[]{:S(2)}) collective-permute-start(bf16[96,1536]{1,0:T(8,128)(2,1)S(1)} %get-tuple-element.45), channel_id=1, source_target_pairs={{1,0},{3,2},{5,4},{7,6},{9,8},{11,10},{13,12},{15,14},{16,17},{18,... | collective-permute-start | bytes 884744 | tf_op jit(solution)/shard_map/ppermute | solution.py:233
  28.5 7.2 %collective-permute-start.11 = (bf16[24,1536]{1,0:T(8,128)(2,1)S(1)}, bf16[24,1536]{1,0:T(8,128)(2,1)S(1)}, u32[]{:S(2)}, u32[]{:S(2)}) collective-permute-start(bf16[24,1536]{1,0:T(8,128)(2,1)S(1)} %get-tuple-element.37), channel_id=1, source_target_pairs={{0,12},{1,13},{2,14},{3,15},{4,8},{5,9},{6,10},{7,11},{8,4},{9,5},... | collective-permute-start | bytes 221192 | tf_op jit(solution)/shard_map/ppermute | solution.py:218
  30.6 8.0 %collective-permute-start.12 = (bf16[24,1536]{1,0:T(8,128)(2,1)S(1)}, bf16[24,1536]{1,0:T(8,128)(2,1)S(1)}, u32[]{:S(2)}, u32[]{:S(2)}) collective-permute-start(bf16[24,1536]{1,0:T(8,128)(2,1)S(1)} %get-tuple-element.38), channel_id=1, source_target_pairs={{0,8},{1,9},{2,10},{3,11},{4,12},{5,13},{6,14},{7,15},{8,0},{9,1},... | collective-permute-start | bytes 221192 | tf_op jit(solution)/shard_map/ppermute | solution.py:218
  30.6 8.0 %collective-permute-start.13 = (bf16[24,1536]{1,0:T(8,128)(2,1)S(1)}, bf16[24,1536]{1,0:T(8,128)(2,1)S(1)}, u32[]{:S(2)}, u32[]{:S(2)}) collective-permute-start(bf16[24,1536]{1,0:T(8,128)(2,1)S(1)} %get-tuple-element.39), channel_id=1, source_target_pairs={{0,4},{1,5},{2,6},{3,7},{4,0},{5,1},{6,2},{7,3},{8,12},{9,13},{10,... | collective-permute-start | bytes 221192 | tf_op jit(solution)/shard_map/ppermute | solution.py:218
  32.9 12.1 %copy-start = (f32[3072]{0:T(1024)S(1)}, f32[3072]{0:T(1024)}, u32[]{:S(2)}) copy-start(f32[3072]{0:T(1024)} %param.15) | copy-start | bytes 36868
  33.6 7.2 %collective-permute-start.15 = (bf16[24,1536]{1,0:T(8,128)(2,1)S(1)}, bf16[24,1536]{1,0:T(8,128)(2,1)S(1)}, u32[]{:S(2)}, u32[]{:S(2)}) collective-permute-start(bf16[24,1536]{1,0:T(8,128)(2,1)S(1)} %get-tuple-element.42), channel_id=1, source_target_pairs={{0,12},{1,13},{2,14},{3,15},{4,8},{5,9},{6,10},{7,11},{8,4},{9,5},... | collective-permute-start | bytes 221192 | tf_op jit(solution)/shard_map/ppermute | solution.py:218
  35.7 9.3 %collective-permute-start.16 = (bf16[24,1536]{1,0:T(8,128)(2,1)S(1)}, bf16[24,1536]{1,0:T(8,128)(2,1)S(1)}, u32[]{:S(2)}, u32[]{:S(2)}) collective-permute-start(bf16[24,1536]{1,0:T(8,128)(2,1)S(1)} %get-tuple-element.43), channel_id=1, source_target_pairs={{0,8},{1,9},{2,10},{3,11},{4,12},{5,13},{6,14},{7,15},{8,0},{9,1},... | collective-permute-start | bytes 221192 | tf_op jit(solution)/shard_map/ppermute | solution.py:218
  35.7 9.3 %collective-permute-start.17 = (bf16[24,1536]{1,0:T(8,128)(2,1)S(1)}, bf16[24,1536]{1,0:T(8,128)(2,1)S(1)}, u32[]{:S(2)}, u32[]{:S(2)}) collective-permute-start(bf16[24,1536]{1,0:T(8,128)(2,1)S(1)} %get-tuple-element.44), channel_id=1, source_target_pairs={{0,4},{1,5},{2,6},{3,7},{4,0},{5,1},{6,2},{7,3},{8,12},{9,13},{10,... | collective-permute-start | bytes 221192 | tf_op jit(solution)/shard_map/ppermute | solution.py:218

commit v13 on v11

--- a/solution.py
+++ b/solution.py
@@ -10,7 +10,6 @@
 
 CLIP_LIMIT = 2.0
 VMEM = pl.BlockSpec(memory_space=pltpu.VMEM)
-ANY = pl.BlockSpec(memory_space=pl.ANY)
 HBM = pl.BlockSpec(memory_space=pltpu.HBM)
 
 
@@ -105,6 +104,27 @@
     return result[0], result[1 : 1 + groups], result[-1]
 
 
+def share_kernel(w_ref, out_ref, sem):
+    size = out_ref.shape[0]
+    top = pl.multiple_of((lax.axis_index("groups") & 1) * size, size)
+    copy = pltpu.make_async_copy(w_ref.at[pl.ds(top, size)], out_ref, sem)
+    copy.start()
+    copy.wait()
+
+
+def share_rows(w_out):
+    depth, model = w_out.shape
+    return pl.pallas_call(
+        share_kernel,
+        out_shape=jax.ShapeDtypeStruct((depth // 2, model), w_out.dtype),
+        in_specs=[HBM],
+        out_specs=VMEM,
+        scratch_shapes=[pltpu.SemaphoreType.DMA],
+        compiler_params=pltpu.CompilerParams(vmem_limit_bytes=24 * 1024 * 1024),
+        cost_estimate=pl.CostEstimate(flops=0, bytes_accessed=2 * depth * model, transcendentals=0),
+    )(pltpu.with_memory_space_constraint(w_out, pltpu.HBM))
+
+
 def attend_kernel(groups, dim, *refs):
     queries = refs[:groups]
     kvs = refs[groups:-2]
@@ -154,12 +174,11 @@
 def project_kernel(groups, members, places, att, *refs):
     ws = refs[: len(places)]
     outs = refs[len(places) : len(places) + groups]
-    wide, sems = refs[len(places) + groups :]
+    wide = refs[-1]
     rows, width = outs[0].shape
     q = lax.axis_index("patch") % members
-    side = lax.axis_index("groups") % 2
-    copies = []
-    for i, (piece, (j, flip, left)) in enumerate(zip(ws, places)):
+    side = lax.axis_index("groups") & 1
+    for piece, (j, flip, left) in zip(ws, places):
         size = piece.shape[0]
         row = 0
         if j is not None:
@@ -167,12 +186,8 @@
             if flip is not None:
                 row = row + (side ^ flip) * size
             row = pl.multiple_of(row, size)
-        copies.append(pltpu.make_async_copy(piece.at[:, pl.ds(left, width)], wide.at[pl.ds(row, size)], sems.at[i]))
-    for c in copies:
-        c.start()
-    for c in copies:
-        c.wait()
-    tile = 512 if width % 512 == 0 else width
+        wide[pl.ds(row, size), :] = piece[:, left : left + width]
+    tile = 256 if width % 256 == 0 else width
     for t in range(width // tile):
         cols = slice(t * tile, (t + 1) * tile)
         part = jnp.dot(att[...], wide[:, cols], preferred_element_type=jnp.float32)
@@ -187,9 +202,9 @@
         functools.partial(project_kernel, groups, members, places),
         out_shape=[jax.ShapeDtypeStruct((rows, width), jnp.bfloat16)] * (groups - 1)
         + [jax.ShapeDtypeStruct((rows, width), jnp.float32)],
-        in_specs=[VMEM] + [ANY] * len(pieces),
+        in_specs=[VMEM] * (1 + len(pieces)),
         out_specs=[VMEM] * groups,
-        scratch_shapes=[pltpu.VMEM((share, width), jnp.bfloat16), pltpu.SemaphoreType.DMA((len(pieces),))],
+        scratch_shapes=[pltpu.VMEM((share, width), jnp.bfloat16)],
         compiler_params=pltpu.CompilerParams(vmem_limit_bytes=24 * 1024 * 1024),
         cost_estimate=pl.CostEstimate(
             flops=2 * groups * rows * share * width, bytes_accessed=2 * share * width, transcendentals=0
@@ -213,7 +228,7 @@
     depth, model = w_out.shape
     far = members // 2
     shared = parts % 2 == 0 and members == 4 and depth % 32 == 0
-    half = model // 2
+    first = model // 2
 
     def send(x, k, j):
         return lax.ppermute(x, "patch", [(p, ((p // members) ^ k) * members + (p % members) ^ j) for p in range(patch)])
@@ -229,8 +244,7 @@
         return [pieces[j] for j in range(members)]
 
     if shared:
-        side = lax.axis_index("groups") & 1
-        w_part = lax.dynamic_slice_in_dim(w_out, side * (depth // 2), depth // 2, 0)
+        w_part = share_rows(w_out)
         y_part = send(w_part, 0, far)
     own_query, fresh, w_own = prepare(
         groups, members, query, key_new, value_new, key_stale, value_stale, exponents.T, w_out
@@ -248,7 +262,7 @@
         w_core = send(after(w_own, both), 0, 1)
         y_core = send(after(y_part, both), 0, 1)
         x_part = swap(y_part)
-        edges = (0, half, model)
+        edges = (0, first, model)
         for left, right in zip(edges, edges[1:]):
             x_core = send(after(x_part, kvs[far])[:, left:right], 0, 1)
             pieces = [w_own, w_core, y_part, x_part, y_core, x_core]

time: 39.2 us -> 38.8 us (0.990)
  local copies, waits for them, and re-layouts: 1.02 us -> 0.03 us
  waiting for transfers between devices: 13.3 us -> 13.7 us
    dynamic_slice x1 -> x0, local copies, waits for them, and re-layouts: 0.98 us -> none  [per_device(): w_part = lax.dynamic_slice_in_dim(w_out, side * (depth // 2), depth // 2, 0)]
    pallas_call x0 -> x1, Pallas kernels: none -> 0.97 us  [share_rows(): pl.pallas_call(share_kernel, out_shape=jax.ShapeDtypeStruct((depth // 2,...]
    pallas_call x2, Pallas kernels: 1.6 us -> 0.88 us  [project(): pl.pallas_call(functools.partial(project_kernel, groups, members, places)...]
  transfers between devices with their start and end apart: 18 -> 18, of which waited for: 7 -> 7; matrix products, arithmetic and copies ran while one was open for 0% -> 0% of each run, Pallas kernels for 10% -> 8%
where the time goes in v13:
time: 38.8 us; the launch traced here: 38.6 us
  starting transfers between devices  19.8 us (51%)
  waiting for transfers between devices  13.7 us (35%)
  Pallas kernels  4.17 us (11%)
  other arithmetic  0.78 us (2%)
    ppermute x17, starting transfers between devices, send(): lax.ppermute(x, 'patch', [(p, (p // members ^ k) * members + p % members...  18.1 us
    ppermute x17, waiting for transfers between devices, send(): lax.ppermute(x, 'patch', [(p, (p // members ^ k) * members + p % members...  13.7 us
    ppermute x1, starting transfers between devices, swap(): return lax.ppermute(x, 'groups', [(g, g ^ 1) for g in range(parts)])  1.71 us
    pallas_call x1, Pallas kernels, prepare(): pl.pallas_call(functools.partial(prepare_kernel, groups, members), out_sh...  1.4 us
    pallas_call x1, Pallas kernels, share_rows(): pl.pallas_call(share_kernel, out_shape=jax.ShapeDtypeStruct((depth // 2,...  0.97 us
    pallas_call x1, Pallas kernels, attend(): pl.pallas_call(functools.partial(attend_kernel, groups, dim), out_shape=j...  0.92 us
    pallas_call x2, Pallas kernels, project(): pl.pallas_call(functools.partial(project_kernel, groups, members, places)...  0.88 us
  transfers between devices with their start and end apart: 18, of which 7 were waited for; matrix products, arithmetic and copies ran while one was open for 0% of the time, Pallas kernels for 8%

profile of v13, /device:TPU:0, one launch (start us, length us, event | category | flops | bytes accessed | tf_op | source)
XLA Modules:
  0.0 38.6 jit_solution(17109379062847297217)
XLA Ops:
  0.0 1.0 %shard_map.83 = bf16[48,3072]{1,0:T(8,128)(2,1)S(1)} custom-call(bf16[96,3072]{1,0:T(8,128)(2,1)} %w_ref.1), custom_call_target="tpu_custom_call" | custom-call | bytes 589824 | tf_op jit(solution)/shard_map/pallas_call | solution.py:117
  1.0 3.0 %collective-permute-start.3 = (bf16[48,3072]{1,0:T(8,128)(2,1)S(1)}, bf16[48,3072]{1,0:T(8,128)(2,1)S(1)}, u32[]{:S(2)}, u32[]{:S(2)}) collective-permute-start(bf16[48,3072]{1,0:T(8,128)(2,1)S(1)} %shard_map.83), channel_id=1, source_target_pairs={{0,2},{1,3},{2,0},{3,1},{4,6},{5,7},{6,4},{7,5},{8,10},{9,11},{10,... | collective-permute-start | bytes 884744 | tf_op jit(solution)/shard_map/ppermute | solution.py:234
  4.0 1.4 %shard_map.82 = (bf16[24,384]{1,0:T(8,128)(2,1)S(1)}, bf16[24,768]{1,0:T(8,128)(2,1)S(1)}, bf16[24,1152]{1,0:T(8,128)(2,1)S(1)}, bf16[24,1152]{1,0:T(8,128)(2,1)...) custom-call(bf16[24,1536]{1,0:T(8,128)(2,1)} %refs_0_.1, bf16[24,1536]{1,0:T(8,128)(2,1)} %refs_1_.1, ...), custom_call_target="tpu_custom_call" | custom-call | flops 368640 | bytes 1695744 | tf_op jit(solution)/shard_map/pallas_call | solution.py:87
  5.4 3.7 %collective-permute-start = (bf16[24,1152]{1,0:T(8,128)(2,1)S(1)}, bf16[24,1152]{1,0:T(8,128)(2,1)S(1)}, u32[]{:S(2)}, u32[]{:S(2)}) collective-permute-start(bf16[24,1152]{1,0:T(8,128)(2,1)S(1)} %get-tuple-element.24), channel_id=1, source_target_pairs={{0,12},{1,13},{2,14},{3,15},{4,8},{5,9},{6,10},{7,11},{8,4},{9,5},... | collective-permute-start | bytes 165896 | tf_op jit(solution)/shard_map/ppermute | solution.py:234
  9.1 0.0 collective-permute-start.1
  9.1 0.8 %collective-permute-start.2 = (bf16[24,1152]{1,0:T(8,128)(2,1)S(1)}, bf16[24,1152]{1,0:T(8,128)(2,1)S(1)}, u32[]{:S(2)}, u32[]{:S(2)}) collective-permute-start(bf16[24,1152]{1,0:T(8,128)(2,1)S(1)} %get-tuple-element.26), channel_id=1, source_target_pairs={{0,4},{1,5},{2,6},{3,7},{4,0},{5,1},{6,2},{7,3},{8,12},{9,13},{10,... | collective-permute-start | bytes 165896 | tf_op jit(solution)/shard_map/ppermute | solution.py:234
  9.9 1.1 %collective-permute-done.3.refs_2_ = bf16[48,3072]{1,0:T(8,128)(2,1)S(1)} collective-permute-done((bf16[48,3072]{1,0:T(8,128)(2,1)S(1)}, bf16[48,3072]{1,0:T(8,128)(2,1)S(1)}, u32[]{:S(2)}, u32[]{:S(2)}) %collective-permute-start.3) | collective-permute-done | bytes 294944 | tf_op jit(solution)/shard_map/ppermute | solution.py:234
  11.0 1.7 %collective-permute-start.8 = (bf16[48,3072]{1,0:T(8,128)(2,1)S(1)}, bf16[48,3072]{1,0:T(8,128)(2,1)S(1)}, u32[]{:S(2)}, u32[]{:S(2)}) collective-permute-start(bf16[48,3072]{1,0:T(8,128)(2,1)S(1)} %collective-permute-done.3.refs_2_), channel_id=1, source_target_pairs={{0,16},{16,0},{1,17},{17,1},{2,18},{18,2},{3,19},{19,3},{4,20},{20... | collective-permute-start | bytes 884744 | tf_op jit(solution)/shard_map/ppermute | solution.py:237
  12.7 0.0 collective-permute-done.refs_0_
  12.7 1.4 %collective-permute-done.1.refs_1_ = bf16[24,1152]{1,0:T(8,128)(2,1)S(1)} collective-permute-done((bf16[24,1152]{1,0:T(8,128)(2,1)S(1)}, bf16[24,1152]{1,0:T(8,128)(2,1)S(1)}, u32[]{:S(2)}, u32[]{:S(2)}) %collective-permute-start.1) | collective-permute-done | bytes 55328 | tf_op jit(solution)/shard_map/ppermute | solution.py:234
  14.1 0.0 collective-permute-done.2.refs_2_
  14.2 0.6 %collective-permute-start.5 = (bf16[96,768]{1,0:T(8,128)(2,1)S(1)}, bf16[96,768]{1,0:T(8,128)(2,1)S(1)}, u32[]{:S(2)}, u32[]{:S(2)}) collective-permute-start(bf16[96,768]{1,0:T(8,128)(2,1)S(1)} %pad_maximum_fusion.refs_4_), channel_id=1, source_target_pairs={{0,2},{1,3},{2,0},{3,1},{4,6},{5,7},{6,4},{7,5},{8,10},{9,11},{10,... | collective-permute-start | bytes 442376 | tf_op jit(solution)/shard_map/ppermute | solution.py:234
  14.8 0.0 collective-permute-start.4
  14.8 0.5 %collective-permute-start.9 = (bf16[48,3072]{1,0:T(8,128)(2,1)S(1)}, bf16[48,3072]{1,0:T(8,128)(2,1)S(1)}, u32[]{:S(2)}, u32[]{:S(2)}) collective-permute-start(bf16[48,3072]{1,0:T(8,128)(2,1)S(1)} %collective-permute-done.3.refs_2_), channel_id=1, source_target_pairs={{0,1},{1,0},{2,3},{3,2},{4,5},{5,4},{6,7},{7,6},{8,9},{9,8},{10,11... | collective-permute-start | bytes 884744 | tf_op jit(solution)/shard_map/ppermute | solution.py:234
  15.3 0.0 collective-permute-start.7
  15.3 4.1 %collective-permute-done.5.refs_6_ = bf16[96,768]{1,0:T(8,128)(2,1)S(1)} collective-permute-done((bf16[96,768]{1,0:T(8,128)(2,1)S(1)}, bf16[96,768]{1,0:T(8,128)(2,1)S(1)}, u32[]{:S(2)}, u32[]{:S(2)}) %collective-permute-start.5) | collective-permute-done | bytes 147488 | tf_op jit(solution)/shard_map/ppermute | solution.py:234
  19.4 0.0 collective-permute-start.6
  19.4 0.0 collective-permute-done.8.refs_3_
  19.4 0.6 %collective-permute-start.10 = (bf16[48,1536]{1,0:T(8,128)(2,1)S(1)}, bf16[48,1536]{1,0:T(8,128)(2,1)S(1)}, u32[]{:S(2)}, u32[]{:S(2)}) collective-permute-start(bf16[48,1536]{1,0:T(8,128)(2,1)S(1)} %get-tuple-element.44), channel_id=1, source_target_pairs={{0,1},{1,0},{2,3},{3,2},{4,5},{5,4},{6,7},{7,6},{8,9},{9,8},{10,11... | collective-permute-start | bytes 442376 | tf_op jit(solution)/shard_map/ppermute | solution.py:234
  20.0 0.0 collective-permute-done.4.refs_5_
  20.0 0.1 collective-permute-start.14
  20.1 0.7 %collective-permute-done.6.refs_7_ = bf16[96,768]{1,0:T(8,128)(2,1)S(1)} collective-permute-done((bf16[96,768]{1,0:T(8,128)(2,1)S(1)}, bf16[96,768]{1,0:T(8,128)(2,1)S(1)}, u32[]{:S(2)}, u32[]{:S(2)}) %collective-permute-start.6) | collective-permute-done | bytes 147488 | tf_op jit(solution)/shard_map/ppermute | solution.py:234
  20.8 0.9 %shard_map.84.att = bf16[96,384]{1,0:T(8,128)(2,1)S(1)} custom-call(bf16[24,1152]{1,0:T(8,128)(2,1)S(1)} %collective-permute-done.refs_0_, bf16[24,1152]{1,0:T(8,128)(2,1)S(1)} %collective-permute-done.1.refs_1_, bf16[24,1152]{1,0:T(8,128)(2,1)S(1)} %collective-permute-done.2.refs_2_, bf16[24,384]{1,0:T(8,128)(2,1)S(1)} %get-tuple-element.27.refs_3_, ...), custom_call_target="tpu_custom_call" | custom-call | flops 56623104 | bytes 589824 | tf_op jit(solution)/shard_map/pallas_call | solution.py:159
  21.7 0.0 collective-permute-done.9.refs_4_
  21.7 0.0 collective-permute-done.10.refs_5_
  21.7 0.0 collective-permute-done.7.refs_1_
  21.7 0.4 %shard_map.85 = (bf16[24,1536]{1,0:T(8,128)(2,1)S(1)}, bf16[24,1536]{1,0:T(8,128)(2,1)S(1)}, bf16[24,1536]{1,0:T(8,128)(2,1)S(1)}, f32[24,1536]{1,0:T(8,128)S(1)}) custom-call(bf16[96,384]{1,0:T(8,128)(2,1)S(1)} %shard_map.84.att, bf16[96,3072]{1,0:T(8,128)(2,1)S(1)} %get-tuple-element.31.refs_0_, bf16[96,3072]{1,0:T(8,128)(2,1)S(1)} %collective-permute-done.7.refs_1_, ...), custom_call_target="tpu_custom_call" | custom-call | flops 113246208 | bytes 1179648 | tf_op jit(solution)/shard_map/pallas_call | solution.py:201
  22.2 2.6 %collective-permute-start.11 = (bf16[24,1536]{1,0:T(8,128)(2,1)S(1)}, bf16[24,1536]{1,0:T(8,128)(2,1)S(1)}, u32[]{:S(2)}, u32[]{:S(2)}) collective-permute-start(bf16[24,1536]{1,0:T(8,128)(2,1)S(1)} %get-tuple-element.35), channel_id=1, source_target_pairs={{0,12},{1,13},{2,14},{3,15},{4,8},{5,9},{6,10},{7,11},{8,4},{9,5},... | collective-permute-start | bytes 221192 | tf_op jit(solution)/shard_map/ppermute | solution.py:234
  24.8 0.0 collective-permute-start.12
  24.8 1.8 %collective-permute-start.13 = (bf16[24,1536]{1,0:T(8,128)(2,1)S(1)}, bf16[24,1536]{1,0:T(8,128)(2,1)S(1)}, u32[]{:S(2)}, u32[]{:S(2)}) collective-permute-start(bf16[24,1536]{1,0:T(8,128)(2,1)S(1)} %get-tuple-element.37), channel_id=1, source_target_pairs={{0,4},{1,5},{2,6},{3,7},{4,0},{5,1},{6,2},{7,3},{8,12},{9,13},{10,... | collective-permute-start | bytes 221192 | tf_op jit(solution)/shard_map/ppermute | solution.py:234
  26.6 0.0 copy-start
  26.6 0.0 collective-permute-done.14.refs_5_
  26.6 0.4 %shard_map.86 = (bf16[24,1536]{1,0:T(8,128)(2,1)S(1)}, bf16[24,1536]{1,0:T(8,128)(2,1)S(1)}, bf16[24,1536]{1,0:T(8,128)(2,1)S(1)}, f32[24,1536]{1,0:T(8,128)S(1)}) custom-call(bf16[96,384]{1,0:T(8,128)(2,1)S(1)} %shard_map.84.att, bf16[96,3072]{1,0:T(8,128)(2,1)S(1)} %get-tuple-element.31.refs_0_, bf16[96,3072]{1,0:T(8,128)(2,1)S(1)} %collective-permute-done.7.refs_1_, ...), custom_call_target="tpu_custom_call" | custom-call | flops 113246208 | bytes 1179648 | tf_op jit(solution)/shard_map/pallas_call | solution.py:201
  27.1 2.6 %collective-permute-start.15 = (bf16[24,1536]{1,0:T(8,128)(2,1)S(1)}, bf16[24,1536]{1,0:T(8,128)(2,1)S(1)}, u32[]{:S(2)}, u32[]{:S(2)}) collective-permute-start(bf16[24,1536]{1,0:T(8,128)(2,1)S(1)} %get-tuple-element.40), channel_id=1, source_target_pairs={{0,12},{1,13},{2,14},{3,15},{4,8},{5,9},{6,10},{7,11},{8,4},{9,5},... | collective-permute-start | bytes 221192 | tf_op jit(solution)/shard_map/ppermute | solution.py:234
  29.7 0.0 collective-permute-start.16
  29.7 0.0 collective-permute-done.11
  29.7 1.8 %collective-permute-start.17 = (bf16[24,1536]{1,0:T(8,128)(2,1)S(1)}, bf16[24,1536]{1,0:T(8,128)(2,1)S(1)}, u32[]{:S(2)}, u32[]{:S(2)}) collective-permute-start(bf16[24,1536]{1,0:T(8,128)(2,1)S(1)} %get-tuple-element.42), channel_id=1, source_target_pairs={{0,4},{1,5},{2,6},{3,7},{4,0},{5,1},{6,2},{7,3},{8,12},{9,13},{10,... | collective-permute-start | bytes 221192 | tf_op jit(solution)/shard_map/ppermute | solution.py:234
  31.5 2.3 %collective-permute-done.12 = bf16[24,1536]{1,0:T(8,128)(2,1)S(1)} collective-permute-done((bf16[24,1536]{1,0:T(8,128)(2,1)S(1)}, bf16[24,1536]{1,0:T(8,128)(2,1)S(1)}, u32[]{:S(2)}, u32[]{:S(2)}) %collective-permute-start.12) | collective-permute-done | bytes 73760 | tf_op jit(solution)/shard_map/ppermute | solution.py:234
  33.8 0.0 collective-permute-done.13
  33.9 0.3 collective-permute-done.15
  34.1 3.7 %collective-permute-done.16 = bf16[24,1536]{1,0:T(8,128)(2,1)S(1)} collective-permute-done((bf16[24,1536]{1,0:T(8,128)(2,1)S(1)}, bf16[24,1536]{1,0:T(8,128)(2,1)S(1)}, u32[]{:S(2)}, u32[]{:S(2)}) %collective-permute-start.16) | collective-permute-done | bytes 73760 | tf_op jit(solution)/shard_map/ppermute | solution.py:234
  37.9 0.0 collective-permute-done.17
  37.9 0.0 copy-done
  37.9 0.7 %fusion = bf16[24,3072]{1,0:T(8,128)(2,1)} fusion(f32[24,1536]{1,0:T(8,128)S(1)} %convert_add_fusion, f32[24,1536]{1,0:T(8,128)S(1)} %convert_add_fusion.1, f32[3072]{0:T(1024)S(1)} %copy-done), kind=kLoop, calls=%fused_computation.1 | loop fusion | flops 221184 | bytes 454656 | tf_op jit(solution)/shard_map/convert_element_type | solution.py:282
  (7 shorter events, 0.1 us)
Async XLA Ops:
  1.0 10.0 %collective-permute-start.3 = (bf16[48,3072]{1,0:T(8,128)(2,1)S(1)}, bf16[48,3072]{1,0:T(8,128)(2,1)S(1)}, u32[]{:S(2)}, u32[]{:S(2)}) collective-permute-start(bf16[48,3072]{1,0:T(8,128)(2,1)S(1)} %shard_map.83), channel_id=1, source_target_pairs={{0,2},{1,3},{2,0},{3,1},{4,6},{5,7},{6,4},{7,5},{8,10},{9,11},{10,... | collective-permute-start | bytes 884744 | tf_op jit(solution)/shard_map/ppermute | solution.py:234
  5.4 7.3 %collective-permute-start = (bf16[24,1152]{1,0:T(8,128)(2,1)S(1)}, bf16[24,1152]{1,0:T(8,128)(2,1)S(1)}, u32[]{:S(2)}, u32[]{:S(2)}) collective-permute-start(bf16[24,1152]{1,0:T(8,128)(2,1)S(1)} %get-tuple-element.24), channel_id=1, source_target_pairs={{0,12},{1,13},{2,14},{3,15},{4,8},{5,9},{6,10},{7,11},{8,4},{9,5},... | collective-permute-start | bytes 165896 | tf_op jit(solution)/shard_map/ppermute | solution.py:234
  9.1 5.1 %collective-permute-start.1 = (bf16[24,1152]{1,0:T(8,128)(2,1)S(1)}, bf16[24,1152]{1,0:T(8,128)(2,1)S(1)}, u32[]{:S(2)}, u32[]{:S(2)}) collective-permute-start(bf16[24,1152]{1,0:T(8,128)(2,1)S(1)} %get-tuple-element.25), channel_id=1, source_target_pairs={{0,8},{1,9},{2,10},{3,11},{4,12},{5,13},{6,14},{7,15},{8,0},{9,1},... | collective-permute-start | bytes 165896 | tf_op jit(solution)/shard_map/ppermute | solution.py:234
  9.1 5.1 %collective-permute-start.2 = (bf16[24,1152]{1,0:T(8,128)(2,1)S(1)}, bf16[24,1152]{1,0:T(8,128)(2,1)S(1)}, u32[]{:S(2)}, u32[]{:S(2)}) collective-permute-start(bf16[24,1152]{1,0:T(8,128)(2,1)S(1)} %get-tuple-element.26), channel_id=1, source_target_pairs={{0,4},{1,5},{2,6},{3,7},{4,0},{5,1},{6,2},{7,3},{8,12},{9,13},{10,... | collective-permute-start | bytes 165896 | tf_op jit(solution)/shard_map/ppermute | solution.py:234
  11.0 8.4 %collective-permute-start.8 = (bf16[48,3072]{1,0:T(8,128)(2,1)S(1)}, bf16[48,3072]{1,0:T(8,128)(2,1)S(1)}, u32[]{:S(2)}, u32[]{:S(2)}) collective-permute-start(bf16[48,3072]{1,0:T(8,128)(2,1)S(1)} %collective-permute-done.3.refs_2_), channel_id=1, source_target_pairs={{0,16},{16,0},{1,17},{17,1},{2,18},{18,2},{3,19},{19,3},{4,20},{20... | collective-permute-start | bytes 884744 | tf_op jit(solution)/shard_map/ppermute | solution.py:237
  14.2 5.2 %collective-permute-start.5 = (bf16[96,768]{1,0:T(8,128)(2,1)S(1)}, bf16[96,768]{1,0:T(8,128)(2,1)S(1)}, u32[]{:S(2)}, u32[]{:S(2)}) collective-permute-start(bf16[96,768]{1,0:T(8,128)(2,1)S(1)} %pad_maximum_fusion.refs_4_), channel_id=1, source_target_pairs={{0,2},{1,3},{2,0},{3,1},{4,6},{5,7},{6,4},{7,5},{8,10},{9,11},{10,... | collective-permute-start | bytes 442376 | tf_op jit(solution)/shard_map/ppermute | solution.py:234
  14.8 5.2 %collective-permute-start.4 = (bf16[96,768]{1,0:T(8,128)(2,1)S(1)}, bf16[96,768]{1,0:T(8,128)(2,1)S(1)}, u32[]{:S(2)}, u32[]{:S(2)}) collective-permute-start(bf16[96,768]{1,0:T(8,128)(2,1)S(1)} %pad_maximum_fusion.refs_4_), channel_id=1, source_target_pairs={{0,1},{1,0},{2,3},{3,2},{4,5},{5,4},{6,7},{7,6},{8,9},{9,8},{10,11... | collective-permute-start | bytes 442376 | tf_op jit(solution)/shard_map/ppermute | solution.py:234
  14.8 6.9 %collective-permute-start.9 = (bf16[48,3072]{1,0:T(8,128)(2,1)S(1)}, bf16[48,3072]{1,0:T(8,128)(2,1)S(1)}, u32[]{:S(2)}, u32[]{:S(2)}) collective-permute-start(bf16[48,3072]{1,0:T(8,128)(2,1)S(1)} %collective-permute-done.3.refs_2_), channel_id=1, source_target_pairs={{0,1},{1,0},{2,3},{3,2},{4,5},{5,4},{6,7},{7,6},{8,9},{9,8},{10,11... | collective-permute-start | bytes 884744 | tf_op jit(solution)/shard_map/ppermute | solution.py:234
  15.3 6.4 %collective-permute-start.7 = (bf16[96,3072]{1,0:T(8,128)(2,1)S(1)}, bf16[96,3072]{1,0:T(8,128)(2,1)S(1)}, u32[]{:S(2)}, u32[]{:S(2)}) collective-permute-start(bf16[96,3072]{1,0:T(8,128)(2,1)S(1)} %get-tuple-element.31.refs_0_), channel_id=1, source_target_pairs={{0,1},{1,0},{2,3},{3,2},{4,5},{5,4},{6,7},{7,6},{8,9},{9,8},{10,11... | collective-permute-start | bytes 1769480 | tf_op jit(solution)/shard_map/ppermute | solution.py:234
  19.4 1.4 %collective-permute-start.6 = (bf16[96,768]{1,0:T(8,128)(2,1)S(1)}, bf16[96,768]{1,0:T(8,128)(2,1)S(1)}, u32[]{:S(2)}, u32[]{:S(2)}) collective-permute-start(bf16[96,768]{1,0:T(8,128)(2,1)S(1)} %collective-permute-done.5.refs_6_), channel_id=1, source_target_pairs={{0,1},{1,0},{2,3},{3,2},{4,5},{5,4},{6,7},{7,6},{8,9},{9,8},{10,11... | collective-permute-start | bytes 442376 | tf_op jit(solution)/shard_map/ppermute | solution.py:234
  19.4 2.3 %collective-permute-start.10 = (bf16[48,1536]{1,0:T(8,128)(2,1)S(1)}, bf16[48,1536]{1,0:T(8,128)(2,1)S(1)}, u32[]{:S(2)}, u32[]{:S(2)}) collective-permute-start(bf16[48,1536]{1,0:T(8,128)(2,1)S(1)} %get-tuple-element.44), channel_id=1, source_target_pairs={{0,1},{1,0},{2,3},{3,2},{4,5},{5,4},{6,7},{7,6},{8,9},{9,8},{10,11... | collective-permute-start | bytes 442376 | tf_op jit(solution)/shard_map/ppermute | solution.py:234
  20.0 6.6 %collective-permute-start.14 = (bf16[48,1536]{1,0:T(8,128)(2,1)S(1)}, bf16[48,1536]{1,0:T(8,128)(2,1)S(1)}, u32[]{:S(2)}, u32[]{:S(2)}) collective-permute-start(bf16[48,1536]{1,0:T(8,128)(2,1)S(1)} %get-tuple-element.43), channel_id=1, source_target_pairs={{0,1},{1,0},{2,3},{3,2},{4,5},{5,4},{6,7},{7,6},{8,9},{9,8},{10,11... | collective-permute-start | bytes 442376 | tf_op jit(solution)/shard_map/ppermute | solution.py:234
  22.2 7.5 %collective-permute-start.11 = (bf16[24,1536]{1,0:T(8,128)(2,1)S(1)}, bf16[24,1536]{1,0:T(8,128)(2,1)S(1)}, u32[]{:S(2)}, u32[]{:S(2)}) collective-permute-start(bf16[24,1536]{1,0:T(8,128)(2,1)S(1)} %get-tuple-element.35), channel_id=1, source_target_pairs={{0,12},{1,13},{2,14},{3,15},{4,8},{5,9},{6,10},{7,11},{8,4},{9,5},... | collective-permute-start | bytes 221192 | tf_op jit(solution)/shard_map/ppermute | solution.py:234
  24.8 9.0 %collective-permute-start.12 = (bf16[24,1536]{1,0:T(8,128)(2,1)S(1)}, bf16[24,1536]{1,0:T(8,128)(2,1)S(1)}, u32[]{:S(2)}, u32[]{:S(2)}) collective-permute-start(bf16[24,1536]{1,0:T(8,128)(2,1)S(1)} %get-tuple-element.36), channel_id=1, source_target_pairs={{0,8},{1,9},{2,10},{3,11},{4,12},{5,13},{6,14},{7,15},{8,0},{9,1},... | collective-permute-start | bytes 221192 | tf_op jit(solution)/shard_map/ppermute | solution.py:234
  24.8 9.0 %collective-permute-start.13 = (bf16[24,1536]{1,0:T(8,128)(2,1)S(1)}, bf16[24,1536]{1,0:T(8,128)(2,1)S(1)}, u32[]{:S(2)}, u32[]{:S(2)}) collective-permute-start(bf16[24,1536]{1,0:T(8,128)(2,1)S(1)} %get-tuple-element.37), channel_id=1, source_target_pairs={{0,4},{1,5},{2,6},{3,7},{4,0},{5,1},{6,2},{7,3},{8,12},{9,13},{10,... | collective-permute-start | bytes 221192 | tf_op jit(solution)/shard_map/ppermute | solution.py:234
  26.6 11.3 %copy-start = (f32[3072]{0:T(1024)S(1)}, f32[3072]{0:T(1024)}, u32[]{:S(2)}) copy-start(f32[3072]{0:T(1024)} %param.15) | copy-start | bytes 36868
  27.1 7.1 %collective-permute-start.15 = (bf16[24,1536]{1,0:T(8,128)(2,1)S(1)}, bf16[24,1536]{1,0:T(8,128)(2,1)S(1)}, u32[]{:S(2)}, u32[]{:S(2)}) collective-permute-start(bf16[24,1536]{1,0:T(8,128)(2,1)S(1)} %get-tuple-element.40), channel_id=1, source_target_pairs={{0,12},{1,13},{2,14},{3,15},{4,8},{5,9},{6,10},{7,11},{8,4},{9,5},... | collective-permute-start | bytes 221192 | tf_op jit(solution)/shard_map/ppermute | solution.py:234
  29.7 8.2 %collective-permute-start.16 = (bf16[24,1536]{1,0:T(8,128)(2,1)S(1)}, bf16[24,1536]{1,0:T(8,128)(2,1)S(1)}, u32[]{:S(2)}, u32[]{:S(2)}) collective-permute-start(bf16[24,1536]{1,0:T(8,128)(2,1)S(1)} %get-tuple-element.41), channel_id=1, source_target_pairs={{0,8},{1,9},{2,10},{3,11},{4,12},{5,13},{6,14},{7,15},{8,0},{9,1},... | collective-permute-start | bytes 221192 | tf_op jit(solution)/shard_map/ppermute | solution.py:234
  29.7 8.2 %collective-permute-start.17 = (bf16[24,1536]{1,0:T(8,128)(2,1)S(1)}, bf16[24,1536]{1,0:T(8,128)(2,1)S(1)}, u32[]{:S(2)}, u32[]{:S(2)}) collective-permute-start(bf16[24,1536]{1,0:T(8,128)(2,1)S(1)} %get-tuple-element.42), channel_id=1, source_target_pairs={{0,4},{1,5},{2,6},{3,7},{4,0},{5,1},{6,2},{7,3},{8,12},{9,13},{10,... | collective-permute-start | bytes 221192 | tf_op jit(solution)/shard_map/ppermute | solution.py:234

commit v14 on v13

--- a/solution.py
+++ b/solution.py
@@ -30,7 +30,9 @@
     }
     for i in order:
         copies[i].start()
-    move = pltpu.make_async_copy(w_ref, wout, sems.at[6])
+    size = wout.shape[0]
+    top = pl.multiple_of((lax.axis_index("groups") & 1) * size, size) if size < w_ref.shape[0] else 0
+    move = pltpu.make_async_copy(w_ref.at[pl.ds(top, size)], wout, sems.at[6])
     move.start()
     heads = est.shape[0] // 2
     dim = width // heads
@@ -74,14 +76,14 @@
     move.wait()
 
 
-def prepare(groups, members, query, key_new, value_new, key_stale, value_stale, powers, w_out):
+def prepare(groups, members, split, query, key_new, value_new, key_stale, value_stale, powers, w_out):
     rows, width = query.shape
     share = width // groups
     depth, model = w_out.shape
     outs = (
         [((rows, share), jnp.bfloat16), ((rows, 2 * share), jnp.bfloat16)]
         + [((rows, 3 * share), jnp.bfloat16)] * (groups - 1)
-        + [((depth, model), jnp.bfloat16)]
+        + [((depth // split, model), jnp.bfloat16)]
     )
     sources = (query, key_new, value_new, key_stale, value_stale, powers, w_out)
     result = pl.pallas_call(
@@ -98,37 +100,18 @@
         ],
         compiler_params=pltpu.CompilerParams(vmem_limit_bytes=24 * 1024 * 1024),
         cost_estimate=pl.CostEstimate(
-            flops=10 * rows * width, bytes_accessed=14 * rows * width + 4 * depth * model, transcendentals=0
+            flops=10 * rows * width, bytes_accessed=14 * rows * width + 4 * (depth // split) * model, transcendentals=0
         ),
     )(*(pltpu.with_memory_space_constraint(x, pltpu.HBM) for x in sources))
     return result[0], result[1 : 1 + groups], result[-1]
 
 
-def share_kernel(w_ref, out_ref, sem):
-    size = out_ref.shape[0]
-    top = pl.multiple_of((lax.axis_index("groups") & 1) * size, size)
-    copy = pltpu.make_async_copy(w_ref.at[pl.ds(top, size)], out_ref, sem)
-    copy.start()
-    copy.wait()
-
-
-def share_rows(w_out):
-    depth, model = w_out.shape
-    return pl.pallas_call(
-        share_kernel,
-        out_shape=jax.ShapeDtypeStruct((depth // 2, model), w_out.dtype),
-        in_specs=[HBM],
-        out_specs=VMEM,
-        scratch_shapes=[pltpu.SemaphoreType.DMA],
-        compiler_params=pltpu.CompilerParams(vmem_limit_bytes=24 * 1024 * 1024),
-        cost_estimate=pl.CostEstimate(flops=0, bytes_accessed=2 * depth * model, transcendentals=0),
-    )(pltpu.with_memory_space_constraint(w_out, pltpu.HBM))
-
-
 def attend_kernel(groups, dim, *refs):
     queries = refs[:groups]
-    kvs = refs[groups:-2]
-    att, kv = refs[-2:]
+    kvs = refs[groups:-5]
+    w_ref, att, w_own, kv, sem = refs[-5:]
+    copy = pltpu.make_async_copy(w_ref, w_own, sem)
+    copy.start()
     share = att.shape[1]
     block = kvs[0].shape[0]
     for j in range(len(kvs)):
@@ -150,25 +133,29 @@
             preferred_element_type=jnp.float32,
         )
         att[:, cols] = (numer / total).astype(jnp.bfloat16)
-
-
-def attend(groups, dim, queries, kvs):
+    copy.wait()
+
+
+def attend(groups, dim, queries, kvs, w_out):
     rows, share = queries[-1].shape
     block = kvs[0].shape[0]
     pieces = len(kvs)
     return pl.pallas_call(
         functools.partial(attend_kernel, groups, dim),
-        out_shape=jax.ShapeDtypeStruct((groups * rows, share), jnp.bfloat16),
-        in_specs=[VMEM] * (groups + pieces),
-        out_specs=VMEM,
-        scratch_shapes=[pltpu.VMEM((pieces * block, 2 * share), jnp.bfloat16)],
+        out_shape=[
+            jax.ShapeDtypeStruct((groups * rows, share), jnp.bfloat16),
+            jax.ShapeDtypeStruct(w_out.shape, w_out.dtype),
+        ],
+        in_specs=[VMEM] * (groups + pieces) + [HBM],
+        out_specs=[VMEM] * 2,
+        scratch_shapes=[pltpu.VMEM((pieces * block, 2 * share), jnp.bfloat16), pltpu.SemaphoreType.DMA],
         compiler_params=pltpu.CompilerParams(vmem_limit_bytes=24 * 1024 * 1024),
         cost_estimate=pl.CostEstimate(
             flops=4 * groups * rows * pieces * block * share,
             bytes_accessed=4 * pieces * block * share,
             transcendentals=groups * rows * pieces * block * share // dim,
         ),
-    )(*queries, *kvs)
+    )(*queries, *kvs, pltpu.with_memory_space_constraint(w_out, pltpu.HBM))
 
 
 def project_kernel(groups, members, places, att, *refs):
@@ -243,23 +230,21 @@
             bit //= 2
         return [pieces[j] for j in range(members)]
 
-    if shared:
-        w_part = share_rows(w_out)
-        y_part = send(w_part, 0, far)
-    own_query, fresh, w_own = prepare(
-        groups, members, query, key_new, value_new, key_stale, value_stale, exponents.T, w_out
+    own_query, fresh, w_part = prepare(
+        groups, members, 2 if shared else 1, query, key_new, value_new, key_stale, value_stale, exponents.T, w_out
     )
     order = range(groups - 1, 0, -1)
     arrived = [send(fresh[k], k, 0) for k in order]
     both = jnp.concatenate([x[:, share:] for x in arrived] + [fresh[0]], axis=0)
     if shared:
+        y_part = send(w_part, 0, 2)
         both = after(both, y_part)
     kvs = spread({0: both}, far)
-    att = attend(groups, dim, arrived + [own_query], kvs)
+    att, w_own = attend(groups, dim, arrived + [own_query], kvs, w_out)
 
     jobs = []
     if shared:
-        w_core = send(after(w_own, both), 0, 1)
+        w_core = send(after(w_out, both), 0, 1)
         y_core = send(after(y_part, both), 0, 1)
         x_part = swap(y_part)
         edges = (0, first, model)
@@ -270,7 +255,7 @@
             jobs.append((right - left, pieces, places))
     else:
         spots = (lax.axis_index("patch") % members) ^ jnp.arange(members)
-        jobs.append((model, [jnp.stack(spread({0: w_own}, far))[spots].reshape(-1, model)], [(None, None, 0)]))
+        jobs.append((model, [jnp.stack(spread({0: w_out}, far))[spots].reshape(-1, model)], [(None, None, 0)]))
     totals = []
     for width, pieces, places in jobs:
         sums = project(groups, members, att, width, pieces, places)

time: 38.8 us -> 39.7 us (1.023)
  starting transfers between devices: 19.8 us -> 22 us
  waiting for transfers between devices: 13.7 us -> 12.6 us
    ppermute x17, waiting for transfers between devices: 13.7 us -> 11.4 us  [send(): lax.ppermute(x, 'patch', [(p, (p // members ^ k) * members + p % members...]
    ppermute x17, starting transfers between devices: 18.1 us -> 20.3 us  [send(): lax.ppermute(x, 'patch', [(p, (p // members ^ k) * members + p % members...]
    ppermute x1, waiting for transfers between devices: 0.01 us -> 1.2 us  [swap(): return lax.ppermute(x, 'groups', [(g, g ^ 1) for g in range(parts)])]
    pallas_call x2 -> x1, Pallas kernels: 1.89 us -> 1.62 us  [attend(): pl.pallas_call(functools.partial(attend_kernel, groups, dim), out_shape=[...]
  transfers between devices with their start and end apart: 18 -> 18, of which waited for: 7 -> 5; matrix products, arithmetic and copies ran while one was open for 0% -> 0% of each run, Pallas kernels for 8% -> 6%
where the time goes in v14:
time: 39.7 us; the launch traced here: 39.6 us
  starting transfers between devices  22 us (55%)
  waiting for transfers between devices  12.6 us (32%)
  Pallas kernels  3.96 us (10%)
  other arithmetic  0.78 us (2%)
    ppermute x17, starting transfers between devices, send(): lax.ppermute(x, 'patch', [(p, (p // members ^ k) * members + p % members...  20.3 us
    ppermute x17, waiting for transfers between devices, send(): lax.ppermute(x, 'patch', [(p, (p // members ^ k) * members + p % members...  11.4 us
    ppermute x1, starting transfers between devices, swap(): return lax.ppermute(x, 'groups', [(g, g ^ 1) for g in range(parts)])  1.71 us
    pallas_call x1, Pallas kernels, attend(): pl.pallas_call(functools.partial(attend_kernel, groups, dim), out_shape=[...  1.62 us
    pallas_call x1, Pallas kernels, prepare(): pl.pallas_call(functools.partial(prepare_kernel, groups, members), out_sh...  1.46 us
    ppermute x1, waiting for transfers between devices, swap(): return lax.ppermute(x, 'groups', [(g, g ^ 1) for g in range(parts)])  1.2 us
    pallas_call x2, Pallas kernels, project(): pl.pallas_call(functools.partial(project_kernel, groups, members, places)...  0.88 us
  transfers between devices with their start and end apart: 18, of which 5 were waited for; matrix products, arithmetic and copies ran while one was open for 0% of the time, Pallas kernels for 6%

profile of v14, /device:TPU:0, one launch (start us, length us, event | category | flops | bytes accessed | tf_op | source)
XLA Modules:
  0.0 39.6 jit_solution(3096711938499996306)
XLA Ops:
  0.0 0.0 copy-start
  0.0 1.5 %shard_map.82 = (bf16[24,384]{1,0:T(8,128)(2,1)S(1)}, bf16[24,768]{1,0:T(8,128)(2,1)S(1)}, bf16[24,1152]{1,0:T(8,128)(2,1)S(1)}, bf16[24,1152]{1,0:T(8,128)(2,1)...) custom-call(bf16[24,1536]{1,0:T(8,128)(2,1)} %refs_0_.1, bf16[24,1536]{1,0:T(8,128)(2,1)} %refs_1_.1, ...), custom_call_target="tpu_custom_call" | custom-call | flops 368640 | bytes 1105920 | tf_op jit(solution)/shard_map/pallas_call | solution.py:89
  1.5 3.0 %collective-permute-start.3 = (bf16[48,3072]{1,0:T(8,128)(2,1)S(1)}, bf16[48,3072]{1,0:T(8,128)(2,1)S(1)}, u32[]{:S(2)}, u32[]{:S(2)}) collective-permute-start(bf16[48,3072]{1,0:T(8,128)(2,1)S(1)} %get-tuple-element.31), channel_id=1, source_target_pairs={{0,2},{1,3},{2,0},{3,1},{4,6},{5,7},{6,4},{7,5},{8,10},{9,11},{10,... | collective-permute-start | bytes 884744 | tf_op jit(solution)/shard_map/ppermute | solution.py:221
  4.5 3.6 %collective-permute-start = (bf16[24,1152]{1,0:T(8,128)(2,1)S(1)}, bf16[24,1152]{1,0:T(8,128)(2,1)S(1)}, u32[]{:S(2)}, u32[]{:S(2)}) collective-permute-start(bf16[24,1152]{1,0:T(8,128)(2,1)S(1)} %get-tuple-element.26), channel_id=1, source_target_pairs={{0,12},{1,13},{2,14},{3,15},{4,8},{5,9},{6,10},{7,11},{8,4},{9,5},... | collective-permute-start | bytes 165896 | tf_op jit(solution)/shard_map/ppermute | solution.py:221
  8.1 0.0 collective-permute-start.1
  8.1 0.8 %collective-permute-start.2 = (bf16[24,1152]{1,0:T(8,128)(2,1)S(1)}, bf16[24,1152]{1,0:T(8,128)(2,1)S(1)}, u32[]{:S(2)}, u32[]{:S(2)}) collective-permute-start(bf16[24,1152]{1,0:T(8,128)(2,1)S(1)} %get-tuple-element.28), channel_id=1, source_target_pairs={{0,4},{1,5},{2,6},{3,7},{4,0},{5,1},{6,2},{7,3},{8,12},{9,13},{10,... | collective-permute-start | bytes 165896 | tf_op jit(solution)/shard_map/ppermute | solution.py:221
  8.9 2.6 %collective-permute-done.3.refs_2_ = bf16[48,3072]{1,0:T(8,128)(2,1)S(1)} collective-permute-done((bf16[48,3072]{1,0:T(8,128)(2,1)S(1)}, bf16[48,3072]{1,0:T(8,128)(2,1)S(1)}, u32[]{:S(2)}, u32[]{:S(2)}) %collective-permute-start.3) | collective-permute-done | bytes 294944 | tf_op jit(solution)/shard_map/ppermute | solution.py:221
  11.5 1.7 %collective-permute-start.8 = (bf16[48,3072]{1,0:T(8,128)(2,1)S(1)}, bf16[48,3072]{1,0:T(8,128)(2,1)S(1)}, u32[]{:S(2)}, u32[]{:S(2)}) collective-permute-start(bf16[48,3072]{1,0:T(8,128)(2,1)S(1)} %collective-permute-done.3.refs_2_), channel_id=1, source_target_pairs={{0,16},{16,0},{1,17},{17,1},{2,18},{18,2},{3,19},{19,3},{4,20},{20... | collective-permute-start | bytes 884744 | tf_op jit(solution)/shard_map/ppermute | solution.py:224
  13.2 0.0 collective-permute-done.refs_0_
  13.2 0.0 collective-permute-done.1.refs_1_
  13.3 0.0 collective-permute-done.2.refs_2_
  13.3 1.6 %collective-permute-start.5 = (bf16[96,768]{1,0:T(8,128)(2,1)S(1)}, bf16[96,768]{1,0:T(8,128)(2,1)S(1)}, u32[]{:S(2)}, u32[]{:S(2)}) collective-permute-start(bf16[96,768]{1,0:T(8,128)(2,1)S(1)} %pad_maximum_fusion.refs_4_), channel_id=1, source_target_pairs={{0,2},{1,3},{2,0},{3,1},{4,6},{5,7},{6,4},{7,5},{8,10},{9,11},{10,... | collective-permute-start | bytes 442376 | tf_op jit(solution)/shard_map/ppermute | solution.py:221
  14.9 0.0 collective-permute-start.4
  14.9 0.5 %collective-permute-start.9 = (bf16[48,3072]{1,0:T(8,128)(2,1)S(1)}, bf16[48,3072]{1,0:T(8,128)(2,1)S(1)}, u32[]{:S(2)}, u32[]{:S(2)}) collective-permute-start(bf16[48,3072]{1,0:T(8,128)(2,1)S(1)} %collective-permute-done.3.refs_2_), channel_id=1, source_target_pairs={{0,1},{1,0},{2,3},{3,2},{4,5},{5,4},{6,7},{7,6},{8,9},{9,8},{10,11... | collective-permute-start | bytes 884744 | tf_op jit(solution)/shard_map/ppermute | solution.py:221
  15.4 0.0 copy-done
  15.4 0.0 collective-permute-start.7
  15.4 3.1 %collective-permute-done.5.refs_6_ = bf16[96,768]{1,0:T(8,128)(2,1)S(1)} collective-permute-done((bf16[96,768]{1,0:T(8,128)(2,1)S(1)}, bf16[96,768]{1,0:T(8,128)(2,1)S(1)}, u32[]{:S(2)}, u32[]{:S(2)}) %collective-permute-start.5) | collective-permute-done | bytes 147488 | tf_op jit(solution)/shard_map/ppermute | solution.py:221
  18.5 0.0 collective-permute-start.6
  18.5 1.2 %collective-permute-done.8.refs_3_ = bf16[48,3072]{1,0:T(8,128)(2,1)S(1)} collective-permute-done((bf16[48,3072]{1,0:T(8,128)(2,1)S(1)}, bf16[48,3072]{1,0:T(8,128)(2,1)S(1)}, u32[]{:S(2)}, u32[]{:S(2)}) %collective-permute-start.8) | collective-permute-done | bytes 294944 | tf_op jit(solution)/shard_map/ppermute | solution.py:224
  19.7 0.1 collective-permute-start.10
  19.8 0.0 collective-permute-done.4.refs_5_
  19.8 0.5 %collective-permute-start.14 = (bf16[48,1536]{1,0:T(8,128)(2,1)S(1)}, bf16[48,1536]{1,0:T(8,128)(2,1)S(1)}, u32[]{:S(2)}, u32[]{:S(2)}) collective-permute-start(bf16[48,1536]{1,0:T(8,128)(2,1)S(1)} %get-tuple-element.47), channel_id=1, source_target_pairs={{0,1},{1,0},{2,3},{3,2},{4,5},{5,4},{6,7},{7,6},{8,9},{9,8},{10,11... | collective-permute-start | bytes 442376 | tf_op jit(solution)/shard_map/ppermute | solution.py:221
  20.3 0.0 collective-permute-done.6.refs_7_
  20.3 1.6 %shard_map.83 = (bf16[96,384]{1,0:T(8,128)(2,1)S(1)}, bf16[96,3072]{1,0:T(8,128)(2,1)S(1)}) custom-call(bf16[24,1152]{1,0:T(8,128)(2,1)S(1)} %collective-permute-done.refs_0_, bf16[24,1152]{1,0:T(8,128)(2,1)S(1)} %collective-permute-done.1.refs_1_, bf16[24,1152]{1,0:T(8,128)(2,1)S(1)} %collective-permute-done.2.refs_2_, ...), custom_call_target="tpu_custom_call" | custom-call | flops 56623104 | bytes 589824 | tf_op jit(solution)/shard_map/pallas_call | solution.py:143
  21.9 0.0 collective-permute-done.9.refs_4_
  22.0 0.0 collective-permute-done.10.refs_5_
  22.0 0.0 collective-permute-done.7.refs_1_
  22.0 0.4 %shard_map.84 = (bf16[24,1536]{1,0:T(8,128)(2,1)S(1)}, bf16[24,1536]{1,0:T(8,128)(2,1)S(1)}, bf16[24,1536]{1,0:T(8,128)(2,1)S(1)}, f32[24,1536]{1,0:T(8,128)S(1)}) custom-call(bf16[96,384]{1,0:T(8,128)(2,1)S(1)} %get-tuple-element.42.att, bf16[96,3072]{1,0:T(8,128)(2,1)S(1)} %get-tuple-element.34.refs_0_, ...), custom_call_target="tpu_custom_call" | custom-call | flops 113246208 | bytes 1179648 | tf_op jit(solution)/shard_map/pallas_call | solution.py:188
  22.4 3.6 %collective-permute-start.11 = (bf16[24,1536]{1,0:T(8,128)(2,1)S(1)}, bf16[24,1536]{1,0:T(8,128)(2,1)S(1)}, u32[]{:S(2)}, u32[]{:S(2)}) collective-permute-start(bf16[24,1536]{1,0:T(8,128)(2,1)S(1)} %get-tuple-element.39), channel_id=1, source_target_pairs={{0,12},{1,13},{2,14},{3,15},{4,8},{5,9},{6,10},{7,11},{8,4},{9,5},... | collective-permute-start | bytes 221192 | tf_op jit(solution)/shard_map/ppermute | solution.py:221
  26.0 0.0 collective-permute-start.12
  26.0 0.9 %collective-permute-start.13 = (bf16[24,1536]{1,0:T(8,128)(2,1)S(1)}, bf16[24,1536]{1,0:T(8,128)(2,1)S(1)}, u32[]{:S(2)}, u32[]{:S(2)}) collective-permute-start(bf16[24,1536]{1,0:T(8,128)(2,1)S(1)} %get-tuple-element.41), channel_id=1, source_target_pairs={{0,4},{1,5},{2,6},{3,7},{4,0},{5,1},{6,2},{7,3},{8,12},{9,13},{10,... | collective-permute-start | bytes 221192 | tf_op jit(solution)/shard_map/ppermute | solution.py:221
  26.9 0.0 copy-start.1
  26.9 0.0 collective-permute-done.14.refs_5_
  26.9 0.4 %shard_map.85 = (bf16[24,1536]{1,0:T(8,128)(2,1)S(1)}, bf16[24,1536]{1,0:T(8,128)(2,1)S(1)}, bf16[24,1536]{1,0:T(8,128)(2,1)S(1)}, f32[24,1536]{1,0:T(8,128)S(1)}) custom-call(bf16[96,384]{1,0:T(8,128)(2,1)S(1)} %get-tuple-element.42.att, bf16[96,3072]{1,0:T(8,128)(2,1)S(1)} %get-tuple-element.34.refs_0_, ...), custom_call_target="tpu_custom_call" | custom-call | flops 113246208 | bytes 1179648 | tf_op jit(solution)/shard_map/pallas_call | solution.py:188
  27.3 3.6 %collective-permute-start.15 = (bf16[24,1536]{1,0:T(8,128)(2,1)S(1)}, bf16[24,1536]{1,0:T(8,128)(2,1)S(1)}, u32[]{:S(2)}, u32[]{:S(2)}) collective-permute-start(bf16[24,1536]{1,0:T(8,128)(2,1)S(1)} %get-tuple-element.44), channel_id=1, source_target_pairs={{0,12},{1,13},{2,14},{3,15},{4,8},{5,9},{6,10},{7,11},{8,4},{9,5},... | collective-permute-start | bytes 221192 | tf_op jit(solution)/shard_map/ppermute | solution.py:221
  30.9 0.0 collective-permute-start.16
  30.9 0.0 collective-permute-done.11
  30.9 2.2 %collective-permute-start.17 = (bf16[24,1536]{1,0:T(8,128)(2,1)S(1)}, bf16[24,1536]{1,0:T(8,128)(2,1)S(1)}, u32[]{:S(2)}, u32[]{:S(2)}) collective-permute-start(bf16[24,1536]{1,0:T(8,128)(2,1)S(1)} %get-tuple-element.46), channel_id=1, source_target_pairs={{0,4},{1,5},{2,6},{3,7},{4,0},{5,1},{6,2},{7,3},{8,12},{9,13},{10,... | collective-permute-start | bytes 221192 | tf_op jit(solution)/shard_map/ppermute | solution.py:221
  33.1 3.2 %collective-permute-done.12 = bf16[24,1536]{1,0:T(8,128)(2,1)S(1)} collective-permute-done((bf16[24,1536]{1,0:T(8,128)(2,1)S(1)}, bf16[24,1536]{1,0:T(8,128)(2,1)S(1)}, u32[]{:S(2)}, u32[]{:S(2)}) %collective-permute-start.12) | collective-permute-done | bytes 73760 | tf_op jit(solution)/shard_map/ppermute | solution.py:221
  36.3 0.0 collective-permute-done.13
  36.3 0.0 collective-permute-done.15
  36.4 2.5 %collective-permute-done.16 = bf16[24,1536]{1,0:T(8,128)(2,1)S(1)} collective-permute-done((bf16[24,1536]{1,0:T(8,128)(2,1)S(1)}, bf16[24,1536]{1,0:T(8,128)(2,1)S(1)}, u32[]{:S(2)}, u32[]{:S(2)}) %collective-permute-start.16) | collective-permute-done | bytes 73760 | tf_op jit(solution)/shard_map/ppermute | solution.py:221
  38.8 0.0 collective-permute-done.17
  38.9 0.0 copy-done.1
  38.9 0.7 %fusion = bf16[24,3072]{1,0:T(8,128)(2,1)} fusion(f32[24,1536]{1,0:T(8,128)S(1)} %convert_add_fusion, f32[24,1536]{1,0:T(8,128)S(1)} %convert_add_fusion.1, f32[3072]{0:T(1024)S(1)} %copy-done.1), kind=kLoop, calls=%fused_computation.1 | loop fusion | flops 221184 | bytes 454656 | tf_op jit(solution)/shard_map/convert_element_type | solution.py:267
  (7 shorter events, 0.1 us)
Async XLA Ops:
  0.0 15.4 %copy-start = (bf16[96,3072]{1,0:T(8,128)(2,1)S(1)}, bf16[96,3072]{1,0:T(8,128)(2,1)}, u32[]{:S(2)}) copy-start(bf16[96,3072]{1,0:T(8,128)(2,1)} %refs_8_.1) | copy-start | bytes 1769476
  1.5 10.0 %collective-permute-start.3 = (bf16[48,3072]{1,0:T(8,128)(2,1)S(1)}, bf16[48,3072]{1,0:T(8,128)(2,1)S(1)}, u32[]{:S(2)}, u32[]{:S(2)}) collective-permute-start(bf16[48,3072]{1,0:T(8,128)(2,1)S(1)} %get-tuple-element.31), channel_id=1, source_target_pairs={{0,2},{1,3},{2,0},{3,1},{4,6},{5,7},{6,4},{7,5},{8,10},{9,11},{10,... | collective-permute-start | bytes 884744 | tf_op jit(solution)/shard_map/ppermute | solution.py:221
  4.5 8.7 %collective-permute-start = (bf16[24,1152]{1,0:T(8,128)(2,1)S(1)}, bf16[24,1152]{1,0:T(8,128)(2,1)S(1)}, u32[]{:S(2)}, u32[]{:S(2)}) collective-permute-start(bf16[24,1152]{1,0:T(8,128)(2,1)S(1)} %get-tuple-element.26), channel_id=1, source_target_pairs={{0,12},{1,13},{2,14},{3,15},{4,8},{5,9},{6,10},{7,11},{8,4},{9,5},... | collective-permute-start | bytes 165896 | tf_op jit(solution)/shard_map/ppermute | solution.py:221
  8.1 5.1 %collective-permute-start.1 = (bf16[24,1152]{1,0:T(8,128)(2,1)S(1)}, bf16[24,1152]{1,0:T(8,128)(2,1)S(1)}, u32[]{:S(2)}, u32[]{:S(2)}) collective-permute-start(bf16[24,1152]{1,0:T(8,128)(2,1)S(1)} %get-tuple-element.27), channel_id=1, source_target_pairs={{0,8},{1,9},{2,10},{3,11},{4,12},{5,13},{6,14},{7,15},{8,0},{9,1},... | collective-permute-start | bytes 165896 | tf_op jit(solution)/shard_map/ppermute | solution.py:221
  8.1 5.1 %collective-permute-start.2 = (bf16[24,1152]{1,0:T(8,128)(2,1)S(1)}, bf16[24,1152]{1,0:T(8,128)(2,1)S(1)}, u32[]{:S(2)}, u32[]{:S(2)}) collective-permute-start(bf16[24,1152]{1,0:T(8,128)(2,1)S(1)} %get-tuple-element.28), channel_id=1, source_target_pairs={{0,4},{1,5},{2,6},{3,7},{4,0},{5,1},{6,2},{7,3},{8,12},{9,13},{10,... | collective-permute-start | bytes 165896 | tf_op jit(solution)/shard_map/ppermute | solution.py:221
  11.5 8.2 %collective-permute-start.8 = (bf16[48,3072]{1,0:T(8,128)(2,1)S(1)}, bf16[48,3072]{1,0:T(8,128)(2,1)S(1)}, u32[]{:S(2)}, u32[]{:S(2)}) collective-permute-start(bf16[48,3072]{1,0:T(8,128)(2,1)S(1)} %collective-permute-done.3.refs_2_), channel_id=1, source_target_pairs={{0,16},{16,0},{1,17},{17,1},{2,18},{18,2},{3,19},{19,3},{4,20},{20... | collective-permute-start | bytes 884744 | tf_op jit(solution)/shard_map/ppermute | solution.py:224
  13.3 5.2 %collective-permute-start.5 = (bf16[96,768]{1,0:T(8,128)(2,1)S(1)}, bf16[96,768]{1,0:T(8,128)(2,1)S(1)}, u32[]{:S(2)}, u32[]{:S(2)}) collective-permute-start(bf16[96,768]{1,0:T(8,128)(2,1)S(1)} %pad_maximum_fusion.refs_4_), channel_id=1, source_target_pairs={{0,2},{1,3},{2,0},{3,1},{4,6},{5,7},{6,4},{7,5},{8,10},{9,11},{10,... | collective-permute-start | bytes 442376 | tf_op jit(solution)/shard_map/ppermute | solution.py:221
  14.9 4.9 %collective-permute-start.4 = (bf16[96,768]{1,0:T(8,128)(2,1)S(1)}, bf16[96,768]{1,0:T(8,128)(2,1)S(1)}, u32[]{:S(2)}, u32[]{:S(2)}) collective-permute-start(bf16[96,768]{1,0:T(8,128)(2,1)S(1)} %pad_maximum_fusion.refs_4_), channel_id=1, source_target_pairs={{0,1},{1,0},{2,3},{3,2},{4,5},{5,4},{6,7},{7,6},{8,9},{9,8},{10,11... | collective-permute-start | bytes 442376 | tf_op jit(solution)/shard_map/ppermute | solution.py:221
  14.9 7.1 %collective-permute-start.9 = (bf16[48,3072]{1,0:T(8,128)(2,1)S(1)}, bf16[48,3072]{1,0:T(8,128)(2,1)S(1)}, u32[]{:S(2)}, u32[]{:S(2)}) collective-permute-start(bf16[48,3072]{1,0:T(8,128)(2,1)S(1)} %collective-permute-done.3.refs_2_), channel_id=1, source_target_pairs={{0,1},{1,0},{2,3},{3,2},{4,5},{5,4},{6,7},{7,6},{8,9},{9,8},{10,11... | collective-permute-start | bytes 884744 | tf_op jit(solution)/shard_map/ppermute | solution.py:221
  15.4 6.6 %collective-permute-start.7 = (bf16[96,3072]{1,0:T(8,128)(2,1)S(1)}, bf16[96,3072]{1,0:T(8,128)(2,1)S(1)}, u32[]{:S(2)}, u32[]{:S(2)}) collective-permute-start(bf16[96,3072]{1,0:T(8,128)(2,1)S(1)} %copy-done), channel_id=1, source_target_pairs={{0,1},{1,0},{2,3},{3,2},{4,5},{5,4},{6,7},{7,6},{8,9},{9,8},{10,11... | collective-permute-start | bytes 1769480 | tf_op jit(solution)/shard_map/ppermute | solution.py:221
  18.5 1.8 %collective-permute-start.6 = (bf16[96,768]{1,0:T(8,128)(2,1)S(1)}, bf16[96,768]{1,0:T(8,128)(2,1)S(1)}, u32[]{:S(2)}, u32[]{:S(2)}) collective-permute-start(bf16[96,768]{1,0:T(8,128)(2,1)S(1)} %collective-permute-done.5.refs_6_), channel_id=1, source_target_pairs={{0,1},{1,0},{2,3},{3,2},{4,5},{5,4},{6,7},{7,6},{8,9},{9,8},{10,11... | collective-permute-start | bytes 442376 | tf_op jit(solution)/shard_map/ppermute | solution.py:221
  19.7 2.2 %collective-permute-start.10 = (bf16[48,1536]{1,0:T(8,128)(2,1)S(1)}, bf16[48,1536]{1,0:T(8,128)(2,1)S(1)}, u32[]{:S(2)}, u32[]{:S(2)}) collective-permute-start(bf16[48,1536]{1,0:T(8,128)(2,1)S(1)} %get-tuple-element.48), channel_id=1, source_target_pairs={{0,1},{1,0},{2,3},{3,2},{4,5},{5,4},{6,7},{7,6},{8,9},{9,8},{10,11... | collective-permute-start | bytes 442376 | tf_op jit(solution)/shard_map/ppermute | solution.py:221
  19.8 7.1 %collective-permute-start.14 = (bf16[48,1536]{1,0:T(8,128)(2,1)S(1)}, bf16[48,1536]{1,0:T(8,128)(2,1)S(1)}, u32[]{:S(2)}, u32[]{:S(2)}) collective-permute-start(bf16[48,1536]{1,0:T(8,128)(2,1)S(1)} %get-tuple-element.47), channel_id=1, source_target_pairs={{0,1},{1,0},{2,3},{3,2},{4,5},{5,4},{6,7},{7,6},{8,9},{9,8},{10,11... | collective-permute-start | bytes 442376 | tf_op jit(solution)/shard_map/ppermute | solution.py:221
  22.4 8.5 %collective-permute-start.11 = (bf16[24,1536]{1,0:T(8,128)(2,1)S(1)}, bf16[24,1536]{1,0:T(8,128)(2,1)S(1)}, u32[]{:S(2)}, u32[]{:S(2)}) collective-permute-start(bf16[24,1536]{1,0:T(8,128)(2,1)S(1)} %get-tuple-element.39), channel_id=1, source_target_pairs={{0,12},{1,13},{2,14},{3,15},{4,8},{5,9},{6,10},{7,11},{8,4},{9,5},... | collective-permute-start | bytes 221192 | tf_op jit(solution)/shard_map/ppermute | solution.py:221
  26.0 10.3 %collective-permute-start.12 = (bf16[24,1536]{1,0:T(8,128)(2,1)S(1)}, bf16[24,1536]{1,0:T(8,128)(2,1)S(1)}, u32[]{:S(2)}, u32[]{:S(2)}) collective-permute-start(bf16[24,1536]{1,0:T(8,128)(2,1)S(1)} %get-tuple-element.40), channel_id=1, source_target_pairs={{0,8},{1,9},{2,10},{3,11},{4,12},{5,13},{6,14},{7,15},{8,0},{9,1},... | collective-permute-start | bytes 221192 | tf_op jit(solution)/shard_map/ppermute | solution.py:221
  26.0 10.3 %collective-permute-start.13 = (bf16[24,1536]{1,0:T(8,128)(2,1)S(1)}, bf16[24,1536]{1,0:T(8,128)(2,1)S(1)}, u32[]{:S(2)}, u32[]{:S(2)}) collective-permute-start(bf16[24,1536]{1,0:T(8,128)(2,1)S(1)} %get-tuple-element.41), channel_id=1, source_target_pairs={{0,4},{1,5},{2,6},{3,7},{4,0},{5,1},{6,2},{7,3},{8,12},{9,13},{10,... | collective-permute-start | bytes 221192 | tf_op jit(solution)/shard_map/ppermute | solution.py:221
  26.9 12.0 %copy-start.1 = (f32[3072]{0:T(1024)S(1)}, f32[3072]{0:T(1024)}, u32[]{:S(2)}) copy-start(f32[3072]{0:T(1024)} %param.15) | copy-start | bytes 36868
  27.3 9.0 %collective-permute-start.15 = (bf16[24,1536]{1,0:T(8,128)(2,1)S(1)}, bf16[24,1536]{1,0:T(8,128)(2,1)S(1)}, u32[]{:S(2)}, u32[]{:S(2)}) collective-permute-start(bf16[24,1536]{1,0:T(8,128)(2,1)S(1)} %get-tuple-element.44), channel_id=1, source_target_pairs={{0,12},{1,13},{2,14},{3,15},{4,8},{5,9},{6,10},{7,11},{8,4},{9,5},... | collective-permute-start | bytes 221192 | tf_op jit(solution)/shard_map/ppermute | solution.py:221
  30.9 7.9 %collective-permute-start.16 = (bf16[24,1536]{1,0:T(8,128)(2,1)S(1)}, bf16[24,1536]{1,0:T(8,128)(2,1)S(1)}, u32[]{:S(2)}, u32[]{:S(2)}) collective-permute-start(bf16[24,1536]{1,0:T(8,128)(2,1)S(1)} %get-tuple-element.45), channel_id=1, source_target_pairs={{0,8},{1,9},{2,10},{3,11},{4,12},{5,13},{6,14},{7,15},{8,0},{9,1},... | collective-permute-start | bytes 221192 | tf_op jit(solution)/shard_map/ppermute | solution.py:221
  30.9 7.9 %collective-permute-start.17 = (bf16[24,1536]{1,0:T(8,128)(2,1)S(1)}, bf16[24,1536]{1,0:T(8,128)(2,1)S(1)}, u32[]{:S(2)}, u32[]{:S(2)}) collective-permute-start(bf16[24,1536]{1,0:T(8,128)(2,1)S(1)} %get-tuple-element.46), channel_id=1, source_target_pairs={{0,4},{1,5},{2,6},{3,7},{4,0},{5,1},{6,2},{7,3},{8,12},{9,13},{10,... | collective-permute-start | bytes 221192 | tf_op jit(solution)/shard_map/ppermute | solution.py:221

commit v15 on v13

--- a/solution.py
+++ b/solution.py
@@ -14,11 +14,10 @@
 
 
 def prepare_kernel(groups, members, *refs):
-    sources, w_ref = refs[:6], refs[6]
-    outs = refs[7:]
+    sources = refs[:6]
+    outs = refs[6:]
     qout, kvout, fulls = outs[0], outs[1], outs[1 : 1 + groups]
-    wout = outs[1 + groups]
-    query, key_new, value_new, kst, vst, est, packed, sems = outs[2 + groups :]
+    query, key_new, value_new, kst, vst, est, packed, sems = outs[1 + groups :]
     rows, width = query.shape
     me = lax.axis_index("patch")
     first = pl.multiple_of((me // 2) * (2 * rows), 2 * rows)
@@ -30,8 +29,6 @@
     }
     for i in order:
         copies[i].start()
-    move = pltpu.make_async_copy(w_ref, wout, sems.at[6])
-    move.start()
     heads = est.shape[0] // 2
     dim = width // heads
     share = width // groups
@@ -71,45 +68,48 @@
         else:
             fulls[k][:, :share] = wanted
             fulls[k][:, share:] = packed[target]
-    move.wait()
-
-
-def prepare(groups, members, query, key_new, value_new, key_stale, value_stale, powers, w_out):
+
+
+def prepare(groups, members, query, key_new, value_new, key_stale, value_stale, powers):
     rows, width = query.shape
     share = width // groups
-    depth, model = w_out.shape
     outs = (
         [((rows, share), jnp.bfloat16), ((rows, 2 * share), jnp.bfloat16)]
         + [((rows, 3 * share), jnp.bfloat16)] * (groups - 1)
-        + [((depth, model), jnp.bfloat16)]
     )
-    sources = (query, key_new, value_new, key_stale, value_stale, powers, w_out)
+    sources = (query, key_new, value_new, key_stale, value_stale, powers)
     result = pl.pallas_call(
         functools.partial(prepare_kernel, groups, members),
         out_shape=[jax.ShapeDtypeStruct(*o) for o in outs],
-        in_specs=[HBM] * 7,
+        in_specs=[HBM] * 6,
         out_specs=[VMEM] * len(outs),
         scratch_shapes=[pltpu.VMEM((rows, width), jnp.bfloat16)] * 3
         + [pltpu.VMEM((2 * rows, width), jnp.bfloat16)] * 2
         + [
             pltpu.VMEM(powers.shape, jnp.int32),
             pltpu.VMEM((groups, rows, 2 * share), jnp.bfloat16),
-            pltpu.SemaphoreType.DMA((7,)),
+            pltpu.SemaphoreType.DMA((6,)),
         ],
         compiler_params=pltpu.CompilerParams(vmem_limit_bytes=24 * 1024 * 1024),
         cost_estimate=pl.CostEstimate(
-            flops=10 * rows * width, bytes_accessed=14 * rows * width + 4 * depth * model, transcendentals=0
+            flops=10 * rows * width, bytes_accessed=14 * rows * width, transcendentals=0
         ),
     )(*(pltpu.with_memory_space_constraint(x, pltpu.HBM) for x in sources))
-    return result[0], result[1 : 1 + groups], result[-1]
-
-
-def share_kernel(w_ref, out_ref, sem):
-    size = out_ref.shape[0]
-    top = pl.multiple_of((lax.axis_index("groups") & 1) * size, size)
-    copy = pltpu.make_async_copy(w_ref.at[pl.ds(top, size)], out_ref, sem)
-    copy.start()
-    copy.wait()
+    return result[0], result[1:]
+
+
+def share_kernel(w_ref, out_ref, sems):
+    size, model = out_ref.shape
+    top = (lax.axis_index("groups") & 1) * size
+    copies = []
+    for i in range(sems.shape[0]):
+        cols = pl.ds(i * (model // sems.shape[0]), model // sems.shape[0])
+        source = w_ref.at[pl.ds(pl.multiple_of(top, size), size), cols]
+        copies.append(pltpu.make_async_copy(source, out_ref.at[:, cols], sems.at[i]))
+    for c in copies:
+        c.start()
+    for c in copies:
+        c.wait()
 
 
 def share_rows(w_out):
@@ -119,7 +119,7 @@
         out_shape=jax.ShapeDtypeStruct((depth // 2, model), w_out.dtype),
         in_specs=[HBM],
         out_specs=VMEM,
-        scratch_shapes=[pltpu.SemaphoreType.DMA],
+        scratch_shapes=[pltpu.SemaphoreType.DMA((4,))],
         compiler_params=pltpu.CompilerParams(vmem_limit_bytes=24 * 1024 * 1024),
         cost_estimate=pl.CostEstimate(flops=0, bytes_accessed=2 * depth * model, transcendentals=0),
     )(pltpu.with_memory_space_constraint(w_out, pltpu.HBM))
@@ -246,9 +246,8 @@
     if shared:
         w_part = share_rows(w_out)
         y_part = send(w_part, 0, far)
-    own_query, fresh, w_own = prepare(
-        groups, members, query, key_new, value_new, key_stale, value_stale, exponents.T, w_out
-    )
+    own_query, fresh = prepare(groups, members, query, key_new, value_new, key_stale, value_stale, exponents.T)
+    w_own = w_out
     order = range(groups - 1, 0, -1)
     arrived = [send(fresh[k], k, 0) for k in order]
     both = jnp.concatenate([x[:, share:] for x in arrived] + [fresh[0]], axis=0)

time: 38.8 us -> 38.9 us (level)
  no operation moved by 1% of the time
where the time goes in v15:
time: 38.9 us; the launch traced here: 38.7 us
  starting transfers between devices  19.8 us (51%)
  waiting for transfers between devices  13.7 us (35%)
  Pallas kernels  4.28 us (11%)
  other arithmetic  0.78 us (2%)
    ppermute x17, starting transfers between devices, send(): lax.ppermute(x, 'patch', [(p, (p // members ^ k) * members + p % members...  18.1 us
    ppermute x17, waiting for transfers between devices, send(): lax.ppermute(x, 'patch', [(p, (p // members ^ k) * members + p % members...  13.7 us
    ppermute x1, starting transfers between devices, swap(): return lax.ppermute(x, 'groups', [(g, g ^ 1) for g in range(parts)])  1.71 us
    pallas_call x1, Pallas kernels, prepare(): pl.pallas_call(functools.partial(prepare_kernel, groups, members), out_sh...  1.45 us
    pallas_call x1, Pallas kernels, share_rows(): pl.pallas_call(share_kernel, out_shape=jax.ShapeDtypeStruct((depth // 2,...  1.03 us
    pallas_call x1, Pallas kernels, attend(): pl.pallas_call(functools.partial(attend_kernel, groups, dim), out_shape=j...  0.93 us
    pallas_call x2, Pallas kernels, project(): pl.pallas_call(functools.partial(project_kernel, groups, members, places)...  0.88 us
  transfers between devices with their start and end apart: 18, of which 7 were waited for; matrix products, arithmetic and copies ran while one was open for 0% of the time, Pallas kernels for 8%

profile of v15, /device:TPU:0, one launch (start us, length us, event | category | flops | bytes accessed | tf_op | source)
XLA Modules:
  0.0 38.7 jit_solution(8939074966764571260)
XLA Ops:
  0.0 1.0 %shard_map.83 = bf16[48,3072]{1,0:T(8,128)(2,1)S(1)} custom-call(bf16[96,3072]{1,0:T(8,128)(2,1)} %refs_0_.5), custom_call_target="tpu_custom_call" | custom-call | bytes 589824 | tf_op jit(solution)/shard_map/pallas_call | solution.py:117
  1.0 3.0 %collective-permute-start.3 = (bf16[48,3072]{1,0:T(8,128)(2,1)S(1)}, bf16[48,3072]{1,0:T(8,128)(2,1)S(1)}, u32[]{:S(2)}, u32[]{:S(2)}) collective-permute-start(bf16[48,3072]{1,0:T(8,128)(2,1)S(1)} %shard_map.83), channel_id=1, source_target_pairs={{0,2},{1,3},{2,0},{3,1},{4,6},{5,7},{6,4},{7,5},{8,10},{9,11},{10,... | collective-permute-start | bytes 884744 | tf_op jit(solution)/shard_map/ppermute | solution.py:234
  4.1 0.0 copy-start
  4.1 1.5 %shard_map.82 = (bf16[24,384]{1,0:T(8,128)(2,1)S(1)}, bf16[24,768]{1,0:T(8,128)(2,1)S(1)}, bf16[24,1152]{1,0:T(8,128)(2,1)S(1)}, bf16[24,1152]{1,0:T(8,128)(2,1)S(1)}, bf16[24,1152]{1,0:T(8,128)(2,1)S(1)}) custom-call(bf16[24,1536]{1,0:T(8,128)(2,1)} %refs_0_.3, bf16[24,1536]{1,0:T(8,128)(2,1)} %refs_1_.1, bf16[24,1536]{1,0:T(8,128)(2,1)} %refs_2_.1, ...), custom_call_target="tpu_custom_call" | custom-call | flops 368640 | bytes 516096 | tf_op jit(solution)/shard_map/pallas_call | solution.py:81
  5.5 3.7 %collective-permute-start = (bf16[24,1152]{1,0:T(8,128)(2,1)S(1)}, bf16[24,1152]{1,0:T(8,128)(2,1)S(1)}, u32[]{:S(2)}, u32[]{:S(2)}) collective-permute-start(bf16[24,1152]{1,0:T(8,128)(2,1)S(1)} %get-tuple-element.23), channel_id=1, source_target_pairs={{0,12},{1,13},{2,14},{3,15},{4,8},{5,9},{6,10},{7,11},{8,4},{9,5},... | collective-permute-start | bytes 165896 | tf_op jit(solution)/shard_map/ppermute | solution.py:234
  9.2 0.0 collective-permute-start.1
  9.2 0.8 %collective-permute-start.2 = (bf16[24,1152]{1,0:T(8,128)(2,1)S(1)}, bf16[24,1152]{1,0:T(8,128)(2,1)S(1)}, u32[]{:S(2)}, u32[]{:S(2)}) collective-permute-start(bf16[24,1152]{1,0:T(8,128)(2,1)S(1)} %get-tuple-element.25), channel_id=1, source_target_pairs={{0,4},{1,5},{2,6},{3,7},{4,0},{5,1},{6,2},{7,3},{8,12},{9,13},{10,... | collective-permute-start | bytes 165896 | tf_op jit(solution)/shard_map/ppermute | solution.py:234
  10.0 1.1 %collective-permute-done.3.refs_2_ = bf16[48,3072]{1,0:T(8,128)(2,1)S(1)} collective-permute-done((bf16[48,3072]{1,0:T(8,128)(2,1)S(1)}, bf16[48,3072]{1,0:T(8,128)(2,1)S(1)}, u32[]{:S(2)}, u32[]{:S(2)}) %collective-permute-start.3) | collective-permute-done | bytes 294944 | tf_op jit(solution)/shard_map/ppermute | solution.py:234
  11.1 1.7 %collective-permute-start.8 = (bf16[48,3072]{1,0:T(8,128)(2,1)S(1)}, bf16[48,3072]{1,0:T(8,128)(2,1)S(1)}, u32[]{:S(2)}, u32[]{:S(2)}) collective-permute-start(bf16[48,3072]{1,0:T(8,128)(2,1)S(1)} %collective-permute-done.3.refs_2_), channel_id=1, source_target_pairs={{0,16},{16,0},{1,17},{17,1},{2,18},{18,2},{3,19},{19,3},{4,20},{20... | collective-permute-start | bytes 884744 | tf_op jit(solution)/shard_map/ppermute | solution.py:237
  12.8 0.0 collective-permute-done.refs_0_
  12.8 1.5 %collective-permute-done.1.refs_1_ = bf16[24,1152]{1,0:T(8,128)(2,1)S(1)} collective-permute-done((bf16[24,1152]{1,0:T(8,128)(2,1)S(1)}, bf16[24,1152]{1,0:T(8,128)(2,1)S(1)}, u32[]{:S(2)}, u32[]{:S(2)}) %collective-permute-start.1) | collective-permute-done | bytes 55328 | tf_op jit(solution)/shard_map/ppermute | solution.py:234
  14.3 0.0 collective-permute-done.2.refs_2_
  14.3 0.6 %collective-permute-start.5 = (bf16[96,768]{1,0:T(8,128)(2,1)S(1)}, bf16[96,768]{1,0:T(8,128)(2,1)S(1)}, u32[]{:S(2)}, u32[]{:S(2)}) collective-permute-start(bf16[96,768]{1,0:T(8,128)(2,1)S(1)} %pad_maximum_fusion.refs_4_), channel_id=1, source_target_pairs={{0,2},{1,3},{2,0},{3,1},{4,6},{5,7},{6,4},{7,5},{8,10},{9,11},{10,... | collective-permute-start | bytes 442376 | tf_op jit(solution)/shard_map/ppermute | solution.py:234
  14.9 0.0 collective-permute-start.4
  14.9 0.5 %collective-permute-start.9 = (bf16[48,3072]{1,0:T(8,128)(2,1)S(1)}, bf16[48,3072]{1,0:T(8,128)(2,1)S(1)}, u32[]{:S(2)}, u32[]{:S(2)}) collective-permute-start(bf16[48,3072]{1,0:T(8,128)(2,1)S(1)} %collective-permute-done.3.refs_2_), channel_id=1, source_target_pairs={{0,1},{1,0},{2,3},{3,2},{4,5},{5,4},{6,7},{7,6},{8,9},{9,8},{10,11... | collective-permute-start | bytes 884744 | tf_op jit(solution)/shard_map/ppermute | solution.py:234
  15.4 0.0 copy-done
  15.4 0.0 collective-permute-start.7
  15.4 4.1 %collective-permute-done.5.refs_6_ = bf16[96,768]{1,0:T(8,128)(2,1)S(1)} collective-permute-done((bf16[96,768]{1,0:T(8,128)(2,1)S(1)}, bf16[96,768]{1,0:T(8,128)(2,1)S(1)}, u32[]{:S(2)}, u32[]{:S(2)}) %collective-permute-start.5) | collective-permute-done | bytes 147488 | tf_op jit(solution)/shard_map/ppermute | solution.py:234
  19.5 0.0 collective-permute-start.6
  19.5 0.0 collective-permute-done.8.refs_3_
  19.5 0.6 %collective-permute-start.10 = (bf16[48,1536]{1,0:T(8,128)(2,1)S(1)}, bf16[48,1536]{1,0:T(8,128)(2,1)S(1)}, u32[]{:S(2)}, u32[]{:S(2)}) collective-permute-start(bf16[48,1536]{1,0:T(8,128)(2,1)S(1)} %get-tuple-element.42), channel_id=1, source_target_pairs={{0,1},{1,0},{2,3},{3,2},{4,5},{5,4},{6,7},{7,6},{8,9},{9,8},{10,11... | collective-permute-start | bytes 442376 | tf_op jit(solution)/shard_map/ppermute | solution.py:234
  20.1 0.0 collective-permute-done.4.refs_5_
  20.1 0.1 collective-permute-start.14
  20.2 0.7 %collective-permute-done.6.refs_7_ = bf16[96,768]{1,0:T(8,128)(2,1)S(1)} collective-permute-done((bf16[96,768]{1,0:T(8,128)(2,1)S(1)}, bf16[96,768]{1,0:T(8,128)(2,1)S(1)}, u32[]{:S(2)}, u32[]{:S(2)}) %collective-permute-start.6) | collective-permute-done | bytes 147488 | tf_op jit(solution)/shard_map/ppermute | solution.py:234
  20.9 0.9 %shard_map.84.att = bf16[96,384]{1,0:T(8,128)(2,1)S(1)} custom-call(bf16[24,1152]{1,0:T(8,128)(2,1)S(1)} %collective-permute-done.refs_0_, bf16[24,1152]{1,0:T(8,128)(2,1)S(1)} %collective-permute-done.1.refs_1_, bf16[24,1152]{1,0:T(8,128)(2,1)S(1)} %collective-permute-done.2.refs_2_, bf16[24,384]{1,0:T(8,128)(2,1)S(1)} %get-tuple-element.26.refs_3_, ...), custom_call_target="tpu_custom_call" | custom-call | flops 56623104 | bytes 589824 | tf_op jit(solution)/shard_map/pallas_call | solution.py:159
  21.8 0.0 collective-permute-done.9.refs_4_
  21.8 0.0 collective-permute-done.10.refs_5_
  21.8 0.0 collective-permute-done.7.refs_1_
  21.8 0.4 %shard_map.85 = (bf16[24,1536]{1,0:T(8,128)(2,1)S(1)}, bf16[24,1536]{1,0:T(8,128)(2,1)S(1)}, bf16[24,1536]{1,0:T(8,128)(2,1)S(1)}, f32[24,1536]{1,0:T(8,128)S(1)}) custom-call(bf16[96,384]{1,0:T(8,128)(2,1)S(1)} %shard_map.84.att, bf16[96,3072]{1,0:T(8,128)(2,1)S(1)} %copy-done, bf16[96,3072]{1,0:T(8,128)(2,1)S(1)} %collective-permute-done.7.refs_1_, ...), custom_call_target="tpu_custom_call" | custom-call | flops 113246208 | bytes 1179648 | tf_op jit(solution)/shard_map/pallas_call | solution.py:201
  22.3 2.6 %collective-permute-start.11 = (bf16[24,1536]{1,0:T(8,128)(2,1)S(1)}, bf16[24,1536]{1,0:T(8,128)(2,1)S(1)}, u32[]{:S(2)}, u32[]{:S(2)}) collective-permute-start(bf16[24,1536]{1,0:T(8,128)(2,1)S(1)} %get-tuple-element.33), channel_id=1, source_target_pairs={{0,12},{1,13},{2,14},{3,15},{4,8},{5,9},{6,10},{7,11},{8,4},{9,5},... | collective-permute-start | bytes 221192 | tf_op jit(solution)/shard_map/ppermute | solution.py:234
  24.9 0.0 collective-permute-start.12
  24.9 1.9 %collective-permute-start.13 = (bf16[24,1536]{1,0:T(8,128)(2,1)S(1)}, bf16[24,1536]{1,0:T(8,128)(2,1)S(1)}, u32[]{:S(2)}, u32[]{:S(2)}) collective-permute-start(bf16[24,1536]{1,0:T(8,128)(2,1)S(1)} %get-tuple-element.35), channel_id=1, source_target_pairs={{0,4},{1,5},{2,6},{3,7},{4,0},{5,1},{6,2},{7,3},{8,12},{9,13},{10,... | collective-permute-start | bytes 221192 | tf_op jit(solution)/shard_map/ppermute | solution.py:234
  26.7 0.0 copy-start.1
  26.7 0.0 collective-permute-done.14.refs_5_
  26.7 0.4 %shard_map.86 = (bf16[24,1536]{1,0:T(8,128)(2,1)S(1)}, bf16[24,1536]{1,0:T(8,128)(2,1)S(1)}, bf16[24,1536]{1,0:T(8,128)(2,1)S(1)}, f32[24,1536]{1,0:T(8,128)S(1)}) custom-call(bf16[96,384]{1,0:T(8,128)(2,1)S(1)} %shard_map.84.att, bf16[96,3072]{1,0:T(8,128)(2,1)S(1)} %copy-done, bf16[96,3072]{1,0:T(8,128)(2,1)S(1)} %collective-permute-done.7.refs_1_, ...), custom_call_target="tpu_custom_call" | custom-call | flops 113246208 | bytes 1179648 | tf_op jit(solution)/shard_map/pallas_call | solution.py:201
  27.2 2.6 %collective-permute-start.15 = (bf16[24,1536]{1,0:T(8,128)(2,1)S(1)}, bf16[24,1536]{1,0:T(8,128)(2,1)S(1)}, u32[]{:S(2)}, u32[]{:S(2)}) collective-permute-start(bf16[24,1536]{1,0:T(8,128)(2,1)S(1)} %get-tuple-element.38), channel_id=1, source_target_pairs={{0,12},{1,13},{2,14},{3,15},{4,8},{5,9},{6,10},{7,11},{8,4},{9,5},... | collective-permute-start | bytes 221192 | tf_op jit(solution)/shard_map/ppermute | solution.py:234
  29.8 0.0 collective-permute-start.16
  29.8 0.0 collective-permute-done.11
  29.8 1.9 %collective-permute-start.17 = (bf16[24,1536]{1,0:T(8,128)(2,1)S(1)}, bf16[24,1536]{1,0:T(8,128)(2,1)S(1)}, u32[]{:S(2)}, u32[]{:S(2)}) collective-permute-start(bf16[24,1536]{1,0:T(8,128)(2,1)S(1)} %get-tuple-element.40), channel_id=1, source_target_pairs={{0,4},{1,5},{2,6},{3,7},{4,0},{5,1},{6,2},{7,3},{8,12},{9,13},{10,... | collective-permute-start | bytes 221192 | tf_op jit(solution)/shard_map/ppermute | solution.py:234
  31.6 2.3 %collective-permute-done.12 = bf16[24,1536]{1,0:T(8,128)(2,1)S(1)} collective-permute-done((bf16[24,1536]{1,0:T(8,128)(2,1)S(1)}, bf16[24,1536]{1,0:T(8,128)(2,1)S(1)}, u32[]{:S(2)}, u32[]{:S(2)}) %collective-permute-start.12) | collective-permute-done | bytes 73760 | tf_op jit(solution)/shard_map/ppermute | solution.py:234
  33.9 0.0 collective-permute-done.13
  34.0 0.3 collective-permute-done.15
  34.2 3.7 %collective-permute-done.16 = bf16[24,1536]{1,0:T(8,128)(2,1)S(1)} collective-permute-done((bf16[24,1536]{1,0:T(8,128)(2,1)S(1)}, bf16[24,1536]{1,0:T(8,128)(2,1)S(1)}, u32[]{:S(2)}, u32[]{:S(2)}) %collective-permute-start.16) | collective-permute-done | bytes 73760 | tf_op jit(solution)/shard_map/ppermute | solution.py:234
  38.0 0.0 collective-permute-done.17
  38.0 0.0 copy-done.1
  38.0 0.7 %fusion = bf16[24,3072]{1,0:T(8,128)(2,1)} fusion(f32[24,1536]{1,0:T(8,128)S(1)} %convert_add_fusion, f32[24,1536]{1,0:T(8,128)S(1)} %convert_add_fusion.1, f32[3072]{0:T(1024)S(1)} %copy-done.1), kind=kLoop, calls=%fused_computation.1 | loop fusion | flops 221184 | bytes 454656 | tf_op jit(solution)/shard_map/convert_element_type | solution.py:281
  (7 shorter events, 0.1 us)
Async XLA Ops:
  1.0 10.0 %collective-permute-start.3 = (bf16[48,3072]{1,0:T(8,128)(2,1)S(1)}, bf16[48,3072]{1,0:T(8,128)(2,1)S(1)}, u32[]{:S(2)}, u32[]{:S(2)}) collective-permute-start(bf16[48,3072]{1,0:T(8,128)(2,1)S(1)} %shard_map.83), channel_id=1, source_target_pairs={{0,2},{1,3},{2,0},{3,1},{4,6},{5,7},{6,4},{7,5},{8,10},{9,11},{10,... | collective-permute-start | bytes 884744 | tf_op jit(solution)/shard_map/ppermute | solution.py:234
  4.1 11.3 %copy-start = (bf16[96,3072]{1,0:T(8,128)(2,1)S(1)}, bf16[96,3072]{1,0:T(8,128)(2,1)}, u32[]{:S(2)}) copy-start(bf16[96,3072]{1,0:T(8,128)(2,1)} %refs_0_.5) | copy-start | bytes 1769476
  5.5 7.3 %collective-permute-start = (bf16[24,1152]{1,0:T(8,128)(2,1)S(1)}, bf16[24,1152]{1,0:T(8,128)(2,1)S(1)}, u32[]{:S(2)}, u32[]{:S(2)}) collective-permute-start(bf16[24,1152]{1,0:T(8,128)(2,1)S(1)} %get-tuple-element.23), channel_id=1, source_target_pairs={{0,12},{1,13},{2,14},{3,15},{4,8},{5,9},{6,10},{7,11},{8,4},{9,5},... | collective-permute-start | bytes 165896 | tf_op jit(solution)/shard_map/ppermute | solution.py:234
  9.2 5.1 %collective-permute-start.1 = (bf16[24,1152]{1,0:T(8,128)(2,1)S(1)}, bf16[24,1152]{1,0:T(8,128)(2,1)S(1)}, u32[]{:S(2)}, u32[]{:S(2)}) collective-permute-start(bf16[24,1152]{1,0:T(8,128)(2,1)S(1)} %get-tuple-element.24), channel_id=1, source_target_pairs={{0,8},{1,9},{2,10},{3,11},{4,12},{5,13},{6,14},{7,15},{8,0},{9,1},... | collective-permute-start | bytes 165896 | tf_op jit(solution)/shard_map/ppermute | solution.py:234
  9.2 5.1 %collective-permute-start.2 = (bf16[24,1152]{1,0:T(8,128)(2,1)S(1)}, bf16[24,1152]{1,0:T(8,128)(2,1)S(1)}, u32[]{:S(2)}, u32[]{:S(2)}) collective-permute-start(bf16[24,1152]{1,0:T(8,128)(2,1)S(1)} %get-tuple-element.25), channel_id=1, source_target_pairs={{0,4},{1,5},{2,6},{3,7},{4,0},{5,1},{6,2},{7,3},{8,12},{9,13},{10,... | collective-permute-start | bytes 165896 | tf_op jit(solution)/shard_map/ppermute | solution.py:234
  11.1 8.4 %collective-permute-start.8 = (bf16[48,3072]{1,0:T(8,128)(2,1)S(1)}, bf16[48,3072]{1,0:T(8,128)(2,1)S(1)}, u32[]{:S(2)}, u32[]{:S(2)}) collective-permute-start(bf16[48,3072]{1,0:T(8,128)(2,1)S(1)} %collective-permute-done.3.refs_2_), channel_id=1, source_target_pairs={{0,16},{16,0},{1,17},{17,1},{2,18},{18,2},{3,19},{19,3},{4,20},{20... | collective-permute-start | bytes 884744 | tf_op jit(solution)/shard_map/ppermute | solution.py:237
  14.3 5.2 %collective-permute-start.5 = (bf16[96,768]{1,0:T(8,128)(2,1)S(1)}, bf16[96,768]{1,0:T(8,128)(2,1)S(1)}, u32[]{:S(2)}, u32[]{:S(2)}) collective-permute-start(bf16[96,768]{1,0:T(8,128)(2,1)S(1)} %pad_maximum_fusion.refs_4_), channel_id=1, source_target_pairs={{0,2},{1,3},{2,0},{3,1},{4,6},{5,7},{6,4},{7,5},{8,10},{9,11},{10,... | collective-permute-start | bytes 442376 | tf_op jit(solution)/shard_map/ppermute | solution.py:234
  14.9 5.2 %collective-permute-start.4 = (bf16[96,768]{1,0:T(8,128)(2,1)S(1)}, bf16[96,768]{1,0:T(8,128)(2,1)S(1)}, u32[]{:S(2)}, u32[]{:S(2)}) collective-permute-start(bf16[96,768]{1,0:T(8,128)(2,1)S(1)} %pad_maximum_fusion.refs_4_), channel_id=1, source_target_pairs={{0,1},{1,0},{2,3},{3,2},{4,5},{5,4},{6,7},{7,6},{8,9},{9,8},{10,11... | collective-permute-start | bytes 442376 | tf_op jit(solution)/shard_map/ppermute | solution.py:234
  14.9 6.9 %collective-permute-start.9 = (bf16[48,3072]{1,0:T(8,128)(2,1)S(1)}, bf16[48,3072]{1,0:T(8,128)(2,1)S(1)}, u32[]{:S(2)}, u32[]{:S(2)}) collective-permute-start(bf16[48,3072]{1,0:T(8,128)(2,1)S(1)} %collective-permute-done.3.refs_2_), channel_id=1, source_target_pairs={{0,1},{1,0},{2,3},{3,2},{4,5},{5,4},{6,7},{7,6},{8,9},{9,8},{10,11... | collective-permute-start | bytes 884744 | tf_op jit(solution)/shard_map/ppermute | solution.py:234
  15.4 6.4 %collective-permute-start.7 = (bf16[96,3072]{1,0:T(8,128)(2,1)S(1)}, bf16[96,3072]{1,0:T(8,128)(2,1)S(1)}, u32[]{:S(2)}, u32[]{:S(2)}) collective-permute-start(bf16[96,3072]{1,0:T(8,128)(2,1)S(1)} %copy-done), channel_id=1, source_target_pairs={{0,1},{1,0},{2,3},{3,2},{4,5},{5,4},{6,7},{7,6},{8,9},{9,8},{10,11... | collective-permute-start | bytes 1769480 | tf_op jit(solution)/shard_map/ppermute | solution.py:234
  19.5 1.4 %collective-permute-start.6 = (bf16[96,768]{1,0:T(8,128)(2,1)S(1)}, bf16[96,768]{1,0:T(8,128)(2,1)S(1)}, u32[]{:S(2)}, u32[]{:S(2)}) collective-permute-start(bf16[96,768]{1,0:T(8,128)(2,1)S(1)} %collective-permute-done.5.refs_6_), channel_id=1, source_target_pairs={{0,1},{1,0},{2,3},{3,2},{4,5},{5,4},{6,7},{7,6},{8,9},{9,8},{10,11... | collective-permute-start | bytes 442376 | tf_op jit(solution)/shard_map/ppermute | solution.py:234
  19.5 2.3 %collective-permute-start.10 = (bf16[48,1536]{1,0:T(8,128)(2,1)S(1)}, bf16[48,1536]{1,0:T(8,128)(2,1)S(1)}, u32[]{:S(2)}, u32[]{:S(2)}) collective-permute-start(bf16[48,1536]{1,0:T(8,128)(2,1)S(1)} %get-tuple-element.42), channel_id=1, source_target_pairs={{0,1},{1,0},{2,3},{3,2},{4,5},{5,4},{6,7},{7,6},{8,9},{9,8},{10,11... | collective-permute-start | bytes 442376 | tf_op jit(solution)/shard_map/ppermute | solution.py:234
  20.1 6.6 %collective-permute-start.14 = (bf16[48,1536]{1,0:T(8,128)(2,1)S(1)}, bf16[48,1536]{1,0:T(8,128)(2,1)S(1)}, u32[]{:S(2)}, u32[]{:S(2)}) collective-permute-start(bf16[48,1536]{1,0:T(8,128)(2,1)S(1)} %get-tuple-element.41), channel_id=1, source_target_pairs={{0,1},{1,0},{2,3},{3,2},{4,5},{5,4},{6,7},{7,6},{8,9},{9,8},{10,11... | collective-permute-start | bytes 442376 | tf_op jit(solution)/shard_map/ppermute | solution.py:234
  22.3 7.5 %collective-permute-start.11 = (bf16[24,1536]{1,0:T(8,128)(2,1)S(1)}, bf16[24,1536]{1,0:T(8,128)(2,1)S(1)}, u32[]{:S(2)}, u32[]{:S(2)}) collective-permute-start(bf16[24,1536]{1,0:T(8,128)(2,1)S(1)} %get-tuple-element.33), channel_id=1, source_target_pairs={{0,12},{1,13},{2,14},{3,15},{4,8},{5,9},{6,10},{7,11},{8,4},{9,5},... | collective-permute-start | bytes 221192 | tf_op jit(solution)/shard_map/ppermute | solution.py:234
  24.9 9.1 %collective-permute-start.12 = (bf16[24,1536]{1,0:T(8,128)(2,1)S(1)}, bf16[24,1536]{1,0:T(8,128)(2,1)S(1)}, u32[]{:S(2)}, u32[]{:S(2)}) collective-permute-start(bf16[24,1536]{1,0:T(8,128)(2,1)S(1)} %get-tuple-element.34), channel_id=1, source_target_pairs={{0,8},{1,9},{2,10},{3,11},{4,12},{5,13},{6,14},{7,15},{8,0},{9,1},... | collective-permute-start | bytes 221192 | tf_op jit(solution)/shard_map/ppermute | solution.py:234
  24.9 9.1 %collective-permute-start.13 = (bf16[24,1536]{1,0:T(8,128)(2,1)S(1)}, bf16[24,1536]{1,0:T(8,128)(2,1)S(1)}, u32[]{:S(2)}, u32[]{:S(2)}) collective-permute-start(bf16[24,1536]{1,0:T(8,128)(2,1)S(1)} %get-tuple-element.35), channel_id=1, source_target_pairs={{0,4},{1,5},{2,6},{3,7},{4,0},{5,1},{6,2},{7,3},{8,12},{9,13},{10,... | collective-permute-start | bytes 221192 | tf_op jit(solution)/shard_map/ppermute | solution.py:234
  26.7 11.3 %copy-start.1 = (f32[3072]{0:T(1024)S(1)}, f32[3072]{0:T(1024)}, u32[]{:S(2)}) copy-start(f32[3072]{0:T(1024)} %param.15) | copy-start | bytes 36868
  27.2 7.1 %collective-permute-start.15 = (bf16[24,1536]{1,0:T(8,128)(2,1)S(1)}, bf16[24,1536]{1,0:T(8,128)(2,1)S(1)}, u32[]{:S(2)}, u32[]{:S(2)}) collective-permute-start(bf16[24,1536]{1,0:T(8,128)(2,1)S(1)} %get-tuple-element.38), channel_id=1, source_target_pairs={{0,12},{1,13},{2,14},{3,15},{4,8},{5,9},{6,10},{7,11},{8,4},{9,5},... | collective-permute-start | bytes 221192 | tf_op jit(solution)/shard_map/ppermute | solution.py:234
  29.8 8.2 %collective-permute-start.16 = (bf16[24,1536]{1,0:T(8,128)(2,1)S(1)}, bf16[24,1536]{1,0:T(8,128)(2,1)S(1)}, u32[]{:S(2)}, u32[]{:S(2)}) collective-permute-start(bf16[24,1536]{1,0:T(8,128)(2,1)S(1)} %get-tuple-element.39), channel_id=1, source_target_pairs={{0,8},{1,9},{2,10},{3,11},{4,12},{5,13},{6,14},{7,15},{8,0},{9,1},... | collective-permute-start | bytes 221192 | tf_op jit(solution)/shard_map/ppermute | solution.py:234
  29.8 8.2 %collective-permute-start.17 = (bf16[24,1536]{1,0:T(8,128)(2,1)S(1)}, bf16[24,1536]{1,0:T(8,128)(2,1)S(1)}, u32[]{:S(2)}, u32[]{:S(2)}) collective-permute-start(bf16[24,1536]{1,0:T(8,128)(2,1)S(1)} %get-tuple-element.40), channel_id=1, source_target_pairs={{0,4},{1,5},{2,6},{3,7},{4,0},{5,1},{6,2},{7,3},{8,12},{9,13},{10,... | collective-permute-start | bytes 221192 | tf_op jit(solution)/shard_map/ppermute | solution.py:234

commit v16 on v15

--- a/solution.py
+++ b/solution.py
@@ -153,7 +153,8 @@
 
 
 def attend(groups, dim, queries, kvs):
-    rows, share = queries[-1].shape
+    rows = queries[0].shape[0]
+    share = min(q.shape[1] for q in queries)
     block = kvs[0].shape[0]
     pieces = len(kvs)
     return pl.pallas_call(
@@ -171,11 +172,11 @@
     )(*queries, *kvs)
 
 
-def project_kernel(groups, members, places, att, *refs):
+def project_kernel(members, places, att, *refs):
     ws = refs[: len(places)]
-    outs = refs[len(places) : len(places) + groups]
+    outs = refs[len(places) : -1]
     wide = refs[-1]
-    rows, width = outs[0].shape
+    width = outs[0].shape[1]
     q = lax.axis_index("patch") % members
     side = lax.axis_index("groups") & 1
     for piece, (j, flip, left) in zip(ws, places):
@@ -191,23 +192,23 @@
     for t in range(width // tile):
         cols = slice(t * tile, (t + 1) * tile)
         part = jnp.dot(att[...], wide[:, cols], preferred_element_type=jnp.float32)
-        for i in range(groups):
-            outs[i][:, cols] = part[i * rows : (i + 1) * rows].astype(outs[i].dtype)
-
-
-def project(groups, members, att, width, pieces, places):
-    rows = att.shape[0] // groups
+        first = 0
+        for out in outs:
+            out[:, cols] = part[first : first + out.shape[0]].astype(out.dtype)
+            first += out.shape[0]
+
+
+def project(members, att, width, pieces, places, outs):
     share = att.shape[1]
     return pl.pallas_call(
-        functools.partial(project_kernel, groups, members, places),
-        out_shape=[jax.ShapeDtypeStruct((rows, width), jnp.bfloat16)] * (groups - 1)
-        + [jax.ShapeDtypeStruct((rows, width), jnp.float32)],
+        functools.partial(project_kernel, members, places),
+        out_shape=[jax.ShapeDtypeStruct((count, width), kind) for count, kind in outs],
         in_specs=[VMEM] * (1 + len(pieces)),
-        out_specs=[VMEM] * groups,
+        out_specs=[VMEM] * len(outs),
         scratch_shapes=[pltpu.VMEM((share, width), jnp.bfloat16)],
         compiler_params=pltpu.CompilerParams(vmem_limit_bytes=24 * 1024 * 1024),
         cost_estimate=pl.CostEstimate(
-            flops=2 * groups * rows * share * width, bytes_accessed=2 * share * width, transcendentals=0
+            flops=2 * att.shape[0] * share * width, bytes_accessed=2 * share * width, transcendentals=0
         ),
     )(att, *pieces)
 
@@ -254,7 +255,10 @@
     if shared:
         both = after(both, y_part)
     kvs = spread({0: both}, far)
-    att = attend(groups, dim, arrived + [own_query], kvs)
+    blocks = dict(zip(order, arrived))
+    blocks[0] = own_query
+    line = [3, 1, 2, 0] if groups == 4 else [*order, 0]
+    att = attend(groups, dim, [blocks[k] for k in line], kvs)
 
     jobs = []
     if shared:
@@ -270,14 +274,30 @@
     else:
         spots = (lax.axis_index("patch") % members) ^ jnp.arange(members)
         jobs.append((model, [jnp.stack(spread({0: w_own}, far))[spots].reshape(-1, model)], [(None, None, 0)]))
-    totals = []
-    for width, pieces, places in jobs:
-        sums = project(groups, members, att, width, pieces, places)
-        att = after(att, *sums)
+    half, full = jnp.bfloat16, jnp.float32
+
+    def straight(att, width, pieces, places):
+        sums = project(members, att, width, pieces, places, [(rows, half)] * (groups - 1) + [(rows, full)])
         total = sums[-1]
-        for k, part in zip(order, sums):
-            total = total + send(part, k, 0).astype(jnp.float32)
-        totals.append(total)
+        taken = [send(part, k, 0) for k, part in sorted(zip(line, sums[:-1]), key=lambda x: -x[0])]
+        for part in taken:
+            total = total + part.astype(full)
+        return sums, taken, total
+
+    def paired(att, width, pieces, places):
+        sums = project(members, att, width, pieces, places, [(2 * rows, half), (rows, full), (rows, full)])
+        return sums, send(sums[0], 1, 0)
+
+    def close(sums, near, gate_on):
+        across = (sums[1] + near[:rows].astype(full)).astype(half)
+        return sums[2] + near[rows:].astype(full) + send(after(across, *gate_on), 2, 0).astype(full)
+
+    if len(jobs) == 2 and groups == 4:
+        sums, near = paired(att, *jobs[0])
+        _, taken, total = straight(after(att, *sums), *jobs[1])
+        totals = [close(sums, near, []), total]
+    else:
+        totals = [straight(att, *job)[2] for job in jobs]
     return (jnp.concatenate(totals, axis=1) * gate[None, :]).astype(jnp.bfloat16)
 
 

time: 38.9 us -> 37.8 us (0.972)
  starting transfers between devices: 19.8 us -> 18.2 us
  waiting for transfers between devices: 13.7 us -> 14.3 us
    ppermute x17 -> x16, starting transfers between devices: 18.1 us -> 16.5 us  [send(): lax.ppermute(x, 'patch', [(p, (p // members ^ k) * members + p % members...]
    ppermute x17 -> x16, waiting for transfers between devices: 13.7 us -> 14.3 us  [send(): lax.ppermute(x, 'patch', [(p, (p // members ^ k) * members + p % members...]
  transfers between devices with their start and end apart: 18 -> 17, of which waited for: 7 -> 8; matrix products, arithmetic and copies ran while one was open for 0% -> 0% of each run, Pallas kernels for 8% -> 9%
where the time goes in v16:
time: 37.8 us; the launch traced here: 37.7 us
  starting transfers between devices  18.2 us (48%)
  waiting for transfers between devices  14.3 us (38%)
  Pallas kernels  4.28 us (11%)
  other arithmetic  0.79 us (2%)
    ppermute x16, starting transfers between devices, send(): lax.ppermute(x, 'patch', [(p, (p // members ^ k) * members + p % members...  16.5 us
    ppermute x16, waiting for transfers between devices, send(): lax.ppermute(x, 'patch', [(p, (p // members ^ k) * members + p % members...  14.3 us
    ppermute x1, starting transfers between devices, swap(): return lax.ppermute(x, 'groups', [(g, g ^ 1) for g in range(parts)])  1.71 us
    pallas_call x1, Pallas kernels, prepare(): pl.pallas_call(functools.partial(prepare_kernel, groups, members), out_sh...  1.45 us
    pallas_call x1, Pallas kernels, share_rows(): pl.pallas_call(share_kernel, out_shape=jax.ShapeDtypeStruct((depth // 2,...  1.03 us
    pallas_call x1, Pallas kernels, attend(): pl.pallas_call(functools.partial(attend_kernel, groups, dim), out_shape=j...  0.93 us
    pallas_call x2, Pallas kernels, project(): pl.pallas_call(functools.partial(project_kernel, members, places), out_sh...  0.88 us
  transfers between devices with their start and end apart: 17, of which 8 were waited for; matrix products, arithmetic and copies ran while one was open for 0% of the time, Pallas kernels for 9%

profile of v16, /device:TPU:0, one launch (start us, length us, event | category | flops | bytes accessed | tf_op | source)
XLA Modules:
  0.0 37.7 jit_solution(9763059304973353609)
XLA Ops:
  0.0 1.0 %shard_map.83 = bf16[48,3072]{1,0:T(8,128)(2,1)S(1)} custom-call(bf16[96,3072]{1,0:T(8,128)(2,1)} %refs_0_.5), custom_call_target="tpu_custom_call" | custom-call | bytes 589824 | tf_op jit(solution)/shard_map/pallas_call | solution.py:117
  1.0 3.0 %collective-permute-start.3 = (bf16[48,3072]{1,0:T(8,128)(2,1)S(1)}, bf16[48,3072]{1,0:T(8,128)(2,1)S(1)}, u32[]{:S(2)}, u32[]{:S(2)}) collective-permute-start(bf16[48,3072]{1,0:T(8,128)(2,1)S(1)} %shard_map.83), channel_id=1, source_target_pairs={{0,2},{1,3},{2,0},{3,1},{4,6},{5,7},{6,4},{7,5},{8,10},{9,11},{10,... | collective-permute-start | bytes 884744 | tf_op jit(solution)/shard_map/ppermute | solution.py:235
  4.1 0.0 copy-start
  4.1 1.5 %shard_map.82 = (bf16[24,384]{1,0:T(8,128)(2,1)S(1)}, bf16[24,768]{1,0:T(8,128)(2,1)S(1)}, bf16[24,1152]{1,0:T(8,128)(2,1)S(1)}, bf16[24,1152]{1,0:T(8,128)(2,1)S(1)}, bf16[24,1152]{1,0:T(8,128)(2,1)S(1)}) custom-call(bf16[24,1536]{1,0:T(8,128)(2,1)} %refs_0_.3, bf16[24,1536]{1,0:T(8,128)(2,1)} %refs_1_.1, bf16[24,1536]{1,0:T(8,128)(2,1)} %refs_2_.1, ...), custom_call_target="tpu_custom_call" | custom-call | flops 368640 | bytes 516096 | tf_op jit(solution)/shard_map/pallas_call | solution.py:81
  5.5 3.7 %collective-permute-start = (bf16[24,1152]{1,0:T(8,128)(2,1)S(1)}, bf16[24,1152]{1,0:T(8,128)(2,1)S(1)}, u32[]{:S(2)}, u32[]{:S(2)}) collective-permute-start(bf16[24,1152]{1,0:T(8,128)(2,1)S(1)} %get-tuple-element.22), channel_id=1, source_target_pairs={{0,12},{1,13},{2,14},{3,15},{4,8},{5,9},{6,10},{7,11},{8,4},{9,5},... | collective-permute-start | bytes 165896 | tf_op jit(solution)/shard_map/ppermute | solution.py:235
  9.2 0.0 collective-permute-start.1
  9.2 0.8 %collective-permute-start.2 = (bf16[24,1152]{1,0:T(8,128)(2,1)S(1)}, bf16[24,1152]{1,0:T(8,128)(2,1)S(1)}, u32[]{:S(2)}, u32[]{:S(2)}) collective-permute-start(bf16[24,1152]{1,0:T(8,128)(2,1)S(1)} %get-tuple-element.24), channel_id=1, source_target_pairs={{0,8},{1,9},{2,10},{3,11},{4,12},{5,13},{6,14},{7,15},{8,0},{9,1},... | collective-permute-start | bytes 165896 | tf_op jit(solution)/shard_map/ppermute | solution.py:235
  10.0 1.1 %collective-permute-done.3.refs_2_ = bf16[48,3072]{1,0:T(8,128)(2,1)S(1)} collective-permute-done((bf16[48,3072]{1,0:T(8,128)(2,1)S(1)}, bf16[48,3072]{1,0:T(8,128)(2,1)S(1)}, u32[]{:S(2)}, u32[]{:S(2)}) %collective-permute-start.3) | collective-permute-done | bytes 294944 | tf_op jit(solution)/shard_map/ppermute | solution.py:235
  11.1 1.7 %collective-permute-start.8 = (bf16[48,3072]{1,0:T(8,128)(2,1)S(1)}, bf16[48,3072]{1,0:T(8,128)(2,1)S(1)}, u32[]{:S(2)}, u32[]{:S(2)}) collective-permute-start(bf16[48,3072]{1,0:T(8,128)(2,1)S(1)} %collective-permute-done.3.refs_2_), channel_id=1, source_target_pairs={{0,16},{16,0},{1,17},{17,1},{2,18},{18,2},{3,19},{19,3},{4,20},{20... | collective-permute-start | bytes 884744 | tf_op jit(solution)/shard_map/ppermute | solution.py:238
  12.8 0.0 collective-permute-done.refs_0_
  12.8 0.6 %collective-permute-done.1.refs_1_ = bf16[24,1152]{1,0:T(8,128)(2,1)S(1)} collective-permute-done((bf16[24,1152]{1,0:T(8,128)(2,1)S(1)}, bf16[24,1152]{1,0:T(8,128)(2,1)S(1)}, u32[]{:S(2)}, u32[]{:S(2)}) %collective-permute-start.1) | collective-permute-done | bytes 55328 | tf_op jit(solution)/shard_map/ppermute | solution.py:235
  13.4 1.0 %collective-permute-done.2.refs_2_ = bf16[24,1152]{1,0:T(8,128)(2,1)S(1)} collective-permute-done((bf16[24,1152]{1,0:T(8,128)(2,1)S(1)}, bf16[24,1152]{1,0:T(8,128)(2,1)S(1)}, u32[]{:S(2)}, u32[]{:S(2)}) %collective-permute-start.2) | collective-permute-done | bytes 55328 | tf_op jit(solution)/shard_map/ppermute | solution.py:235
  14.3 0.6 %collective-permute-start.5 = (bf16[96,768]{1,0:T(8,128)(2,1)S(1)}, bf16[96,768]{1,0:T(8,128)(2,1)S(1)}, u32[]{:S(2)}, u32[]{:S(2)}) collective-permute-start(bf16[96,768]{1,0:T(8,128)(2,1)S(1)} %pad_maximum_fusion.refs_4_), channel_id=1, source_target_pairs={{0,2},{1,3},{2,0},{3,1},{4,6},{5,7},{6,4},{7,5},{8,10},{9,11},{10,... | collective-permute-start | bytes 442376 | tf_op jit(solution)/shard_map/ppermute | solution.py:235
  14.9 0.0 collective-permute-start.4
  14.9 0.5 %collective-permute-start.9 = (bf16[48,3072]{1,0:T(8,128)(2,1)S(1)}, bf16[48,3072]{1,0:T(8,128)(2,1)S(1)}, u32[]{:S(2)}, u32[]{:S(2)}) collective-permute-start(bf16[48,3072]{1,0:T(8,128)(2,1)S(1)} %collective-permute-done.3.refs_2_), channel_id=1, source_target_pairs={{0,1},{1,0},{2,3},{3,2},{4,5},{5,4},{6,7},{7,6},{8,9},{9,8},{10,11... | collective-permute-start | bytes 884744 | tf_op jit(solution)/shard_map/ppermute | solution.py:235
  15.4 0.0 copy-done
  15.4 0.0 collective-permute-start.7
  15.4 4.1 %collective-permute-done.5.refs_6_ = bf16[96,768]{1,0:T(8,128)(2,1)S(1)} collective-permute-done((bf16[96,768]{1,0:T(8,128)(2,1)S(1)}, bf16[96,768]{1,0:T(8,128)(2,1)S(1)}, u32[]{:S(2)}, u32[]{:S(2)}) %collective-permute-start.5) | collective-permute-done | bytes 147488 | tf_op jit(solution)/shard_map/ppermute | solution.py:235
  19.6 0.0 collective-permute-start.6
  19.6 0.0 collective-permute-done.8.refs_3_
  19.6 0.6 %collective-permute-start.10 = (bf16[48,1536]{1,0:T(8,128)(2,1)S(1)}, bf16[48,1536]{1,0:T(8,128)(2,1)S(1)}, u32[]{:S(2)}, u32[]{:S(2)}) collective-permute-start(bf16[48,1536]{1,0:T(8,128)(2,1)S(1)} %get-tuple-element.40), channel_id=1, source_target_pairs={{0,1},{1,0},{2,3},{3,2},{4,5},{5,4},{6,7},{7,6},{8,9},{9,8},{10,11... | collective-permute-start | bytes 442376 | tf_op jit(solution)/shard_map/ppermute | solution.py:235
  20.2 0.0 collective-permute-done.4.refs_5_
  20.2 0.1 collective-permute-start.13
  20.3 0.7 %collective-permute-done.6.refs_7_ = bf16[96,768]{1,0:T(8,128)(2,1)S(1)} collective-permute-done((bf16[96,768]{1,0:T(8,128)(2,1)S(1)}, bf16[96,768]{1,0:T(8,128)(2,1)S(1)}, u32[]{:S(2)}, u32[]{:S(2)}) %collective-permute-start.6) | collective-permute-done | bytes 147488 | tf_op jit(solution)/shard_map/ppermute | solution.py:235
  20.9 0.9 %shard_map.84.att = bf16[96,384]{1,0:T(8,128)(2,1)S(1)} custom-call(bf16[24,1152]{1,0:T(8,128)(2,1)S(1)} %collective-permute-done.refs_0_, bf16[24,1152]{1,0:T(8,128)(2,1)S(1)} %collective-permute-done.1.refs_1_, bf16[24,1152]{1,0:T(8,128)(2,1)S(1)} %collective-permute-done.2.refs_2_, bf16[24,384]{1,0:T(8,128)(2,1)S(1)} %get-tuple-element.25.refs_3_, ...), custom_call_target="tpu_custom_call" | custom-call | flops 56623104 | bytes 589824 | tf_op jit(solution)/shard_map/pallas_call | solution.py:160
  21.9 0.0 collective-permute-done.9.refs_4_
  21.9 0.0 collective-permute-done.10.refs_5_
  21.9 0.0 collective-permute-done.7.refs_1_
  21.9 0.4 %shard_map.85 = (bf16[48,1536]{1,0:T(8,128)(2,1)S(1)}, f32[24,1536]{1,0:T(8,128)S(1)}, f32[24,1536]{1,0:T(8,128)S(1)}) custom-call(bf16[96,384]{1,0:T(8,128)(2,1)S(1)} %shard_map.84.att, bf16[96,3072]{1,0:T(8,128)(2,1)S(1)} %copy-done, bf16[96,3072]{1,0:T(8,128)(2,1)S(1)} %collective-permute-done.7.refs_1_, ...), custom_call_target="tpu_custom_call" | custom-call | flops 113246208 | bytes 1179648 | tf_op jit(solution)/shard_map/pallas_call | solution.py:203
  22.3 2.0 %collective-permute-start.11 = (bf16[48,1536]{1,0:T(8,128)(2,1)S(1)}, bf16[48,1536]{1,0:T(8,128)(2,1)S(1)}, u32[]{:S(2)}, u32[]{:S(2)}) collective-permute-start(bf16[48,1536]{1,0:T(8,128)(2,1)S(1)} %get-tuple-element.32), channel_id=1, source_target_pairs={{0,4},{1,5},{2,6},{3,7},{4,0},{5,1},{6,2},{7,3},{8,12},{9,13},{10,... | collective-permute-start | bytes 442376 | tf_op jit(solution)/shard_map/ppermute | solution.py:235
  24.4 0.0 collective-permute-done.13.refs_5_
  24.4 0.4 %shard_map.86 = (bf16[24,1536]{1,0:T(8,128)(2,1)S(1)}, bf16[24,1536]{1,0:T(8,128)(2,1)S(1)}, bf16[24,1536]{1,0:T(8,128)(2,1)S(1)}, f32[24,1536]{1,0:T(8,128)S(1)}) custom-call(bf16[96,384]{1,0:T(8,128)(2,1)S(1)} %shard_map.84.att, bf16[96,3072]{1,0:T(8,128)(2,1)S(1)} %copy-done, bf16[96,3072]{1,0:T(8,128)(2,1)S(1)} %collective-permute-done.7.refs_1_, ...), custom_call_target="tpu_custom_call" | custom-call | flops 113246208 | bytes 1179648 | tf_op jit(solution)/shard_map/pallas_call | solution.py:203
  24.8 0.0 copy-start.1
  24.8 1.1 %collective-permute-start.14 = (bf16[24,1536]{1,0:T(8,128)(2,1)S(1)}, bf16[24,1536]{1,0:T(8,128)(2,1)S(1)}, u32[]{:S(2)}, u32[]{:S(2)}) collective-permute-start(bf16[24,1536]{1,0:T(8,128)(2,1)S(1)} %get-tuple-element.36), channel_id=1, source_target_pairs={{0,12},{1,13},{2,14},{3,15},{4,8},{5,9},{6,10},{7,11},{8,4},{9,5},... | collective-permute-start | bytes 221192 | tf_op jit(solution)/shard_map/ppermute | solution.py:235
  26.0 0.5 %collective-permute-start.15 = (bf16[24,1536]{1,0:T(8,128)(2,1)S(1)}, bf16[24,1536]{1,0:T(8,128)(2,1)S(1)}, u32[]{:S(2)}, u32[]{:S(2)}) collective-permute-start(bf16[24,1536]{1,0:T(8,128)(2,1)S(1)} %get-tuple-element.37), channel_id=1, source_target_pairs={{0,8},{1,9},{2,10},{3,11},{4,12},{5,13},{6,14},{7,15},{8,0},{9,1},... | collective-permute-start | bytes 221192 | tf_op jit(solution)/shard_map/ppermute | solution.py:235
  26.4 2.8 %collective-permute-start.16 = (bf16[24,1536]{1,0:T(8,128)(2,1)S(1)}, bf16[24,1536]{1,0:T(8,128)(2,1)S(1)}, u32[]{:S(2)}, u32[]{:S(2)}) collective-permute-start(bf16[24,1536]{1,0:T(8,128)(2,1)S(1)} %get-tuple-element.38), channel_id=1, source_target_pairs={{0,4},{1,5},{2,6},{3,7},{4,0},{5,1},{6,2},{7,3},{8,12},{9,13},{10,... | collective-permute-start | bytes 221192 | tf_op jit(solution)/shard_map/ppermute | solution.py:235
  29.3 0.0 collective-permute-done.11
  29.3 0.8 %collective-permute-start.12 = (bf16[24,1536]{1,0:T(8,128)(2,1)S(1)}, bf16[24,1536]{1,0:T(8,128)(2,1)S(1)}, u32[]{:S(2)}, u32[]{:S(2)}) collective-permute-start(bf16[24,1536]{1,0:T(8,128)(2,1)S(1)} %add_convert_fusion), channel_id=1, source_target_pairs={{0,8},{1,9},{2,10},{3,11},{4,12},{5,13},{6,14},{7,15},{8,0},{9,1},... | collective-permute-start | bytes 221192 | tf_op jit(solution)/shard_map/ppermute | solution.py:235
  30.1 1.8 %collective-permute-done.14 = bf16[24,1536]{1,0:T(8,128)(2,1)S(1)} collective-permute-done((bf16[24,1536]{1,0:T(8,128)(2,1)S(1)}, bf16[24,1536]{1,0:T(8,128)(2,1)S(1)}, u32[]{:S(2)}, u32[]{:S(2)}) %collective-permute-start.14) | collective-permute-done | bytes 73760 | tf_op jit(solution)/shard_map/ppermute | solution.py:235
  31.9 3.1 %collective-permute-done.15 = bf16[24,1536]{1,0:T(8,128)(2,1)S(1)} collective-permute-done((bf16[24,1536]{1,0:T(8,128)(2,1)S(1)}, bf16[24,1536]{1,0:T(8,128)(2,1)S(1)}, u32[]{:S(2)}, u32[]{:S(2)}) %collective-permute-start.15) | collective-permute-done | bytes 73760 | tf_op jit(solution)/shard_map/ppermute | solution.py:235
  35.0 0.0 collective-permute-done.16
  35.0 1.9 %collective-permute-done.12 = bf16[24,1536]{1,0:T(8,128)(2,1)S(1)} collective-permute-done((bf16[24,1536]{1,0:T(8,128)(2,1)S(1)}, bf16[24,1536]{1,0:T(8,128)(2,1)S(1)}, u32[]{:S(2)}, u32[]{:S(2)}) %collective-permute-start.12) | collective-permute-done | bytes 73760 | tf_op jit(solution)/shard_map/ppermute | solution.py:235
  37.0 0.0 copy-done.1
  37.0 0.7 %fusion = bf16[24,3072]{1,0:T(8,128)(2,1)} fusion(f32[24,1536]{1,0:T(8,128)S(1)} %convert_add_fusion, f32[24,1536]{1,0:T(8,128)S(1)} %convert_add_fusion.1, f32[3072]{0:T(1024)S(1)} %copy-done.1), kind=kLoop, calls=%fused_computation.1 | loop fusion | flops 221184 | bytes 454656 | tf_op jit(solution)/shard_map/convert_element_type | solution.py:301
  (8 shorter events, 0.1 us)
Async XLA Ops:
  1.0 10.0 %collective-permute-start.3 = (bf16[48,3072]{1,0:T(8,128)(2,1)S(1)}, bf16[48,3072]{1,0:T(8,128)(2,1)S(1)}, u32[]{:S(2)}, u32[]{:S(2)}) collective-permute-start(bf16[48,3072]{1,0:T(8,128)(2,1)S(1)} %shard_map.83), channel_id=1, source_target_pairs={{0,2},{1,3},{2,0},{3,1},{4,6},{5,7},{6,4},{7,5},{8,10},{9,11},{10,... | collective-permute-start | bytes 884744 | tf_op jit(solution)/shard_map/ppermute | solution.py:235
  4.1 11.4 %copy-start = (bf16[96,3072]{1,0:T(8,128)(2,1)S(1)}, bf16[96,3072]{1,0:T(8,128)(2,1)}, u32[]{:S(2)}) copy-start(bf16[96,3072]{1,0:T(8,128)(2,1)} %refs_0_.5) | copy-start | bytes 1769476
  5.5 7.3 %collective-permute-start = (bf16[24,1152]{1,0:T(8,128)(2,1)S(1)}, bf16[24,1152]{1,0:T(8,128)(2,1)S(1)}, u32[]{:S(2)}, u32[]{:S(2)}) collective-permute-start(bf16[24,1152]{1,0:T(8,128)(2,1)S(1)} %get-tuple-element.22), channel_id=1, source_target_pairs={{0,12},{1,13},{2,14},{3,15},{4,8},{5,9},{6,10},{7,11},{8,4},{9,5},... | collective-permute-start | bytes 165896 | tf_op jit(solution)/shard_map/ppermute | solution.py:235
  9.2 4.2 %collective-permute-start.1 = (bf16[24,1152]{1,0:T(8,128)(2,1)S(1)}, bf16[24,1152]{1,0:T(8,128)(2,1)S(1)}, u32[]{:S(2)}, u32[]{:S(2)}) collective-permute-start(bf16[24,1152]{1,0:T(8,128)(2,1)S(1)} %get-tuple-element.23), channel_id=1, source_target_pairs={{0,4},{1,5},{2,6},{3,7},{4,0},{5,1},{6,2},{7,3},{8,12},{9,13},{10,... | collective-permute-start | bytes 165896 | tf_op jit(solution)/shard_map/ppermute | solution.py:235
  9.2 5.1 %collective-permute-start.2 = (bf16[24,1152]{1,0:T(8,128)(2,1)S(1)}, bf16[24,1152]{1,0:T(8,128)(2,1)S(1)}, u32[]{:S(2)}, u32[]{:S(2)}) collective-permute-start(bf16[24,1152]{1,0:T(8,128)(2,1)S(1)} %get-tuple-element.24), channel_id=1, source_target_pairs={{0,8},{1,9},{2,10},{3,11},{4,12},{5,13},{6,14},{7,15},{8,0},{9,1},... | collective-permute-start | bytes 165896 | tf_op jit(solution)/shard_map/ppermute | solution.py:235
  11.1 8.5 %collective-permute-start.8 = (bf16[48,3072]{1,0:T(8,128)(2,1)S(1)}, bf16[48,3072]{1,0:T(8,128)(2,1)S(1)}, u32[]{:S(2)}, u32[]{:S(2)}) collective-permute-start(bf16[48,3072]{1,0:T(8,128)(2,1)S(1)} %collective-permute-done.3.refs_2_), channel_id=1, source_target_pairs={{0,16},{16,0},{1,17},{17,1},{2,18},{18,2},{3,19},{19,3},{4,20},{20... | collective-permute-start | bytes 884744 | tf_op jit(solution)/shard_map/ppermute | solution.py:238
  14.3 5.2 %collective-permute-start.5 = (bf16[96,768]{1,0:T(8,128)(2,1)S(1)}, bf16[96,768]{1,0:T(8,128)(2,1)S(1)}, u32[]{:S(2)}, u32[]{:S(2)}) collective-permute-start(bf16[96,768]{1,0:T(8,128)(2,1)S(1)} %pad_maximum_fusion.refs_4_), channel_id=1, source_target_pairs={{0,2},{1,3},{2,0},{3,1},{4,6},{5,7},{6,4},{7,5},{8,10},{9,11},{10,... | collective-permute-start | bytes 442376 | tf_op jit(solution)/shard_map/ppermute | solution.py:235
  14.9 5.2 %collective-permute-start.4 = (bf16[96,768]{1,0:T(8,128)(2,1)S(1)}, bf16[96,768]{1,0:T(8,128)(2,1)S(1)}, u32[]{:S(2)}, u32[]{:S(2)}) collective-permute-start(bf16[96,768]{1,0:T(8,128)(2,1)S(1)} %pad_maximum_fusion.refs_4_), channel_id=1, source_target_pairs={{0,1},{1,0},{2,3},{3,2},{4,5},{5,4},{6,7},{7,6},{8,9},{9,8},{10,11... | collective-permute-start | bytes 442376 | tf_op jit(solution)/shard_map/ppermute | solution.py:235
  14.9 6.9 %collective-permute-start.9 = (bf16[48,3072]{1,0:T(8,128)(2,1)S(1)}, bf16[48,3072]{1,0:T(8,128)(2,1)S(1)}, u32[]{:S(2)}, u32[]{:S(2)}) collective-permute-start(bf16[48,3072]{1,0:T(8,128)(2,1)S(1)} %collective-permute-done.3.refs_2_), channel_id=1, source_target_pairs={{0,1},{1,0},{2,3},{3,2},{4,5},{5,4},{6,7},{7,6},{8,9},{9,8},{10,11... | collective-permute-start | bytes 884744 | tf_op jit(solution)/shard_map/ppermute | solution.py:235
  15.4 6.5 %collective-permute-start.7 = (bf16[96,3072]{1,0:T(8,128)(2,1)S(1)}, bf16[96,3072]{1,0:T(8,128)(2,1)S(1)}, u32[]{:S(2)}, u32[]{:S(2)}) collective-permute-start(bf16[96,3072]{1,0:T(8,128)(2,1)S(1)} %copy-done), channel_id=1, source_target_pairs={{0,1},{1,0},{2,3},{3,2},{4,5},{5,4},{6,7},{7,6},{8,9},{9,8},{10,11... | collective-permute-start | bytes 1769480 | tf_op jit(solution)/shard_map/ppermute | solution.py:235
  19.6 1.4 %collective-permute-start.6 = (bf16[96,768]{1,0:T(8,128)(2,1)S(1)}, bf16[96,768]{1,0:T(8,128)(2,1)S(1)}, u32[]{:S(2)}, u32[]{:S(2)}) collective-permute-start(bf16[96,768]{1,0:T(8,128)(2,1)S(1)} %collective-permute-done.5.refs_6_), channel_id=1, source_target_pairs={{0,1},{1,0},{2,3},{3,2},{4,5},{5,4},{6,7},{7,6},{8,9},{9,8},{10,11... | collective-permute-start | bytes 442376 | tf_op jit(solution)/shard_map/ppermute | solution.py:235
  19.6 2.3 %collective-permute-start.10 = (bf16[48,1536]{1,0:T(8,128)(2,1)S(1)}, bf16[48,1536]{1,0:T(8,128)(2,1)S(1)}, u32[]{:S(2)}, u32[]{:S(2)}) collective-permute-start(bf16[48,1536]{1,0:T(8,128)(2,1)S(1)} %get-tuple-element.40), channel_id=1, source_target_pairs={{0,1},{1,0},{2,3},{3,2},{4,5},{5,4},{6,7},{7,6},{8,9},{9,8},{10,11... | collective-permute-start | bytes 442376 | tf_op jit(solution)/shard_map/ppermute | solution.py:235
  20.2 4.2 %collective-permute-start.13 = (bf16[48,1536]{1,0:T(8,128)(2,1)S(1)}, bf16[48,1536]{1,0:T(8,128)(2,1)S(1)}, u32[]{:S(2)}, u32[]{:S(2)}) collective-permute-start(bf16[48,1536]{1,0:T(8,128)(2,1)S(1)} %get-tuple-element.39), channel_id=1, source_target_pairs={{0,1},{1,0},{2,3},{3,2},{4,5},{5,4},{6,7},{7,6},{8,9},{9,8},{10,11... | collective-permute-start | bytes 442376 | tf_op jit(solution)/shard_map/ppermute | solution.py:235
  22.3 6.9 %collective-permute-start.11 = (bf16[48,1536]{1,0:T(8,128)(2,1)S(1)}, bf16[48,1536]{1,0:T(8,128)(2,1)S(1)}, u32[]{:S(2)}, u32[]{:S(2)}) collective-permute-start(bf16[48,1536]{1,0:T(8,128)(2,1)S(1)} %get-tuple-element.32), channel_id=1, source_target_pairs={{0,4},{1,5},{2,6},{3,7},{4,0},{5,1},{6,2},{7,3},{8,12},{9,13},{10,... | collective-permute-start | bytes 442376 | tf_op jit(solution)/shard_map/ppermute | solution.py:235
  24.8 12.2 %copy-start.1 = (f32[3072]{0:T(1024)S(1)}, f32[3072]{0:T(1024)}, u32[]{:S(2)}) copy-start(f32[3072]{0:T(1024)} %param.15) | copy-start | bytes 36868
  24.8 7.1 %collective-permute-start.14 = (bf16[24,1536]{1,0:T(8,128)(2,1)S(1)}, bf16[24,1536]{1,0:T(8,128)(2,1)S(1)}, u32[]{:S(2)}, u32[]{:S(2)}) collective-permute-start(bf16[24,1536]{1,0:T(8,128)(2,1)S(1)} %get-tuple-element.36), channel_id=1, source_target_pairs={{0,12},{1,13},{2,14},{3,15},{4,8},{5,9},{6,10},{7,11},{8,4},{9,5},... | collective-permute-start | bytes 221192 | tf_op jit(solution)/shard_map/ppermute | solution.py:235
  26.0 9.0 %collective-permute-start.15 = (bf16[24,1536]{1,0:T(8,128)(2,1)S(1)}, bf16[24,1536]{1,0:T(8,128)(2,1)S(1)}, u32[]{:S(2)}, u32[]{:S(2)}) collective-permute-start(bf16[24,1536]{1,0:T(8,128)(2,1)S(1)} %get-tuple-element.37), channel_id=1, source_target_pairs={{0,8},{1,9},{2,10},{3,11},{4,12},{5,13},{6,14},{7,15},{8,0},{9,1},... | collective-permute-start | bytes 221192 | tf_op jit(solution)/shard_map/ppermute | solution.py:235
  26.4 8.6 %collective-permute-start.16 = (bf16[24,1536]{1,0:T(8,128)(2,1)S(1)}, bf16[24,1536]{1,0:T(8,128)(2,1)S(1)}, u32[]{:S(2)}, u32[]{:S(2)}) collective-permute-start(bf16[24,1536]{1,0:T(8,128)(2,1)S(1)} %get-tuple-element.38), channel_id=1, source_target_pairs={{0,4},{1,5},{2,6},{3,7},{4,0},{5,1},{6,2},{7,3},{8,12},{9,13},{10,... | collective-permute-start | bytes 221192 | tf_op jit(solution)/shard_map/ppermute | solution.py:235
  29.3 7.6 %collective-permute-start.12 = (bf16[24,1536]{1,0:T(8,128)(2,1)S(1)}, bf16[24,1536]{1,0:T(8,128)(2,1)S(1)}, u32[]{:S(2)}, u32[]{:S(2)}) collective-permute-start(bf16[24,1536]{1,0:T(8,128)(2,1)S(1)} %add_convert_fusion), channel_id=1, source_target_pairs={{0,8},{1,9},{2,10},{3,11},{4,12},{5,13},{6,14},{7,15},{8,0},{9,1},... | collective-permute-start | bytes 221192 | tf_op jit(solution)/shard_map/ppermute | solution.py:235

commit v17 on v16

--- a/solution.py
+++ b/solution.py
@@ -229,7 +229,7 @@
     depth, model = w_out.shape
     far = members // 2
     shared = parts % 2 == 0 and members == 4 and depth % 32 == 0
-    first = model // 2
+    first = model * 2 // 3 // 256 * 256
 
     def send(x, k, j):
         return lax.ppermute(x, "patch", [(p, ((p // members) ^ k) * members + (p % members) ^ j) for p in range(patch)])
@@ -265,11 +265,11 @@
         w_core = send(after(w_own, both), 0, 1)
         y_core = send(after(y_part, both), 0, 1)
         x_part = swap(y_part)
+        x_core = send(after(x_part, *kvs), 0, 1)
         edges = (0, first, model)
         for left, right in zip(edges, edges[1:]):
-            x_core = send(after(x_part, kvs[far])[:, left:right], 0, 1)
             pieces = [w_own, w_core, y_part, x_part, y_core, x_core]
-            places = [(0, None, left), (1, None, left), (2, 0, left), (2, 1, left), (3, 0, left), (3, 1, 0)]
+            places = [(0, None, left), (1, None, left), (2, 0, left), (2, 1, left), (3, 0, left), (3, 1, left)]
             jobs.append((right - left, pieces, places))
     else:
         spots = (lax.axis_index("patch") % members) ^ jnp.arange(members)

time: 37.8 us -> 40 us (1.058)
  waiting for transfers between devices: 14.3 us -> 16.6 us
    ppermute x16 -> x15, waiting for transfers between devices: 14.3 us -> 15.9 us  [send(): lax.ppermute(x, 'patch', [(p, (p // members ^ k) * members + p % members...]
    ppermute x1, waiting for transfers between devices: 0.01 us -> 0.72 us  [swap(): return lax.ppermute(x, 'groups', [(g, g ^ 1) for g in range(parts)])]
    ppermute x16 -> x15, starting transfers between devices: 16.5 us -> 16.6 us  [send(): lax.ppermute(x, 'patch', [(p, (p // members ^ k) * members + p % members...]
  transfers between devices with their start and end apart: 17 -> 16, of which waited for: 8 -> 11; matrix products, arithmetic and copies ran while one was open for 0% -> 0% of each run, Pallas kernels for 9% -> 7%
where the time goes in v17:
time: 40 us; the launch traced here: 39.9 us
  starting transfers between devices  18.1 us (45%)
  waiting for transfers between devices  16.6 us (42%)
  Pallas kernels  4.29 us (11%)
  other arithmetic  0.8 us (2%)
    ppermute x15, starting transfers between devices, send(): lax.ppermute(x, 'patch', [(p, (p // members ^ k) * members + p % members...  16.6 us
    ppermute x15, waiting for transfers between devices, send(): lax.ppermute(x, 'patch', [(p, (p // members ^ k) * members + p % members...  15.9 us
    ppermute x1, starting transfers between devices, swap(): return lax.ppermute(x, 'groups', [(g, g ^ 1) for g in range(parts)])  1.49 us
    pallas_call x1, Pallas kernels, prepare(): pl.pallas_call(functools.partial(prepare_kernel, groups, members), out_sh...  1.45 us
    pallas_call x1, Pallas kernels, share_rows(): pl.pallas_call(share_kernel, out_shape=jax.ShapeDtypeStruct((depth // 2,...  1.03 us
    pallas_call x1, Pallas kernels, attend(): pl.pallas_call(functools.partial(attend_kernel, groups, dim), out_shape=j...  0.92 us
    pallas_call x2, Pallas kernels, project(): pl.pallas_call(functools.partial(project_kernel, members, places), out_sh...  0.89 us
  transfers between devices with their start and end apart: 16, of which 11 were waited for; matrix products, arithmetic and copies ran while one was open for 0% of the time, Pallas kernels for 7%

profile of v17, /device:TPU:0, one launch (start us, length us, event | category | flops | bytes accessed | tf_op | source)
XLA Modules:
  0.0 39.9 jit_solution(1993280385138104494)
XLA Ops:
  0.0 1.0 %shard_map.83 = bf16[48,3072]{1,0:T(8,128)(2,1)S(1)} custom-call(bf16[96,3072]{1,0:T(8,128)(2,1)} %refs_0_.5), custom_call_target="tpu_custom_call" | custom-call | bytes 589824 | tf_op jit(solution)/shard_map/pallas_call | solution.py:117
  1.0 3.0 %collective-permute-start.3 = (bf16[48,3072]{1,0:T(8,128)(2,1)S(1)}, bf16[48,3072]{1,0:T(8,128)(2,1)S(1)}, u32[]{:S(2)}, u32[]{:S(2)}) collective-permute-start(bf16[48,3072]{1,0:T(8,128)(2,1)S(1)} %shard_map.83), channel_id=1, source_target_pairs={{0,2},{1,3},{2,0},{3,1},{4,6},{5,7},{6,4},{7,5},{8,10},{9,11},{10,... | collective-permute-start | bytes 884744 | tf_op jit(solution)/shard_map/ppermute | solution.py:235
  4.1 0.0 copy-start
  4.1 1.5 %shard_map.82 = (bf16[24,384]{1,0:T(8,128)(2,1)S(1)}, bf16[24,768]{1,0:T(8,128)(2,1)S(1)}, bf16[24,1152]{1,0:T(8,128)(2,1)S(1)}, bf16[24,1152]{1,0:T(8,128)(2,1)S(1)}, bf16[24,1152]{1,0:T(8,128)(2,1)S(1)}) custom-call(bf16[24,1536]{1,0:T(8,128)(2,1)} %refs_0_.3, bf16[24,1536]{1,0:T(8,128)(2,1)} %refs_1_.1, bf16[24,1536]{1,0:T(8,128)(2,1)} %refs_2_.1, ...), custom_call_target="tpu_custom_call" | custom-call | flops 368640 | bytes 516096 | tf_op jit(solution)/shard_map/pallas_call | solution.py:81
  5.5 3.7 %collective-permute-start = (bf16[24,1152]{1,0:T(8,128)(2,1)S(1)}, bf16[24,1152]{1,0:T(8,128)(2,1)S(1)}, u32[]{:S(2)}, u32[]{:S(2)}) collective-permute-start(bf16[24,1152]{1,0:T(8,128)(2,1)S(1)} %get-tuple-element.22), channel_id=1, source_target_pairs={{0,12},{1,13},{2,14},{3,15},{4,8},{5,9},{6,10},{7,11},{8,4},{9,5},... | collective-permute-start | bytes 165896 | tf_op jit(solution)/shard_map/ppermute | solution.py:235
  9.2 0.0 collective-permute-start.1
  9.2 0.8 %collective-permute-start.2 = (bf16[24,1152]{1,0:T(8,128)(2,1)S(1)}, bf16[24,1152]{1,0:T(8,128)(2,1)S(1)}, u32[]{:S(2)}, u32[]{:S(2)}) collective-permute-start(bf16[24,1152]{1,0:T(8,128)(2,1)S(1)} %get-tuple-element.24), channel_id=1, source_target_pairs={{0,8},{1,9},{2,10},{3,11},{4,12},{5,13},{6,14},{7,15},{8,0},{9,1},... | collective-permute-start | bytes 165896 | tf_op jit(solution)/shard_map/ppermute | solution.py:235
  10.0 1.6 %collective-permute-done.refs_0_ = bf16[24,1152]{1,0:T(8,128)(2,1)S(1)} collective-permute-done((bf16[24,1152]{1,0:T(8,128)(2,1)S(1)}, bf16[24,1152]{1,0:T(8,128)(2,1)S(1)}, u32[]{:S(2)}, u32[]{:S(2)}) %collective-permute-start) | collective-permute-done | bytes 55328 | tf_op jit(solution)/shard_map/ppermute | solution.py:235
  11.6 1.8 %collective-permute-done.1.refs_1_ = bf16[24,1152]{1,0:T(8,128)(2,1)S(1)} collective-permute-done((bf16[24,1152]{1,0:T(8,128)(2,1)S(1)}, bf16[24,1152]{1,0:T(8,128)(2,1)S(1)}, u32[]{:S(2)}, u32[]{:S(2)}) %collective-permute-start.1) | collective-permute-done | bytes 55328 | tf_op jit(solution)/shard_map/ppermute | solution.py:235
  13.4 1.0 %collective-permute-done.2.refs_2_ = bf16[24,1152]{1,0:T(8,128)(2,1)S(1)} collective-permute-done((bf16[24,1152]{1,0:T(8,128)(2,1)S(1)}, bf16[24,1152]{1,0:T(8,128)(2,1)S(1)}, u32[]{:S(2)}, u32[]{:S(2)}) %collective-permute-start.2) | collective-permute-done | bytes 55328 | tf_op jit(solution)/shard_map/ppermute | solution.py:235
  14.3 0.0 collective-permute-done.3.refs_2_
  14.4 0.6 %collective-permute-start.5 = (bf16[96,768]{1,0:T(8,128)(2,1)S(1)}, bf16[96,768]{1,0:T(8,128)(2,1)S(1)}, u32[]{:S(2)}, u32[]{:S(2)}) collective-permute-start(bf16[96,768]{1,0:T(8,128)(2,1)S(1)} %pad_maximum_fusion.refs_4_), channel_id=1, source_target_pairs={{0,2},{1,3},{2,0},{3,1},{4,6},{5,7},{6,4},{7,5},{8,10},{9,11},{10,... | collective-permute-start | bytes 442376 | tf_op jit(solution)/shard_map/ppermute | solution.py:235
  14.9 1.5 %collective-permute-start.8 = (bf16[48,3072]{1,0:T(8,128)(2,1)S(1)}, bf16[48,3072]{1,0:T(8,128)(2,1)S(1)}, u32[]{:S(2)}, u32[]{:S(2)}) collective-permute-start(bf16[48,3072]{1,0:T(8,128)(2,1)S(1)} %collective-permute-done.3.refs_2_), channel_id=1, source_target_pairs={{0,16},{16,0},{1,17},{17,1},{2,18},{18,2},{3,19},{19,3},{4,20},{20... | collective-permute-start | bytes 884744 | tf_op jit(solution)/shard_map/ppermute | solution.py:238
  16.4 0.0 copy-done
  16.4 0.0 collective-permute-start.7
  16.4 0.5 %collective-permute-start.4 = (bf16[96,768]{1,0:T(8,128)(2,1)S(1)}, bf16[96,768]{1,0:T(8,128)(2,1)S(1)}, u32[]{:S(2)}, u32[]{:S(2)}) collective-permute-start(bf16[96,768]{1,0:T(8,128)(2,1)S(1)} %pad_maximum_fusion.refs_4_), channel_id=1, source_target_pairs={{0,1},{1,0},{2,3},{3,2},{4,5},{5,4},{6,7},{7,6},{8,9},{9,8},{10,11... | collective-permute-start | bytes 442376 | tf_op jit(solution)/shard_map/ppermute | solution.py:235
  16.9 2.6 %collective-permute-done.5.refs_6_ = bf16[96,768]{1,0:T(8,128)(2,1)S(1)} collective-permute-done((bf16[96,768]{1,0:T(8,128)(2,1)S(1)}, bf16[96,768]{1,0:T(8,128)(2,1)S(1)}, u32[]{:S(2)}, u32[]{:S(2)}) %collective-permute-start.5) | collective-permute-done | bytes 147488 | tf_op jit(solution)/shard_map/ppermute | solution.py:235
  19.6 0.0 collective-permute-start.6
  19.6 0.5 %collective-permute-start.9 = (bf16[48,3072]{1,0:T(8,128)(2,1)S(1)}, bf16[48,3072]{1,0:T(8,128)(2,1)S(1)}, u32[]{:S(2)}, u32[]{:S(2)}) collective-permute-start(bf16[48,3072]{1,0:T(8,128)(2,1)S(1)} %collective-permute-done.3.refs_2_), channel_id=1, source_target_pairs={{0,1},{1,0},{2,3},{3,2},{4,5},{5,4},{6,7},{7,6},{8,9},{9,8},{10,11... | collective-permute-start | bytes 884744 | tf_op jit(solution)/shard_map/ppermute | solution.py:235
  20.1 0.0 collective-permute-done.4.refs_5_
  20.1 0.9 %collective-permute-done.6.refs_7_ = bf16[96,768]{1,0:T(8,128)(2,1)S(1)} collective-permute-done((bf16[96,768]{1,0:T(8,128)(2,1)S(1)}, bf16[96,768]{1,0:T(8,128)(2,1)S(1)}, u32[]{:S(2)}, u32[]{:S(2)}) %collective-permute-start.6) | collective-permute-done | bytes 147488 | tf_op jit(solution)/shard_map/ppermute | solution.py:235
  20.9 0.7 %collective-permute-done.8.refs_3_ = bf16[48,3072]{1,0:T(8,128)(2,1)S(1)} collective-permute-done((bf16[48,3072]{1,0:T(8,128)(2,1)S(1)}, bf16[48,3072]{1,0:T(8,128)(2,1)S(1)}, u32[]{:S(2)}, u32[]{:S(2)}) %collective-permute-start.8) | collective-permute-done | bytes 294944 | tf_op jit(solution)/shard_map/ppermute | solution.py:238
  21.7 0.0 collective-permute-start.10
  21.7 0.9 %shard_map.84.att = bf16[96,384]{1,0:T(8,128)(2,1)S(1)} custom-call(bf16[24,1152]{1,0:T(8,128)(2,1)S(1)} %collective-permute-done.refs_0_, bf16[24,1152]{1,0:T(8,128)(2,1)S(1)} %collective-permute-done.1.refs_1_, bf16[24,1152]{1,0:T(8,128)(2,1)S(1)} %collective-permute-done.2.refs_2_, bf16[24,384]{1,0:T(8,128)(2,1)S(1)} %get-tuple-element.25.refs_3_, ...), custom_call_target="tpu_custom_call" | custom-call | flops 56623104 | bytes 589824 | tf_op jit(solution)/shard_map/pallas_call | solution.py:160
  22.6 0.0 collective-permute-done.9.refs_4_
  22.6 0.6 %collective-permute-done.10.refs_5_ = bf16[48,3072]{1,0:T(8,128)(2,1)S(1)} collective-permute-done((bf16[48,3072]{1,0:T(8,128)(2,1)S(1)}, bf16[48,3072]{1,0:T(8,128)(2,1)S(1)}, u32[]{:S(2)}, u32[]{:S(2)}) %collective-permute-start.10) | collective-permute-done | bytes 294944 | tf_op jit(solution)/shard_map/ppermute | solution.py:235
  23.2 0.0 collective-permute-done.7.refs_1_
  23.2 0.5 %shard_map.85 = (bf16[48,2048]{1,0:T(8,128)(2,1)S(1)}, f32[24,2048]{1,0:T(8,128)S(1)}, f32[24,2048]{1,0:T(8,128)S(1)}) custom-call(bf16[96,384]{1,0:T(8,128)(2,1)S(1)} %shard_map.84.att, bf16[96,3072]{1,0:T(8,128)(2,1)S(1)} %copy-done, bf16[96,3072]{1,0:T(8,128)(2,1)S(1)} %collective-permute-done.7.refs_1_, ...), custom_call_target="tpu_custom_call" | custom-call | flops 150994944 | bytes 1572864 | tf_op jit(solution)/shard_map/pallas_call | solution.py:203
  23.8 2.0 %collective-permute-start.11 = (bf16[48,2048]{1,0:T(8,128)(2,1)S(1)}, bf16[48,2048]{1,0:T(8,128)(2,1)S(1)}, u32[]{:S(2)}, u32[]{:S(2)}) collective-permute-start(bf16[48,2048]{1,0:T(8,128)(2,1)S(1)} %get-tuple-element.32), channel_id=1, source_target_pairs={{0,4},{1,5},{2,6},{3,7},{4,0},{5,1},{6,2},{7,3},{8,12},{9,13},{10,... | collective-permute-start | bytes 589832 | tf_op jit(solution)/shard_map/ppermute | solution.py:235
  25.8 0.3 shard_map.86
  26.2 0.0 copy-start.1
  26.2 1.4 %collective-permute-start.13 = (bf16[24,1024]{1,0:T(8,128)(2,1)S(1)}, bf16[24,1024]{1,0:T(8,128)(2,1)S(1)}, u32[]{:S(2)}, u32[]{:S(2)}) collective-permute-start(bf16[24,1024]{1,0:T(8,128)(2,1)S(1)} %get-tuple-element.36), channel_id=1, source_target_pairs={{0,12},{1,13},{2,14},{3,15},{4,8},{5,9},{6,10},{7,11},{8,4},{9,5},... | collective-permute-start | bytes 147464 | tf_op jit(solution)/shard_map/ppermute | solution.py:235
  27.6 0.2 collective-permute-start.14
  27.8 2.9 %collective-permute-start.15 = (bf16[24,1024]{1,0:T(8,128)(2,1)S(1)}, bf16[24,1024]{1,0:T(8,128)(2,1)S(1)}, u32[]{:S(2)}, u32[]{:S(2)}) collective-permute-start(bf16[24,1024]{1,0:T(8,128)(2,1)S(1)} %get-tuple-element.38), channel_id=1, source_target_pairs={{0,4},{1,5},{2,6},{3,7},{4,0},{5,1},{6,2},{7,3},{8,12},{9,13},{10,... | collective-permute-start | bytes 147464 | tf_op jit(solution)/shard_map/ppermute | solution.py:235
  30.6 1.8 %collective-permute-done.11 = bf16[48,2048]{1,0:T(8,128)(2,1)S(1)} collective-permute-done((bf16[48,2048]{1,0:T(8,128)(2,1)S(1)}, bf16[48,2048]{1,0:T(8,128)(2,1)S(1)}, u32[]{:S(2)}, u32[]{:S(2)}) %collective-permute-start.11) | collective-permute-done | bytes 196640 | tf_op jit(solution)/shard_map/ppermute | solution.py:235
  32.5 1.0 %collective-permute-start.12 = (bf16[24,2048]{1,0:T(8,128)(2,1)S(1)}, bf16[24,2048]{1,0:T(8,128)(2,1)S(1)}, u32[]{:S(2)}, u32[]{:S(2)}) collective-permute-start(bf16[24,2048]{1,0:T(8,128)(2,1)S(1)} %add_convert_fusion), channel_id=1, source_target_pairs={{0,8},{1,9},{2,10},{3,11},{4,12},{5,13},{6,14},{7,15},{8,0},{9,1},... | collective-permute-start | bytes 294920 | tf_op jit(solution)/shard_map/ppermute | solution.py:235
  33.5 0.4 collective-permute-done.13
  33.9 0.0 collective-permute-done.14
  33.9 0.3 collective-permute-done.15
  34.3 4.9 %collective-permute-done.12 = bf16[24,2048]{1,0:T(8,128)(2,1)S(1)} collective-permute-done((bf16[24,2048]{1,0:T(8,128)(2,1)S(1)}, bf16[24,2048]{1,0:T(8,128)(2,1)S(1)}, u32[]{:S(2)}, u32[]{:S(2)}) %collective-permute-start.12) | collective-permute-done | bytes 98336 | tf_op jit(solution)/shard_map/ppermute | solution.py:235
  39.2 0.0 copy-done.1
  39.2 0.7 %fusion = bf16[24,3072]{1,0:T(8,128)(2,1)} fusion(f32[24,1024]{1,0:T(8,128)S(1)} %convert_add_fusion.1, f32[24,2048]{1,0:T(8,128)S(1)} %convert_add_fusion, f32[3072]{0:T(1024)S(1)} %copy-done.1), kind=kLoop, calls=%fused_computation.1 | loop fusion | flops 221184 | bytes 454656 | tf_op jit(solution)/shard_map/convert_element_type | solution.py:301
  (7 shorter events, 0.1 us)
Async XLA Ops:
  1.0 13.3 %collective-permute-start.3 = (bf16[48,3072]{1,0:T(8,128)(2,1)S(1)}, bf16[48,3072]{1,0:T(8,128)(2,1)S(1)}, u32[]{:S(2)}, u32[]{:S(2)}) collective-permute-start(bf16[48,3072]{1,0:T(8,128)(2,1)S(1)} %shard_map.83), channel_id=1, source_target_pairs={{0,2},{1,3},{2,0},{3,1},{4,6},{5,7},{6,4},{7,5},{8,10},{9,11},{10,... | collective-permute-start | bytes 884744 | tf_op jit(solution)/shard_map/ppermute | solution.py:235
  4.1 12.4 %copy-start = (bf16[96,3072]{1,0:T(8,128)(2,1)S(1)}, bf16[96,3072]{1,0:T(8,128)(2,1)}, u32[]{:S(2)}) copy-start(bf16[96,3072]{1,0:T(8,128)(2,1)} %refs_0_.5) | copy-start | bytes 1769476
  5.5 6.1 %collective-permute-start = (bf16[24,1152]{1,0:T(8,128)(2,1)S(1)}, bf16[24,1152]{1,0:T(8,128)(2,1)S(1)}, u32[]{:S(2)}, u32[]{:S(2)}) collective-permute-start(bf16[24,1152]{1,0:T(8,128)(2,1)S(1)} %get-tuple-element.22), channel_id=1, source_target_pairs={{0,12},{1,13},{2,14},{3,15},{4,8},{5,9},{6,10},{7,11},{8,4},{9,5},... | collective-permute-start | bytes 165896 | tf_op jit(solution)/shard_map/ppermute | solution.py:235
  9.2 4.2 %collective-permute-start.1 = (bf16[24,1152]{1,0:T(8,128)(2,1)S(1)}, bf16[24,1152]{1,0:T(8,128)(2,1)S(1)}, u32[]{:S(2)}, u32[]{:S(2)}) collective-permute-start(bf16[24,1152]{1,0:T(8,128)(2,1)S(1)} %get-tuple-element.23), channel_id=1, source_target_pairs={{0,4},{1,5},{2,6},{3,7},{4,0},{5,1},{6,2},{7,3},{8,12},{9,13},{10,... | collective-permute-start | bytes 165896 | tf_op jit(solution)/shard_map/ppermute | solution.py:235
  9.2 5.1 %collective-permute-start.2 = (bf16[24,1152]{1,0:T(8,128)(2,1)S(1)}, bf16[24,1152]{1,0:T(8,128)(2,1)S(1)}, u32[]{:S(2)}, u32[]{:S(2)}) collective-permute-start(bf16[24,1152]{1,0:T(8,128)(2,1)S(1)} %get-tuple-element.24), channel_id=1, source_target_pairs={{0,8},{1,9},{2,10},{3,11},{4,12},{5,13},{6,14},{7,15},{8,0},{9,1},... | collective-permute-start | bytes 165896 | tf_op jit(solution)/shard_map/ppermute | solution.py:235
  14.4 5.2 %collective-permute-start.5 = (bf16[96,768]{1,0:T(8,128)(2,1)S(1)}, bf16[96,768]{1,0:T(8,128)(2,1)S(1)}, u32[]{:S(2)}, u32[]{:S(2)}) collective-permute-start(bf16[96,768]{1,0:T(8,128)(2,1)S(1)} %pad_maximum_fusion.refs_4_), channel_id=1, source_target_pairs={{0,2},{1,3},{2,0},{3,1},{4,6},{5,7},{6,4},{7,5},{8,10},{9,11},{10,... | collective-permute-start | bytes 442376 | tf_op jit(solution)/shard_map/ppermute | solution.py:235
  14.9 6.7 %collective-permute-start.8 = (bf16[48,3072]{1,0:T(8,128)(2,1)S(1)}, bf16[48,3072]{1,0:T(8,128)(2,1)S(1)}, u32[]{:S(2)}, u32[]{:S(2)}) collective-permute-start(bf16[48,3072]{1,0:T(8,128)(2,1)S(1)} %collective-permute-done.3.refs_2_), channel_id=1, source_target_pairs={{0,16},{16,0},{1,17},{17,1},{2,18},{18,2},{3,19},{19,3},{4,20},{20... | collective-permute-start | bytes 884744 | tf_op jit(solution)/shard_map/ppermute | solution.py:238
  16.4 6.8 %collective-permute-start.7 = (bf16[96,3072]{1,0:T(8,128)(2,1)S(1)}, bf16[96,3072]{1,0:T(8,128)(2,1)S(1)}, u32[]{:S(2)}, u32[]{:S(2)}) collective-permute-start(bf16[96,3072]{1,0:T(8,128)(2,1)S(1)} %copy-done), channel_id=1, source_target_pairs={{0,1},{1,0},{2,3},{3,2},{4,5},{5,4},{6,7},{7,6},{8,9},{9,8},{10,11... | collective-permute-start | bytes 1769480 | tf_op jit(solution)/shard_map/ppermute | solution.py:235
  16.4 3.7 %collective-permute-start.4 = (bf16[96,768]{1,0:T(8,128)(2,1)S(1)}, bf16[96,768]{1,0:T(8,128)(2,1)S(1)}, u32[]{:S(2)}, u32[]{:S(2)}) collective-permute-start(bf16[96,768]{1,0:T(8,128)(2,1)S(1)} %pad_maximum_fusion.refs_4_), channel_id=1, source_target_pairs={{0,1},{1,0},{2,3},{3,2},{4,5},{5,4},{6,7},{7,6},{8,9},{9,8},{10,11... | collective-permute-start | bytes 442376 | tf_op jit(solution)/shard_map/ppermute | solution.py:235
  19.6 1.4 %collective-permute-start.6 = (bf16[96,768]{1,0:T(8,128)(2,1)S(1)}, bf16[96,768]{1,0:T(8,128)(2,1)S(1)}, u32[]{:S(2)}, u32[]{:S(2)}) collective-permute-start(bf16[96,768]{1,0:T(8,128)(2,1)S(1)} %collective-permute-done.5.refs_6_), channel_id=1, source_target_pairs={{0,1},{1,0},{2,3},{3,2},{4,5},{5,4},{6,7},{7,6},{8,9},{9,8},{10,11... | collective-permute-start | bytes 442376 | tf_op jit(solution)/shard_map/ppermute | solution.py:235
  19.6 3.0 %collective-permute-start.9 = (bf16[48,3072]{1,0:T(8,128)(2,1)S(1)}, bf16[48,3072]{1,0:T(8,128)(2,1)S(1)}, u32[]{:S(2)}, u32[]{:S(2)}) collective-permute-start(bf16[48,3072]{1,0:T(8,128)(2,1)S(1)} %collective-permute-done.3.refs_2_), channel_id=1, source_target_pairs={{0,1},{1,0},{2,3},{3,2},{4,5},{5,4},{6,7},{7,6},{8,9},{9,8},{10,11... | collective-permute-start | bytes 884744 | tf_op jit(solution)/shard_map/ppermute | solution.py:235
  21.7 1.6 %collective-permute-start.10 = (bf16[48,3072]{1,0:T(8,128)(2,1)S(1)}, bf16[48,3072]{1,0:T(8,128)(2,1)S(1)}, u32[]{:S(2)}, u32[]{:S(2)}) collective-permute-start(bf16[48,3072]{1,0:T(8,128)(2,1)S(1)} %collective-permute-done.8.refs_3_), channel_id=1, source_target_pairs={{0,1},{1,0},{2,3},{3,2},{4,5},{5,4},{6,7},{7,6},{8,9},{9,8},{10,11... | collective-permute-start | bytes 884744 | tf_op jit(solution)/shard_map/ppermute | solution.py:235
  23.8 8.7 %collective-permute-start.11 = (bf16[48,2048]{1,0:T(8,128)(2,1)S(1)}, bf16[48,2048]{1,0:T(8,128)(2,1)S(1)}, u32[]{:S(2)}, u32[]{:S(2)}) collective-permute-start(bf16[48,2048]{1,0:T(8,128)(2,1)S(1)} %get-tuple-element.32), channel_id=1, source_target_pairs={{0,4},{1,5},{2,6},{3,7},{4,0},{5,1},{6,2},{7,3},{8,12},{9,13},{10,... | collective-permute-start | bytes 589832 | tf_op jit(solution)/shard_map/ppermute | solution.py:235
  26.2 13.0 %copy-start.1 = (f32[3072]{0:T(1024)S(1)}, f32[3072]{0:T(1024)}, u32[]{:S(2)}) copy-start(f32[3072]{0:T(1024)} %param.15) | copy-start | bytes 36868
  26.2 7.8 %collective-permute-start.13 = (bf16[24,1024]{1,0:T(8,128)(2,1)S(1)}, bf16[24,1024]{1,0:T(8,128)(2,1)S(1)}, u32[]{:S(2)}, u32[]{:S(2)}) collective-permute-start(bf16[24,1024]{1,0:T(8,128)(2,1)S(1)} %get-tuple-element.36), channel_id=1, source_target_pairs={{0,12},{1,13},{2,14},{3,15},{4,8},{5,9},{6,10},{7,11},{8,4},{9,5},... | collective-permute-start | bytes 147464 | tf_op jit(solution)/shard_map/ppermute | solution.py:235
  27.6 6.4 %collective-permute-start.14 = (bf16[24,1024]{1,0:T(8,128)(2,1)S(1)}, bf16[24,1024]{1,0:T(8,128)(2,1)S(1)}, u32[]{:S(2)}, u32[]{:S(2)}) collective-permute-start(bf16[24,1024]{1,0:T(8,128)(2,1)S(1)} %get-tuple-element.37), channel_id=1, source_target_pairs={{0,8},{1,9},{2,10},{3,11},{4,12},{5,13},{6,14},{7,15},{8,0},{9,1},... | collective-permute-start | bytes 147464 | tf_op jit(solution)/shard_map/ppermute | solution.py:235
  27.8 6.5 %collective-permute-start.15 = (bf16[24,1024]{1,0:T(8,128)(2,1)S(1)}, bf16[24,1024]{1,0:T(8,128)(2,1)S(1)}, u32[]{:S(2)}, u32[]{:S(2)}) collective-permute-start(bf16[24,1024]{1,0:T(8,128)(2,1)S(1)} %get-tuple-element.38), channel_id=1, source_target_pairs={{0,4},{1,5},{2,6},{3,7},{4,0},{5,1},{6,2},{7,3},{8,12},{9,13},{10,... | collective-permute-start | bytes 147464 | tf_op jit(solution)/shard_map/ppermute | solution.py:235
  32.5 6.6 %collective-permute-start.12 = (bf16[24,2048]{1,0:T(8,128)(2,1)S(1)}, bf16[24,2048]{1,0:T(8,128)(2,1)S(1)}, u32[]{:S(2)}, u32[]{:S(2)}) collective-permute-start(bf16[24,2048]{1,0:T(8,128)(2,1)S(1)} %add_convert_fusion), channel_id=1, source_target_pairs={{0,8},{1,9},{2,10},{3,11},{4,12},{5,13},{6,14},{7,15},{8,0},{9,1},... | collective-permute-start | bytes 294920 | tf_op jit(solution)/shard_map/ppermute | solution.py:235

commit v18 on v17

--- a/solution.py
+++ b/solution.py
@@ -229,7 +229,7 @@
     depth, model = w_out.shape
     far = members // 2
     shared = parts % 2 == 0 and members == 4 and depth % 32 == 0
-    first = model * 2 // 3 // 256 * 256
+    first = model // 2
 
     def send(x, k, j):
         return lax.ppermute(x, "patch", [(p, ((p // members) ^ k) * members + (p % members) ^ j) for p in range(patch)])
@@ -265,7 +265,7 @@
         w_core = send(after(w_own, both), 0, 1)
         y_core = send(after(y_part, both), 0, 1)
         x_part = swap(y_part)
-        x_core = send(after(x_part, *kvs), 0, 1)
+        x_core = send(after(x_part, kvs[far]), 0, 1)
         edges = (0, first, model)
         for left, right in zip(edges, edges[1:]):
             pieces = [w_own, w_core, y_part, x_part, y_core, x_core]

time: 40 us -> 41.2 us (1.030)
  waiting for transfers between devices: 16.6 us -> 17.5 us
    ppermute x15, waiting for transfers between devices: 15.9 us -> 17.5 us  [send(): lax.ppermute(x, 'patch', [(p, (p // members ^ k) * members + p % members...]
    ppermute x1, waiting for transfers between devices: 0.72 us -> 0.01 us  [swap(): return lax.ppermute(x, 'groups', [(g, g ^ 1) for g in range(parts)])]
  transfers between devices with their start and end apart: 16 -> 16, of which waited for: 11 -> 9; matrix products, arithmetic and copies ran while one was open for 0% -> 0% of each run, Pallas kernels for 7% -> 7%
where the time goes in v18:
time: 41.2 us; the launch traced here: 41.1 us
  starting transfers between devices  18.4 us (45%)
  waiting for transfers between devices  17.5 us (42%)
  Pallas kernels  4.28 us (10%)
  other arithmetic  0.77 us (2%)
    ppermute x15, waiting for transfers between devices, send(): lax.ppermute(x, 'patch', [(p, (p // members ^ k) * members + p % members...  17.5 us
    ppermute x15, starting transfers between devices, send(): lax.ppermute(x, 'patch', [(p, (p // members ^ k) * members + p % members...  16.8 us
    ppermute x1, starting transfers between devices, swap(): return lax.ppermute(x, 'groups', [(g, g ^ 1) for g in range(parts)])  1.56 us
    pallas_call x1, Pallas kernels, prepare(): pl.pallas_call(functools.partial(prepare_kernel, groups, members), out_sh...  1.45 us
    pallas_call x1, Pallas kernels, share_rows(): pl.pallas_call(share_kernel, out_shape=jax.ShapeDtypeStruct((depth // 2,...  1.03 us
    pallas_call x1, Pallas kernels, attend(): pl.pallas_call(functools.partial(attend_kernel, groups, dim), out_shape=j...  0.92 us
    pallas_call x2, Pallas kernels, project(): pl.pallas_call(functools.partial(project_kernel, members, places), out_sh...  0.88 us
  transfers between devices with their start and end apart: 16, of which 9 were waited for; matrix products, arithmetic and copies ran while one was open for 0% of the time, Pallas kernels for 7%

profile of v18, /device:TPU:0, one launch (start us, length us, event | category | flops | bytes accessed | tf_op | source)
XLA Modules:
  0.0 41.1 jit_solution(8499945134873173402)
XLA Ops:
  0.0 1.0 %shard_map.83 = bf16[48,3072]{1,0:T(8,128)(2,1)S(1)} custom-call(bf16[96,3072]{1,0:T(8,128)(2,1)} %refs_0_.5), custom_call_target="tpu_custom_call" | custom-call | bytes 589824 | tf_op jit(solution)/shard_map/pallas_call | solution.py:117
  1.0 3.0 %collective-permute-start.3 = (bf16[48,3072]{1,0:T(8,128)(2,1)S(1)}, bf16[48,3072]{1,0:T(8,128)(2,1)S(1)}, u32[]{:S(2)}, u32[]{:S(2)}) collective-permute-start(bf16[48,3072]{1,0:T(8,128)(2,1)S(1)} %shard_map.83), channel_id=1, source_target_pairs={{0,2},{1,3},{2,0},{3,1},{4,6},{5,7},{6,4},{7,5},{8,10},{9,11},{10,... | collective-permute-start | bytes 884744 | tf_op jit(solution)/shard_map/ppermute | solution.py:235
  4.1 0.0 copy-start
  4.1 1.5 %shard_map.82 = (bf16[24,384]{1,0:T(8,128)(2,1)S(1)}, bf16[24,768]{1,0:T(8,128)(2,1)S(1)}, bf16[24,1152]{1,0:T(8,128)(2,1)S(1)}, bf16[24,1152]{1,0:T(8,128)(2,1)S(1)}, bf16[24,1152]{1,0:T(8,128)(2,1)S(1)}) custom-call(bf16[24,1536]{1,0:T(8,128)(2,1)} %refs_0_.3, bf16[24,1536]{1,0:T(8,128)(2,1)} %refs_1_.1, bf16[24,1536]{1,0:T(8,128)(2,1)} %refs_2_.1, ...), custom_call_target="tpu_custom_call" | custom-call | flops 368640 | bytes 516096 | tf_op jit(solution)/shard_map/pallas_call | solution.py:81
  5.5 3.7 %collective-permute-start = (bf16[24,1152]{1,0:T(8,128)(2,1)S(1)}, bf16[24,1152]{1,0:T(8,128)(2,1)S(1)}, u32[]{:S(2)}, u32[]{:S(2)}) collective-permute-start(bf16[24,1152]{1,0:T(8,128)(2,1)S(1)} %get-tuple-element.22), channel_id=1, source_target_pairs={{0,12},{1,13},{2,14},{3,15},{4,8},{5,9},{6,10},{7,11},{8,4},{9,5},... | collective-permute-start | bytes 165896 | tf_op jit(solution)/shard_map/ppermute | solution.py:235
  9.2 0.0 collective-permute-start.2
  9.2 0.8 %collective-permute-start.1 = (bf16[24,1152]{1,0:T(8,128)(2,1)S(1)}, bf16[24,1152]{1,0:T(8,128)(2,1)S(1)}, u32[]{:S(2)}, u32[]{:S(2)}) collective-permute-start(bf16[24,1152]{1,0:T(8,128)(2,1)S(1)} %get-tuple-element.23), channel_id=1, source_target_pairs={{0,4},{1,5},{2,6},{3,7},{4,0},{5,1},{6,2},{7,3},{8,12},{9,13},{10,... | collective-permute-start | bytes 165896 | tf_op jit(solution)/shard_map/ppermute | solution.py:235
  10.0 2.2 %collective-permute-done.refs_0_ = bf16[24,1152]{1,0:T(8,128)(2,1)S(1)} collective-permute-done((bf16[24,1152]{1,0:T(8,128)(2,1)S(1)}, bf16[24,1152]{1,0:T(8,128)(2,1)S(1)}, u32[]{:S(2)}, u32[]{:S(2)}) %collective-permute-start) | collective-permute-done | bytes 55328 | tf_op jit(solution)/shard_map/ppermute | solution.py:235
  12.2 2.0 %collective-permute-done.2.refs_2_ = bf16[24,1152]{1,0:T(8,128)(2,1)S(1)} collective-permute-done((bf16[24,1152]{1,0:T(8,128)(2,1)S(1)}, bf16[24,1152]{1,0:T(8,128)(2,1)S(1)}, u32[]{:S(2)}, u32[]{:S(2)}) %collective-permute-start.2) | collective-permute-done | bytes 55328 | tf_op jit(solution)/shard_map/ppermute | solution.py:235
  14.3 0.0 collective-permute-done.1.refs_1_
  14.3 0.0 collective-permute-done.3.refs_2_
  14.3 1.6 %collective-permute-start.8 = (bf16[48,3072]{1,0:T(8,128)(2,1)S(1)}, bf16[48,3072]{1,0:T(8,128)(2,1)S(1)}, u32[]{:S(2)}, u32[]{:S(2)}) collective-permute-start(bf16[48,3072]{1,0:T(8,128)(2,1)S(1)} %collective-permute-done.3.refs_2_), channel_id=1, source_target_pairs={{0,16},{16,0},{1,17},{17,1},{2,18},{18,2},{3,19},{19,3},{4,20},{20... | collective-permute-start | bytes 884744 | tf_op jit(solution)/shard_map/ppermute | solution.py:238
  15.9 0.0 copy-done
  15.9 0.0 collective-permute-start.7
  15.9 0.5 %collective-permute-start.5 = (bf16[96,768]{1,0:T(8,128)(2,1)S(1)}, bf16[96,768]{1,0:T(8,128)(2,1)S(1)}, u32[]{:S(2)}, u32[]{:S(2)}) collective-permute-start(bf16[96,768]{1,0:T(8,128)(2,1)S(1)} %pad_maximum_fusion.refs_4_), channel_id=1, source_target_pairs={{0,2},{1,3},{2,0},{3,1},{4,6},{5,7},{6,4},{7,5},{8,10},{9,11},{10,... | collective-permute-start | bytes 442376 | tf_op jit(solution)/shard_map/ppermute | solution.py:235
  16.4 0.2 collective-permute-start.9
  16.6 5.5 %collective-permute-done.5.refs_6_ = bf16[96,768]{1,0:T(8,128)(2,1)S(1)} collective-permute-done((bf16[96,768]{1,0:T(8,128)(2,1)S(1)}, bf16[96,768]{1,0:T(8,128)(2,1)S(1)}, u32[]{:S(2)}, u32[]{:S(2)}) %collective-permute-start.5) | collective-permute-done | bytes 147488 | tf_op jit(solution)/shard_map/ppermute | solution.py:235
  22.1 0.0 collective-permute-done.8.refs_3_
  22.1 0.0 collective-permute-start.10
  22.1 0.5 %collective-permute-start.4 = (bf16[96,768]{1,0:T(8,128)(2,1)S(1)}, bf16[96,768]{1,0:T(8,128)(2,1)S(1)}, u32[]{:S(2)}, u32[]{:S(2)}) collective-permute-start(bf16[96,768]{1,0:T(8,128)(2,1)S(1)} %pad_maximum_fusion.refs_4_), channel_id=1, source_target_pairs={{0,1},{1,0},{2,3},{3,2},{4,5},{5,4},{6,7},{7,6},{8,9},{9,8},{10,11... | collective-permute-start | bytes 442376 | tf_op jit(solution)/shard_map/ppermute | solution.py:235
  22.6 0.0 collective-permute-start.6
  22.6 1.3 %collective-permute-done.4.refs_5_ = bf16[96,768]{1,0:T(8,128)(2,1)S(1)} collective-permute-done((bf16[96,768]{1,0:T(8,128)(2,1)S(1)}, bf16[96,768]{1,0:T(8,128)(2,1)S(1)}, u32[]{:S(2)}, u32[]{:S(2)}) %collective-permute-start.4) | collective-permute-done | bytes 147488 | tf_op jit(solution)/shard_map/ppermute | solution.py:235
  23.9 0.2 collective-permute-done.6.refs_7_
  24.1 0.9 %shard_map.84.att = bf16[96,384]{1,0:T(8,128)(2,1)S(1)} custom-call(bf16[24,1152]{1,0:T(8,128)(2,1)S(1)} %collective-permute-done.refs_0_, bf16[24,1152]{1,0:T(8,128)(2,1)S(1)} %collective-permute-done.1.refs_1_, bf16[24,1152]{1,0:T(8,128)(2,1)S(1)} %collective-permute-done.2.refs_2_, bf16[24,384]{1,0:T(8,128)(2,1)S(1)} %get-tuple-element.25.refs_3_, ...), custom_call_target="tpu_custom_call" | custom-call | flops 56623104 | bytes 589824 | tf_op jit(solution)/shard_map/pallas_call | solution.py:160
  25.1 0.0 collective-permute-done.9.refs_4_
  25.1 0.0 collective-permute-done.10.refs_5_
  25.1 0.0 collective-permute-done.7.refs_1_
  25.1 0.4 %shard_map.85 = (bf16[48,1536]{1,0:T(8,128)(2,1)S(1)}, f32[24,1536]{1,0:T(8,128)S(1)}, f32[24,1536]{1,0:T(8,128)S(1)}) custom-call(bf16[96,384]{1,0:T(8,128)(2,1)S(1)} %shard_map.84.att, bf16[96,3072]{1,0:T(8,128)(2,1)S(1)} %copy-done, bf16[96,3072]{1,0:T(8,128)(2,1)S(1)} %collective-permute-done.7.refs_1_, ...), custom_call_target="tpu_custom_call" | custom-call | flops 113246208 | bytes 1179648 | tf_op jit(solution)/shard_map/pallas_call | solution.py:203
  25.5 0.7 %collective-permute-start.11 = (bf16[48,1536]{1,0:T(8,128)(2,1)S(1)}, bf16[48,1536]{1,0:T(8,128)(2,1)S(1)}, u32[]{:S(2)}, u32[]{:S(2)}) collective-permute-start(bf16[48,1536]{1,0:T(8,128)(2,1)S(1)} %get-tuple-element.32), channel_id=1, source_target_pairs={{0,4},{1,5},{2,6},{3,7},{4,0},{5,1},{6,2},{7,3},{8,12},{9,13},{10,... | collective-permute-start | bytes 442376 | tf_op jit(solution)/shard_map/ppermute | solution.py:235
  26.3 0.4 %shard_map.86 = (bf16[24,1536]{1,0:T(8,128)(2,1)S(1)}, bf16[24,1536]{1,0:T(8,128)(2,1)S(1)}, bf16[24,1536]{1,0:T(8,128)(2,1)S(1)}, f32[24,1536]{1,0:T(8,128)S(1)}) custom-call(bf16[96,384]{1,0:T(8,128)(2,1)S(1)} %shard_map.84.att, bf16[96,3072]{1,0:T(8,128)(2,1)S(1)} %copy-done, bf16[96,3072]{1,0:T(8,128)(2,1)S(1)} %collective-permute-done.7.refs_1_, ...), custom_call_target="tpu_custom_call" | custom-call | flops 113246208 | bytes 1179648 | tf_op jit(solution)/shard_map/pallas_call | solution.py:203
  26.7 0.0 copy-start.1
  26.7 2.9 %collective-permute-start.13 = (bf16[24,1536]{1,0:T(8,128)(2,1)S(1)}, bf16[24,1536]{1,0:T(8,128)(2,1)S(1)}, u32[]{:S(2)}, u32[]{:S(2)}) collective-permute-start(bf16[24,1536]{1,0:T(8,128)(2,1)S(1)} %get-tuple-element.36), channel_id=1, source_target_pairs={{0,12},{1,13},{2,14},{3,15},{4,8},{5,9},{6,10},{7,11},{8,4},{9,5},... | collective-permute-start | bytes 221192 | tf_op jit(solution)/shard_map/ppermute | solution.py:235
  29.6 0.0 collective-permute-start.14
  29.6 1.6 %collective-permute-start.15 = (bf16[24,1536]{1,0:T(8,128)(2,1)S(1)}, bf16[24,1536]{1,0:T(8,128)(2,1)S(1)}, u32[]{:S(2)}, u32[]{:S(2)}) collective-permute-start(bf16[24,1536]{1,0:T(8,128)(2,1)S(1)} %get-tuple-element.38), channel_id=1, source_target_pairs={{0,4},{1,5},{2,6},{3,7},{4,0},{5,1},{6,2},{7,3},{8,12},{9,13},{10,... | collective-permute-start | bytes 221192 | tf_op jit(solution)/shard_map/ppermute | solution.py:235
  31.2 0.3 collective-permute-done.11
  31.5 2.9 %collective-permute-start.12 = (bf16[24,1536]{1,0:T(8,128)(2,1)S(1)}, bf16[24,1536]{1,0:T(8,128)(2,1)S(1)}, u32[]{:S(2)}, u32[]{:S(2)}) collective-permute-start(bf16[24,1536]{1,0:T(8,128)(2,1)S(1)} %add_convert_fusion), channel_id=1, source_target_pairs={{0,8},{1,9},{2,10},{3,11},{4,12},{5,13},{6,14},{7,15},{8,0},{9,1},... | collective-permute-start | bytes 221192 | tf_op jit(solution)/shard_map/ppermute | solution.py:235
  34.4 1.0 %collective-permute-done.13 = bf16[24,1536]{1,0:T(8,128)(2,1)S(1)} collective-permute-done((bf16[24,1536]{1,0:T(8,128)(2,1)S(1)}, bf16[24,1536]{1,0:T(8,128)(2,1)S(1)}, u32[]{:S(2)}, u32[]{:S(2)}) %collective-permute-start.13) | collective-permute-done | bytes 73760 | tf_op jit(solution)/shard_map/ppermute | solution.py:235
  35.4 4.0 %collective-permute-done.14 = bf16[24,1536]{1,0:T(8,128)(2,1)S(1)} collective-permute-done((bf16[24,1536]{1,0:T(8,128)(2,1)S(1)}, bf16[24,1536]{1,0:T(8,128)(2,1)S(1)}, u32[]{:S(2)}, u32[]{:S(2)}) %collective-permute-start.14) | collective-permute-done | bytes 73760 | tf_op jit(solution)/shard_map/ppermute | solution.py:235
  39.4 0.0 collective-permute-done.15
  39.4 0.9 %collective-permute-done.12 = bf16[24,1536]{1,0:T(8,128)(2,1)S(1)} collective-permute-done((bf16[24,1536]{1,0:T(8,128)(2,1)S(1)}, bf16[24,1536]{1,0:T(8,128)(2,1)S(1)}, u32[]{:S(2)}, u32[]{:S(2)}) %collective-permute-start.12) | collective-permute-done | bytes 73760 | tf_op jit(solution)/shard_map/ppermute | solution.py:235
  40.4 0.0 copy-done.1
  40.4 0.7 %fusion = bf16[24,3072]{1,0:T(8,128)(2,1)} fusion(f32[24,1536]{1,0:T(8,128)S(1)} %convert_add_fusion, f32[24,1536]{1,0:T(8,128)S(1)} %convert_add_fusion.1, f32[3072]{0:T(1024)S(1)} %copy-done.1), kind=kLoop, calls=%fused_computation.1 | loop fusion | flops 221184 | bytes 454656 | tf_op jit(solution)/shard_map/convert_element_type | solution.py:301
  (7 shorter events, 0.1 us)
Async XLA Ops:
  1.0 13.3 %collective-permute-start.3 = (bf16[48,3072]{1,0:T(8,128)(2,1)S(1)}, bf16[48,3072]{1,0:T(8,128)(2,1)S(1)}, u32[]{:S(2)}, u32[]{:S(2)}) collective-permute-start(bf16[48,3072]{1,0:T(8,128)(2,1)S(1)} %shard_map.83), channel_id=1, source_target_pairs={{0,2},{1,3},{2,0},{3,1},{4,6},{5,7},{6,4},{7,5},{8,10},{9,11},{10,... | collective-permute-start | bytes 884744 | tf_op jit(solution)/shard_map/ppermute | solution.py:235
  4.1 11.8 %copy-start = (bf16[96,3072]{1,0:T(8,128)(2,1)S(1)}, bf16[96,3072]{1,0:T(8,128)(2,1)}, u32[]{:S(2)}) copy-start(bf16[96,3072]{1,0:T(8,128)(2,1)} %refs_0_.5) | copy-start | bytes 1769476
  5.5 6.7 %collective-permute-start = (bf16[24,1152]{1,0:T(8,128)(2,1)S(1)}, bf16[24,1152]{1,0:T(8,128)(2,1)S(1)}, u32[]{:S(2)}, u32[]{:S(2)}) collective-permute-start(bf16[24,1152]{1,0:T(8,128)(2,1)S(1)} %get-tuple-element.22), channel_id=1, source_target_pairs={{0,12},{1,13},{2,14},{3,15},{4,8},{5,9},{6,10},{7,11},{8,4},{9,5},... | collective-permute-start | bytes 165896 | tf_op jit(solution)/shard_map/ppermute | solution.py:235
  9.2 5.1 %collective-permute-start.2 = (bf16[24,1152]{1,0:T(8,128)(2,1)S(1)}, bf16[24,1152]{1,0:T(8,128)(2,1)S(1)}, u32[]{:S(2)}, u32[]{:S(2)}) collective-permute-start(bf16[24,1152]{1,0:T(8,128)(2,1)S(1)} %get-tuple-element.24), channel_id=1, source_target_pairs={{0,8},{1,9},{2,10},{3,11},{4,12},{5,13},{6,14},{7,15},{8,0},{9,1},... | collective-permute-start | bytes 165896 | tf_op jit(solution)/shard_map/ppermute | solution.py:235
  9.2 5.1 %collective-permute-start.1 = (bf16[24,1152]{1,0:T(8,128)(2,1)S(1)}, bf16[24,1152]{1,0:T(8,128)(2,1)S(1)}, u32[]{:S(2)}, u32[]{:S(2)}) collective-permute-start(bf16[24,1152]{1,0:T(8,128)(2,1)S(1)} %get-tuple-element.23), channel_id=1, source_target_pairs={{0,4},{1,5},{2,6},{3,7},{4,0},{5,1},{6,2},{7,3},{8,12},{9,13},{10,... | collective-permute-start | bytes 165896 | tf_op jit(solution)/shard_map/ppermute | solution.py:235
  14.3 7.8 %collective-permute-start.8 = (bf16[48,3072]{1,0:T(8,128)(2,1)S(1)}, bf16[48,3072]{1,0:T(8,128)(2,1)S(1)}, u32[]{:S(2)}, u32[]{:S(2)}) collective-permute-start(bf16[48,3072]{1,0:T(8,128)(2,1)S(1)} %collective-permute-done.3.refs_2_), channel_id=1, source_target_pairs={{0,16},{16,0},{1,17},{17,1},{2,18},{18,2},{3,19},{19,3},{4,20},{20... | collective-permute-start | bytes 884744 | tf_op jit(solution)/shard_map/ppermute | solution.py:238
  15.9 9.2 %collective-permute-start.7 = (bf16[96,3072]{1,0:T(8,128)(2,1)S(1)}, bf16[96,3072]{1,0:T(8,128)(2,1)S(1)}, u32[]{:S(2)}, u32[]{:S(2)}) collective-permute-start(bf16[96,3072]{1,0:T(8,128)(2,1)S(1)} %copy-done), channel_id=1, source_target_pairs={{0,1},{1,0},{2,3},{3,2},{4,5},{5,4},{6,7},{7,6},{8,9},{9,8},{10,11... | collective-permute-start | bytes 1769480 | tf_op jit(solution)/shard_map/ppermute | solution.py:235
  15.9 6.3 %collective-permute-start.5 = (bf16[96,768]{1,0:T(8,128)(2,1)S(1)}, bf16[96,768]{1,0:T(8,128)(2,1)S(1)}, u32[]{:S(2)}, u32[]{:S(2)}) collective-permute-start(bf16[96,768]{1,0:T(8,128)(2,1)S(1)} %pad_maximum_fusion.refs_4_), channel_id=1, source_target_pairs={{0,2},{1,3},{2,0},{3,1},{4,6},{5,7},{6,4},{7,5},{8,10},{9,11},{10,... | collective-permute-start | bytes 442376 | tf_op jit(solution)/shard_map/ppermute | solution.py:235
  16.4 8.7 %collective-permute-start.9 = (bf16[48,3072]{1,0:T(8,128)(2,1)S(1)}, bf16[48,3072]{1,0:T(8,128)(2,1)S(1)}, u32[]{:S(2)}, u32[]{:S(2)}) collective-permute-start(bf16[48,3072]{1,0:T(8,128)(2,1)S(1)} %collective-permute-done.3.refs_2_), channel_id=1, source_target_pairs={{0,1},{1,0},{2,3},{3,2},{4,5},{5,4},{6,7},{7,6},{8,9},{9,8},{10,11... | collective-permute-start | bytes 884744 | tf_op jit(solution)/shard_map/ppermute | solution.py:235
  22.1 2.9 %collective-permute-start.10 = (bf16[48,3072]{1,0:T(8,128)(2,1)S(1)}, bf16[48,3072]{1,0:T(8,128)(2,1)S(1)}, u32[]{:S(2)}, u32[]{:S(2)}) collective-permute-start(bf16[48,3072]{1,0:T(8,128)(2,1)S(1)} %collective-permute-done.8.refs_3_), channel_id=1, source_target_pairs={{0,1},{1,0},{2,3},{3,2},{4,5},{5,4},{6,7},{7,6},{8,9},{9,8},{10,11... | collective-permute-start | bytes 884744 | tf_op jit(solution)/shard_map/ppermute | solution.py:235
  22.1 1.8 %collective-permute-start.4 = (bf16[96,768]{1,0:T(8,128)(2,1)S(1)}, bf16[96,768]{1,0:T(8,128)(2,1)S(1)}, u32[]{:S(2)}, u32[]{:S(2)}) collective-permute-start(bf16[96,768]{1,0:T(8,128)(2,1)S(1)} %pad_maximum_fusion.refs_4_), channel_id=1, source_target_pairs={{0,1},{1,0},{2,3},{3,2},{4,5},{5,4},{6,7},{7,6},{8,9},{9,8},{10,11... | collective-permute-start | bytes 442376 | tf_op jit(solution)/shard_map/ppermute | solution.py:235
  22.6 1.5 %collective-permute-start.6 = (bf16[96,768]{1,0:T(8,128)(2,1)S(1)}, bf16[96,768]{1,0:T(8,128)(2,1)S(1)}, u32[]{:S(2)}, u32[]{:S(2)}) collective-permute-start(bf16[96,768]{1,0:T(8,128)(2,1)S(1)} %collective-permute-done.5.refs_6_), channel_id=1, source_target_pairs={{0,1},{1,0},{2,3},{3,2},{4,5},{5,4},{6,7},{7,6},{8,9},{9,8},{10,11... | collective-permute-start | bytes 442376 | tf_op jit(solution)/shard_map/ppermute | solution.py:235
  25.5 6.0 %collective-permute-start.11 = (bf16[48,1536]{1,0:T(8,128)(2,1)S(1)}, bf16[48,1536]{1,0:T(8,128)(2,1)S(1)}, u32[]{:S(2)}, u32[]{:S(2)}) collective-permute-start(bf16[48,1536]{1,0:T(8,128)(2,1)S(1)} %get-tuple-element.32), channel_id=1, source_target_pairs={{0,4},{1,5},{2,6},{3,7},{4,0},{5,1},{6,2},{7,3},{8,12},{9,13},{10,... | collective-permute-start | bytes 442376 | tf_op jit(solution)/shard_map/ppermute | solution.py:235
  26.7 13.7 %copy-start.1 = (f32[3072]{0:T(1024)S(1)}, f32[3072]{0:T(1024)}, u32[]{:S(2)}) copy-start(f32[3072]{0:T(1024)} %param.15) | copy-start | bytes 36868
  26.7 8.7 %collective-permute-start.13 = (bf16[24,1536]{1,0:T(8,128)(2,1)S(1)}, bf16[24,1536]{1,0:T(8,128)(2,1)S(1)}, u32[]{:S(2)}, u32[]{:S(2)}) collective-permute-start(bf16[24,1536]{1,0:T(8,128)(2,1)S(1)} %get-tuple-element.36), channel_id=1, source_target_pairs={{0,12},{1,13},{2,14},{3,15},{4,8},{5,9},{6,10},{7,11},{8,4},{9,5},... | collective-permute-start | bytes 221192 | tf_op jit(solution)/shard_map/ppermute | solution.py:235
  29.6 9.8 %collective-permute-start.14 = (bf16[24,1536]{1,0:T(8,128)(2,1)S(1)}, bf16[24,1536]{1,0:T(8,128)(2,1)S(1)}, u32[]{:S(2)}, u32[]{:S(2)}) collective-permute-start(bf16[24,1536]{1,0:T(8,128)(2,1)S(1)} %get-tuple-element.37), channel_id=1, source_target_pairs={{0,8},{1,9},{2,10},{3,11},{4,12},{5,13},{6,14},{7,15},{8,0},{9,1},... | collective-permute-start | bytes 221192 | tf_op jit(solution)/shard_map/ppermute | solution.py:235
  29.6 9.8 %collective-permute-start.15 = (bf16[24,1536]{1,0:T(8,128)(2,1)S(1)}, bf16[24,1536]{1,0:T(8,128)(2,1)S(1)}, u32[]{:S(2)}, u32[]{:S(2)}) collective-permute-start(bf16[24,1536]{1,0:T(8,128)(2,1)S(1)} %get-tuple-element.38), channel_id=1, source_target_pairs={{0,4},{1,5},{2,6},{3,7},{4,0},{5,1},{6,2},{7,3},{8,12},{9,13},{10,... | collective-permute-start | bytes 221192 | tf_op jit(solution)/shard_map/ppermute | solution.py:235
  31.5 8.8 %collective-permute-start.12 = (bf16[24,1536]{1,0:T(8,128)(2,1)S(1)}, bf16[24,1536]{1,0:T(8,128)(2,1)S(1)}, u32[]{:S(2)}, u32[]{:S(2)}) collective-permute-start(bf16[24,1536]{1,0:T(8,128)(2,1)S(1)} %add_convert_fusion), channel_id=1, source_target_pairs={{0,8},{1,9},{2,10},{3,11},{4,12},{5,13},{6,14},{7,15},{8,0},{9,1},... | collective-permute-start | bytes 221192 | tf_op jit(solution)/shard_map/ppermute | solution.py:235

commit v19 on v16

--- a/solution.py
+++ b/solution.py
@@ -267,7 +267,7 @@
         x_part = swap(y_part)
         edges = (0, first, model)
         for left, right in zip(edges, edges[1:]):
-            x_core = send(after(x_part, kvs[far])[:, left:right], 0, 1)
+            x_core = send(after(x_part, att if left else kvs[far])[:, left:right], 0, 1)
             pieces = [w_own, w_core, y_part, x_part, y_core, x_core]
             places = [(0, None, left), (1, None, left), (2, 0, left), (2, 1, left), (3, 0, left), (3, 1, 0)]
             jobs.append((right - left, pieces, places))

time: 37.8 us -> 41.4 us (1.095)
  waiting for transfers between devices: 14.3 us -> 17 us
  starting transfers between devices: 18.2 us -> 18.9 us
    ppermute x1, waiting for transfers between devices: 0.01 us -> 1.94 us  [swap(): return lax.ppermute(x, 'groups', [(g, g ^ 1) for g in range(parts)])]
    ppermute x16, starting transfers between devices: 16.5 us -> 17.4 us  [send(): lax.ppermute(x, 'patch', [(p, (p // members ^ k) * members + p % members...]
    ppermute x16, waiting for transfers between devices: 14.3 us -> 15.1 us  [send(): lax.ppermute(x, 'patch', [(p, (p // members ^ k) * members + p % members...]
  transfers between devices with their start and end apart: 17 -> 17, of which waited for: 8 -> 8; matrix products, arithmetic and copies ran while one was open for 0% -> 0% of each run, Pallas kernels for 9% -> 8%
where the time goes in v19:
time: 41.4 us; the launch traced here: 41.2 us
  starting transfers between devices  18.9 us (46%)
  waiting for transfers between devices  17 us (41%)
  Pallas kernels  4.29 us (10%)
  other arithmetic  0.79 us (2%)
    ppermute x16, starting transfers between devices, send(): lax.ppermute(x, 'patch', [(p, (p // members ^ k) * members + p % members...  17.4 us
    ppermute x16, waiting for transfers between devices, send(): lax.ppermute(x, 'patch', [(p, (p // members ^ k) * members + p % members...  15.1 us
    ppermute x1, waiting for transfers between devices, swap(): return lax.ppermute(x, 'groups', [(g, g ^ 1) for g in range(parts)])  1.94 us
    ppermute x1, starting transfers between devices, swap(): return lax.ppermute(x, 'groups', [(g, g ^ 1) for g in range(parts)])  1.56 us
    pallas_call x1, Pallas kernels, prepare(): pl.pallas_call(functools.partial(prepare_kernel, groups, members), out_sh...  1.45 us
    pallas_call x1, Pallas kernels, share_rows(): pl.pallas_call(share_kernel, out_shape=jax.ShapeDtypeStruct((depth // 2,...  1.03 us
    pallas_call x1, Pallas kernels, attend(): pl.pallas_call(functools.partial(attend_kernel, groups, dim), out_shape=j...  0.93 us
    pallas_call x2, Pallas kernels, project(): pl.pallas_call(functools.partial(project_kernel, members, places), out_sh...  0.88 us
  transfers between devices with their start and end apart: 17, of which 8 were waited for; matrix products, arithmetic and copies ran while one was open for 0% of the time, Pallas kernels for 8%

profile of v19, /device:TPU:0, one launch (start us, length us, event | category | flops | bytes accessed | tf_op | source)
XLA Modules:
  0.0 41.2 jit_solution(5638761444782861615)
XLA Ops:
  0.0 1.0 %shard_map.83 = bf16[48,3072]{1,0:T(8,128)(2,1)S(1)} custom-call(bf16[96,3072]{1,0:T(8,128)(2,1)} %refs_0_.5), custom_call_target="tpu_custom_call" | custom-call | bytes 589824 | tf_op jit(solution)/shard_map/pallas_call | solution.py:117
  1.0 3.0 %collective-permute-start.3 = (bf16[48,3072]{1,0:T(8,128)(2,1)S(1)}, bf16[48,3072]{1,0:T(8,128)(2,1)S(1)}, u32[]{:S(2)}, u32[]{:S(2)}) collective-permute-start(bf16[48,3072]{1,0:T(8,128)(2,1)S(1)} %shard_map.83), channel_id=1, source_target_pairs={{0,2},{1,3},{2,0},{3,1},{4,6},{5,7},{6,4},{7,5},{8,10},{9,11},{10,... | collective-permute-start | bytes 884744 | tf_op jit(solution)/shard_map/ppermute | solution.py:235
  4.1 0.0 copy-start
  4.1 1.5 %shard_map.82 = (bf16[24,384]{1,0:T(8,128)(2,1)S(1)}, bf16[24,768]{1,0:T(8,128)(2,1)S(1)}, bf16[24,1152]{1,0:T(8,128)(2,1)S(1)}, bf16[24,1152]{1,0:T(8,128)(2,1)S(1)}, bf16[24,1152]{1,0:T(8,128)(2,1)S(1)}) custom-call(bf16[24,1536]{1,0:T(8,128)(2,1)} %refs_0_.3, bf16[24,1536]{1,0:T(8,128)(2,1)} %refs_1_.1, bf16[24,1536]{1,0:T(8,128)(2,1)} %refs_2_.1, ...), custom_call_target="tpu_custom_call" | custom-call | flops 368640 | bytes 516096 | tf_op jit(solution)/shard_map/pallas_call | solution.py:81
  5.5 3.7 %collective-permute-start = (bf16[24,1152]{1,0:T(8,128)(2,1)S(1)}, bf16[24,1152]{1,0:T(8,128)(2,1)S(1)}, u32[]{:S(2)}, u32[]{:S(2)}) collective-permute-start(bf16[24,1152]{1,0:T(8,128)(2,1)S(1)} %get-tuple-element.23), channel_id=1, source_target_pairs={{0,12},{1,13},{2,14},{3,15},{4,8},{5,9},{6,10},{7,11},{8,4},{9,5},... | collective-permute-start | bytes 165896 | tf_op jit(solution)/shard_map/ppermute | solution.py:235
  9.2 0.0 collective-permute-start.2
  9.2 0.8 %collective-permute-start.1 = (bf16[24,1152]{1,0:T(8,128)(2,1)S(1)}, bf16[24,1152]{1,0:T(8,128)(2,1)S(1)}, u32[]{:S(2)}, u32[]{:S(2)}) collective-permute-start(bf16[24,1152]{1,0:T(8,128)(2,1)S(1)} %get-tuple-element.24), channel_id=1, source_target_pairs={{0,4},{1,5},{2,6},{3,7},{4,0},{5,1},{6,2},{7,3},{8,12},{9,13},{10,... | collective-permute-start | bytes 165896 | tf_op jit(solution)/shard_map/ppermute | solution.py:235
  10.0 2.2 %collective-permute-done.refs_0_ = bf16[24,1152]{1,0:T(8,128)(2,1)S(1)} collective-permute-done((bf16[24,1152]{1,0:T(8,128)(2,1)S(1)}, bf16[24,1152]{1,0:T(8,128)(2,1)S(1)}, u32[]{:S(2)}, u32[]{:S(2)}) %collective-permute-start) | collective-permute-done | bytes 55328 | tf_op jit(solution)/shard_map/ppermute | solution.py:235
  12.2 2.0 %collective-permute-done.2.refs_2_ = bf16[24,1152]{1,0:T(8,128)(2,1)S(1)} collective-permute-done((bf16[24,1152]{1,0:T(8,128)(2,1)S(1)}, bf16[24,1152]{1,0:T(8,128)(2,1)S(1)}, u32[]{:S(2)}, u32[]{:S(2)}) %collective-permute-start.2) | collective-permute-done | bytes 55328 | tf_op jit(solution)/shard_map/ppermute | solution.py:235
  14.3 0.0 collective-permute-done.1.refs_1_
  14.3 0.0 collective-permute-done.3.refs_2_
  14.3 0.0 copy-done
  14.3 0.1 collective-permute-start.7
  14.4 1.6 %collective-permute-start.8 = (bf16[48,3072]{1,0:T(8,128)(2,1)S(1)}, bf16[48,3072]{1,0:T(8,128)(2,1)S(1)}, u32[]{:S(2)}, u32[]{:S(2)}) collective-permute-start(bf16[48,3072]{1,0:T(8,128)(2,1)S(1)} %collective-permute-done.3.refs_2_), channel_id=1, source_target_pairs={{0,16},{16,0},{1,17},{17,1},{2,18},{18,2},{3,19},{19,3},{4,20},{20... | collective-permute-start | bytes 884744 | tf_op jit(solution)/shard_map/ppermute | solution.py:238
  15.9 0.5 %collective-permute-start.5 = (bf16[96,768]{1,0:T(8,128)(2,1)S(1)}, bf16[96,768]{1,0:T(8,128)(2,1)S(1)}, u32[]{:S(2)}, u32[]{:S(2)}) collective-permute-start(bf16[96,768]{1,0:T(8,128)(2,1)S(1)} %pad_maximum_fusion.refs_4_), channel_id=1, source_target_pairs={{0,2},{1,3},{2,0},{3,1},{4,6},{5,7},{6,4},{7,5},{8,10},{9,11},{10,... | collective-permute-start | bytes 442376 | tf_op jit(solution)/shard_map/ppermute | solution.py:235
  16.4 0.0 collective-permute-start.9
  16.5 0.5 %collective-permute-start.4 = (bf16[96,768]{1,0:T(8,128)(2,1)S(1)}, bf16[96,768]{1,0:T(8,128)(2,1)S(1)}, u32[]{:S(2)}, u32[]{:S(2)}) collective-permute-start(bf16[96,768]{1,0:T(8,128)(2,1)S(1)} %pad_maximum_fusion.refs_4_), channel_id=1, source_target_pairs={{0,1},{1,0},{2,3},{3,2},{4,5},{5,4},{6,7},{7,6},{8,9},{9,8},{10,11... | collective-permute-start | bytes 442376 | tf_op jit(solution)/shard_map/ppermute | solution.py:235
  17.0 4.9 %collective-permute-done.5.refs_6_ = bf16[96,768]{1,0:T(8,128)(2,1)S(1)} collective-permute-done((bf16[96,768]{1,0:T(8,128)(2,1)S(1)}, bf16[96,768]{1,0:T(8,128)(2,1)S(1)}, u32[]{:S(2)}, u32[]{:S(2)}) %collective-permute-start.5) | collective-permute-done | bytes 147488 | tf_op jit(solution)/shard_map/ppermute | solution.py:235
  21.9 0.0 collective-permute-start.6
  21.9 1.9 %collective-permute-done.8.refs_3_ = bf16[48,3072]{1,0:T(8,128)(2,1)S(1)} collective-permute-done((bf16[48,3072]{1,0:T(8,128)(2,1)S(1)}, bf16[48,3072]{1,0:T(8,128)(2,1)S(1)}, u32[]{:S(2)}, u32[]{:S(2)}) %collective-permute-start.8) | collective-permute-done | bytes 294944 | tf_op jit(solution)/shard_map/ppermute | solution.py:238
  23.8 0.1 collective-permute-start.10
  23.9 0.0 collective-permute-done.4.refs_5_
  23.9 0.0 collective-permute-done.6.refs_7_
  23.9 0.9 %shard_map.84.att = bf16[96,384]{1,0:T(8,128)(2,1)S(1)} custom-call(bf16[24,1152]{1,0:T(8,128)(2,1)S(1)} %collective-permute-done.refs_0_, bf16[24,1152]{1,0:T(8,128)(2,1)S(1)} %collective-permute-done.1.refs_1_, bf16[24,1152]{1,0:T(8,128)(2,1)S(1)} %collective-permute-done.2.refs_2_, bf16[24,384]{1,0:T(8,128)(2,1)S(1)} %get-tuple-element.26.refs_3_, ...), custom_call_target="tpu_custom_call" | custom-call | flops 56623104 | bytes 589824 | tf_op jit(solution)/shard_map/pallas_call | solution.py:160
  24.9 0.5 %collective-permute-start.13 = (bf16[48,1536]{1,0:T(8,128)(2,1)S(1)}, bf16[48,1536]{1,0:T(8,128)(2,1)S(1)}, u32[]{:S(2)}, u32[]{:S(2)}) collective-permute-start(bf16[48,1536]{1,0:T(8,128)(2,1)S(1)} %slice.27), channel_id=1, source_target_pairs={{0,1},{1,0},{2,3},{3,2},{4,5},{5,4},{6,7},{7,6},{8,9},{9,8},{10,11... | collective-permute-start | bytes 442376 | tf_op jit(solution)/shard_map/ppermute | solution.py:235
  25.4 0.0 collective-permute-done.9.refs_4_
  25.4 0.0 collective-permute-done.10.refs_5_
  25.4 0.0 collective-permute-done.7.refs_1_
  25.4 0.4 %shard_map.85 = (bf16[48,1536]{1,0:T(8,128)(2,1)S(1)}, f32[24,1536]{1,0:T(8,128)S(1)}, f32[24,1536]{1,0:T(8,128)S(1)}) custom-call(bf16[96,384]{1,0:T(8,128)(2,1)S(1)} %shard_map.84.att, bf16[96,3072]{1,0:T(8,128)(2,1)S(1)} %copy-done, bf16[96,3072]{1,0:T(8,128)(2,1)S(1)} %collective-permute-done.7.refs_1_, ...), custom_call_target="tpu_custom_call" | custom-call | flops 113246208 | bytes 1179648 | tf_op jit(solution)/shard_map/pallas_call | solution.py:203
  25.9 0.7 %collective-permute-start.11 = (bf16[48,1536]{1,0:T(8,128)(2,1)S(1)}, bf16[48,1536]{1,0:T(8,128)(2,1)S(1)}, u32[]{:S(2)}, u32[]{:S(2)}) collective-permute-start(bf16[48,1536]{1,0:T(8,128)(2,1)S(1)} %get-tuple-element.33), channel_id=1, source_target_pairs={{0,4},{1,5},{2,6},{3,7},{4,0},{5,1},{6,2},{7,3},{8,12},{9,13},{10,... | collective-permute-start | bytes 442376 | tf_op jit(solution)/shard_map/ppermute | solution.py:235
  26.6 0.0 collective-permute-done.13.refs_5_
  26.6 0.4 %shard_map.86 = (bf16[24,1536]{1,0:T(8,128)(2,1)S(1)}, bf16[24,1536]{1,0:T(8,128)(2,1)S(1)}, bf16[24,1536]{1,0:T(8,128)(2,1)S(1)}, f32[24,1536]{1,0:T(8,128)S(1)}) custom-call(bf16[96,384]{1,0:T(8,128)(2,1)S(1)} %shard_map.84.att, bf16[96,3072]{1,0:T(8,128)(2,1)S(1)} %copy-done, bf16[96,3072]{1,0:T(8,128)(2,1)S(1)} %collective-permute-done.7.refs_1_, ...), custom_call_target="tpu_custom_call" | custom-call | flops 113246208 | bytes 1179648 | tf_op jit(solution)/shard_map/pallas_call | solution.py:203
  27.1 0.0 copy-start.1
  27.1 2.9 %collective-permute-start.14 = (bf16[24,1536]{1,0:T(8,128)(2,1)S(1)}, bf16[24,1536]{1,0:T(8,128)(2,1)S(1)}, u32[]{:S(2)}, u32[]{:S(2)}) collective-permute-start(bf16[24,1536]{1,0:T(8,128)(2,1)S(1)} %get-tuple-element.38), channel_id=1, source_target_pairs={{0,12},{1,13},{2,14},{3,15},{4,8},{5,9},{6,10},{7,11},{8,4},{9,5},... | collective-permute-start | bytes 221192 | tf_op jit(solution)/shard_map/ppermute | solution.py:235
  29.9 0.0 collective-permute-start.15
  30.0 1.6 %collective-permute-start.16 = (bf16[24,1536]{1,0:T(8,128)(2,1)S(1)}, bf16[24,1536]{1,0:T(8,128)(2,1)S(1)}, u32[]{:S(2)}, u32[]{:S(2)}) collective-permute-start(bf16[24,1536]{1,0:T(8,128)(2,1)S(1)} %get-tuple-element.40), channel_id=1, source_target_pairs={{0,4},{1,5},{2,6},{3,7},{4,0},{5,1},{6,2},{7,3},{8,12},{9,13},{10,... | collective-permute-start | bytes 221192 | tf_op jit(solution)/shard_map/ppermute | solution.py:235
  31.5 0.2 collective-permute-done.11
  31.8 3.0 %collective-permute-start.12 = (bf16[24,1536]{1,0:T(8,128)(2,1)S(1)}, bf16[24,1536]{1,0:T(8,128)(2,1)S(1)}, u32[]{:S(2)}, u32[]{:S(2)}) collective-permute-start(bf16[24,1536]{1,0:T(8,128)(2,1)S(1)} %add_convert_fusion), channel_id=1, source_target_pairs={{0,8},{1,9},{2,10},{3,11},{4,12},{5,13},{6,14},{7,15},{8,0},{9,1},... | collective-permute-start | bytes 221192 | tf_op jit(solution)/shard_map/ppermute | solution.py:235
  34.8 1.0 %collective-permute-done.14 = bf16[24,1536]{1,0:T(8,128)(2,1)S(1)} collective-permute-done((bf16[24,1536]{1,0:T(8,128)(2,1)S(1)}, bf16[24,1536]{1,0:T(8,128)(2,1)S(1)}, u32[]{:S(2)}, u32[]{:S(2)}) %collective-permute-start.14) | collective-permute-done | bytes 73760 | tf_op jit(solution)/shard_map/ppermute | solution.py:235
  35.7 3.9 %collective-permute-done.15 = bf16[24,1536]{1,0:T(8,128)(2,1)S(1)} collective-permute-done((bf16[24,1536]{1,0:T(8,128)(2,1)S(1)}, bf16[24,1536]{1,0:T(8,128)(2,1)S(1)}, u32[]{:S(2)}, u32[]{:S(2)}) %collective-permute-start.15) | collective-permute-done | bytes 73760 | tf_op jit(solution)/shard_map/ppermute | solution.py:235
  39.6 0.0 collective-permute-done.16
  39.6 0.9 %collective-permute-done.12 = bf16[24,1536]{1,0:T(8,128)(2,1)S(1)} collective-permute-done((bf16[24,1536]{1,0:T(8,128)(2,1)S(1)}, bf16[24,1536]{1,0:T(8,128)(2,1)S(1)}, u32[]{:S(2)}, u32[]{:S(2)}) %collective-permute-start.12) | collective-permute-done | bytes 73760 | tf_op jit(solution)/shard_map/ppermute | solution.py:235
  40.5 0.0 copy-done.1
  40.5 0.7 %fusion = bf16[24,3072]{1,0:T(8,128)(2,1)} fusion(f32[24,1536]{1,0:T(8,128)S(1)} %convert_add_fusion, f32[24,1536]{1,0:T(8,128)S(1)} %convert_add_fusion.1, f32[3072]{0:T(1024)S(1)} %copy-done.1), kind=kLoop, calls=%fused_computation.1 | loop fusion | flops 221184 | bytes 454656 | tf_op jit(solution)/shard_map/convert_element_type | solution.py:301
  (9 shorter events, 0.1 us)
Async XLA Ops:
  1.0 13.3 %collective-permute-start.3 = (bf16[48,3072]{1,0:T(8,128)(2,1)S(1)}, bf16[48,3072]{1,0:T(8,128)(2,1)S(1)}, u32[]{:S(2)}, u32[]{:S(2)}) collective-permute-start(bf16[48,3072]{1,0:T(8,128)(2,1)S(1)} %shard_map.83), channel_id=1, source_target_pairs={{0,2},{1,3},{2,0},{3,1},{4,6},{5,7},{6,4},{7,5},{8,10},{9,11},{10,... | collective-permute-start | bytes 884744 | tf_op jit(solution)/shard_map/ppermute | solution.py:235
  4.1 10.2 %copy-start = (bf16[96,3072]{1,0:T(8,128)(2,1)S(1)}, bf16[96,3072]{1,0:T(8,128)(2,1)}, u32[]{:S(2)}) copy-start(bf16[96,3072]{1,0:T(8,128)(2,1)} %refs_0_.5) | copy-start | bytes 1769476
  5.5 6.7 %collective-permute-start = (bf16[24,1152]{1,0:T(8,128)(2,1)S(1)}, bf16[24,1152]{1,0:T(8,128)(2,1)S(1)}, u32[]{:S(2)}, u32[]{:S(2)}) collective-permute-start(bf16[24,1152]{1,0:T(8,128)(2,1)S(1)} %get-tuple-element.23), channel_id=1, source_target_pairs={{0,12},{1,13},{2,14},{3,15},{4,8},{5,9},{6,10},{7,11},{8,4},{9,5},... | collective-permute-start | bytes 165896 | tf_op jit(solution)/shard_map/ppermute | solution.py:235
  9.2 5.1 %collective-permute-start.2 = (bf16[24,1152]{1,0:T(8,128)(2,1)S(1)}, bf16[24,1152]{1,0:T(8,128)(2,1)S(1)}, u32[]{:S(2)}, u32[]{:S(2)}) collective-permute-start(bf16[24,1152]{1,0:T(8,128)(2,1)S(1)} %get-tuple-element.25), channel_id=1, source_target_pairs={{0,8},{1,9},{2,10},{3,11},{4,12},{5,13},{6,14},{7,15},{8,0},{9,1},... | collective-permute-start | bytes 165896 | tf_op jit(solution)/shard_map/ppermute | solution.py:235
  9.2 5.1 %collective-permute-start.1 = (bf16[24,1152]{1,0:T(8,128)(2,1)S(1)}, bf16[24,1152]{1,0:T(8,128)(2,1)S(1)}, u32[]{:S(2)}, u32[]{:S(2)}) collective-permute-start(bf16[24,1152]{1,0:T(8,128)(2,1)S(1)} %get-tuple-element.24), channel_id=1, source_target_pairs={{0,4},{1,5},{2,6},{3,7},{4,0},{5,1},{6,2},{7,3},{8,12},{9,13},{10,... | collective-permute-start | bytes 165896 | tf_op jit(solution)/shard_map/ppermute | solution.py:235
  14.3 11.1 %collective-permute-start.7 = (bf16[96,3072]{1,0:T(8,128)(2,1)S(1)}, bf16[96,3072]{1,0:T(8,128)(2,1)S(1)}, u32[]{:S(2)}, u32[]{:S(2)}) collective-permute-start(bf16[96,3072]{1,0:T(8,128)(2,1)S(1)} %copy-done), channel_id=1, source_target_pairs={{0,1},{1,0},{2,3},{3,2},{4,5},{5,4},{6,7},{7,6},{8,9},{9,8},{10,11... | collective-permute-start | bytes 1769480 | tf_op jit(solution)/shard_map/ppermute | solution.py:235
  14.4 9.4 %collective-permute-start.8 = (bf16[48,3072]{1,0:T(8,128)(2,1)S(1)}, bf16[48,3072]{1,0:T(8,128)(2,1)S(1)}, u32[]{:S(2)}, u32[]{:S(2)}) collective-permute-start(bf16[48,3072]{1,0:T(8,128)(2,1)S(1)} %collective-permute-done.3.refs_2_), channel_id=1, source_target_pairs={{0,16},{16,0},{1,17},{17,1},{2,18},{18,2},{3,19},{19,3},{4,20},{20... | collective-permute-start | bytes 884744 | tf_op jit(solution)/shard_map/ppermute | solution.py:238
  15.9 5.9 %collective-permute-start.5 = (bf16[96,768]{1,0:T(8,128)(2,1)S(1)}, bf16[96,768]{1,0:T(8,128)(2,1)S(1)}, u32[]{:S(2)}, u32[]{:S(2)}) collective-permute-start(bf16[96,768]{1,0:T(8,128)(2,1)S(1)} %pad_maximum_fusion.refs_4_), channel_id=1, source_target_pairs={{0,2},{1,3},{2,0},{3,1},{4,6},{5,7},{6,4},{7,5},{8,10},{9,11},{10,... | collective-permute-start | bytes 442376 | tf_op jit(solution)/shard_map/ppermute | solution.py:235
  16.4 9.0 %collective-permute-start.9 = (bf16[48,3072]{1,0:T(8,128)(2,1)S(1)}, bf16[48,3072]{1,0:T(8,128)(2,1)S(1)}, u32[]{:S(2)}, u32[]{:S(2)}) collective-permute-start(bf16[48,3072]{1,0:T(8,128)(2,1)S(1)} %collective-permute-done.3.refs_2_), channel_id=1, source_target_pairs={{0,1},{1,0},{2,3},{3,2},{4,5},{5,4},{6,7},{7,6},{8,9},{9,8},{10,11... | collective-permute-start | bytes 884744 | tf_op jit(solution)/shard_map/ppermute | solution.py:235
  16.5 7.5 %collective-permute-start.4 = (bf16[96,768]{1,0:T(8,128)(2,1)S(1)}, bf16[96,768]{1,0:T(8,128)(2,1)S(1)}, u32[]{:S(2)}, u32[]{:S(2)}) collective-permute-start(bf16[96,768]{1,0:T(8,128)(2,1)S(1)} %pad_maximum_fusion.refs_4_), channel_id=1, source_target_pairs={{0,1},{1,0},{2,3},{3,2},{4,5},{5,4},{6,7},{7,6},{8,9},{9,8},{10,11... | collective-permute-start | bytes 442376 | tf_op jit(solution)/shard_map/ppermute | solution.py:235
  21.9 2.1 %collective-permute-start.6 = (bf16[96,768]{1,0:T(8,128)(2,1)S(1)}, bf16[96,768]{1,0:T(8,128)(2,1)S(1)}, u32[]{:S(2)}, u32[]{:S(2)}) collective-permute-start(bf16[96,768]{1,0:T(8,128)(2,1)S(1)} %collective-permute-done.5.refs_6_), channel_id=1, source_target_pairs={{0,1},{1,0},{2,3},{3,2},{4,5},{5,4},{6,7},{7,6},{8,9},{9,8},{10,11... | collective-permute-start | bytes 442376 | tf_op jit(solution)/shard_map/ppermute | solution.py:235
  23.8 1.6 %collective-permute-start.10 = (bf16[48,1536]{1,0:T(8,128)(2,1)S(1)}, bf16[48,1536]{1,0:T(8,128)(2,1)S(1)}, u32[]{:S(2)}, u32[]{:S(2)}) collective-permute-start(bf16[48,1536]{1,0:T(8,128)(2,1)S(1)} %slice.24), channel_id=1, source_target_pairs={{0,1},{1,0},{2,3},{3,2},{4,5},{5,4},{6,7},{7,6},{8,9},{9,8},{10,11... | collective-permute-start | bytes 442376 | tf_op jit(solution)/shard_map/ppermute | solution.py:235
  24.9 1.7 %collective-permute-start.13 = (bf16[48,1536]{1,0:T(8,128)(2,1)S(1)}, bf16[48,1536]{1,0:T(8,128)(2,1)S(1)}, u32[]{:S(2)}, u32[]{:S(2)}) collective-permute-start(bf16[48,1536]{1,0:T(8,128)(2,1)S(1)} %slice.27), channel_id=1, source_target_pairs={{0,1},{1,0},{2,3},{3,2},{4,5},{5,4},{6,7},{7,6},{8,9},{9,8},{10,11... | collective-permute-start | bytes 442376 | tf_op jit(solution)/shard_map/ppermute | solution.py:235
  25.9 5.9 %collective-permute-start.11 = (bf16[48,1536]{1,0:T(8,128)(2,1)S(1)}, bf16[48,1536]{1,0:T(8,128)(2,1)S(1)}, u32[]{:S(2)}, u32[]{:S(2)}) collective-permute-start(bf16[48,1536]{1,0:T(8,128)(2,1)S(1)} %get-tuple-element.33), channel_id=1, source_target_pairs={{0,4},{1,5},{2,6},{3,7},{4,0},{5,1},{6,2},{7,3},{8,12},{9,13},{10,... | collective-permute-start | bytes 442376 | tf_op jit(solution)/shard_map/ppermute | solution.py:235
  27.1 13.5 %copy-start.1 = (f32[3072]{0:T(1024)S(1)}, f32[3072]{0:T(1024)}, u32[]{:S(2)}) copy-start(f32[3072]{0:T(1024)} %param.15) | copy-start | bytes 36868
  27.1 8.6 %collective-permute-start.14 = (bf16[24,1536]{1,0:T(8,128)(2,1)S(1)}, bf16[24,1536]{1,0:T(8,128)(2,1)S(1)}, u32[]{:S(2)}, u32[]{:S(2)}) collective-permute-start(bf16[24,1536]{1,0:T(8,128)(2,1)S(1)} %get-tuple-element.38), channel_id=1, source_target_pairs={{0,12},{1,13},{2,14},{3,15},{4,8},{5,9},{6,10},{7,11},{8,4},{9,5},... | collective-permute-start | bytes 221192 | tf_op jit(solution)/shard_map/ppermute | solution.py:235
  29.9 9.6 %collective-permute-start.15 = (bf16[24,1536]{1,0:T(8,128)(2,1)S(1)}, bf16[24,1536]{1,0:T(8,128)(2,1)S(1)}, u32[]{:S(2)}, u32[]{:S(2)}) collective-permute-start(bf16[24,1536]{1,0:T(8,128)(2,1)S(1)} %get-tuple-element.39), channel_id=1, source_target_pairs={{0,8},{1,9},{2,10},{3,11},{4,12},{5,13},{6,14},{7,15},{8,0},{9,1},... | collective-permute-start | bytes 221192 | tf_op jit(solution)/shard_map/ppermute | solution.py:235
  30.0 9.6 %collective-permute-start.16 = (bf16[24,1536]{1,0:T(8,128)(2,1)S(1)}, bf16[24,1536]{1,0:T(8,128)(2,1)S(1)}, u32[]{:S(2)}, u32[]{:S(2)}) collective-permute-start(bf16[24,1536]{1,0:T(8,128)(2,1)S(1)} %get-tuple-element.40), channel_id=1, source_target_pairs={{0,4},{1,5},{2,6},{3,7},{4,0},{5,1},{6,2},{7,3},{8,12},{9,13},{10,... | collective-permute-start | bytes 221192 | tf_op jit(solution)/shard_map/ppermute | solution.py:235
  31.8 8.7 %collective-permute-start.12 = (bf16[24,1536]{1,0:T(8,128)(2,1)S(1)}, bf16[24,1536]{1,0:T(8,128)(2,1)S(1)}, u32[]{:S(2)}, u32[]{:S(2)}) collective-permute-start(bf16[24,1536]{1,0:T(8,128)(2,1)S(1)} %add_convert_fusion), channel_id=1, source_target_pairs={{0,8},{1,9},{2,10},{3,11},{4,12},{5,13},{6,14},{7,15},{8,0},{9,1},... | collective-permute-start | bytes 221192 | tf_op jit(solution)/shard_map/ppermute | solution.py:235
